TPU v7x, 32 devices: a whole 2x2x4 slice. The times are simulated.
32 devices in a mesh: dp: 4 (over z), fsdp: 8 (over y, x, core).
Axes of the slice: x: 2, y: 2, z: 4, core: 2. Of those that a mesh axis runs over, the one named last changes fastest.
Arguments:
- layer_input: bfloat16 [4, 1536, 2048], P('dp', 'fsdp'), may hold values from -6 to 6
- output_grad: bfloat16 [4, 1536, 2048], P('dp', 'fsdp'), may hold values from -6 to 6
- layer_keep: int32 [4], P('dp'), may hold values 0 or 1
- group_ids: int32 [4], P('dp'), may hold values from 0 to 1
- exit_scale: float32 [2], replicated, may hold values from 0.5 to 2
- doc_lengths: int32 [4, 4], P('dp'), may hold values from 1 to 1392, 1536 in all within a row
- attention_gain: bfloat16 [2048], P(('dp', 'fsdp')), may hold values from 0.25 to 1.75
- query_weight: bfloat16 [2048, 2048], P(('dp', 'fsdp')), may hold values from -0.125 to 0.125
- key_weight: bfloat16 [2048, 512], P(('dp', 'fsdp')), may hold values from -0.125 to 0.125
- value_weight: bfloat16 [2048, 512], P(('dp', 'fsdp')), may hold values from -0.125 to 0.125
- output_weight: bfloat16 [2048, 2048], P(('dp', 'fsdp')), may hold values from -4 to 4
- feedforward_gain: bfloat16 [2048], P(('dp', 'fsdp')), may hold values from 0.25 to 1.75
- gate_weight: bfloat16 [2048, 5632], P('fsdp', 'dp'), may hold values from -0.125 to 0.125
- up_weight: bfloat16 [2048, 5632], P('fsdp', 'dp'), may hold values from -0.125 to 0.125
- down_weight: bfloat16 [5632, 2048], P(('dp', 'fsdp')), may hold values from -0.078125 to 0.078125
Outputs:
- layer_output: bfloat16 [4, 1536, 2048], P('dp', 'fsdp')
- input_gradient: float32 [4, 1536, 2048], P('dp', 'fsdp')
- attention_gain_gradient: float32 [2048], P(('dp', 'fsdp'))
- query_gradient: float32 [2048, 2048], P(('dp', 'fsdp'))
- key_gradient: float32 [2048, 512], P(('dp', 'fsdp'))
- value_gradient: float32 [2048, 512], P(('dp', 'fsdp'))
- output_gradient: float32 [2048, 2048], P(('dp', 'fsdp'))
- feedforward_gain_gradient: float32 [2048], P(('dp', 'fsdp'))
- gate_gradient: float32 [2048, 5632], P('fsdp', 'dp')
- up_gradient: float32 [2048, 5632], P('fsdp', 'dp')
- down_gradient: float32 [5632, 2048], P(('dp', 'fsdp'))
Inputs may be any that keep to these rules, and one draw needn't show every extreme that they name: `layer_keep`: 1 applies the layer to the sequence, 0 skips it. `doc_lengths`: each row sums to 1536; its longest document has exactly 1392 tokens.
All inputs are finite; a program needn't handle non-finite values. No bound on the sum of `layer_keep` on one device may be relied on, other than what follows from the above.
Results may differ from a plain program's by a relative error of at most 0.019.
Values may be sent and summed in bfloat16 or wider, within the bound.
No kernel may reach another device: no remote copies, remote signals or barrier semaphores. Data moves between devices by JAX's collectives and lax.ppermute only.
A program may use at most 512 MiB of HBM per device.

v0:
```python
import math

import jax
import jax.numpy as jnp
from jax import lax
from jax.sharding import PartitionSpec as P

HEADS = 16
KV_HEADS = 4
HEAD_DIM = 128


norm_eps = 1e-05
rope_base = 10000.0
mask_fill = -1e30


def dot_plain(left, right):
    return jnp.dot(left, right, preferred_element_type=jnp.float32)


def dot_right_t(left, right):
    return lax.dot_general(
        left, right, (((1,), (1,)), ((), ())), preferred_element_type=jnp.float32
    )


def dot_left_t(left, right):
    return lax.dot_general(
        left, right, (((0,), (0,)), ((), ())), preferred_element_type=jnp.float32
    )


def rotary_tables(positions):
    half_dim = HEAD_DIM // 2
    frequency = rope_base ** (-(2.0 * jnp.arange(half_dim, dtype=jnp.float32)) / HEAD_DIM)
    angles = positions.astype(jnp.float32)[:, None] * frequency[None, :]
    return (jnp.cos(angles)[:, None, :], jnp.sin(angles)[:, None, :])


def rotate(vectors, cosine, sine_part):
    half_dim = vectors.shape[-1] // 2
    lower_half = vectors[..., :half_dim]
    upper_half = vectors[..., half_dim:]
    return jnp.concatenate(
        [
            lower_half * cosine - upper_half * sine_part,
            upper_half * cosine + lower_half * sine_part,
        ],
        -1,
    )


def rms_scale(rows):
    return lax.rsqrt(jnp.mean(rows * rows, -1, keepdims=True) + norm_eps)


def norm_back(grad_normed, rows, inv_rms, gain):
    weighted = grad_normed * gain.astype(jnp.float32)
    gain_grad = jnp.sum(grad_normed * rows * inv_rms, 0)
    grad_rows = inv_rms * weighted - rows * inv_rms**3 * jnp.mean(
        weighted * rows, -1, keepdims=True
    )
    return (gain_grad, grad_rows)


def allowed_mask(query_pos, query_doc, key_pos, key_doc):
    return (key_pos[None, :] <= query_pos[:, None]) & (key_doc[None, :] == query_doc[:, None])


def block_scores(queries, key_block, allowed):
    scores = jnp.einsum(
        "tkgd,skd->kgts", queries, key_block, preferred_element_type=jnp.float32
    ) * (1.0 / math.sqrt(HEAD_DIM))
    return jnp.where(allowed[None, None], scores, mask_fill)


def log_normalizer(queries, layout):
    query_pos, query_doc, key_blocks, value_blocks, key_pos_blocks, key_doc_blocks = layout
    shape_rows = (queries.shape[1], queries.shape[2], queries.shape[0])
    initial = (jnp.full(shape_rows, mask_fill, jnp.float32), jnp.zeros(shape_rows, jnp.float32))

    def advance(carry, sliced):
        run_max, run_sum = carry
        key_block, key_pos, key_doc = sliced
        allowed = allowed_mask(query_pos, query_doc, key_pos, key_doc)
        scores = block_scores(queries, key_block, allowed)
        new_max = jnp.maximum(run_max, jnp.max(scores, -1))
        expo = jnp.where(allowed[None, None], jnp.exp(scores - new_max[..., None]), 0.0)
        run_sum = run_sum * jnp.exp(run_max - new_max) + jnp.sum(expo, -1)
        return ((new_max, run_sum), None)

    (run_max, run_sum), _ = lax.scan(advance, initial, (key_blocks, key_pos_blocks, key_doc_blocks))
    return run_max + jnp.log(run_sum)


def attend_values(queries, layout, normalizer):
    query_pos, query_doc, key_blocks, value_blocks, key_pos_blocks, key_doc_blocks = layout
    initial = jnp.zeros(queries.shape, jnp.float32)

    def advance(carry, sliced):
        key_block, value_block, key_pos, key_doc = sliced
        allowed = allowed_mask(query_pos, query_doc, key_pos, key_doc)
        scores = block_scores(queries, key_block, allowed)
        probs_low = jnp.where(
            allowed[None, None], jnp.exp(scores - normalizer[..., None]), 0.0
        ).astype(jnp.bfloat16)
        return (
            carry
            + jnp.einsum(
                "kgts,skd->tkgd", probs_low, value_block, preferred_element_type=jnp.float32
            ),
            None,
        )

    summed, _ = lax.scan(
        advance, initial, (key_blocks, value_blocks, key_pos_blocks, key_doc_blocks)
    )
    return summed


def attend_back(queries, layout, normalizer, grad_out_low, delta):
    query_pos, query_doc, key_blocks, value_blocks, key_pos_blocks, key_doc_blocks = layout
    initial = jnp.zeros(queries.shape, jnp.float32)

    def advance(carry, sliced):
        key_block, value_block, key_pos, key_doc = sliced
        allowed = allowed_mask(query_pos, query_doc, key_pos, key_doc)
        scores = block_scores(queries, key_block, allowed)
        probs = jnp.where(allowed[None, None], jnp.exp(scores - normalizer[..., None]), 0.0)
        probs_low = probs.astype(jnp.bfloat16)
        grad_prob = jnp.einsum(
            "tkgd,skd->kgts", grad_out_low, value_block, preferred_element_type=jnp.float32
        )
        grad_score = (probs * (grad_prob - delta[..., None])).astype(jnp.bfloat16)
        carry = carry + jnp.einsum(
            "kgts,skd->tkgd", grad_score, key_block, preferred_element_type=jnp.float32
        )
        key_part = jnp.einsum(
            "kgts,tkgd->skd", grad_score, queries, preferred_element_type=jnp.float32
        )
        value_part = jnp.einsum(
            "kgts,tkgd->skd", probs_low, grad_out_low, preferred_element_type=jnp.float32
        )
        return (carry, (key_part, value_part))

    query_acc, (key_parts, value_parts) = lax.scan(
        advance, initial, (key_blocks, value_blocks, key_pos_blocks, key_doc_blocks)
    )
    seq_length = key_parts.shape[0] * key_parts.shape[1]
    return (
        query_acc,
        key_parts.reshape(seq_length, KV_HEADS * HEAD_DIM),
        value_parts.reshape(seq_length, KV_HEADS * HEAD_DIM),
    )


def front(rows, attention_set, cosine, sine_part):
    attention_gain, query_weight, key_weight, value_weight = attention_set
    tokens = rows.shape[0]
    inv_first = rms_scale(rows)
    normed = (rows * inv_first * attention_gain.astype(jnp.float32)).astype(jnp.bfloat16)
    query_raw = dot_plain(normed, query_weight).reshape(tokens, HEADS, HEAD_DIM)
    query_rot = (
        rotate(query_raw, cosine, sine_part)
        .astype(jnp.bfloat16)
        .reshape(tokens, KV_HEADS, HEADS // KV_HEADS, HEAD_DIM)
    )
    key_raw = dot_plain(normed, key_weight).reshape(tokens, KV_HEADS, HEAD_DIM)
    key_rot = (
        rotate(key_raw, cosine, sine_part).astype(jnp.bfloat16).reshape(tokens, KV_HEADS * HEAD_DIM)
    )
    value_low = dot_plain(normed, value_weight).astype(jnp.bfloat16)
    return (inv_first, normed, query_rot, key_rot, value_low)


def make_layout(query_pos, query_doc, all_doc, keys_all, values_all):
    seq_length = keys_all.shape[0]
    block_rows = math.gcd(seq_length, 512)
    count = seq_length // block_rows
    key_blocks = keys_all.reshape(count, block_rows, KV_HEADS, HEAD_DIM)
    value_blocks = values_all.reshape(count, block_rows, KV_HEADS, HEAD_DIM)
    key_pos_blocks = jnp.arange(seq_length, dtype=jnp.int32).reshape(count, block_rows)
    key_doc_blocks = all_doc.reshape(count, block_rows)
    return (query_pos, query_doc, key_blocks, value_blocks, key_pos_blocks, key_doc_blocks)


def per_device(
    layer_input,
    output_grad,
    layer_keep,
    group_ids,
    exit_scale,
    doc_lengths,
    attention_gain,
    query_weight,
    key_weight,
    value_weight,
    output_weight,
    feedforward_gain,
    gate_weight,
    up_weight,
    down_weight,
):
    tokens = layer_input.shape[1]
    rows = layer_input[0].astype(jnp.float32)
    seq_length = tokens * lax.axis_size("fsdp")
    all_pos = jnp.arange(seq_length, dtype=jnp.int32)
    first_row = lax.axis_index("fsdp") * tokens
    query_pos = first_row + jnp.arange(tokens, dtype=jnp.int32)
    ends = jnp.cumsum(doc_lengths[0])
    all_doc = jnp.sum((all_pos[:, None] >= ends[None, :]).astype(jnp.int32), 1)
    query_doc = lax.dynamic_slice_in_dim(all_doc, first_row, tokens)
    cosine, sine_part = rotary_tables(query_pos)
    keep = layer_keep[0].astype(jnp.float32)
    gathered = (
        lax.all_gather(attention_gain, ("dp", "fsdp"), axis=0, tiled=True),
        lax.all_gather(feedforward_gain, ("dp", "fsdp"), axis=0, tiled=True),
        lax.all_gather(query_weight, ("dp", "fsdp"), axis=0, tiled=True),
        lax.all_gather(key_weight, ("dp", "fsdp"), axis=0, tiled=True),
        lax.all_gather(value_weight, ("dp", "fsdp"), axis=0, tiled=True),
        lax.all_gather(output_weight, ("dp", "fsdp"), axis=0, tiled=True),
    )
    gain_first, gain_second, query_full, key_full, value_full, output_full = gathered
    feed_block = (
        lax.all_gather(gate_weight, "fsdp", axis=0, tiled=True),
        lax.all_gather(up_weight, "fsdp", axis=0, tiled=True),
        lax.all_gather(down_weight, "fsdp", axis=0, tiled=True),
    )
    gate_use, up_use = (
        lax.all_gather(feed_block[0], "dp", axis=1, tiled=True),
        lax.all_gather(feed_block[1], "dp", axis=1, tiled=True),
    )
    down_use = lax.all_gather(feed_block[2], "dp", axis=0, tiled=True)
    front_parts = front(rows, (gain_first, query_full, key_full, value_full), cosine, sine_part)
    inv_first, normed, query_rot, key_rot, value_low = front_parts
    keys_all, values_all = (
        lax.all_gather(key_rot, "fsdp", axis=0, tiled=True),
        lax.all_gather(value_low, "fsdp", axis=0, tiled=True),
    )
    layout = make_layout(query_pos, query_doc, all_doc, keys_all, values_all)
    normalizer = log_normalizer(query_rot, layout)
    attended = attend_values(query_rot, layout, normalizer)
    attended_low = attended.reshape(tokens, HEADS * HEAD_DIM).astype(jnp.bfloat16)
    branch_attention = dot_plain(attended_low, output_full)
    middle = rows + branch_attention
    inv_second = rms_scale(middle)
    normed_second = (middle * inv_second * gain_second.astype(jnp.float32)).astype(jnp.bfloat16)
    gate_pre = dot_plain(normed_second, gate_use)
    upward = dot_plain(normed_second, up_use)
    sigmoid_gate = 1.0 / (1.0 + jnp.exp(-gate_pre))
    silu_gate = gate_pre * sigmoid_gate
    hidden_low = (silu_gate * upward).astype(jnp.bfloat16)
    branch_feed = dot_plain(hidden_low, down_use)
    output = (rows + keep * (branch_attention + branch_feed)).astype(jnp.bfloat16)
    picked = jnp.sum(
        jnp.where(jnp.arange(exit_scale.shape[0], dtype=jnp.int32) == group_ids[0], exit_scale, 0.0)
    )
    cotangent = output_grad[0].astype(jnp.float32) * picked
    direct = keep * cotangent
    direct_low = direct.astype(jnp.bfloat16)
    grad_hidden = dot_right_t(direct_low, down_use)
    down_term = dot_left_t(hidden_low, direct_low)
    grad_gate_low = (
        grad_hidden * upward * sigmoid_gate * (1.0 + gate_pre * (1.0 - sigmoid_gate))
    ).astype(jnp.bfloat16)
    grad_up_low = (grad_hidden * silu_gate).astype(jnp.bfloat16)
    normed_term = dot_right_t(grad_gate_low, gate_use) + dot_right_t(grad_up_low, up_use)
    gate_term = dot_left_t(normed_second, grad_gate_low)
    up_term = dot_left_t(normed_second, grad_up_low)
    gate_part, up_part = (
        lax.psum_scatter(
            gate_term.astype(jnp.bfloat16), "dp", scatter_dimension=1, tiled=True
        ).astype(jnp.float32),
        lax.psum_scatter(
            up_term.astype(jnp.bfloat16), "dp", scatter_dimension=1, tiled=True
        ).astype(jnp.float32),
    )
    down_part = lax.psum_scatter(
        down_term.astype(jnp.bfloat16), "dp", scatter_dimension=0, tiled=True
    )
    feed_grads = (
        lax.psum_scatter(
            gate_part.astype(jnp.bfloat16), "fsdp", scatter_dimension=0, tiled=True
        ).astype(jnp.float32),
        lax.psum_scatter(
            up_part.astype(jnp.bfloat16), "fsdp", scatter_dimension=0, tiled=True
        ).astype(jnp.float32),
        lax.psum_scatter(down_part, "fsdp", scatter_dimension=0, tiled=True).astype(jnp.float32),
    )
    second_gain_grad, grad_middle = norm_back(normed_term, middle, inv_second, gain_second)
    grad_branch_low = (direct + grad_middle).astype(jnp.bfloat16)
    grad_attended_low = dot_right_t(grad_branch_low, output_full).astype(jnp.bfloat16)
    output_grad_weight = dot_left_t(attended_low, grad_branch_low)
    grad_heads = grad_attended_low.reshape(attended.shape)
    delta = jnp.transpose(jnp.sum(grad_heads.astype(jnp.float32) * attended, -1), (1, 2, 0))
    query_acc, key_grad_all, value_grad_all = attend_back(
        query_rot, layout, normalizer, grad_heads, delta
    )
    key_grad_mine, value_grad_mine = (
        lax.psum_scatter(
            key_grad_all.astype(jnp.bfloat16), "fsdp", scatter_dimension=0, tiled=True
        ).astype(jnp.float32),
        lax.psum_scatter(
            value_grad_all.astype(jnp.bfloat16), "fsdp", scatter_dimension=0, tiled=True
        ).astype(jnp.float32),
    )
    score_scale = 1.0 / math.sqrt(HEAD_DIM)
    grad_query_low = (
        rotate((query_acc * score_scale).reshape(tokens, HEADS, HEAD_DIM), cosine, -sine_part)
        .astype(jnp.bfloat16)
        .reshape(tokens, HEADS * HEAD_DIM)
    )
    grad_key_low = (
        rotate(
            (key_grad_mine * score_scale).reshape(tokens, KV_HEADS, HEAD_DIM), cosine, -sine_part
        )
        .astype(jnp.bfloat16)
        .reshape(tokens, KV_HEADS * HEAD_DIM)
    )
    grad_value_low = value_grad_mine.astype(jnp.bfloat16)
    grad_normed = (
        dot_right_t(grad_query_low, query_full)
        + dot_right_t(grad_key_low, key_full)
        + dot_right_t(grad_value_low, value_full)
    )
    query_grad = dot_left_t(normed, grad_query_low)
    key_grad = dot_left_t(normed, grad_key_low)
    value_grad = dot_left_t(normed, grad_value_low)
    first_gain_grad, grad_rows = norm_back(grad_normed, rows, inv_first, gain_first)
    input_grad = cotangent + grad_middle + grad_rows
    attention_grads = (
        lax.psum_scatter(first_gain_grad, ("dp", "fsdp"), scatter_dimension=0, tiled=True),
        lax.psum_scatter(query_grad, ("dp", "fsdp"), scatter_dimension=0, tiled=True),
        lax.psum_scatter(key_grad, ("dp", "fsdp"), scatter_dimension=0, tiled=True),
        lax.psum_scatter(value_grad, ("dp", "fsdp"), scatter_dimension=0, tiled=True),
        lax.psum_scatter(output_grad_weight, ("dp", "fsdp"), scatter_dimension=0, tiled=True),
        lax.psum_scatter(second_gain_grad, ("dp", "fsdp"), scatter_dimension=0, tiled=True),
    )
    return (
        output[None],
        input_grad[None],
        attention_grads[0],
        attention_grads[1],
        attention_grads[2],
        attention_grads[3],
        attention_grads[4],
        attention_grads[5],
        feed_grads[0],
        feed_grads[1],
        feed_grads[2],
    )


def solution(mesh):
    placed = (
        P("dp", "fsdp", None),
        P("dp", "fsdp", None),
        P("dp"),
        P("dp"),
        P(),
        P("dp", None),
        P(("dp", "fsdp")),
        P(("dp", "fsdp"), None),
        P(("dp", "fsdp"), None),
        P(("dp", "fsdp"), None),
        P(("dp", "fsdp"), None),
        P(("dp", "fsdp")),
        P("fsdp", "dp"),
        P("fsdp", "dp"),
        P(("dp", "fsdp"), None),
    )
    return jax.shard_map(
        per_device,
        mesh=mesh,
        in_specs=placed,
        out_specs=(
            P("dp", "fsdp", None),
            P("dp", "fsdp", None),
            P(("dp", "fsdp")),
            P(("dp", "fsdp"), None),
            P(("dp", "fsdp"), None),
            P(("dp", "fsdp"), None),
            P(("dp", "fsdp"), None),
            P(("dp", "fsdp")),
            P("fsdp", "dp"),
            P("fsdp", "dp"),
            P(("dp", "fsdp"), None),
        ),
        check_vma=False,
    )
```

profile of v0, /device:TPU:0, one launch (start us, length us, event | category | flops | bytes accessed | tf_op | source)
XLA Modules:
  0.0 3794.1 jit_solution(2999831533036421814)
XLA Ops:
  11.2 42.1 %all-reduce.5 = (bf16[2048]{0:T(1024)(128)(2,1)S(1)}, bf16[2048]{0:T(1024)(128)(2,1)S(1)}) all-reduce(bf16[2048]{0:T(1024)(128)(2,1)S(1)} %dynamic-update-slice, bf16[2048]{0:T(1024)(128)(2,1)S(1)} %dynamic-update-slice.1), channel_id=1, replica_groups=mesh['dp'=4,'fsdp'=8] {'dp','fsdp'}, use_global_device_ids=true, to_apply=%add | all-reduce | flops 4096 | bytes 16384
  54.1 16.0 all-gather.13.cloned.1.call-done
  74.2 54.0 %all-gather.17.cloned.1.call-done = bf16[2048,512]{1,0:T(8,128)(2,1)} async-done(((bf16[64,512]{1,0:T(8,128)(2,1)}), bf16[2048,512]{1,0:T(8,128)(2,1)}) %all-gather.17.cloned.1.call-update) | async-done | bytes 2097168 | tf_op jit(solution)/shard_map/all_gather | solution.py:220
  134.6 37.7 all-gather.25.cloned.1.call-done
  172.4 45.0 %all-gather.29.cloned.1.call-done = bf16[2048,1408]{1,0:T(8,128)(2,1)} async-done(((bf16[256,1408]{1,0:T(8,128)(2,1)}), bf16[2048,1408]{1,0:T(8,128)(2,1)}) %all-gather.29.cloned.1.call-update) | async-done | bytes 5767184 | tf_op jit(solution)/shard_map/all_gather | solution.py:227
  217.5 45.0 %all-gather.33.cloned.1.call-done = bf16[1408,2048]{1,0:T(8,128)(2,1)} async-done(((bf16[176,2048]{1,0:T(8,128)(2,1)}), bf16[1408,2048]{1,0:T(8,128)(2,1)}) %all-gather.33.cloned.1.call-update) | async-done | bytes 5767184 | tf_op jit(solution)/shard_map/all_gather | solution.py:228
  265.5 25.0 all-gather.15.cloned.1.call-done
  294.3 24.4 all-gather.19.cloned.1.call-done
  323.9 75.1 %all-gather.21.cloned.1.call-done = bf16[2048,2048]{1,0:T(8,128)(2,1)} async-done(((bf16[64,2048]{1,0:T(8,128)(2,1)}), bf16[2048,2048]{1,0:T(8,128)(2,1)}) %all-gather.21.cloned.1.call-update) | async-done | bytes 8388624 | tf_op jit(solution)/shard_map/all_gather | solution.py:219
  399.0 12.2 copy.70
  417.7 23.9 while.39
  441.6 15.8 while.40
  446.6 5.4 bitcast_add_fusion.5
  463.0 14.7 all-gather.23.cloned.1.call-done
  477.7 5.6 multiply_reduce_fusion.3
  485.7 383.3 %all-gather.27.cloned.1.call-done = bf16[2048,5632]{1,0:T(8,128)(2,1)} async-done(((bf16[2048,1408]{1,0:T(8,128)(2,1)}), bf16[2048,5632]{1,0:T(8,128)(2,1)}) %all-gather.27.cloned.1.call-update) | async-done | bytes 23068688 | tf_op jit(solution)/shard_map/all_gather | solution.py:231
  868.9 15.5 fusion.119
  884.4 375.5 %all-gather.31.cloned.1.call-done = bf16[2048,5632]{1,0:T(8,128)(2,1)} async-done(((bf16[2048,1408]{1,0:T(8,128)(2,1)}), bf16[2048,5632]{1,0:T(8,128)(2,1)}) %all-gather.31.cloned.1.call-update) | async-done | bytes 23068688 | tf_op jit(solution)/shard_map/all_gather | solution.py:232
  1259.9 15.5 fusion.120
  1275.5 375.3 %all-gather.35.cloned.1.call-done = bf16[5632,2048]{1,0:T(8,128)(2,1)} async-done(((bf16[1408,2048]{1,0:T(8,128)(2,1)}), bf16[5632,2048]{1,0:T(8,128)(2,1)}) %all-gather.35.cloned.1.call-update) | async-done | bytes 23068688 | tf_op jit(solution)/shard_map/all_gather | solution.py:234
  1650.8 16.9 multiply_convert_fusion
  1669.0 11.4 convolution_convert_fusion.1
  1680.5 30.6 copy.92
  1711.1 12.6 convolution_convert_fusion
  1723.8 30.6 copy.94
  1754.4 13.5 convolution_convert_fusion.2
  1768.1 14.0 fusion.121
  1782.0 15.2 multiply_reduce_fusion
  1801.5 7.5 convolution_convert_fusion.3
  1813.9 57.3 %while.41 = (s32[]{:T(128)}, f32[192,4,4,128]{3,0,2,1:T(8,128)}, bf16[3,512,4,128]{3,1,2,0:T(8,128)(2,1)}, bf16[3,512,4,128]{3,1,2,0:T(8,128)(2,1)}, bf16[3,512,...) while((s32[]{:T(128)}, f32[192,4,4,128]{3,0,2,1:T(8,128)}, ...), condition=%wide.region_14.15_spmd.clone, body=%wide.region_13.14_spmd.clone.sunk | while | flops 2033221888 | bytes 139287344 | solution.py:147
  1879.4 210.7 %reduce-scatter.37.cloned.1.call-done = bf16[1408,2048]{1,0:T(8,128)(2,1)} async-done(((bf16[5632,2048]{1,0:T(8,128)(2,1)}), bf16[1408,2048]{1,0:T(8,128)(2,1)}) %reduce-scatter.37.cloned.1.call-update) | async-done | bytes 5767184
  2090.2 8.3 copy.93
  2098.6 376.4 %reduce-scatter.39.cloned.1.call-done = bf16[1408,2048]{1,0:T(8,128)(2,1)} async-done(((bf16[5632,2048]{1,0:T(8,128)(2,1)}), bf16[1408,2048]{1,0:T(8,128)(2,1)}) %reduce-scatter.39.cloned.1.call-update) | async-done | bytes 5767184
  2475.0 8.3 copy.95
  2483.4 376.2 %reduce-scatter.33.cloned.1.call-done = bf16[1408,2048]{1,0:T(8,128)(2,1)} async-done(((bf16[5632,2048]{1,0:T(8,128)(2,1)}), bf16[1408,2048]{1,0:T(8,128)(2,1)}) %reduce-scatter.33.cloned.1.call-update) | async-done | bytes 5767184 | tf_op jit(solution)/shard_map/reduce_scatter | solution.py:279
  2859.7 44.2 %reduce-scatter.17.cloned.1.call-done = bf16[192,512]{1,0:T(8,128)(2,1)} async-done(((bf16[1536,512]{1,0:T(8,128)(2,1)}), bf16[192,512]{1,0:T(8,128)(2,1)}) %reduce-scatter.17.cloned.1.call-update) | async-done | bytes 196624 | tf_op jit(solution)/shard_map/reduce_scatter | solution.py:301
  2909.1 36.8 reduce-scatter.19.cloned.1.call-done
  2952.7 10.3 fusion.88
  2964.5 8.3 fusion.122
  2972.8 7.2 fusion.90
  2980.0 11.7 fusion.67
  2995.5 40.3 %all-reduce.4 = (f32[2048]{0:T(1024)S(1)}, f32[2048]{0:T(1024)S(1)}) all-reduce(f32[2048]{0:T(1024)S(1)} %get-tuple-element.433, f32[2048]{0:T(1024)S(1)} %copy-done.49), channel_id=4, replica_groups=mesh['dp'=4,'fsdp'=8] {'dp','fsdp'}, use_global_device_ids=true, to_apply=%region_19.20.clone | all-reduce | flops 4096 | bytes 32768
  3044.1 27.7 reduce-scatter.31.cloned.1.call-done
  3074.1 60.4 %reduce-scatter.35.cloned.1.call-done = bf16[176,2048]{1,0:T(8,128)(2,1)} async-done(((bf16[1408,2048]{1,0:T(8,128)(2,1)}), bf16[176,2048]{1,0:T(8,128)(2,1)}) %reduce-scatter.35.cloned.1.call-update) | async-done | bytes 720912 | tf_op jit(solution)/shard_map/reduce_scatter | solution.py:289
  3136.9 141.0 %reduce-scatter.23.cloned.1.call-done = f32[64,512]{1,0:T(8,128)} async-done(((f32[2048,512]{1,0:T(8,128)}), f32[64,512]{1,0:T(8,128)}) %reduce-scatter.23.cloned.1.call-update) | async-done | bytes 131088 | tf_op jit(solution)/shard_map/reduce_scatter | solution.py:335
  3277.9 139.8 %reduce-scatter.25.cloned.1.call-done = f32[64,512]{1,0:T(8,128)} async-done(((f32[2048,512]{1,0:T(8,128)}), f32[64,512]{1,0:T(8,128)}) %reduce-scatter.25.cloned.1.call-update) | async-done | bytes 131088 | tf_op jit(solution)/shard_map/reduce_scatter | solution.py:336
  3417.7 181.6 %reduce-scatter.21.cloned.1.call-done = f32[64,2048]{1,0:T(8,128)} async-done(((f32[2048,2048]{1,0:T(8,128)}), f32[64,2048]{1,0:T(8,128)}) %reduce-scatter.21.cloned.1.call-update) | async-done | bytes 524304 | tf_op jit(solution)/shard_map/reduce_scatter | solution.py:334
  3599.4 187.4 %reduce-scatter.27.cloned.1.call-done = f32[64,2048]{1,0:T(8,128)} async-done(((f32[2048,2048]{1,0:T(8,128)}), f32[64,2048]{1,0:T(8,128)}) %reduce-scatter.27.cloned.1.call-update) | async-done | bytes 524304 | tf_op jit(solution)/shard_map/reduce_scatter | solution.py:337
  (333 shorter events, 179.9 us)
Async XLA Ops:
  7.2 46.1 %copy-start.7 = (bf16[1,192,2048]{2,1,0:T(8,128)(2,1)S(1)}, bf16[1,192,2048]{2,1,0:T(8,128)(2,1)}, u32[]{:S(2)}) copy-start(bf16[1,192,2048]{2,1,0:T(8,128)(2,1)} %param.21) | copy-start | bytes 2359300
  7.2 62.9 %all-gather.13.cloned.1.call-start = ((), (), s32[]{:S(2)}) async-start(), calls=%async_computation.12 | async-start | bytes 2162688 | tf_op jit(solution)/shard_map/all_gather | solution.py:221
  7.9 120.3 %all-gather.17.cloned.1.call-start = ((), (), s32[]{:S(2)}) async-start(), calls=%async_computation.14 | async-start | bytes 2162688 | tf_op jit(solution)/shard_map/all_gather | solution.py:220
  8.7 163.6 %all-gather.25.cloned.1.call-start = ((), (), s32[]{:S(2)}) async-start(), calls=%async_computation.18 | async-start | bytes 6488064 | tf_op jit(solution)/shard_map/all_gather | solution.py:226
  9.4 208.0 %all-gather.29.cloned.1.call-start = ((), (), s32[]{:S(2)}) async-start(), calls=%async_computation.20 | async-start | bytes 6488064 | tf_op jit(solution)/shard_map/all_gather | solution.py:227
  10.0 252.5 %all-gather.33.cloned.1.call-start = ((), (), s32[]{:S(2)}) async-start(), calls=%async_computation.22 | async-start | bytes 6488064 | tf_op jit(solution)/shard_map/all_gather | solution.py:228
  10.6 279.9 %all-gather.15.cloned.1.call-start = ((), (), s32[]{:S(2)}) async-start(), calls=%async_computation.13 | async-start | bytes 1769472 | tf_op jit(solution)/shard_map/all_gather | solution.py:239
  53.3 357.9 %copy-start.35 = (f32[2048]{0:T(1024)}, f32[2048]{0:T(1024)S(1)}, u32[]{:S(2)}) copy-start(f32[2048]{0:T(1024)S(1)} %convert_element_type.174) | copy-start | bytes 24580
  54.1 357.1 %copy-start.37 = (f32[192]{0:T(256)}, f32[192]{0:T(256)S(1)}, u32[]{:S(2)}) copy-start(f32[192]{0:T(256)S(1)} %get-tuple-element.530) | copy-start | bytes 2308
  73.0 245.7 %all-gather.19.cloned.1.call-start = ((), (), s32[]{:S(2)}) async-start(), calls=%async_computation.15 | async-start | bytes 1769472 | tf_op jit(solution)/shard_map/all_gather | solution.py:238
  74.2 342.4 %copy-start.20 = (f32[192,64]{1,0:T(8,128)}, f32[192,64]{1,0:T(8,128)S(1)}, u32[]{:S(2)}) copy-start(f32[192,64]{1,0:T(8,128)S(1)} %get-tuple-element.528) | copy-start | bytes 147460
  133.0 266.0 %all-gather.21.cloned.1.call-start = ((), (), s32[]{:S(2)}) async-start(), calls=%async_computation.16 | async-start | bytes 8650752 | tf_op jit(solution)/shard_map/all_gather | solution.py:219
  133.8 343.9 %all-gather.23.cloned.1.call-start = ((), (), s32[]{:S(2)}) async-start(), calls=%async_computation.17 | async-start | bytes 8650752 | tf_op jit(solution)/shard_map/all_gather | solution.py:222
  134.5 734.4 %all-gather.27.cloned.1.call-start = ((), (), s32[]{:S(2)}) async-start(), calls=%async_computation.19 | async-start | bytes 28835840 | tf_op jit(solution)/shard_map/all_gather | solution.py:231
  172.3 1087.6 %all-gather.31.cloned.1.call-start = ((), (), s32[]{:S(2)}) async-start(), calls=%async_computation.21 | async-start | bytes 28835840 | tf_op jit(solution)/shard_map/all_gather | solution.py:232
  217.4 1433.4 %all-gather.35.cloned.1.call-start = ((), (), s32[]{:S(2)}) async-start(), calls=%async_computation.23 | async-start | bytes 28835840 | tf_op jit(solution)/shard_map/all_gather | solution.py:234
  262.5 1827.7 %reduce-scatter.37.cloned.1.call-start = ((), (), s32[]{:S(2)}) async-start(), calls=%async_computation.34 | async-start | bytes 28835840
  483.3 1313.8 %copy-start.41 = (f32[192]{0:T(256)}, f32[192]{0:T(256)S(1)}, u32[]{:S(2)}) copy-start(f32[192]{0:T(256)S(1)} %get-tuple-element.532) | copy-start | bytes 2308
  483.4 1313.8 %copy-start.45 = (f32[192]{0:T(256)}, f32[192]{0:T(256)S(1)}, u32[]{:S(2)}) copy-start(f32[192]{0:T(256)S(1)} %get-tuple-element.531) | copy-start | bytes 2308
  1650.8 18.3 copy-start.12
  1711.1 763.9 %reduce-scatter.39.cloned.1.call-start = ((), (), s32[]{:S(2)}) async-start(), calls=%async_computation.35 | async-start | bytes 28835840
  1754.4 1105.2 %reduce-scatter.33.cloned.1.call-start = ((), (), s32[]{:S(2)}) async-start(), calls=%async_computation.32 | async-start | bytes 28835840 | tf_op jit(solution)/shard_map/reduce_scatter | solution.py:279
  1768.0 1136.0 %reduce-scatter.17.cloned.1.call-start = ((), (), s32[]{:S(2)}) async-start(), calls=%async_computation.24 | async-start | bytes 1769472 | tf_op jit(solution)/shard_map/reduce_scatter | solution.py:301
  1821.8 6.1 copy-start.28
  1828.5 4.3 copy-start.6
  1840.6 6.7 copy-start.28
  1847.7 4.3 copy-start.6
  1859.7 6.7 copy-start.28
  1866.9 4.3 copy-start.6
  1875.3 1070.6 %reduce-scatter.19.cloned.1.call-start = ((), (), s32[]{:S(2)}) async-start(), calls=%async_computation.25 | async-start | bytes 1769472 | tf_op jit(solution)/shard_map/reduce_scatter | solution.py:304
  1879.4 1162.4 %reduce-scatter.29.cloned.1.call-start = ((), (), s32[]{:S(2)}) async-start(), calls=%async_computation.30 | async-start | bytes 6488064 | tf_op jit(solution)/shard_map/reduce_scatter | solution.py:283
  2098.5 973.3 %reduce-scatter.31.cloned.1.call-start = ((), (), s32[]{:S(2)}) async-start(), calls=%async_computation.31 | async-start | bytes 6488064 | tf_op jit(solution)/shard_map/reduce_scatter | solution.py:286
  2483.3 651.2 %reduce-scatter.35.cloned.1.call-start = ((), (), s32[]{:S(2)}) async-start(), calls=%async_computation.33 | async-start | bytes 6488064 | tf_op jit(solution)/shard_map/reduce_scatter | solution.py:289
  2859.6 45.7 %copy-start.21 = (f32[192,64]{1,0:T(8,128)S(1)}, f32[192,64]{1,0:T(8,128)}, u32[]{:S(2)}) copy-start(f32[192,64]{1,0:T(8,128)} %copy-done.20) | copy-start | bytes 147460
  2859.6 45.7 %copy-start.31 = (f32[192,64]{1,0:T(8,128)S(1)}, f32[192,64]{1,0:T(8,128)}, u32[]{:S(2)}) copy-start(f32[192,64]{1,0:T(8,128)} %get-tuple-element.526) | copy-start | bytes 147460
  2859.7 418.3 %reduce-scatter.23.cloned.1.call-start = ((), (), s32[]{:S(2)}) async-start(), calls=%async_computation.27 | async-start | bytes 4325376 | tf_op jit(solution)/shard_map/reduce_scatter | solution.py:335
  2909.1 508.7 %reduce-scatter.25.cloned.1.call-start = ((), (), s32[]{:S(2)}) async-start(), calls=%async_computation.28 | async-start | bytes 4325376 | tf_op jit(solution)/shard_map/reduce_scatter | solution.py:336
  2949.7 649.6 %reduce-scatter.21.cloned.1.call-start = ((), (), s32[]{:S(2)}) async-start(), calls=%async_computation.26 | async-start | bytes 17301504 | tf_op jit(solution)/shard_map/reduce_scatter | solution.py:334
  2963.0 823.7 %reduce-scatter.27.cloned.1.call-start = ((), (), s32[]{:S(2)}) async-start(), calls=%async_computation.29 | async-start | bytes 17301504 | tf_op jit(solution)/shard_map/reduce_scatter | solution.py:337
  2972.8 7.2 copy-start.10
  2972.8 7.2 copy-start.16
  2980.0 11.7 copy-start.11
  2980.0 11.7 copy-start.25
  2993.3 43.6 %copy-start.14 = (bf16[1,192,2048]{2,1,0:T(8,128)(2,1)S(1)}, bf16[1,192,2048]{2,1,0:T(8,128)(2,1)}, u32[]{:S(2)}) copy-start(bf16[1,192,2048]{2,1,0:T(8,128)(2,1)} %param.22) | copy-start | bytes 2359300
  2993.3 43.6 %copy-start.42 = (f32[192]{0:T(256)S(1)}, f32[192]{0:T(256)}, u32[]{:S(2)}) copy-start(f32[192]{0:T(256)} %copy-done.41) | copy-start | bytes 2308
  2993.4 43.6 %copy-start.46 = (f32[192]{0:T(256)S(1)}, f32[192]{0:T(256)}, u32[]{:S(2)}) copy-start(f32[192]{0:T(256)} %copy-done.45) | copy-start | bytes 2308
  2993.4 43.6 %copy-start.48 = (f32[192]{0:T(256)S(1)}, f32[192]{0:T(256)}, u32[]{:S(2)}) copy-start(f32[192]{0:T(256)} %copy-done.47) | copy-start | bytes 2308
  2993.4 43.6 %copy-start.50 = (f32[192]{0:T(256)S(1)}, f32[192]{0:T(256)}, u32[]{:S(2)}) copy-start(f32[192]{0:T(256)} %get-tuple-element.529) | copy-start | bytes 2308
  (55 other events, 130.0 us)
Sparse Core Ops, SparseCore 0:
  10.9 59.1 all-gather.12
  72.9 55.2 all-gather.16
  130.1 42.1 all-gather.24
  174.0 43.3 all-gather.28
  219.1 43.3 all-gather.32
  264.8 25.6 all-gather.14
  293.0 25.6 all-gather.18
  321.6 77.4 all-gather.20
  401.9 75.7 all-gather.22
  479.2 389.6 all-gather.26
  870.5 389.3 all-gather.30
  1261.4 389.3 all-gather.34
  1711.2 378.9 reduce-scatter.36
  2092.5 382.3 reduce-scatter.38
  2477.2 382.3 reduce-scatter.32
  2863.7 40.2 reduce-scatter.16
  2907.4 38.4 reduce-scatter.18
  2949.6 59.5 reduce-scatter.28
  3012.7 59.0 reduce-scatter.30
  3075.5 59.0 reduce-scatter.34
  3137.4 140.5 reduce-scatter.22
  3280.8 136.8 reduce-scatter.24
  3420.6 178.7 reduce-scatter.20
  3602.1 184.5 reduce-scatter.26
where the time goes:
time: 3800 us; the launch traced here: 3790 us
  waiting for transfers between devices  3260 us (86%)
  matrix products  253 us (7%)
  local copies, waits for them, and re-layouts  143 us (4%)
  blocking collectives  82.4 us (2%)
  other arithmetic  38.6 us (1%)
    unnamed x26, waiting for transfers between devices  592 us
    all_gather x1, waiting for transfers between devices, per_device(): lax.all_gather(feed_block[0], 'dp', axis=1, tiled=True)  383 us
    reduce_scatter x1, waiting for transfers between devices, per_device(): lax.psum_scatter(down_term.astype(jnp.bfloat16), 'dp', scatter_dimension=...  376 us
    all_gather x1, waiting for transfers between devices, per_device(): lax.all_gather(feed_block[1], 'dp', axis=1, tiled=True)  376 us
    all_gather x1, waiting for transfers between devices, per_device(): down_use = lax.all_gather(feed_block[2], 'dp', axis=0, tiled=True)  375 us
    reduce_scatter x1, waiting for transfers between devices, per_device(): lax.psum_scatter(output_grad_weight, ('dp', 'fsdp'), scatter_dimension=0,...  187 us
    reduce_scatter x1, waiting for transfers between devices, per_device(): lax.psum_scatter(query_grad, ('dp', 'fsdp'), scatter_dimension=0, tiled=T...  182 us
    reduce_scatter x1, waiting for transfers between devices, per_device(): lax.psum_scatter(key_grad, ('dp', 'fsdp'), scatter_dimension=0, tiled=True)  141 us
  transfers between devices with their start and end apart: 24, of which 23 were waited for; matrix products, arithmetic and copies ran while one was open for 9% of the time, Pallas kernels for 0%

commit v1 on v0

--- a/solution.py
+++ b/solution.py
@@ -208,7 +208,8 @@
     all_pos = jnp.arange(seq_length, dtype=jnp.int32)
     first_row = lax.axis_index("fsdp") * tokens
     query_pos = first_row + jnp.arange(tokens, dtype=jnp.int32)
-    ends = jnp.cumsum(doc_lengths[0])
+    order = jnp.arange(doc_lengths.shape[1], dtype=jnp.int32)
+    ends = jnp.sum(jnp.where(order[None, :] <= order[:, None], doc_lengths[0][None, :], 0), 1)
     all_doc = jnp.sum((all_pos[:, None] >= ends[None, :]).astype(jnp.int32), 1)
     query_doc = lax.dynamic_slice_in_dim(all_doc, first_row, tokens)
     cosine, sine_part = rotary_tables(query_pos)

time: 3800 us -> 3800 us (level)
  no operation moved by 1% of the time
where the time goes in v1:
time: 3800 us; the launch traced here: 3790 us
  waiting for transfers between devices  3260 us (86%)
  matrix products  253 us (7%)
  local copies, waits for them, and re-layouts  143 us (4%)
  blocking collectives  82.4 us (2%)
  other arithmetic  38.5 us (1%)
    unnamed x26, waiting for transfers between devices  592 us
    all_gather x1, waiting for transfers between devices, per_device(): lax.all_gather(feed_block[0], 'dp', axis=1, tiled=True)  383 us
    reduce_scatter x1, waiting for transfers between devices, per_device(): lax.psum_scatter(down_term.astype(jnp.bfloat16), 'dp', scatter_dimension=...  376 us
    all_gather x1, waiting for transfers between devices, per_device(): lax.all_gather(feed_block[1], 'dp', axis=1, tiled=True)  376 us
    all_gather x1, waiting for transfers between devices, per_device(): down_use = lax.all_gather(feed_block[2], 'dp', axis=0, tiled=True)  375 us
    reduce_scatter x1, waiting for transfers between devices, per_device(): lax.psum_scatter(output_grad_weight, ('dp', 'fsdp'), scatter_dimension=0,...  187 us
    reduce_scatter x1, waiting for transfers between devices, per_device(): lax.psum_scatter(query_grad, ('dp', 'fsdp'), scatter_dimension=0, tiled=T...  182 us
    reduce_scatter x1, waiting for transfers between devices, per_device(): lax.psum_scatter(key_grad, ('dp', 'fsdp'), scatter_dimension=0, tiled=True)  141 us
  transfers between devices with their start and end apart: 24, of which 23 were waited for; matrix products, arithmetic and copies ran while one was open for 9% of the time, Pallas kernels for 0%

profile of v1, /device:TPU:0, one launch (start us, length us, event | category | flops | bytes accessed | tf_op | source)
XLA Modules:
  0.0 3794.1 jit_solution(652203059127364912)
XLA Ops:
  11.2 42.1 %all-reduce.5 = (bf16[2048]{0:T(1024)(128)(2,1)S(1)}, bf16[2048]{0:T(1024)(128)(2,1)S(1)}) all-reduce(bf16[2048]{0:T(1024)(128)(2,1)S(1)} %dynamic-update-slice, bf16[2048]{0:T(1024)(128)(2,1)S(1)} %dynamic-update-slice.1), channel_id=1, replica_groups=mesh['dp'=4,'fsdp'=8] {'dp','fsdp'}, use_global_device_ids=true, to_apply=%add | all-reduce | flops 4096 | bytes 16384
  54.1 16.0 all-gather.13.cloned.1.call-done
  74.2 54.0 %all-gather.17.cloned.1.call-done = bf16[2048,512]{1,0:T(8,128)(2,1)} async-done(((bf16[64,512]{1,0:T(8,128)(2,1)}), bf16[2048,512]{1,0:T(8,128)(2,1)}) %all-gather.17.cloned.1.call-update) | async-done | bytes 2097168 | tf_op jit(solution)/shard_map/all_gather | solution.py:221
  134.6 37.7 all-gather.25.cloned.1.call-done
  172.4 45.0 %all-gather.29.cloned.1.call-done = bf16[2048,1408]{1,0:T(8,128)(2,1)} async-done(((bf16[256,1408]{1,0:T(8,128)(2,1)}), bf16[2048,1408]{1,0:T(8,128)(2,1)}) %all-gather.29.cloned.1.call-update) | async-done | bytes 5767184 | tf_op jit(solution)/shard_map/all_gather | solution.py:228
  217.5 45.0 %all-gather.33.cloned.1.call-done = bf16[1408,2048]{1,0:T(8,128)(2,1)} async-done(((bf16[176,2048]{1,0:T(8,128)(2,1)}), bf16[1408,2048]{1,0:T(8,128)(2,1)}) %all-gather.33.cloned.1.call-update) | async-done | bytes 5767184 | tf_op jit(solution)/shard_map/all_gather | solution.py:229
  265.4 25.1 all-gather.15.cloned.1.call-done
  294.3 24.4 all-gather.19.cloned.1.call-done
  323.9 75.1 %all-gather.21.cloned.1.call-done = bf16[2048,2048]{1,0:T(8,128)(2,1)} async-done(((bf16[64,2048]{1,0:T(8,128)(2,1)}), bf16[2048,2048]{1,0:T(8,128)(2,1)}) %all-gather.21.cloned.1.call-update) | async-done | bytes 8388624 | tf_op jit(solution)/shard_map/all_gather | solution.py:220
  399.0 12.2 copy.70
  417.7 23.9 while.39
  441.6 15.8 while.40
  446.6 5.4 bitcast_add_fusion.5
  463.0 14.7 all-gather.23.cloned.1.call-done
  477.7 5.6 multiply_reduce_fusion.3
  485.7 383.3 %all-gather.27.cloned.1.call-done = bf16[2048,5632]{1,0:T(8,128)(2,1)} async-done(((bf16[2048,1408]{1,0:T(8,128)(2,1)}), bf16[2048,5632]{1,0:T(8,128)(2,1)}) %all-gather.27.cloned.1.call-update) | async-done | bytes 23068688 | tf_op jit(solution)/shard_map/all_gather | solution.py:232
  868.9 15.5 fusion.119
  884.4 375.5 %all-gather.31.cloned.1.call-done = bf16[2048,5632]{1,0:T(8,128)(2,1)} async-done(((bf16[2048,1408]{1,0:T(8,128)(2,1)}), bf16[2048,5632]{1,0:T(8,128)(2,1)}) %all-gather.31.cloned.1.call-update) | async-done | bytes 23068688 | tf_op jit(solution)/shard_map/all_gather | solution.py:233
  1259.9 15.5 fusion.120
  1275.5 375.3 %all-gather.35.cloned.1.call-done = bf16[5632,2048]{1,0:T(8,128)(2,1)} async-done(((bf16[1408,2048]{1,0:T(8,128)(2,1)}), bf16[5632,2048]{1,0:T(8,128)(2,1)}) %all-gather.35.cloned.1.call-update) | async-done | bytes 23068688 | tf_op jit(solution)/shard_map/all_gather | solution.py:235
  1650.8 16.9 multiply_convert_fusion
  1669.0 11.4 convolution_convert_fusion.1
  1680.5 30.6 copy.92
  1711.1 12.6 convolution_convert_fusion
  1723.8 30.6 copy.94
  1754.4 13.5 convolution_convert_fusion.2
  1768.1 14.0 fusion.121
  1782.0 15.2 multiply_reduce_fusion
  1801.5 7.5 convolution_convert_fusion.3
  1813.9 57.3 %while.41 = (s32[]{:T(128)}, f32[192,4,4,128]{3,0,2,1:T(8,128)}, bf16[3,512,4,128]{3,1,2,0:T(8,128)(2,1)}, bf16[3,512,4,128]{3,1,2,0:T(8,128)(2,1)}, bf16[3,512,...) while((s32[]{:T(128)}, f32[192,4,4,128]{3,0,2,1:T(8,128)}, ...), condition=%wide.region_14.15_spmd.clone, body=%wide.region_13.14_spmd.clone.sunk | while | flops 2033221888 | bytes 139287344 | solution.py:147
  1879.4 210.7 %reduce-scatter.37.cloned.1.call-done = bf16[1408,2048]{1,0:T(8,128)(2,1)} async-done(((bf16[5632,2048]{1,0:T(8,128)(2,1)}), bf16[1408,2048]{1,0:T(8,128)(2,1)}) %reduce-scatter.37.cloned.1.call-update) | async-done | bytes 5767184
  2090.2 8.3 copy.93
  2098.6 376.4 %reduce-scatter.39.cloned.1.call-done = bf16[1408,2048]{1,0:T(8,128)(2,1)} async-done(((bf16[5632,2048]{1,0:T(8,128)(2,1)}), bf16[1408,2048]{1,0:T(8,128)(2,1)}) %reduce-scatter.39.cloned.1.call-update) | async-done | bytes 5767184
  2475.0 8.3 copy.95
  2483.4 376.2 %reduce-scatter.33.cloned.1.call-done = bf16[1408,2048]{1,0:T(8,128)(2,1)} async-done(((bf16[5632,2048]{1,0:T(8,128)(2,1)}), bf16[1408,2048]{1,0:T(8,128)(2,1)}) %reduce-scatter.33.cloned.1.call-update) | async-done | bytes 5767184 | tf_op jit(solution)/shard_map/reduce_scatter | solution.py:280
  2859.7 44.2 %reduce-scatter.17.cloned.1.call-done = bf16[192,512]{1,0:T(8,128)(2,1)} async-done(((bf16[1536,512]{1,0:T(8,128)(2,1)}), bf16[192,512]{1,0:T(8,128)(2,1)}) %reduce-scatter.17.cloned.1.call-update) | async-done | bytes 196624 | tf_op jit(solution)/shard_map/reduce_scatter | solution.py:302
  2909.1 36.8 reduce-scatter.19.cloned.1.call-done
  2952.7 10.3 fusion.88
  2964.5 8.3 fusion.122
  2972.8 7.2 fusion.90
  2980.0 11.7 fusion.67
  2995.5 40.3 %all-reduce.4 = (f32[2048]{0:T(1024)S(1)}, f32[2048]{0:T(1024)S(1)}) all-reduce(f32[2048]{0:T(1024)S(1)} %get-tuple-element.433, f32[2048]{0:T(1024)S(1)} %copy-done.49), channel_id=4, replica_groups=mesh['dp'=4,'fsdp'=8] {'dp','fsdp'}, use_global_device_ids=true, to_apply=%region_19.20.clone | all-reduce | flops 4096 | bytes 32768
  3044.1 27.7 reduce-scatter.31.cloned.1.call-done
  3074.1 60.4 %reduce-scatter.35.cloned.1.call-done = bf16[176,2048]{1,0:T(8,128)(2,1)} async-done(((bf16[1408,2048]{1,0:T(8,128)(2,1)}), bf16[176,2048]{1,0:T(8,128)(2,1)}) %reduce-scatter.35.cloned.1.call-update) | async-done | bytes 720912 | tf_op jit(solution)/shard_map/reduce_scatter | solution.py:290
  3136.9 141.0 %reduce-scatter.23.cloned.1.call-done = f32[64,512]{1,0:T(8,128)} async-done(((f32[2048,512]{1,0:T(8,128)}), f32[64,512]{1,0:T(8,128)}) %reduce-scatter.23.cloned.1.call-update) | async-done | bytes 131088 | tf_op jit(solution)/shard_map/reduce_scatter | solution.py:336
  3277.9 139.8 %reduce-scatter.25.cloned.1.call-done = f32[64,512]{1,0:T(8,128)} async-done(((f32[2048,512]{1,0:T(8,128)}), f32[64,512]{1,0:T(8,128)}) %reduce-scatter.25.cloned.1.call-update) | async-done | bytes 131088 | tf_op jit(solution)/shard_map/reduce_scatter | solution.py:337
  3417.7 181.6 %reduce-scatter.21.cloned.1.call-done = f32[64,2048]{1,0:T(8,128)} async-done(((f32[2048,2048]{1,0:T(8,128)}), f32[64,2048]{1,0:T(8,128)}) %reduce-scatter.21.cloned.1.call-update) | async-done | bytes 524304 | tf_op jit(solution)/shard_map/reduce_scatter | solution.py:335
  3599.4 187.4 %reduce-scatter.27.cloned.1.call-done = f32[64,2048]{1,0:T(8,128)} async-done(((f32[2048,2048]{1,0:T(8,128)}), f32[64,2048]{1,0:T(8,128)}) %reduce-scatter.27.cloned.1.call-update) | async-done | bytes 524304 | tf_op jit(solution)/shard_map/reduce_scatter | solution.py:338
  (333 shorter events, 179.9 us)
Async XLA Ops:
  7.2 46.1 %copy-start.7 = (bf16[1,192,2048]{2,1,0:T(8,128)(2,1)S(1)}, bf16[1,192,2048]{2,1,0:T(8,128)(2,1)}, u32[]{:S(2)}) copy-start(bf16[1,192,2048]{2,1,0:T(8,128)(2,1)} %param.21) | copy-start | bytes 2359300
  7.2 62.9 %all-gather.13.cloned.1.call-start = ((), (), s32[]{:S(2)}) async-start(), calls=%async_computation.12 | async-start | bytes 2162688 | tf_op jit(solution)/shard_map/all_gather | solution.py:222
  7.9 120.3 %all-gather.17.cloned.1.call-start = ((), (), s32[]{:S(2)}) async-start(), calls=%async_computation.14 | async-start | bytes 2162688 | tf_op jit(solution)/shard_map/all_gather | solution.py:221
  8.7 163.6 %all-gather.25.cloned.1.call-start = ((), (), s32[]{:S(2)}) async-start(), calls=%async_computation.18 | async-start | bytes 6488064 | tf_op jit(solution)/shard_map/all_gather | solution.py:227
  9.4 208.0 %all-gather.29.cloned.1.call-start = ((), (), s32[]{:S(2)}) async-start(), calls=%async_computation.20 | async-start | bytes 6488064 | tf_op jit(solution)/shard_map/all_gather | solution.py:228
  10.0 252.5 %all-gather.33.cloned.1.call-start = ((), (), s32[]{:S(2)}) async-start(), calls=%async_computation.22 | async-start | bytes 6488064 | tf_op jit(solution)/shard_map/all_gather | solution.py:229
  10.6 279.9 %all-gather.15.cloned.1.call-start = ((), (), s32[]{:S(2)}) async-start(), calls=%async_computation.13 | async-start | bytes 1769472 | tf_op jit(solution)/shard_map/all_gather | solution.py:240
  53.3 357.9 %copy-start.35 = (f32[2048]{0:T(1024)}, f32[2048]{0:T(1024)S(1)}, u32[]{:S(2)}) copy-start(f32[2048]{0:T(1024)S(1)} %convert_element_type.174) | copy-start | bytes 24580
  54.1 357.1 %copy-start.37 = (f32[192]{0:T(256)}, f32[192]{0:T(256)S(1)}, u32[]{:S(2)}) copy-start(f32[192]{0:T(256)S(1)} %get-tuple-element.530) | copy-start | bytes 2308
  73.0 245.7 %all-gather.19.cloned.1.call-start = ((), (), s32[]{:S(2)}) async-start(), calls=%async_computation.15 | async-start | bytes 1769472 | tf_op jit(solution)/shard_map/all_gather | solution.py:239
  74.2 342.4 %copy-start.20 = (f32[192,64]{1,0:T(8,128)}, f32[192,64]{1,0:T(8,128)S(1)}, u32[]{:S(2)}) copy-start(f32[192,64]{1,0:T(8,128)S(1)} %get-tuple-element.528) | copy-start | bytes 147460
  133.0 266.0 %all-gather.21.cloned.1.call-start = ((), (), s32[]{:S(2)}) async-start(), calls=%async_computation.16 | async-start | bytes 8650752 | tf_op jit(solution)/shard_map/all_gather | solution.py:220
  133.8 343.9 %all-gather.23.cloned.1.call-start = ((), (), s32[]{:S(2)}) async-start(), calls=%async_computation.17 | async-start | bytes 8650752 | tf_op jit(solution)/shard_map/all_gather | solution.py:223
  134.5 734.4 %all-gather.27.cloned.1.call-start = ((), (), s32[]{:S(2)}) async-start(), calls=%async_computation.19 | async-start | bytes 28835840 | tf_op jit(solution)/shard_map/all_gather | solution.py:232
  172.3 1087.6 %all-gather.31.cloned.1.call-start = ((), (), s32[]{:S(2)}) async-start(), calls=%async_computation.21 | async-start | bytes 28835840 | tf_op jit(solution)/shard_map/all_gather | solution.py:233
  217.4 1433.4 %all-gather.35.cloned.1.call-start = ((), (), s32[]{:S(2)}) async-start(), calls=%async_computation.23 | async-start | bytes 28835840 | tf_op jit(solution)/shard_map/all_gather | solution.py:235
  262.5 1827.7 %reduce-scatter.37.cloned.1.call-start = ((), (), s32[]{:S(2)}) async-start(), calls=%async_computation.34 | async-start | bytes 28835840
  483.3 1313.8 %copy-start.41 = (f32[192]{0:T(256)}, f32[192]{0:T(256)S(1)}, u32[]{:S(2)}) copy-start(f32[192]{0:T(256)S(1)} %get-tuple-element.532) | copy-start | bytes 2308
  483.4 1313.8 %copy-start.45 = (f32[192]{0:T(256)}, f32[192]{0:T(256)S(1)}, u32[]{:S(2)}) copy-start(f32[192]{0:T(256)S(1)} %get-tuple-element.531) | copy-start | bytes 2308
  1650.8 18.3 copy-start.12
  1711.1 763.9 %reduce-scatter.39.cloned.1.call-start = ((), (), s32[]{:S(2)}) async-start(), calls=%async_computation.35 | async-start | bytes 28835840
  1754.4 1105.2 %reduce-scatter.33.cloned.1.call-start = ((), (), s32[]{:S(2)}) async-start(), calls=%async_computation.32 | async-start | bytes 28835840 | tf_op jit(solution)/shard_map/reduce_scatter | solution.py:280
  1768.0 1136.0 %reduce-scatter.17.cloned.1.call-start = ((), (), s32[]{:S(2)}) async-start(), calls=%async_computation.24 | async-start | bytes 1769472 | tf_op jit(solution)/shard_map/reduce_scatter | solution.py:302
  1821.8 6.1 copy-start.28
  1828.5 4.3 copy-start.6
  1840.6 6.7 copy-start.28
  1847.7 4.3 copy-start.6
  1859.7 6.7 copy-start.28
  1866.9 4.3 copy-start.6
  1875.3 1070.6 %reduce-scatter.19.cloned.1.call-start = ((), (), s32[]{:S(2)}) async-start(), calls=%async_computation.25 | async-start | bytes 1769472 | tf_op jit(solution)/shard_map/reduce_scatter | solution.py:305
  1879.4 1162.4 %reduce-scatter.29.cloned.1.call-start = ((), (), s32[]{:S(2)}) async-start(), calls=%async_computation.30 | async-start | bytes 6488064 | tf_op jit(solution)/shard_map/reduce_scatter | solution.py:284
  2098.5 973.3 %reduce-scatter.31.cloned.1.call-start = ((), (), s32[]{:S(2)}) async-start(), calls=%async_computation.31 | async-start | bytes 6488064 | tf_op jit(solution)/shard_map/reduce_scatter | solution.py:287
  2483.3 651.2 %reduce-scatter.35.cloned.1.call-start = ((), (), s32[]{:S(2)}) async-start(), calls=%async_computation.33 | async-start | bytes 6488064 | tf_op jit(solution)/shard_map/reduce_scatter | solution.py:290
  2859.6 45.7 %copy-start.21 = (f32[192,64]{1,0:T(8,128)S(1)}, f32[192,64]{1,0:T(8,128)}, u32[]{:S(2)}) copy-start(f32[192,64]{1,0:T(8,128)} %copy-done.20) | copy-start | bytes 147460
  2859.6 45.7 %copy-start.31 = (f32[192,64]{1,0:T(8,128)S(1)}, f32[192,64]{1,0:T(8,128)}, u32[]{:S(2)}) copy-start(f32[192,64]{1,0:T(8,128)} %get-tuple-element.526) | copy-start | bytes 147460
  2859.7 418.3 %reduce-scatter.23.cloned.1.call-start = ((), (), s32[]{:S(2)}) async-start(), calls=%async_computation.27 | async-start | bytes 4325376 | tf_op jit(solution)/shard_map/reduce_scatter | solution.py:336
  2909.1 508.7 %reduce-scatter.25.cloned.1.call-start = ((), (), s32[]{:S(2)}) async-start(), calls=%async_computation.28 | async-start | bytes 4325376 | tf_op jit(solution)/shard_map/reduce_scatter | solution.py:337
  2949.7 649.6 %reduce-scatter.21.cloned.1.call-start = ((), (), s32[]{:S(2)}) async-start(), calls=%async_computation.26 | async-start | bytes 17301504 | tf_op jit(solution)/shard_map/reduce_scatter | solution.py:335
  2963.0 823.7 %reduce-scatter.27.cloned.1.call-start = ((), (), s32[]{:S(2)}) async-start(), calls=%async_computation.29 | async-start | bytes 17301504 | tf_op jit(solution)/shard_map/reduce_scatter | solution.py:338
  2972.8 7.2 copy-start.10
  2972.8 7.2 copy-start.16
  2980.0 11.7 copy-start.11
  2980.0 11.7 copy-start.25
  2993.3 43.6 %copy-start.14 = (bf16[1,192,2048]{2,1,0:T(8,128)(2,1)S(1)}, bf16[1,192,2048]{2,1,0:T(8,128)(2,1)}, u32[]{:S(2)}) copy-start(bf16[1,192,2048]{2,1,0:T(8,128)(2,1)} %param.22) | copy-start | bytes 2359300
  2993.3 43.6 %copy-start.42 = (f32[192]{0:T(256)S(1)}, f32[192]{0:T(256)}, u32[]{:S(2)}) copy-start(f32[192]{0:T(256)} %copy-done.41) | copy-start | bytes 2308
  2993.4 43.6 %copy-start.46 = (f32[192]{0:T(256)S(1)}, f32[192]{0:T(256)}, u32[]{:S(2)}) copy-start(f32[192]{0:T(256)} %copy-done.45) | copy-start | bytes 2308
  2993.4 43.6 %copy-start.48 = (f32[192]{0:T(256)S(1)}, f32[192]{0:T(256)}, u32[]{:S(2)}) copy-start(f32[192]{0:T(256)} %copy-done.47) | copy-start | bytes 2308
  2993.4 43.6 %copy-start.50 = (f32[192]{0:T(256)S(1)}, f32[192]{0:T(256)}, u32[]{:S(2)}) copy-start(f32[192]{0:T(256)} %get-tuple-element.529) | copy-start | bytes 2308
  (55 other events, 129.9 us)
Sparse Core Ops, SparseCore 0:
  10.9 59.1 all-gather.12
  72.9 55.2 all-gather.16
  130.1 42.1 all-gather.24
  174.0 43.3 all-gather.28
  219.1 43.3 all-gather.32
  264.8 25.6 all-gather.14
  293.0 25.6 all-gather.18
  321.6 77.4 all-gather.20
  401.9 75.7 all-gather.22
  479.2 389.6 all-gather.26
  870.5 389.3 all-gather.30
  1261.4 389.3 all-gather.34
  1711.2 378.9 reduce-scatter.36
  2092.5 382.3 reduce-scatter.38
  2477.2 382.3 reduce-scatter.32
  2863.7 40.2 reduce-scatter.16
  2907.4 38.4 reduce-scatter.18
  2949.6 59.5 reduce-scatter.28
  3012.7 59.0 reduce-scatter.30
  3075.5 59.0 reduce-scatter.34
  3137.4 140.5 reduce-scatter.22
  3280.8 136.8 reduce-scatter.24
  3420.6 178.7 reduce-scatter.20
  3602.1 184.5 reduce-scatter.26

commit v2 on v0

v2 whole, which is shorter than its diff:
```python
import functools
import math

import jax
import jax.numpy as jnp
from jax import lax
from jax.experimental import pallas as pl
from jax.experimental.pallas import tpu as pltpu
from jax.sharding import PartitionSpec as P

HEADS = 16
KV_HEADS = 4
HEAD_DIM = 128

norm_eps = 1e-05
rope_base = 10000.0
mask_fill = -1e30
score_scale = 1.0 / math.sqrt(HEAD_DIM)
f32 = jnp.float32
bf16 = jnp.bfloat16


def dot_plain(left, right):
    return jnp.dot(left, right, preferred_element_type=f32)


def dot_right_t(left, right):
    return lax.dot_general(left, right, (((1,), (1,)), ((), ())), preferred_element_type=f32)


def dot_left_t(left, right):
    return lax.dot_general(left, right, (((0,), (0,)), ((), ())), preferred_element_type=f32)


def rotary_tables(length):
    half_dim = HEAD_DIM // 2
    frequency = rope_base ** (-(2.0 * jnp.arange(half_dim, dtype=f32)) / HEAD_DIM)
    angles = jnp.arange(length, dtype=jnp.int32).astype(f32)[:, None] * frequency[None, :]
    return (jnp.cos(angles)[:, None, :], jnp.sin(angles)[:, None, :])


def rotate(vectors, cosine, sine_part):
    half_dim = vectors.shape[-1] // 2
    lower_half = vectors[..., :half_dim]
    upper_half = vectors[..., half_dim:]
    return jnp.concatenate(
        [
            lower_half * cosine - upper_half * sine_part,
            upper_half * cosine + lower_half * sine_part,
        ],
        -1,
    )


def rms_scale(rows):
    return lax.rsqrt(jnp.mean(rows * rows, -1, keepdims=True) + norm_eps)


def after(value, *earlier):
    return lax.optimization_barrier((value, *earlier))[0]


UP = [(0, 1), (1, 2), (2, 3)]
DOWN = [(3, 2), (2, 1), (1, 0)]


def pick(plane, options):
    return lax.select_n(plane, *options)


def plane_gather(block):
    count = lax.axis_size("dp")
    plane = lax.axis_index("dp")
    if count != 4:
        whole = lax.all_gather(block, "dp", axis=0)
        return [whole[i] for i in range(count)], [jnp.int32(i) for i in range(count)]
    up1 = lax.ppermute(block, "dp", UP)
    down1 = lax.ppermute(block, "dp", DOWN)
    up2 = lax.ppermute(up1, "dp", UP[1:])
    down2 = lax.ppermute(down1, "dp", DOWN[1:])
    up3 = lax.ppermute(up2, "dp", UP[2:])
    down3 = lax.ppermute(down2, "dp", DOWN[2:])
    blocks = [
        block,
        pick(plane, [down1, down1, up1, up1]),
        pick(plane, [down2, up1, down1, up2]),
        pick(plane, [down3, down2, up2, up3]),
    ]
    table = jnp.array([[0, 1, 2, 3], [1, 2, 0, 3], [2, 1, 3, 0], [3, 2, 1, 0]], jnp.int32)
    mine = lax.dynamic_index_in_dim(table, plane, 0, keepdims=False)
    return blocks, [mine[i] for i in range(4)]


def add_low(left, right):
    return (left.astype(f32) + right.astype(f32)).astype(left.dtype)


def plane_scatter(parts):
    count = lax.axis_size("dp")
    plane = lax.axis_index("dp")
    if count != 4:
        return lax.psum_scatter(jnp.stack(parts), "dp", scatter_dimension=0, tiled=False).astype(f32)
    own, first, second, third = parts
    up3 = lax.ppermute(third, "dp", UP[:1])
    down3 = lax.ppermute(third, "dp", DOWN[:1])
    middle = pick(plane, [second, third, third, second])
    up2 = lax.ppermute(add_low(middle, up3), "dp", UP[:2])
    down2 = lax.ppermute(add_low(middle, down3), "dp", DOWN[:2])
    up1 = lax.ppermute(add_low(pick(plane, [first, first, second, second]), up2), "dp", UP)
    down1 = lax.ppermute(add_low(pick(plane, [second, second, first, first]), down2), "dp", DOWN)
    return own.astype(f32) + up1.astype(f32) + down1.astype(f32)


def slots_of(whole):
    count = lax.axis_size("dp")
    if count != 4:
        return [whole[i] for i in range(count)]
    plane = lax.axis_index("dp")
    table = jnp.array([[0, 1, 2, 3], [1, 2, 0, 3], [2, 1, 3, 0], [3, 2, 1, 0]], jnp.int32)
    mine = lax.dynamic_index_in_dim(table, plane, 0, keepdims=False)
    return [lax.dynamic_index_in_dim(whole, mine[i], 0, keepdims=False) for i in range(4)]


def in_order(blocks, planes):
    if lax.axis_size("dp") != 4:
        return jnp.stack(blocks)
    whole = jnp.zeros((4, *blocks[0].shape), blocks[0].dtype)
    for block, plane in zip(blocks, planes):
        whole = lax.dynamic_update_index_in_dim(whole, block, plane, 0)
    return whole


def block_rows_of(length):
    return math.gcd(length, 256)


def transposed_scores(keys, queries, starts, low, high, width):
    scores = dot_right_t(keys, queries) * score_scale
    key_pos = lax.broadcasted_iota(jnp.int32, (width, high - low), 0)
    query_pos = lax.broadcasted_iota(jnp.int32, (width, high - low), 1) + low
    allowed = (key_pos <= query_pos) & (key_pos >= starts)
    return scores, allowed


def attend_kernel(rows_of, q_ref, k_ref, vt_ref, starts_ref, out_ref, norm_ref):
    length = q_ref.shape[0]
    for low in range(0, length, rows_of):
        high = low + rows_of
        starts = starts_ref[:, low:high]
        scores, allowed = transposed_scores(
            k_ref[:high, :], q_ref[low:high, :], starts, low, high, high
        )
        scores = jnp.where(allowed, scores, mask_fill)
        top = jnp.max(scores, 0, keepdims=True)
        expo = jnp.exp(scores - top)
        total = jnp.sum(expo, 0, keepdims=True)
        probs = (expo * (1.0 / total)).astype(bf16)
        mixed = dot_plain(vt_ref[:, :high], probs)
        out_ref[low:high, :] = jnp.transpose(mixed).astype(out_ref.dtype)
        norm_ref[0, :, low:high] = top + jnp.log(total)


def attend(queries, keys, values, starts):
    length, width = queries.shape
    heads = width // HEAD_DIM
    return pl.pallas_call(
        functools.partial(attend_kernel, block_rows_of(length)),
        grid=(heads,),
        in_specs=[
            pl.BlockSpec((length, HEAD_DIM), lambda h: (0, h)),
            pl.BlockSpec((length, HEAD_DIM), lambda h: (0, 0)),
            pl.BlockSpec((HEAD_DIM, length), lambda h: (0, 0)),
            pl.BlockSpec((1, length), lambda h: (0, 0)),
        ],
        out_specs=[
            pl.BlockSpec((length, HEAD_DIM), lambda h: (0, h)),
            pl.BlockSpec((1, 1, length), lambda h: (h, 0, 0)),
        ],
        out_shape=[
            jax.ShapeDtypeStruct((length, width), bf16),
            jax.ShapeDtypeStruct((heads, 1, length), f32),
        ],
        compiler_params=pltpu.CompilerParams(vmem_limit_bytes=48 << 20),
        cost_estimate=pl.CostEstimate(
            flops=3 * heads * length * length * HEAD_DIM,
            bytes_accessed=8 * length * width,
            transcendentals=heads * length * length,
        ),
        name="attend",
    )(queries, keys, jnp.transpose(values), starts)


def attend_back_kernel(
    rows_of, q_ref, k_ref, kt_ref, v_ref, starts_ref, norm_ref, out_ref, grad_ref, dq_ref, dk_ref, dv_ref
):
    length = q_ref.shape[0]

    @pl.when(pl.program_id(0) == 0)
    def _():
        dk_ref[...] = jnp.zeros_like(dk_ref)
        dv_ref[...] = jnp.zeros_like(dv_ref)

    for low in range(0, length, rows_of):
        high = low + rows_of
        starts = starts_ref[:, low:high]
        queries = q_ref[low:high, :]
        grads = grad_ref[low:high, :]
        scores, allowed = transposed_scores(k_ref[:high, :], queries, starts, low, high, high)
        probs = jnp.where(allowed, jnp.exp(scores - norm_ref[0, :, low:high]), 0.0)
        grad_prob = dot_right_t(v_ref[:high, :], grads)
        weighed = jnp.transpose(grads.astype(f32) * out_ref[low:high, :].astype(f32))
        delta = jnp.sum(weighed, 0, keepdims=True)
        grad_score = (probs * (grad_prob - delta)).astype(bf16)
        dv_ref[:high, :] += dot_plain(probs.astype(bf16), grads)
        dk_ref[:high, :] += dot_plain(grad_score, queries)
        dq_ref[low:high, :] = jnp.transpose(dot_plain(kt_ref[:, :high], grad_score))


def attend_back(queries, keys, values, starts, norm, out, grads):
    length, width = queries.shape
    heads = width // HEAD_DIM
    by_head = pl.BlockSpec((length, HEAD_DIM), lambda h: (0, h))
    shared = pl.BlockSpec((length, HEAD_DIM), lambda h: (0, 0))
    return pl.pallas_call(
        functools.partial(attend_back_kernel, block_rows_of(length)),
        grid=(heads,),
        in_specs=[
            by_head,
            shared,
            pl.BlockSpec((HEAD_DIM, length), lambda h: (0, 0)),
            shared,
            pl.BlockSpec((1, length), lambda h: (0, 0)),
            pl.BlockSpec((1, 1, length), lambda h: (h, 0, 0)),
            by_head,
            by_head,
        ],
        out_specs=[by_head, shared, shared],
        out_shape=[
            jax.ShapeDtypeStruct((length, width), f32),
            jax.ShapeDtypeStruct((length, HEAD_DIM), f32),
            jax.ShapeDtypeStruct((length, HEAD_DIM), f32),
        ],
        compiler_params=pltpu.CompilerParams(vmem_limit_bytes=56 << 20),
        cost_estimate=pl.CostEstimate(
            flops=7 * heads * length * length * HEAD_DIM,
            bytes_accessed=16 * length * width,
            transcendentals=heads * length * length,
        ),
        name="attend_back",
    )(queries, keys, jnp.transpose(keys), values, starts, norm, out, grads)


def per_device(
    layer_input,
    output_grad,
    layer_keep,
    group_ids,
    exit_scale,
    doc_lengths,
    attention_gain,
    query_weight,
    key_weight,
    value_weight,
    output_weight,
    feedforward_gain,
    gate_weight,
    up_weight,
    down_weight,
):
    tokens, width = layer_input.shape[1:]
    ring = lax.axis_size("fsdp")
    planes = lax.axis_size("dp")
    place = lax.axis_index("fsdp")
    length = tokens * ring
    own_rows = query_weight.shape[0]
    heads = HEADS // ring
    own_width = heads * HEAD_DIM
    ff_own = gate_weight.shape[1]
    rows = layer_input[0].astype(f32)
    keep = layer_keep[0].astype(f32)

    inv_first = rms_scale(rows)
    normed = lax.all_gather((rows * inv_first).astype(bf16), "fsdp", axis=0, tiled=True)

    gain_mine = attention_gain.astype(f32)[:, None]
    sharers = ring // KV_HEADS
    cols = own_width + 2 * HEAD_DIM

    def spread(weight):
        heads_of = (weight.astype(f32) * gain_mine).astype(bf16).reshape(own_rows, KV_HEADS, 1, HEAD_DIM)
        return jnp.broadcast_to(heads_of, (own_rows, KV_HEADS, sharers, HEAD_DIM)).reshape(
            own_rows, ring, HEAD_DIM
        )

    query_scaled = (query_weight.astype(f32) * gain_mine).astype(bf16).reshape(own_rows, ring, own_width)
    sent = jnp.concatenate([query_scaled, spread(key_weight), spread(value_weight)], -1)
    sent = jnp.transpose(sent, (1, 0, 2)).reshape(ring * own_rows, cols)
    plane_cols = lax.all_to_all(sent, "fsdp", split_axis=0, concat_axis=0, tiled=True)
    project = in_order(*plane_gather(plane_cols)).reshape(width, cols)

    picked = jnp.sum(
        jnp.where(jnp.arange(exit_scale.shape[0], dtype=jnp.int32) == group_ids[0], exit_scale, 0.0)
    )
    cotangent = output_grad[0].astype(f32) * picked
    direct = keep * cotangent
    direct_all = plane_gather(after(direct.astype(bf16), plane_cols))[0]
    direct_all = jnp.concatenate(direct_all, 0)

    gain_second = lax.all_gather(
        lax.all_gather(feedforward_gain, "fsdp", axis=0, tiled=False), "dp", axis=0, tiled=False
    ).reshape(width).astype(f32)

    output_full = lax.all_gather(after(output_weight, normed), ("dp", "fsdp"), axis=0, tiled=True)
    gate_up = jnp.concatenate([gate_weight, up_weight], 1)
    gate_up = lax.all_gather(after(gate_up, output_full), "fsdp", axis=0, tiled=True)
    down_use = lax.all_gather(after(down_weight, gate_up), "fsdp", axis=0, tiled=True)

    cosine, sine_part = rotary_tables(length)
    ends = jnp.sum(
        jnp.where(
            jnp.arange(doc_lengths.shape[1])[None, :] <= jnp.arange(doc_lengths.shape[1])[:, None],
            doc_lengths[0][None, :],
            0,
        ),
        1,
    )
    positions = jnp.arange(length, dtype=jnp.int32)
    starts = jnp.max(jnp.where(positions[None, :] >= ends[:, None], ends[:, None], 0), 0)[None, :]
    raw = dot_plain(normed, project)
    rotated = rotate(
        raw[:, : own_width + HEAD_DIM].reshape(length, heads + 1, HEAD_DIM), cosine, sine_part
    ).astype(bf16)
    queries = rotated[:, :heads].reshape(length, own_width)
    keys = rotated[:, heads]
    values = raw[:, own_width + HEAD_DIM :].astype(bf16)
    mixed, norm = attend(queries, keys, values, starts)
    attended_low = lax.all_to_all(mixed, "fsdp", split_axis=0, concat_axis=1, tiled=True)
    branch_attention = dot_plain(attended_low, output_full)
    middle = rows + branch_attention
    inv_second = rms_scale(middle)
    second_mine = (middle * inv_second * gain_second).astype(bf16)

    second_all = jnp.concatenate(plane_gather(second_mine)[0], 0)
    gate_use, up_use = gate_up[:, :ff_own], gate_up[:, ff_own:]
    gate_pre = dot_plain(second_all, gate_use)
    upward = dot_plain(second_all, up_use)
    sigmoid_gate = 1.0 / (1.0 + jnp.exp(-gate_pre))
    silu_gate = gate_pre * sigmoid_gate
    hidden_low = (silu_gate * upward).astype(bf16)
    grad_hidden = dot_right_t(direct_all, down_use)
    grad_gate_low = (
        grad_hidden * upward * sigmoid_gate * (1.0 + gate_pre * (1.0 - sigmoid_gate))
    ).astype(bf16)
    grad_up_low = (grad_hidden * silu_gate).astype(bf16)
    grad_both = jnp.concatenate([grad_gate_low, grad_up_low], 1)
    second_terms = dot_right_t(grad_both, gate_up).astype(bf16).reshape(planes, tokens, width)
    grad_second = plane_scatter([second_terms[i] for i in range(planes)])

    down_term = dot_left_t(hidden_low, direct_all).astype(bf16)
    gate_up_term = dot_left_t(second_all, grad_both).astype(bf16)
    gate_up_grad = lax.psum_scatter(gate_up_term, "fsdp", scatter_dimension=0, tiled=True).astype(f32)
    down_grad = lax.psum_scatter(
        after(down_term, gate_up_grad), "fsdp", scatter_dimension=0, tiled=True
    ).astype(f32)
    branch_terms = dot_plain(hidden_low, down_use).astype(bf16).reshape(planes, tokens, width)
    branch_feed = plane_scatter(
        [after(branch_terms, grad_second)[i] for i in range(planes)]
    )
    output = (rows + keep * (branch_attention + branch_feed)).astype(bf16)

    second_gain_term = jnp.sum(grad_second * middle * inv_second, 0)
    weighted = grad_second * gain_second
    grad_middle = inv_second * weighted - middle * inv_second**3 * jnp.mean(
        weighted * middle, -1, keepdims=True
    )
    grad_branch_low = (direct + grad_middle).astype(bf16)
    grad_attended_low = dot_right_t(grad_branch_low, output_full).astype(bf16)
    grad_heads = lax.all_to_all(grad_attended_low, "fsdp", split_axis=1, concat_axis=0, tiled=True)
    attended_by_owner = jnp.transpose(
        attended_low.reshape(tokens, planes, ring, own_rows), (0, 2, 1, 3)
    ).reshape(tokens, width)
    output_term = dot_left_t(attended_by_owner, grad_branch_low).astype(bf16)
    output_plane = lax.psum_scatter(
        after(output_term, down_grad), "fsdp", scatter_dimension=0, tiled=True
    )

    dq, dk, dv = attend_back(queries, keys, values, starts, norm, mixed, grad_heads)
    turned = rotate(
        (jnp.concatenate([dq, dk], 1) * score_scale).reshape(length, heads + 1, HEAD_DIM),
        cosine,
        -sine_part,
    ).astype(bf16)
    grad_cols = jnp.concatenate([turned.reshape(length, own_width + HEAD_DIM), dv.astype(bf16)], 1)
    normed_terms = dot_right_t(grad_cols, project).astype(bf16)
    weighted_first = lax.psum_scatter(normed_terms, "fsdp", scatter_dimension=0, tiled=True).astype(f32)
    grad_rows = inv_first * weighted_first - rows * inv_first**3 * jnp.mean(
        weighted_first * rows, -1, keepdims=True
    )
    input_grad = cotangent + grad_middle + grad_rows

    project_term = dot_left_t(normed, grad_cols).astype(bf16).reshape(planes, ring * own_rows, cols)
    project_plane = plane_scatter(slots_of(project_term)).astype(bf16)
    back = lax.all_to_all(project_plane, "fsdp", split_axis=0, concat_axis=0, tiled=True)
    back = back.reshape(ring, own_rows, cols).astype(f32)

    def collect(low):
        parts = back[:, :, low : low + HEAD_DIM].reshape(KV_HEADS, sharers, own_rows, HEAD_DIM)
        return jnp.transpose(jnp.sum(parts, 1), (1, 0, 2)).reshape(own_rows, KV_HEADS * HEAD_DIM)

    query_plain = jnp.transpose(back[:, :, :own_width], (1, 0, 2)).reshape(own_rows, width)
    key_plain = collect(own_width)
    value_plain = collect(own_width + HEAD_DIM)
    first_gain_grad = (
        jnp.sum(query_plain * query_weight.astype(f32), 1)
        + jnp.sum(key_plain * key_weight.astype(f32), 1)
        + jnp.sum(value_plain * value_weight.astype(f32), 1)
    )
    output_grad_weight = plane_scatter(slots_of(output_plane.reshape(planes, own_rows, width)))
    second_gain_all = lax.psum(lax.psum(second_gain_term, "fsdp"), "dp")
    mine = (lax.axis_index("dp") * ring + place) * own_rows
    second_gain_grad = lax.dynamic_slice_in_dim(second_gain_all, mine, own_rows)
    return (
        output[None],
        input_grad[None],
        first_gain_grad,
        query_plain * gain_mine,
        key_plain * gain_mine,
        value_plain * gain_mine,
        output_grad_weight,
        second_gain_grad,
        gate_up_grad[:, :ff_own],
        gate_up_grad[:, ff_own:],
        down_grad,
    )


def solution(mesh):
    both = ("dp", "fsdp")
    return jax.shard_map(
        per_device,
        mesh=mesh,
        in_specs=(
            P("dp", "fsdp", None),
            P("dp", "fsdp", None),
            P("dp"),
            P("dp"),
            P(),
            P("dp", None),
            P(both),
            P(both, None),
            P(both, None),
            P(both, None),
            P(both, None),
            P(both),
            P("fsdp", "dp"),
            P("fsdp", "dp"),
            P(both, None),
        ),
        out_specs=(
            P("dp", "fsdp", None),
            P("dp", "fsdp", None),
            P(both),
            P(both, None),
            P(both, None),
            P(both, None),
            P(both, None),
            P(both),
            P("fsdp", "dp"),
            P("fsdp", "dp"),
            P(both, None),
        ),
        check_vma=False,
    )
```

time: 3800 us -> 898 us (0.24)
  waiting for transfers between devices: 3260 us -> 463 us
  matrix products: 253 us -> 116 us
  local copies, waits for them, and re-layouts: 143 us -> 24.8 us
  starting transfers between devices: 1.42 us -> 112 us
    all_gather x12 -> x4, waiting for transfers between devices: 1470 us -> 172 us  [the longest x1 79 us: per_device(): lax.all_gather(after(output_weight, normed), ('dp', 'fsdp'), axis=0, tile...]
    reduce_scatter x10 -> x4, waiting for transfers between devices: 1200 us -> 76.9 us  [the longest x1 76.8 us: per_device(): lax.psum_scatter(gate_up_term, 'fsdp', scatter_dimension=0, tiled=True)]
    unnamed x26 -> x8, waiting for transfers between devices: 592 us -> 0.13 us
    ppermute x0 -> x42, waiting for transfers between devices: none -> 197 us  [the longest x3 43.6 us: plane_gather(): down2 = lax.ppermute(down1, 'dp', DOWN[1:])]
    ppermute x0 -> x42, starting transfers between devices: none -> 100 us  [the longest x4 30.8 us: plane_scatter(): lax.ppermute(add_low(pick(plane, [first, first, second, second]), up2), '...]
    unnamed x101 -> x126, local copies, waits for them, and re-layouts: 97.3 us -> 8.21 us
    dot_general x28 -> x5, matrix products: 126 us -> 42.7 us  [dot_plain(): return jnp.dot(left, right, preferred_element_type=f32)]
    unnamed x2 -> x1, blocking collectives: 82.4 us -> 16.1 us
  transfers between devices with their start and end apart: 24 -> 53, of which waited for: 23 -> 26; matrix products, arithmetic and copies ran while one was open for 9% -> 16% of each run, Pallas kernels for 0% -> 2%
where the time goes in v2:
time: 898 us; the launch traced here: 888 us
  waiting for transfers between devices  463 us (52%)
  matrix products  116 us (13%)
  starting transfers between devices  112 us (12%)
  blocking collectives  66.9 us (7%)
  other arithmetic  57.6 us (6%)
  between operations  25.5 us (3%)
  local copies, waits for them, and re-layouts  24.8 us (3%)
  Pallas kernels  22.1 us (2%)
    all_gather x1, waiting for transfers between devices, per_device(): lax.all_gather(after(output_weight, normed), ('dp', 'fsdp'), axis=0, tile...  79 us
    reduce_scatter x1, waiting for transfers between devices, per_device(): lax.psum_scatter(gate_up_term, 'fsdp', scatter_dimension=0, tiled=True)  76.8 us
    all_gather x1, waiting for transfers between devices, per_device(): lax.all_gather((rows * inv_first).astype(bf16), 'fsdp', axis=0, tiled=True)  48.3 us
    all_gather x1, waiting for transfers between devices, per_device(): lax.all_gather(after(gate_up, output_full), 'fsdp', axis=0, tiled=True)  44.2 us
    ppermute x3, waiting for transfers between devices, plane_gather(): down2 = lax.ppermute(down1, 'dp', DOWN[1:])  43.6 us
    dot_general x5, matrix products, dot_plain(): return jnp.dot(left, right, preferred_element_type=f32)  42.7 us
    dot_general x4, matrix products, dot_left_t(): lax.dot_general(left, right, (((0,), (0,)), ((), ())), preferred_element_...  38.6 us
    ppermute x3, waiting for transfers between devices, plane_gather(): down3 = lax.ppermute(down2, 'dp', DOWN[2:])  38 us
  transfers between devices with their start and end apart: 53, of which 26 were waited for; matrix products, arithmetic and copies ran while one was open for 16% of the time, Pallas kernels for 2%

profile of v2, /device:TPU:0, one launch (start us, length us, event | category | flops | bytes accessed | tf_op | source)
XLA Modules:
  0.0 887.8 jit_solution(3237585360331288523)
XLA Ops:
  11.6 48.3 %all-gather.7.cloned.1.call-done = bf16[1536,2048]{1,0:T(8,128)(2,1)} async-done(((bf16[192,2048]{1,0:T(8,128)(2,1)}), bf16[1536,2048]{1,0:T(8,128)(2,1)}) %all-gather.7.cloned.1.call-update) | async-done | bytes 6291472 | tf_op jit(solution)/shard_map/all_gather | solution.py:283
  61.2 79.0 %all-gather.9.cloned.1.call-done = bf16[2048,2048]{1,0:T(8,128)(2,1)} async-done(((bf16[64,2048]{1,0:T(8,128)(2,1)}), bf16[2048,2048]{1,0:T(8,128)(2,1)}) %all-gather.9.cloned.1.call-update) | async-done | bytes 8388624 | tf_op jit(solution)/shard_map/all_gather | solution.py:313
  146.4 11.4 %all-to-all-done = bf16[8,64,512]{2,1,0:T(8,128)(2,1)S(1)} async-done(((bf16[8,64,512]{2,1,0:T(8,128)(2,1)}), bf16[8,64,512]{2,1,0:T(8,128)(2,1)S(1)}, u32[]{:S(2)}, u32[]{:S(2)}) %all-to-all-start) | async-done | bytes 524320 | tf_op jit(solution)/shard_map/all_to_all | solution.py:298
  159.1 5.3 collective-permute-start.1
  165.0 44.2 %all-gather.11.cloned.1.call-done = bf16[2048,2816]{1,0:T(8,128)(2,1)} async-done(((bf16[256,2816]{1,0:T(8,128)(2,1)}), bf16[2048,2816]{1,0:T(8,128)(2,1)}) %all-gather.11.cloned.1.call-update) | async-done | bytes 11534352 | tf_op jit(solution)/shard_map/all_gather | solution.py:315
  222.5 13.9 %collective-permute-done.2 = bf16[512,512]{1,0:T(8,128)(2,1)S(1)} collective-permute-done((bf16[512,512]{1,0:T(8,128)(2,1)}, bf16[512,512]{1,0:T(8,128)(2,1)S(1)}, u32[]{:S(2)}, u32[]{:S(2)}) %collective-permute-start.2) | collective-permute-done | bytes 524320 | tf_op jit(solution)/shard_map/ppermute | solution.py:80
  240.3 11.3 %collective-permute-done.4 = bf16[512,512]{1,0:T(8,128)(2,1)S(1)} collective-permute-done((bf16[512,512]{1,0:T(8,128)(2,1)S(1)}, bf16[512,512]{1,0:T(8,128)(2,1)S(1)}, u32[]{:S(2)}, u32[]{:S(2)}) %collective-permute-start.4) | collective-permute-done | bytes 524320 | tf_op jit(solution)/shard_map/ppermute | solution.py:82
  251.9 6.5 fusion.52
  262.6 10.4 %attend.1 = (bf16[1536,256]{1,0:T(8,128)(2,1)}, f32[2,1,1536]{2,1,0:T(1,128)S(1)}) custom-call(bf16[1536,256]{1,0:T(8,128)(2,1)S(1)} %copy.116.q_ref, bf16[1536,128]{1,0:T(8,128)(2,1)S(1)} %copy.117.k_ref, bf16[128,1536]{1,0:T(8,128)(2,1)S(1)} %copy.118.vt_ref, s32[1,1536]{1,0:T(1,128)S(1)} %broadcast_in_dim.96.starts_ref), custom_call_target="tpu_custom_call" | custom-call | flops 1811939328 | bytes 3145728 | tf_op jit(solution)/shard_map/attend/pallas_call | solution.py:166
  280.6 16.1 %all-reduce = bf16[512]{0:T(512)(128)(2,1)S(1)} all-reduce(bf16[512]{0:T(512)(128)(2,1)S(1)} %dynamic-update-slice), channel_id=2, replica_groups=mesh['dp'=4,'fsdp'=8] {'fsdp'}, use_global_device_ids=true, to_apply=%add | all-reduce | flops 512 | bytes 2048
  296.8 11.9 %all-gather.1 = bf16[32,64]{1,0:T(8,128)(2,1)S(1)} all-gather(bf16[8,64]{1,0:T(8,128)(2,1)S(1)} %reshape.291), channel_id=3, replica_groups=mesh['dp'=4,'fsdp'=8] {'dp'}, dimensions={0}, use_global_device_ids=true | all-gather | bytes 5120 | tf_op jit(solution)/shard_map/all_gather | solution.py:309
  312.3 5.5 collective-permute-start.13
  318.6 5.5 multiply_reduce_fusion.2
  327.9 7.2 collective-permute-done.13
  337.2 10.5 %collective-permute-done.7 = bf16[192,2048]{1,0:T(8,128)(2,1)S(1)} collective-permute-done((bf16[192,2048]{1,0:T(8,128)(2,1)S(1)}, bf16[192,2048]{1,0:T(8,128)(2,1)S(1)}, u32[]{:S(2)}, u32[]{:S(2)}) %collective-permute-start.7) | collective-permute-done | bytes 786464 | tf_op jit(solution)/shard_map/ppermute | solution.py:77
  351.1 14.8 %collective-permute-done.14 = bf16[192,2048]{1,0:T(8,128)(2,1)S(1)} collective-permute-done((bf16[192,2048]{1,0:T(8,128)(2,1)}, bf16[192,2048]{1,0:T(8,128)(2,1)S(1)}, u32[]{:S(2)}, u32[]{:S(2)}) %collective-permute-start.14) | collective-permute-done | bytes 786464 | tf_op jit(solution)/shard_map/ppermute | solution.py:80
  367.9 14.8 %collective-permute-done.8 = bf16[192,2048]{1,0:T(8,128)(2,1)S(1)} collective-permute-done((bf16[192,2048]{1,0:T(8,128)(2,1)S(1)}, bf16[192,2048]{1,0:T(8,128)(2,1)S(1)}, u32[]{:S(2)}, u32[]{:S(2)}) %collective-permute-start.8) | collective-permute-done | bytes 786464 | tf_op jit(solution)/shard_map/ppermute | solution.py:80
  384.1 15.5 %collective-permute-done.16 = bf16[192,2048]{1,0:T(8,128)(2,1)S(1)} collective-permute-done((bf16[192,2048]{1,0:T(8,128)(2,1)S(1)}, bf16[192,2048]{1,0:T(8,128)(2,1)S(1)}, u32[]{:S(2)}, u32[]{:S(2)}) %collective-permute-start.16) | collective-permute-done | bytes 786464 | tf_op jit(solution)/shard_map/ppermute | solution.py:82
  402.7 11.2 %collective-permute-done.10 = bf16[192,2048]{1,0:T(8,128)(2,1)S(1)} collective-permute-done((bf16[192,2048]{1,0:T(8,128)(2,1)S(1)}, bf16[192,2048]{1,0:T(8,128)(2,1)S(1)}, u32[]{:S(2)}, u32[]{:S(2)}) %collective-permute-start.10) | collective-permute-done | bytes 786464 | tf_op jit(solution)/shard_map/ppermute | solution.py:82
  415.5 8.7 fusion
  424.2 9.5 %fusion.28 = f32[768,1408]{1,0:T(8,128)S(1)} fusion(bf16[1408,2048]{1,0:T(8,128)(2,1)} %all-gather.13.cloned.1.call-done, bf16[192,2048]{1,0:T(8,128)(2,1)} %get-tuple-element.59, bf16[192,2048]{1,0:T(8,128)(2,1)} %get-tuple-element.58, bf16[192,2048]{1,0:T(8,128)(2,1)} %get-tuple-element.57, bf16[192,2048]{1,0:T(8,128)(2,1)} %fusion.20), kind=kOutput, calls=%fused_computation.103 | convolution fusion | flops 4441767936 | bytes 13238272 | tf_op jit(solution)/shard_map/dot_general | solution.py:28
  433.7 13.5 %multiply_convert_fusion.1 = (bf16[768,1408]{1,0:T(8,128)(2,1)}, bf16[768,1408]{1,0:T(8,128)(2,1)}, bf16[768,1408]{1,0:T(8,128)(2,1)}) fusion(f32[768,1408]{1,0:T(8,128)S(1)} %fusion.28, f32[768,1408]{1,0:T(8,128)} %fusion, bf16[2048,2816]{1,0:T(8,128)(2,1)} %all-gather.11.cloned.1.call-done, bf16[192,2048]{1,0:T(8,128)(2,1)S(1)} %copy-done.31, ...), kind=kOutput, calls=%fused_computation.10 | convolution fusion | flops 4457988096 | bytes 24051712 | tf_op jit(solution)/shard_map/dot_general | solution.py:24
  447.2 14.3 %convolution_convert_fusion = bf16[2048,2816]{1,0:T(8,128)(2,1)} fusion(bf16[768,1408]{1,0:T(8,128)(2,1)} %get-tuple-element.41, bf16[768,1408]{1,0:T(8,128)(2,1)} %get-tuple-element.40, bf16[192,2048]{1,0:T(8,128)(2,1)S(1)} %copy-done.31, bf16[192,2048]{1,0:T(8,128)(2,1)S(1)} %copy-done.29, bf16[192,2048]{1,0:T(8,128)(2,1)S(1)} %copy-done.27, ...), kind=kOutput, calls=%fused_computation | convolution fusion | flops 8885370880 | bytes 19005440 | tf_op jit(solution)/shard_map/dot_general | solution.py:32
  461.6 10.5 %convolution_convert_fusion.1 = bf16[1408,2048]{1,0:T(8,128)(2,1)} fusion(bf16[768,1408]{1,0:T(8,128)(2,1)} %get-tuple-element.42, bf16[192,2048]{1,0:T(8,128)(2,1)} %get-tuple-element.59, bf16[192,2048]{1,0:T(8,128)(2,1)} %get-tuple-element.58, bf16[192,2048]{1,0:T(8,128)(2,1)} %get-tuple-element.57, bf16[192,2048]{1,0:T(8,128)(2,1)} %fusion.20), kind=kOutput, calls=%fused_computation.1 | convolution fusion | flops 4444651520 | bytes 11075584 | tf_op jit(solution)/shard_map/dot_general | solution.py:32
  472.1 76.8 %reduce-scatter.7.cloned.1.call-done = bf16[256,2816]{1,0:T(8,128)(2,1)} async-done(((bf16[2048,2816]{1,0:T(8,128)(2,1)}), bf16[256,2816]{1,0:T(8,128)(2,1)}) %reduce-scatter.7.cloned.1.call-update) | async-done | bytes 1441808 | tf_op jit(solution)/shard_map/reduce_scatter | solution.py:361
  549.0 13.3 %convolution_convert_fusion.4 = bf16[768,2048]{1,0:T(8,128)(2,1)S(1)} fusion(bf16[2048,2816]{1,0:T(8,128)(2,1)} %all-gather.11.cloned.1.call-done, bf16[768,1408]{1,0:T(8,128)(2,1)} %get-tuple-element.41, bf16[768,1408]{1,0:T(8,128)(2,1)} %get-tuple-element.40), kind=kOutput, calls=%fused_computation.20 | convolution fusion | flops 8868593664 | bytes 19005440 | tf_op jit(solution)/shard_map/dot_general | solution.py:28
  566.8 15.8 %collective-permute-done.18 = bf16[192,2048]{1,0:T(8,128)(2,1)S(1)} collective-permute-done((bf16[192,2048]{1,0:T(8,128)(2,1)S(1)}, bf16[192,2048]{1,0:T(8,128)(2,1)S(1)}, u32[]{:S(2)}, u32[]{:S(2)}) %collective-permute-start.18) | collective-permute-done | bytes 786464 | tf_op jit(solution)/shard_map/ppermute | solution.py:104
  587.5 15.9 %collective-permute-done.19 = bf16[192,2048]{1,0:T(8,128)(2,1)S(1)} collective-permute-done((bf16[192,2048]{1,0:T(8,128)(2,1)S(1)}, bf16[192,2048]{1,0:T(8,128)(2,1)S(1)}, u32[]{:S(2)}, u32[]{:S(2)}) %collective-permute-start.19) | collective-permute-done | bytes 786464 | tf_op jit(solution)/shard_map/ppermute | solution.py:107
  605.8 5.9 collective-permute-start.20
  617.8 8.3 collective-permute-done.20
  626.1 19.4 %collective-permute-done.23 = bf16[192,2048]{1,0:T(8,128)(2,1)} collective-permute-done((bf16[192,2048]{1,0:T(8,128)(2,1)}, bf16[192,2048]{1,0:T(8,128)(2,1)}, u32[]{:S(2)}, u32[]{:S(2)}) %collective-permute-start.23) | collective-permute-done | bytes 786464 | tf_op jit(solution)/shard_map/ppermute | solution.py:110
  650.2 5.7 convolution_convert_fusion.2
  658.3 6.5 convolution_convert_fusion.7
  664.9 16.1 %all_to_all.56 = bf16[192,8,256]{2,0,1:T(8,128)(2,1)} all-to-all(bf16[192,8,256]{2,0,1:T(8,128)(2,1)S(1)} %bitcast.226), channel_id=1, replica_groups=mesh['dp'=4,'fsdp'=8] {'fsdp'}, dimensions={1} | all-to-all | bytes 1572864 | tf_op jit(solution)/shard_map/all_to_all | solution.py:378
  681.0 11.7 %attend_back.1 = (f32[1536,256]{1,0:T(8,128)}, f32[1536,128]{1,0:T(8,128)}, f32[1536,128]{1,0:T(8,128)}) custom-call(bf16[1536,256]{1,0:T(8,128)(2,1)} %copy-done, bf16[1536,128]{1,0:T(8,128)(2,1)} %copy-done.1, bf16[128,1536]{1,0:T(8,128)(2,1)} %get-tuple-element.67.kt_ref, bf16[1536,128]{1,0:T(8,128)(2,1)} %copy-done.18, s32[1,1536]{1,0:T(1,128)} %copy-done.2, ...), custom_call_target="tpu_custom_call" | custom-call | flops 4227858432 | bytes 6291456 | tf_op jit(solution)/shard_map/attend_back/pallas_call | solution.py:224
  707.2 5.4 convolution_convert_fusion.3
  712.7 8.5 convolution_convert_fusion.5
  721.2 8.1 convolution_convert_fusion.6
  736.0 9.3 %collective-permute-done.30 = bf16[512,512]{1,0:T(8,128)(2,1)S(1)} collective-permute-done((bf16[512,512]{1,0:T(8,128)(2,1)S(1)}, bf16[512,512]{1,0:T(8,128)(2,1)S(1)}, u32[]{:S(2)}, u32[]{:S(2)}) %collective-permute-start.30) | collective-permute-done | bytes 524320 | tf_op jit(solution)/shard_map/ppermute | solution.py:104
  750.8 11.3 %collective-permute-done.24 = bf16[192,2048]{1,0:T(8,128)(2,1)S(1)} collective-permute-done((bf16[192,2048]{1,0:T(8,128)(2,1)S(1)}, bf16[192,2048]{1,0:T(8,128)(2,1)S(1)}, u32[]{:S(2)}, u32[]{:S(2)}) %collective-permute-start.24) | collective-permute-done | bytes 786464 | tf_op jit(solution)/shard_map/ppermute | solution.py:104
  767.0 6.4 collective-permute-done.31
  776.0 5.8 collective-permute-start.32
  781.8 8.4 collective-permute-done.25
  793.7 12.1 %psum.14 = f32[2048]{0:T(1024)S(1)} all-reduce(f32[2048]{0:T(1024)S(1)} %get-tuple-element.35), channel_id=1, replica_groups=mesh['dp'=4,'fsdp'=8] {'fsdp'}, use_global_device_ids=true, to_apply=%region_17.18 | all-reduce | flops 2048 | bytes 16384 | tf_op jit(solution)/shard_map/psum | solution.py:419
  805.8 10.8 %psum.15 = f32[2048]{0:T(1024)S(1)} all-reduce(f32[2048]{0:T(1024)S(1)} %psum.14), channel_id=1, replica_groups=mesh['dp'=4,'fsdp'=8] {'dp'}, use_global_device_ids=true, to_apply=%region_18.19 | all-reduce | flops 2048 | bytes 16384 | tf_op jit(solution)/shard_map/psum | solution.py:419
  832.5 5.4 all-to-all-done.3
  854.5 5.1 fusion.11
  861.3 14.6 %collective-permute-start.38 = (bf16[64,2048]{1,0:T(8,128)(2,1)S(1)}, bf16[64,2048]{1,0:T(8,128)(2,1)S(1)}, u32[]{:S(2)}, u32[]{:S(2)}) collective-permute-start(bf16[64,2048]{1,0:T(8,128)(2,1)S(1)} %get-tuple-element.69), channel_id=1, source_target_pairs={{0,8},{8,16},{16,24},{1,9},{9,17},{17,25},{2,10},{10,18},{18,26},{... | collective-permute-start | bytes 786440 | tf_op jit(solution)/shard_map/ppermute | solution.py:109
  (296 shorter events, 155.8 us)
Async XLA Ops:
  7.2 52.7 %all-gather.7.cloned.1.call-start = ((), (), s32[]{:S(2)}) async-start(), calls=%async_computation.8 | async-start | bytes 7077888 | tf_op jit(solution)/shard_map/all_gather | solution.py:283
  11.5 128.7 %all-gather.9.cloned.1.call-start = ((), (), s32[]{:S(2)}) async-start(), calls=%async_computation.9 | async-start | bytes 8650752 | tf_op jit(solution)/shard_map/all_gather | solution.py:313
  60.0 149.3 %all-gather.11.cloned.1.call-start = ((), (), s32[]{:S(2)}) async-start(), calls=%async_computation.10 | async-start | bytes 12976128 | tf_op jit(solution)/shard_map/all_gather | solution.py:315
  142.1 15.6 %all-to-all-start = ((bf16[8,64,512]{2,1,0:T(8,128)(2,1)}), bf16[8,64,512]{2,1,0:T(8,128)(2,1)S(1)}, u32[]{:S(2)}, u32[]{:S(2)}) async-start(bf16[8,64,512]{2,1,0:T(8,128)(2,1)} %copy.114), calls=%async_computation | async-start | bytes 1048576 | tf_op jit(solution)/shard_map/all_to_all | solution.py:298
  145.6 278.6 %all-gather.13.cloned.1.call-start = ((), (), s32[]{:S(2)}) async-start(), calls=%async_computation.11 | async-start | bytes 6488064 | tf_op jit(solution)/shard_map/all_gather | solution.py:316
  157.8 60.3 %collective-permute-start = (bf16[512,512]{1,0:T(8,128)(2,1)S(1)}, bf16[512,512]{1,0:T(8,128)(2,1)}, u32[]{:S(2)}, u32[]{:S(2)}) collective-permute-start(bf16[512,512]{1,0:T(8,128)(2,1)S(1)} %bitcast.235), channel_id=1, source_target_pairs={{24,16},{16,8},{8,0},{25,17},{17,9},{9,1},{26,18},{18,10},{10,2},{... | collective-permute-start | bytes 1572872 | tf_op jit(solution)/shard_map/ppermute | solution.py:78
  159.1 58.3 %collective-permute-start.1 = (bf16[512,512]{1,0:T(8,128)(2,1)S(1)}, bf16[512,512]{1,0:T(8,128)(2,1)}, u32[]{:S(2)}, u32[]{:S(2)}) collective-permute-start(bf16[512,512]{1,0:T(8,128)(2,1)S(1)} %bitcast.236), channel_id=1, source_target_pairs={{0,8},{8,16},{16,24},{1,9},{9,17},{17,25},{2,10},{10,18},{18,26},{... | collective-permute-start | bytes 1572872 | tf_op jit(solution)/shard_map/ppermute | solution.py:77
  218.1 18.4 %collective-permute-start.2 = (bf16[512,512]{1,0:T(8,128)(2,1)}, bf16[512,512]{1,0:T(8,128)(2,1)S(1)}, u32[]{:S(2)}, u32[]{:S(2)}) collective-permute-start(bf16[512,512]{1,0:T(8,128)(2,1)} %collective-permute-done), channel_id=1, source_target_pairs={{16,8},{8,0},{17,9},{9,1},{18,10},{10,2},{19,11},{11,3},{20,12},{1... | collective-permute-start | bytes 1572872 | tf_op jit(solution)/shard_map/ppermute | solution.py:80
  221.8 18.5 %collective-permute-start.5 = (bf16[512,512]{1,0:T(8,128)(2,1)S(1)}, bf16[512,512]{1,0:T(8,128)(2,1)S(1)}, u32[]{:S(2)}, u32[]{:S(2)}) collective-permute-start(bf16[512,512]{1,0:T(8,128)(2,1)S(1)} %collective-permute-done.3), channel_id=1, source_target_pairs={{16,24},{17,25},{18,26},{19,27},{20,28},{21,29},{22,30},{23,31}} | collective-permute-start | bytes 1572872 | tf_op jit(solution)/shard_map/ppermute | solution.py:81
  236.5 15.2 %collective-permute-start.4 = (bf16[512,512]{1,0:T(8,128)(2,1)S(1)}, bf16[512,512]{1,0:T(8,128)(2,1)S(1)}, u32[]{:S(2)}, u32[]{:S(2)}) collective-permute-start(bf16[512,512]{1,0:T(8,128)(2,1)S(1)} %collective-permute-done.2), channel_id=1, source_target_pairs={{8,0},{9,1},{10,2},{11,3},{12,4},{13,5},{14,6},{15,7}} | collective-permute-start | bytes 1572872 | tf_op jit(solution)/shard_map/ppermute | solution.py:82
  273.6 44.1 %all-to-all-start.1 = ((bf16[8,192,256]{2,1,0:T(8,128)(2,1)}), bf16[8,192,256]{2,1,0:T(8,128)(2,1)S(1)}, u32[]{:S(2)}, u32[]{:S(2)}) async-start(bf16[8,192,256]{2,1,0:T(8,128)(2,1)} %bitcast.21), calls=%async_computation.1 | async-start | bytes 1572864 | tf_op jit(solution)/shard_map/all_to_all | solution.py:337
  277.8 271.2 %reduce-scatter.7.cloned.1.call-start = ((), (), s32[]{:S(2)}) async-start(), calls=%async_computation.13 | async-start | bytes 12976128 | tf_op jit(solution)/shard_map/reduce_scatter | solution.py:361
  311.0 24.8 %collective-permute-start.12 = (bf16[192,2048]{1,0:T(8,128)(2,1)}, bf16[192,2048]{1,0:T(8,128)(2,1)}, u32[]{:S(2)}, u32[]{:S(2)}) collective-permute-start(bf16[192,2048]{1,0:T(8,128)(2,1)} %fusion.20), channel_id=1, source_target_pairs={{24,16},{16,8},{8,0},{25,17},{17,9},{9,1},{26,18},{18,10},{10,2},{... | collective-permute-start | bytes 2359304 | tf_op jit(solution)/shard_map/ppermute | solution.py:78
  312.3 22.9 %collective-permute-start.13 = (bf16[192,2048]{1,0:T(8,128)(2,1)}, bf16[192,2048]{1,0:T(8,128)(2,1)}, u32[]{:S(2)}, u32[]{:S(2)}) collective-permute-start(bf16[192,2048]{1,0:T(8,128)(2,1)} %fusion.20), channel_id=1, source_target_pairs={{0,8},{8,16},{16,24},{1,9},{9,17},{17,25},{2,10},{10,18},{18,26},{... | collective-permute-start | bytes 2359304 | tf_op jit(solution)/shard_map/ppermute | solution.py:77
  325.0 22.6 %collective-permute-start.7 = (bf16[192,2048]{1,0:T(8,128)(2,1)S(1)}, bf16[192,2048]{1,0:T(8,128)(2,1)S(1)}, u32[]{:S(2)}, u32[]{:S(2)}) collective-permute-start(bf16[192,2048]{1,0:T(8,128)(2,1)S(1)} %multiply_convert_fusion.3), channel_id=1, source_target_pairs={{0,8},{8,16},{16,24},{1,9},{9,17},{17,25},{2,10},{10,18},{18,26},{... | collective-permute-start | bytes 2359304 | tf_op jit(solution)/shard_map/ppermute | solution.py:77
  326.6 22.4 %collective-permute-start.6 = (bf16[192,2048]{1,0:T(8,128)(2,1)S(1)}, bf16[192,2048]{1,0:T(8,128)(2,1)S(1)}, u32[]{:S(2)}, u32[]{:S(2)}) collective-permute-start(bf16[192,2048]{1,0:T(8,128)(2,1)S(1)} %multiply_convert_fusion.3), channel_id=1, source_target_pairs={{24,16},{16,8},{8,0},{25,17},{17,9},{9,1},{26,18},{18,10},{10,2},{... | collective-permute-start | bytes 2359304 | tf_op jit(solution)/shard_map/ppermute | solution.py:78
  335.1 15.2 %collective-permute-start.15 = (bf16[192,2048]{1,0:T(8,128)(2,1)}, bf16[192,2048]{1,0:T(8,128)(2,1)S(1)}, u32[]{:S(2)}, u32[]{:S(2)}) collective-permute-start(bf16[192,2048]{1,0:T(8,128)(2,1)} %collective-permute-done.13), channel_id=1, source_target_pairs={{8,16},{16,24},{9,17},{17,25},{10,18},{18,26},{11,19},{19,27},{12,... | collective-permute-start | bytes 2359304 | tf_op jit(solution)/shard_map/ppermute | solution.py:79
  335.9 30.1 %collective-permute-start.14 = (bf16[192,2048]{1,0:T(8,128)(2,1)}, bf16[192,2048]{1,0:T(8,128)(2,1)S(1)}, u32[]{:S(2)}, u32[]{:S(2)}) collective-permute-start(bf16[192,2048]{1,0:T(8,128)(2,1)} %collective-permute-done.12), channel_id=1, source_target_pairs={{16,8},{8,0},{17,9},{9,1},{18,10},{10,2},{19,11},{11,3},{20,12},{1... | collective-permute-start | bytes 2359304 | tf_op jit(solution)/shard_map/ppermute | solution.py:80
  347.6 19.6 %collective-permute-start.9 = (bf16[192,2048]{1,0:T(8,128)(2,1)S(1)}, bf16[192,2048]{1,0:T(8,128)(2,1)S(1)}, u32[]{:S(2)}, u32[]{:S(2)}) collective-permute-start(bf16[192,2048]{1,0:T(8,128)(2,1)S(1)} %collective-permute-done.7), channel_id=1, source_target_pairs={{8,16},{16,24},{9,17},{17,25},{10,18},{18,26},{11,19},{19,27},{12,... | collective-permute-start | bytes 2359304 | tf_op jit(solution)/shard_map/ppermute | solution.py:79
  349.1 33.7 %collective-permute-start.8 = (bf16[192,2048]{1,0:T(8,128)(2,1)S(1)}, bf16[192,2048]{1,0:T(8,128)(2,1)S(1)}, u32[]{:S(2)}, u32[]{:S(2)}) collective-permute-start(bf16[192,2048]{1,0:T(8,128)(2,1)S(1)} %collective-permute-done.6), channel_id=1, source_target_pairs={{16,8},{8,0},{17,9},{9,1},{18,10},{10,2},{19,11},{11,3},{20,12},{1... | collective-permute-start | bytes 2359304 | tf_op jit(solution)/shard_map/ppermute | solution.py:80
  350.4 33.7 %collective-permute-start.17 = (bf16[192,2048]{1,0:T(8,128)(2,1)S(1)}, bf16[192,2048]{1,0:T(8,128)(2,1)S(1)}, u32[]{:S(2)}, u32[]{:S(2)}) collective-permute-start(bf16[192,2048]{1,0:T(8,128)(2,1)S(1)} %collective-permute-done.15), channel_id=1, source_target_pairs={{16,24},{17,25},{18,26},{19,27},{20,28},{21,29},{22,30},{23,31}} | collective-permute-start | bytes 2359304 | tf_op jit(solution)/shard_map/ppermute | solution.py:81
  365.9 33.7 %collective-permute-start.16 = (bf16[192,2048]{1,0:T(8,128)(2,1)S(1)}, bf16[192,2048]{1,0:T(8,128)(2,1)S(1)}, u32[]{:S(2)}, u32[]{:S(2)}) collective-permute-start(bf16[192,2048]{1,0:T(8,128)(2,1)S(1)} %collective-permute-done.14), channel_id=1, source_target_pairs={{8,0},{9,1},{10,2},{11,3},{12,4},{13,5},{14,6},{15,7}} | collective-permute-start | bytes 2359304 | tf_op jit(solution)/shard_map/ppermute | solution.py:82
  367.2 35.5 %collective-permute-start.11 = (bf16[192,2048]{1,0:T(8,128)(2,1)S(1)}, bf16[192,2048]{1,0:T(8,128)(2,1)S(1)}, u32[]{:S(2)}, u32[]{:S(2)}) collective-permute-start(bf16[192,2048]{1,0:T(8,128)(2,1)S(1)} %collective-permute-done.9), channel_id=1, source_target_pairs={{16,24},{17,25},{18,26},{19,27},{20,28},{21,29},{22,30},{23,31}} | collective-permute-start | bytes 2359304 | tf_op jit(solution)/shard_map/ppermute | solution.py:81
  382.8 31.1 %collective-permute-start.10 = (bf16[192,2048]{1,0:T(8,128)(2,1)S(1)}, bf16[192,2048]{1,0:T(8,128)(2,1)S(1)}, u32[]{:S(2)}, u32[]{:S(2)}) collective-permute-start(bf16[192,2048]{1,0:T(8,128)(2,1)S(1)} %collective-permute-done.8), channel_id=1, source_target_pairs={{8,0},{9,1},{10,2},{11,3},{12,4},{13,5},{14,6},{15,7}} | collective-permute-start | bytes 2359304 | tf_op jit(solution)/shard_map/ppermute | solution.py:82
  461.6 194.2 %reduce-scatter.9.cloned.1.call-start = ((), (), s32[]{:S(2)}) async-start(), calls=%async_computation.14 | async-start | bytes 6488064 | tf_op jit(solution)/shard_map/reduce_scatter | solution.py:362
  549.0 292.7 %reduce-scatter.11.cloned.1.call-start = ((), (), s32[]{:S(2)}) async-start(), calls=%async_computation.15 | async-start | bytes 9437184 | tf_op jit(solution)/shard_map/reduce_scatter | solution.py:383
  562.4 20.2 %collective-permute-start.18 = (bf16[192,2048]{1,0:T(8,128)(2,1)S(1)}, bf16[192,2048]{1,0:T(8,128)(2,1)S(1)}, u32[]{:S(2)}, u32[]{:S(2)}) collective-permute-start(bf16[192,2048]{1,0:T(8,128)(2,1)S(1)} %slice.168), channel_id=1, source_target_pairs={{0,8},{1,9},{2,10},{3,11},{4,12},{5,13},{6,14},{7,15}} | collective-permute-start | bytes 2359304 | tf_op jit(solution)/shard_map/ppermute | solution.py:104
  565.9 21.6 %collective-permute-start.21 = (bf16[192,2048]{1,0:T(8,128)(2,1)S(1)}, bf16[192,2048]{1,0:T(8,128)(2,1)S(1)}, u32[]{:S(2)}, u32[]{:S(2)}) collective-permute-start(bf16[192,2048]{1,0:T(8,128)(2,1)S(1)} %slice.168), channel_id=1, source_target_pairs={{24,16},{25,17},{26,18},{27,19},{28,20},{29,21},{30,22},{31,23}} | collective-permute-start | bytes 2359304 | tf_op jit(solution)/shard_map/ppermute | solution.py:105
  583.0 20.4 %collective-permute-start.19 = (bf16[192,2048]{1,0:T(8,128)(2,1)S(1)}, bf16[192,2048]{1,0:T(8,128)(2,1)S(1)}, u32[]{:S(2)}, u32[]{:S(2)}) collective-permute-start(bf16[192,2048]{1,0:T(8,128)(2,1)S(1)} %fusion.5), channel_id=1, source_target_pairs={{0,8},{8,16},{1,9},{9,17},{2,10},{10,18},{3,11},{11,19},{4,12},{12... | collective-permute-start | bytes 2359304 | tf_op jit(solution)/shard_map/ppermute | solution.py:107
  605.8 20.4 %collective-permute-start.20 = (bf16[192,2048]{1,0:T(8,128)(2,1)}, bf16[192,2048]{1,0:T(8,128)(2,1)}, u32[]{:S(2)}, u32[]{:S(2)}) collective-permute-start(bf16[192,2048]{1,0:T(8,128)(2,1)} %get-tuple-element.47), channel_id=1, source_target_pairs={{0,8},{8,16},{16,24},{1,9},{9,17},{17,25},{2,10},{10,18},{18,26},{... | collective-permute-start | bytes 2359304 | tf_op jit(solution)/shard_map/ppermute | solution.py:109
  613.0 32.5 %collective-permute-start.23 = (bf16[192,2048]{1,0:T(8,128)(2,1)}, bf16[192,2048]{1,0:T(8,128)(2,1)}, u32[]{:S(2)}, u32[]{:S(2)}) collective-permute-start(bf16[192,2048]{1,0:T(8,128)(2,1)} %add_convert_fusion.3), channel_id=1, source_target_pairs={{24,16},{16,8},{8,0},{25,17},{17,9},{9,1},{26,18},{18,10},{10,2},{... | collective-permute-start | bytes 2359304 | tf_op jit(solution)/shard_map/ppermute | solution.py:110
  658.2 187.8 %reduce-scatter.5.cloned.1.call-start = ((), (), s32[]{:S(2)}) async-start(), calls=%async_computation.12 | async-start | bytes 7077888 | tf_op jit(solution)/shard_map/reduce_scatter | solution.py:395
  729.4 15.9 %collective-permute-start.30 = (bf16[512,512]{1,0:T(8,128)(2,1)S(1)}, bf16[512,512]{1,0:T(8,128)(2,1)S(1)}, u32[]{:S(2)}, u32[]{:S(2)}) collective-permute-start(bf16[512,512]{1,0:T(8,128)(2,1)S(1)} %dynamic-slice_bitcast_fusion), channel_id=1, source_target_pairs={{0,8},{1,9},{2,10},{3,11},{4,12},{5,13},{6,14},{7,15}} | collective-permute-start | bytes 1572872 | tf_op jit(solution)/shard_map/ppermute | solution.py:104
  733.0 12.3 %collective-permute-start.33 = (bf16[512,512]{1,0:T(8,128)(2,1)S(1)}, bf16[512,512]{1,0:T(8,128)(2,1)S(1)}, u32[]{:S(2)}, u32[]{:S(2)}) collective-permute-start(bf16[512,512]{1,0:T(8,128)(2,1)S(1)} %dynamic-slice_bitcast_fusion), channel_id=1, source_target_pairs={{24,16},{25,17},{26,18},{27,19},{28,20},{29,21},{30,22},{31,23}} | collective-permute-start | bytes 1572872 | tf_op jit(solution)/shard_map/ppermute | solution.py:105
  733.7 28.4 %collective-permute-start.24 = (bf16[192,2048]{1,0:T(8,128)(2,1)S(1)}, bf16[192,2048]{1,0:T(8,128)(2,1)S(1)}, u32[]{:S(2)}, u32[]{:S(2)}) collective-permute-start(bf16[192,2048]{1,0:T(8,128)(2,1)S(1)} %slice_bitcast_fusion), channel_id=1, source_target_pairs={{0,8},{1,9},{2,10},{3,11},{4,12},{5,13},{6,14},{7,15}} | collective-permute-start | bytes 2359304 | tf_op jit(solution)/shard_map/ppermute | solution.py:104
  735.1 46.7 %collective-permute-start.27 = (bf16[192,2048]{1,0:T(8,128)(2,1)S(1)}, bf16[192,2048]{1,0:T(8,128)(2,1)S(1)}, u32[]{:S(2)}, u32[]{:S(2)}) collective-permute-start(bf16[192,2048]{1,0:T(8,128)(2,1)S(1)} %slice_bitcast_fusion), channel_id=1, source_target_pairs={{24,16},{25,17},{26,18},{27,19},{28,20},{29,21},{30,22},{31,23}} | collective-permute-start | bytes 2359304 | tf_op jit(solution)/shard_map/ppermute | solution.py:105
  745.7 27.7 %collective-permute-start.31 = (bf16[512,512]{1,0:T(8,128)(2,1)S(1)}, bf16[512,512]{1,0:T(8,128)(2,1)S(1)}, u32[]{:S(2)}, u32[]{:S(2)}) collective-permute-start(bf16[512,512]{1,0:T(8,128)(2,1)S(1)} %get-tuple-element.51), channel_id=1, source_target_pairs={{0,8},{8,16},{1,9},{9,17},{2,10},{10,18},{3,11},{11,19},{4,12},{12... | collective-permute-start | bytes 1572872 | tf_op jit(solution)/shard_map/ppermute | solution.py:107
  750.1 23.3 %collective-permute-start.34 = (bf16[512,512]{1,0:T(8,128)(2,1)S(1)}, bf16[512,512]{1,0:T(8,128)(2,1)S(1)}, u32[]{:S(2)}, u32[]{:S(2)}) collective-permute-start(bf16[512,512]{1,0:T(8,128)(2,1)S(1)} %get-tuple-element.52), channel_id=1, source_target_pairs={{24,16},{16,8},{25,17},{17,9},{26,18},{18,10},{27,19},{19,11},{28,... | collective-permute-start | bytes 1572872 | tf_op jit(solution)/shard_map/ppermute | solution.py:108
  762.6 27.7 %collective-permute-start.25 = (bf16[192,2048]{1,0:T(8,128)(2,1)S(1)}, bf16[192,2048]{1,0:T(8,128)(2,1)S(1)}, u32[]{:S(2)}, u32[]{:S(2)}) collective-permute-start(bf16[192,2048]{1,0:T(8,128)(2,1)S(1)} %fusion.7), channel_id=1, source_target_pairs={{0,8},{8,16},{1,9},{9,17},{2,10},{10,18},{3,11},{11,19},{4,12},{12... | collective-permute-start | bytes 2359304 | tf_op jit(solution)/shard_map/ppermute | solution.py:107
  774.7 46.9 %collective-permute-start.35 = (bf16[512,512]{1,0:T(8,128)(2,1)}, bf16[512,512]{1,0:T(8,128)(2,1)}, u32[]{:S(2)}, u32[]{:S(2)}) collective-permute-start(bf16[512,512]{1,0:T(8,128)(2,1)} %get-tuple-element.56), channel_id=1, source_target_pairs={{24,16},{16,8},{8,0},{25,17},{17,9},{9,1},{26,18},{18,10},{10,2},{... | collective-permute-start | bytes 1572872 | tf_op jit(solution)/shard_map/ppermute | solution.py:110
  776.0 45.6 %collective-permute-start.32 = (bf16[512,512]{1,0:T(8,128)(2,1)}, bf16[512,512]{1,0:T(8,128)(2,1)}, u32[]{:S(2)}, u32[]{:S(2)}) collective-permute-start(bf16[512,512]{1,0:T(8,128)(2,1)} %get-tuple-element.55), channel_id=1, source_target_pairs={{0,8},{8,16},{16,24},{1,9},{9,17},{17,25},{2,10},{10,18},{18,26},{... | collective-permute-start | bytes 1572872 | tf_op jit(solution)/shard_map/ppermute | solution.py:109
  792.1 36.0 %collective-permute-start.28 = (bf16[192,2048]{1,0:T(8,128)(2,1)}, bf16[192,2048]{1,0:T(8,128)(2,1)}, u32[]{:S(2)}, u32[]{:S(2)}) collective-permute-start(bf16[192,2048]{1,0:T(8,128)(2,1)} %get-tuple-element.46), channel_id=1, source_target_pairs={{24,16},{16,8},{25,17},{17,9},{26,18},{18,10},{27,19},{19,11},{28,... | collective-permute-start | bytes 2359304 | tf_op jit(solution)/shard_map/ppermute | solution.py:108
  817.2 37.3 %collective-permute-start.26 = (bf16[192,2048]{1,0:T(8,128)(2,1)}, bf16[192,2048]{1,0:T(8,128)(2,1)}, u32[]{:S(2)}, u32[]{:S(2)}) collective-permute-start(bf16[192,2048]{1,0:T(8,128)(2,1)} %get-tuple-element.45), channel_id=1, source_target_pairs={{0,8},{8,16},{16,24},{1,9},{9,17},{17,25},{2,10},{10,18},{18,26},{... | collective-permute-start | bytes 2359304 | tf_op jit(solution)/shard_map/ppermute | solution.py:109
  824.0 13.9 %all-to-all-start.3 = ((bf16[8,64,512]{2,1,0:T(8,128)(2,1)}), bf16[8,64,512]{2,1,0:T(8,128)(2,1)}, u32[]{:S(2)}, u32[]{:S(2)}) async-start(bf16[8,64,512]{2,1,0:T(8,128)(2,1)} %bitcast.232), calls=%async_computation.4 | async-start | bytes 1048576 | tf_op jit(solution)/shard_map/all_to_all | solution.py:403
  831.0 23.4 %collective-permute-start.29 = (bf16[192,2048]{1,0:T(8,128)(2,1)}, bf16[192,2048]{1,0:T(8,128)(2,1)}, u32[]{:S(2)}, u32[]{:S(2)}) collective-permute-start(bf16[192,2048]{1,0:T(8,128)(2,1)} %add_convert_fusion.1), channel_id=1, source_target_pairs={{24,16},{16,8},{8,0},{25,17},{17,9},{9,1},{26,18},{18,10},{10,2},{... | collective-permute-start | bytes 2359304 | tf_op jit(solution)/shard_map/ppermute | solution.py:110
  849.2 10.4 %collective-permute-start.37 = (bf16[64,2048]{1,0:T(8,128)(2,1)S(1)}, bf16[64,2048]{1,0:T(8,128)(2,1)S(1)}, u32[]{:S(2)}, u32[]{:S(2)}) collective-permute-start(bf16[64,2048]{1,0:T(8,128)(2,1)S(1)} %get-tuple-element.65), channel_id=1, source_target_pairs={{0,8},{8,16},{1,9},{9,17},{2,10},{10,18},{3,11},{11,19},{4,12},{12... | collective-permute-start | bytes 786440 | tf_op jit(solution)/shard_map/ppermute | solution.py:107
  859.8 18.9 %collective-permute-start.41 = (bf16[64,2048]{1,0:T(8,128)(2,1)S(1)}, bf16[64,2048]{1,0:T(8,128)(2,1)S(1)}, u32[]{:S(2)}, u32[]{:S(2)}) collective-permute-start(bf16[64,2048]{1,0:T(8,128)(2,1)S(1)} %get-tuple-element.70), channel_id=1, source_target_pairs={{24,16},{16,8},{8,0},{25,17},{17,9},{9,1},{26,18},{18,10},{10,2},{... | collective-permute-start | bytes 786440 | tf_op jit(solution)/shard_map/ppermute | solution.py:110
  861.3 18.6 %collective-permute-start.38 = (bf16[64,2048]{1,0:T(8,128)(2,1)S(1)}, bf16[64,2048]{1,0:T(8,128)(2,1)S(1)}, u32[]{:S(2)}, u32[]{:S(2)}) collective-permute-start(bf16[64,2048]{1,0:T(8,128)(2,1)S(1)} %get-tuple-element.69), channel_id=1, source_target_pairs={{0,8},{8,16},{16,24},{1,9},{9,17},{17,25},{2,10},{10,18},{18,26},{... | collective-permute-start | bytes 786440 | tf_op jit(solution)/shard_map/ppermute | solution.py:109
  (65 other events, 1660.9 us)
Sparse Core Ops, SparseCore 0:
  11.6 48.2 all-gather.6
  62.8 77.4 all-gather.8
  142.7 66.4 all-gather.10
  211.0 43.3 all-gather.12
  461.7 87.1 reduce-scatter.6
  552.3 59.0 reduce-scatter.8
  658.4 70.0 reduce-scatter.10
  731.8 61.7 reduce-scatter.4

commit v3 on v2

--- a/solution.py
+++ b/solution.py
@@ -128,6 +128,31 @@
     for block, plane in zip(blocks, planes):
         whole = lax.dynamic_update_index_in_dim(whole, block, plane, 0)
     return whole
+
+
+FLIP = {bit: [(i, i ^ bit) for i in range(8)] for bit in (1, 2, 4, 6)}
+
+
+def flip(block, bit):
+    return lax.ppermute(block, "fsdp", FLIP[bit])
+
+
+def output_rows(term):
+    place = lax.axis_index("fsdp")
+    plane = lax.axis_index("dp")
+    rows = term.shape[0] // 4
+    blocks = term.reshape(4, rows, term.shape[1])
+    y, x, core = place // 4, (place // 2) % 2, place % 2
+    by_group = jnp.zeros_like(blocks)
+    for a in (0, 1):
+        for b in (0, 1):
+            sent = lax.dynamic_index_in_dim(blocks, 2 * (x ^ a) + (y ^ b), 0, keepdims=False)
+            moves = [
+                (i, 4 * (i % 2) + 2 * ((i // 2) % 2 ^ a) + ((i // 4) ^ b)) for i in range(8)
+            ]
+            got = lax.ppermute(sent, "fsdp", moves)
+            by_group = lax.dynamic_update_index_in_dim(by_group, got, 2 * (core ^ b) + (x ^ a), 0)
+    return plane_scatter(slots_of(by_group))
 
 
 def block_rows_of(length):
@@ -303,17 +328,17 @@
     )
     cotangent = output_grad[0].astype(f32) * picked
     direct = keep * cotangent
-    direct_all = plane_gather(after(direct.astype(bf16), plane_cols))[0]
+    direct_all = plane_gather(after(direct.astype(bf16), project))[0]
     direct_all = jnp.concatenate(direct_all, 0)
 
     gain_second = lax.all_gather(
         lax.all_gather(feedforward_gain, "fsdp", axis=0, tiled=False), "dp", axis=0, tiled=False
     ).reshape(width).astype(f32)
 
-    output_full = lax.all_gather(after(output_weight, normed), ("dp", "fsdp"), axis=0, tiled=True)
+    output_full = lax.all_gather(output_weight, ("dp", "fsdp"), axis=0, tiled=True)
     gate_up = jnp.concatenate([gate_weight, up_weight], 1)
-    gate_up = lax.all_gather(after(gate_up, output_full), "fsdp", axis=0, tiled=True)
-    down_use = lax.all_gather(after(down_weight, gate_up), "fsdp", axis=0, tiled=True)
+    gate_up = lax.all_gather(gate_up, "fsdp", axis=0, tiled=True)
+    down_use = lax.all_gather(down_weight, "fsdp", axis=0, tiled=True)
 
     cosine, sine_part = rotary_tables(length)
     ends = jnp.sum(
@@ -358,14 +383,13 @@
 
     down_term = dot_left_t(hidden_low, direct_all).astype(bf16)
     gate_up_term = dot_left_t(second_all, grad_both).astype(bf16)
-    gate_up_grad = lax.psum_scatter(gate_up_term, "fsdp", scatter_dimension=0, tiled=True).astype(f32)
-    down_grad = lax.psum_scatter(
-        after(down_term, gate_up_grad), "fsdp", scatter_dimension=0, tiled=True
+    down_grad = lax.psum_scatter(down_term, "fsdp", scatter_dimension=0, tiled=True).astype(f32)
+    gate_up_grad = lax.psum_scatter(
+        after(gate_up_term, down_term), "fsdp", scatter_dimension=0, tiled=True
     ).astype(f32)
     branch_terms = dot_plain(hidden_low, down_use).astype(bf16).reshape(planes, tokens, width)
-    branch_feed = plane_scatter(
-        [after(branch_terms, grad_second)[i] for i in range(planes)]
-    )
+    branch_terms = after(branch_terms, grad_second)
+    branch_feed = plane_scatter([branch_terms[i] for i in range(planes)])
     output = (rows + keep * (branch_attention + branch_feed)).astype(bf16)
 
     second_gain_term = jnp.sum(grad_second * middle * inv_second, 0)
@@ -376,14 +400,6 @@
     grad_branch_low = (direct + grad_middle).astype(bf16)
     grad_attended_low = dot_right_t(grad_branch_low, output_full).astype(bf16)
     grad_heads = lax.all_to_all(grad_attended_low, "fsdp", split_axis=1, concat_axis=0, tiled=True)
-    attended_by_owner = jnp.transpose(
-        attended_low.reshape(tokens, planes, ring, own_rows), (0, 2, 1, 3)
-    ).reshape(tokens, width)
-    output_term = dot_left_t(attended_by_owner, grad_branch_low).astype(bf16)
-    output_plane = lax.psum_scatter(
-        after(output_term, down_grad), "fsdp", scatter_dimension=0, tiled=True
-    )
-
     dq, dk, dv = attend_back(queries, keys, values, starts, norm, mixed, grad_heads)
     turned = rotate(
         (jnp.concatenate([dq, dk], 1) * score_scale).reshape(length, heads + 1, HEAD_DIM),
@@ -415,7 +431,14 @@
         + jnp.sum(key_plain * key_weight.astype(f32), 1)
         + jnp.sum(value_plain * value_weight.astype(f32), 1)
     )
-    output_grad_weight = plane_scatter(slots_of(output_plane.reshape(planes, own_rows, width)))
+    attended_by_owner = jnp.transpose(
+        attended_low.reshape(tokens, planes, ring, own_rows), (0, 2, 1, 3)
+    ).reshape(tokens, width)
+    output_term = dot_left_t(attended_by_owner, grad_branch_low).astype(bf16)
+    output_plane = lax.psum_scatter(output_term, "fsdp", scatter_dimension=0, tiled=True)
+    output_grad_weight = plane_scatter(
+        slots_of(output_plane.reshape(planes, own_rows, width))
+    )
     second_gain_all = lax.psum(lax.psum(second_gain_term, "fsdp"), "dp")
     mine = (lax.axis_index("dp") * ring + place) * own_rows
     second_gain_grad = lax.dynamic_slice_in_dim(second_gain_all, mine, own_rows)
@@ -434,10 +457,559 @@
     )
 
 
+PIECES = ((0, 0), (2, 0), (4, 0), (6, 0), (6, 1), (1, 0), (3, 0), (5, 0), (7, 0), (7, 1))
+TO_CORE = (7, 3, 5, 1)
+TO_CHIPS = (6, 2, 4, 0)
+SLOT_HOPS = (
+    (("down", 1), ("down", 1), ("up", 1), ("up", 1)),
+    (("down", 2), ("up", 1), ("down", 1), ("up", 2)),
+    (("down", 3), ("down", 2), ("up", 2), ("up", 3)),
+)
+VMEM = pl.BlockSpec(memory_space=pltpu.VMEM)
+SMEM = pl.BlockSpec(memory_space=pltpu.SMEM)
+log2_e = math.log2(math.e)
+
+
+def start_of(place, piece, rows):
+    bit, half = PIECES[piece]
+    return pl.multiple_of((place ^ bit) * rows + half * (rows // 2), rows // 2)
+
+
+def turn(block, cosine, sine, forward):
+    rolled = pltpu.roll(block, HEAD_DIM // 2, 1)
+    return block * cosine + rolled * sine if forward else block * cosine - rolled * sine
+
+
+def masked_scores(keys, queries, starts, low):
+    scores = dot_right_t(keys, queries) * (score_scale * log2_e)
+    key_pos = lax.broadcasted_iota(jnp.int32, scores.shape, 0)
+    query_pos = lax.broadcasted_iota(jnp.int32, scores.shape, 1) + low
+    return scores, (key_pos <= query_pos) & (key_pos >= starts)
+
+
+def front_kernel(tokens, at_ref, *refs):
+    pieces, refs = refs[:10], refs[10:]
+    hops, refs = refs[:7], refs[7:]
+    cos_ref, sin_ref, starts_ref, refs = refs[0], refs[1], refs[2], refs[3:]
+    q_ref, k_ref, v_ref, mixed_ref, norm_ref, project_ref, gain_ref, vt_ref = refs
+    place, plane = at_ref[0], at_ref[1]
+    length = 8 * tokens
+    plane_rows = hops[0].shape[0] - 16
+
+    def put(ref, owner):
+        project_ref[pl.ds(pl.multiple_of(owner * plane_rows, plane_rows), plane_rows), :] = ref[:plane_rows, :]
+        gain_ref[owner] = ref[plane_rows:, :]
+
+    put(hops[0], plane)
+    for hop in (1, 2, 3):
+
+        @pl.when(plane >= hop)
+        def _():
+            put(hops[2 * hop - 1], plane - hop)
+
+        @pl.when(plane + hop <= 3)
+        def _():
+            put(hops[2 * hop], plane + hop)
+
+    q_width = q_ref.shape[1]
+    for piece in range(10):
+        here = pl.ds(start_of(place, piece, tokens), pieces[piece].shape[0])
+        raw = dot_plain(pieces[piece][...], project_ref[...])
+        cosine, sine = cos_ref[here, :], sin_ref[here, :]
+        for low in range(0, q_width, HEAD_DIM):
+            q_ref[here, low : low + HEAD_DIM] = turn(
+                raw[:, low : low + HEAD_DIM], cosine, sine, True
+            ).astype(bf16)
+        k_ref[here, :] = turn(raw[:, q_width : q_width + HEAD_DIM], cosine, sine, True).astype(bf16)
+        v_ref[here, :] = raw[:, q_width + HEAD_DIM :].astype(bf16)
+    vt_ref[...] = jnp.transpose(v_ref[...].astype(f32)).astype(bf16)
+    block = 256
+    for head in range(q_width // HEAD_DIM):
+        cols = slice(head * HEAD_DIM, (head + 1) * HEAD_DIM)
+        for low in range(0, length, block):
+            high = low + block
+            scores, allowed = masked_scores(
+                k_ref[:high, :], q_ref[low:high, cols], starts_ref[:, low:high], low
+            )
+            scores = jnp.where(allowed, scores, mask_fill)
+            top = jnp.max(scores, 0, keepdims=True)
+            expo = jnp.exp2(scores - top)
+            total = jnp.sum(expo, 0, keepdims=True)
+            probs = (expo * (1.0 / total)).astype(bf16)
+            mixed_ref[low:high, cols] = jnp.transpose(dot_plain(vt_ref[:, :high], probs)).astype(bf16)
+            norm_ref[head, :, low:high] = top + jnp.log2(total)
+
+
+def front(at, pieces, hops, cosine, sine, starts):
+    tokens = pieces[0].shape[0]
+    length = 8 * tokens
+    plane_rows, cols = hops[0].shape[0] - 16, hops[0].shape[1]
+    q_width = cols - 2 * HEAD_DIM
+    width = 4 * plane_rows
+    shapes = [
+        jax.ShapeDtypeStruct((length, q_width), bf16),
+        jax.ShapeDtypeStruct((length, HEAD_DIM), bf16),
+        jax.ShapeDtypeStruct((length, HEAD_DIM), bf16),
+        jax.ShapeDtypeStruct((length, q_width), bf16),
+        jax.ShapeDtypeStruct((q_width // HEAD_DIM, 1, length), f32),
+        jax.ShapeDtypeStruct((width, cols), bf16),
+        jax.ShapeDtypeStruct((4, 16, cols), bf16),
+    ]
+    return pl.pallas_call(
+        functools.partial(front_kernel, tokens),
+        in_specs=[SMEM] + [VMEM] * 20,
+        out_specs=[VMEM] * 7,
+        out_shape=shapes,
+        scratch_shapes=[pltpu.VMEM((HEAD_DIM, length), bf16)],
+        compiler_params=pltpu.CompilerParams(vmem_limit_bytes=52 << 20),
+        cost_estimate=pl.CostEstimate(
+            flops=2 * length * width * cols + 4 * length * length * q_width,
+            bytes_accessed=2 * length * width + 4 * width * cols,
+            transcendentals=length * length,
+        ),
+        name="front",
+    )(at, *pieces, *hops, cosine, sine, starts)
+
+
+def back_kernel(tokens, at_ref, q_ref, k_ref, v_ref, mixed_ref, norm_ref, grad_ref, project_ref,
+                cos_ref, sin_ref, starts_ref, core_ref, chips_ref, cols_ref, kt_ref, dk_ref, dv_ref):
+    place = at_ref[0]
+    length, q_width = q_ref.shape
+    block = 256
+    kt_ref[...] = jnp.transpose(k_ref[...].astype(f32)).astype(bf16)
+    dk_ref[...] = jnp.zeros_like(dk_ref)
+    dv_ref[...] = jnp.zeros_like(dv_ref)
+    for head in range(q_width // HEAD_DIM):
+        cols = slice(head * HEAD_DIM, (head + 1) * HEAD_DIM)
+        for low in range(0, length, block):
+            high = low + block
+            queries, grads = q_ref[low:high, cols], grad_ref[low:high, cols]
+            scores, allowed = masked_scores(k_ref[:high, :], queries, starts_ref[:, low:high], low)
+            probs = jnp.where(allowed, jnp.exp2(scores - norm_ref[head, :, low:high]), 0.0)
+            grad_prob = dot_right_t(v_ref[:high, :], grads)
+            weighed = jnp.transpose(grads.astype(f32) * mixed_ref[low:high, cols].astype(f32))
+            grad_score = (probs * (grad_prob - jnp.sum(weighed, 0, keepdims=True))).astype(bf16)
+            dv_ref[:high, :] += dot_plain(probs.astype(bf16), grads)
+            dk_ref[:high, :] += dot_plain(grad_score, queries)
+            dq = jnp.transpose(dot_plain(kt_ref[:, :high], grad_score)) * score_scale
+            cols_ref[low:high, cols] = turn(
+                dq, cos_ref[low:high, :], sin_ref[low:high, :], False
+            ).astype(bf16)
+    cols_ref[:, q_width : q_width + HEAD_DIM] = turn(
+        dk_ref[...] * score_scale, cos_ref[...], sin_ref[...], False
+    ).astype(bf16)
+    cols_ref[:, q_width + HEAD_DIM :] = dv_ref[...].astype(bf16)
+    for out_ref, bits in ((core_ref, TO_CORE), (chips_ref, TO_CHIPS)):
+        for step, bit in enumerate(bits):
+            here = pl.ds(pl.multiple_of((place ^ bit) * tokens, tokens), tokens)
+            out_ref[step] = dot_right_t(cols_ref[here, :], project_ref[...]).astype(bf16)
+
+
+def back(at, queries, keys, values, mixed, norm, grads, project, cosine, sine, starts):
+    length, q_width = queries.shape
+    width, cols = project.shape
+    tokens = length // 8
+    return pl.pallas_call(
+        functools.partial(back_kernel, tokens),
+        in_specs=[SMEM] + [VMEM] * 10,
+        out_specs=[VMEM] * 3,
+        out_shape=[
+            jax.ShapeDtypeStruct((4, tokens, width), bf16),
+            jax.ShapeDtypeStruct((4, tokens, width), bf16),
+            jax.ShapeDtypeStruct((length, cols), bf16),
+        ],
+        scratch_shapes=[
+            pltpu.VMEM((HEAD_DIM, length), bf16),
+            pltpu.VMEM((length, HEAD_DIM), f32),
+            pltpu.VMEM((length, HEAD_DIM), f32),
+        ],
+        compiler_params=pltpu.CompilerParams(vmem_limit_bytes=52 << 20),
+        cost_estimate=pl.CostEstimate(
+            flops=2 * length * width * cols + 7 * length * length * q_width,
+            bytes_accessed=2 * length * width + 2 * width * cols,
+            transcendentals=length * length,
+        ),
+        name="back",
+    )(at, queries, keys, values, mixed, norm, grads, project, cosine, sine, starts)
+
+
+def project_grad_kernel(tokens, at_ref, *refs):
+    pieces, (cols_ref, out_ref) = refs[:10], refs[10:]
+    place = at_ref[0]
+    total = None
+    for piece in range(10):
+        here = pl.ds(start_of(place, piece, tokens), pieces[piece].shape[0])
+        term = dot_left_t(cols_ref[here, :], pieces[piece][...])
+        total = term if total is None else total + term
+    turned = jnp.transpose(total).astype(bf16)
+    out_ref[...] = turned.reshape(out_ref.shape)
+
+
+def project_grad(at, pieces, grad_cols):
+    tokens, width = pieces[0].shape
+    cols = grad_cols.shape[1]
+    return pl.pallas_call(
+        functools.partial(project_grad_kernel, tokens),
+        in_specs=[SMEM] + [VMEM] * 11,
+        out_specs=VMEM,
+        out_shape=jax.ShapeDtypeStruct((4, width // 4, cols), bf16),
+        compiler_params=pltpu.CompilerParams(vmem_limit_bytes=52 << 20),
+        cost_estimate=pl.CostEstimate(
+            flops=16 * tokens * width * cols, bytes_accessed=16 * tokens * width, transcendentals=0
+        ),
+        name="project_grad",
+    )(at, *pieces, grad_cols)
+
+
+def output_grad_kernel(tokens, at_ref, *refs):
+    pieces, (mixed_ref, out_ref, gain_ref) = refs[:10], refs[10:]
+    place = at_ref[0]
+    total = None
+    gain = None
+    for piece in range(10):
+        bit, half = PIECES[piece]
+        rows = tokens // 2 if bit >= 6 else tokens
+        here = pl.ds(start_of(place, piece, tokens), rows)
+        term = dot_left_t(mixed_ref[here, :], pieces[piece][:rows, :])
+        total = term if total is None else total + term
+        if pieces[piece].shape[0] > rows:
+            extra = jnp.sum(pieces[piece][rows:, :].astype(f32), 0, keepdims=True)
+            gain = extra if gain is None else gain + extra
+    out_ref[...] = total.astype(bf16).reshape(out_ref.shape)
+    gain_ref[...] = gain
+
+
+def output_grad_term(at, pieces, mixed):
+    length, own = mixed.shape
+    tokens, width = length // 8, pieces[0].shape[1]
+    return pl.pallas_call(
+        functools.partial(output_grad_kernel, tokens),
+        in_specs=[SMEM] + [VMEM] * 11,
+        out_specs=[VMEM] * 2,
+        out_shape=[
+            jax.ShapeDtypeStruct((4, own // 4, width), bf16),
+            jax.ShapeDtypeStruct((1, width), f32),
+        ],
+        compiler_params=pltpu.CompilerParams(vmem_limit_bytes=52 << 20),
+        cost_estimate=pl.CostEstimate(
+            flops=2 * length * own * width, bytes_accessed=2 * length * width, transcendentals=0
+        ),
+        name="output_grad_term",
+    )(at, *pieces, mixed)
+
+
+def feed_kernel(chosen, count, at_ref, *refs):
+    n_ins = len(chosen[1])
+    n_opts, d_opts, refs = refs[:n_ins], refs[n_ins : 2 * n_ins], refs[2 * n_ins :]
+    both_ref, down_ref, refs = refs[0], refs[1], refs[2 + count :]
+    second_ref, direct_ref, hidden_ref, grads_ref, term_ref, total_ref = refs
+    step = pl.program_id(0)
+    plane = at_ref[1]
+
+    @pl.when(step == 0)
+    def _():
+        total_ref[...] = jnp.zeros_like(total_ref)
+        if n_ins == 1:
+            second_ref[...] = n_opts[0][...]
+            direct_ref[...] = d_opts[0][...]
+        else:
+            for p in range(4):
+
+                @pl.when(plane == p)
+                def _():
+                    second_ref[...] = n_opts[chosen[0][p]][...]
+                    direct_ref[...] = d_opts[chosen[0][p]][...]
+
+    second, direct = second_ref[...], direct_ref[...]
+    both = both_ref[...]
+    raw = dot_plain(second, both)
+    half = raw.shape[1] // 2
+    gate, upward = raw[:, :half], raw[:, half:]
+    sig = 1.0 / (1.0 + jnp.exp(-gate))
+    silu = gate * sig
+    hidden_ref[...] = (silu * upward).astype(bf16)
+    grad_hidden = dot_right_t(direct, down_ref[...])
+    grads = jnp.concatenate(
+        [
+            (grad_hidden * upward * sig * (1.0 + gate * (1.0 - sig))).astype(bf16),
+            (grad_hidden * silu).astype(bf16),
+        ],
+        1,
+    )
+    grads_ref[...] = grads
+    total_ref[...] += dot_right_t(grads, both)
+
+    @pl.when(step == pl.num_programs(0) - 1)
+    def _():
+        term_ref[...] = total_ref[...].astype(bf16)
+
+
+def feed(at, slot, second_hops, direct_hops, both, down, so_far):
+    if slot == 0:
+        names, chosen = [("own", 0)], [0] * 4
+    else:
+        names = list(dict.fromkeys(SLOT_HOPS[slot - 1]))
+        chosen = [names.index(name) for name in SLOT_HOPS[slot - 1]]
+    tokens, width = second_hops["own", 0].shape
+    ff = down.shape[0]
+    unit = 128
+    so_far = so_far or []
+    whole = pl.BlockSpec((tokens, width), lambda i: (0, 0))
+    shapes = [
+        jax.ShapeDtypeStruct((4 * tokens, width), bf16),
+        jax.ShapeDtypeStruct((4 * tokens, width), bf16),
+        jax.ShapeDtypeStruct((4 * tokens, ff), bf16),
+        jax.ShapeDtypeStruct((4 * tokens, 2 * ff), bf16),
+        jax.ShapeDtypeStruct((tokens, width), bf16),
+    ]
+    first = 1 + 2 * len(names) + 2
+    outs = pl.pallas_call(
+        functools.partial(feed_kernel, (chosen, names), len(so_far)),
+        grid=(ff // unit,),
+        in_specs=[SMEM]
+        + [whole] * (2 * len(names))
+        + [
+            pl.BlockSpec((width, 2 * unit), lambda i: (0, i)),
+            pl.BlockSpec((unit, width), lambda i: (i, 0)),
+        ]
+        + [pl.BlockSpec(memory_space=pl.ANY)] * len(so_far),
+        out_specs=[
+            pl.BlockSpec((tokens, width), lambda i: (slot, 0)),
+            pl.BlockSpec((tokens, width), lambda i: (slot, 0)),
+            pl.BlockSpec((tokens, unit), lambda i: (slot, i)),
+            pl.BlockSpec((tokens, 2 * unit), lambda i: (slot, i)),
+            whole,
+        ],
+        out_shape=shapes,
+        scratch_shapes=[pltpu.VMEM((tokens, width), f32)],
+        input_output_aliases={first + i: i for i in range(len(so_far))},
+        compiler_params=pltpu.CompilerParams(vmem_limit_bytes=52 << 20),
+        cost_estimate=pl.CostEstimate(
+            flops=10 * tokens * width * ff,
+            bytes_accessed=6 * width * ff,
+            transcendentals=tokens * ff,
+        ),
+        name="feed",
+    )(
+        at,
+        *[second_hops[name] for name in names],
+        *[direct_hops[name] for name in names],
+        both,
+        down,
+        *so_far,
+    )
+    return outs[:4], outs[4]
+
+
+def hop_on(hops, step, *earlier):
+    before = (("own", 0), ("own", 0)) if step == 1 else (("up", step - 1), ("down", step - 1))
+    for name, moves in ((0, UP), (1, DOWN)):
+        block = hops[before[name]]
+        if earlier:
+            block = after(block, *earlier)
+        hops[("up", "down")[name], step] = lax.ppermute(block, "dp", moves[step - 1 :])
+
+
+def fast_device(
+    layer_input,
+    output_grad,
+    layer_keep,
+    group_ids,
+    exit_scale,
+    doc_lengths,
+    attention_gain,
+    query_weight,
+    key_weight,
+    value_weight,
+    output_weight,
+    feedforward_gain,
+    gate_weight,
+    up_weight,
+    down_weight,
+):
+    tokens, width = layer_input.shape[1:]
+    place, plane = lax.axis_index("fsdp"), lax.axis_index("dp")
+    at = jnp.stack([place, plane]).astype(jnp.int32)
+    length = tokens * 8
+    own_rows = query_weight.shape[0]
+    q_width = HEADS // 8 * HEAD_DIM
+    cols = q_width + 2 * HEAD_DIM
+    ff_own = gate_weight.shape[1]
+    half = tokens // 2
+    rows = layer_input[0].astype(f32)
+    keep = layer_keep[0].astype(f32)
+
+    output_full = lax.all_gather(output_weight, ("dp", "fsdp"), axis=0, tiled=True)
+    both_mine = jnp.stack(
+        [gate_weight.reshape(-1, ff_own // 128, 128), up_weight.reshape(-1, ff_own // 128, 128)], 2
+    ).reshape(-1, 2 * ff_own)
+    both = lax.all_gather(both_mine, "fsdp", axis=0, tiled=True)
+
+    inv_first = rms_scale(rows)
+    normed = (rows * inv_first).astype(bf16)
+    along_x, along_y, on_core = flip(normed, 2), flip(normed, 4), flip(normed, 1)
+    gain_mine = attention_gain.astype(f32)[:, None]
+
+    def spread(weight):
+        scaled = (weight.astype(f32) * gain_mine).astype(bf16).reshape(own_rows, KV_HEADS, 1, HEAD_DIM)
+        return jnp.broadcast_to(scaled, (own_rows, KV_HEADS, 2, HEAD_DIM)).reshape(own_rows, 8, HEAD_DIM)
+
+    query_scaled = (query_weight.astype(f32) * gain_mine).astype(bf16).reshape(own_rows, 8, q_width)
+    sent = jnp.concatenate([query_scaled, spread(key_weight), spread(value_weight)], -1)
+    gain_row = jnp.pad(feedforward_gain[None, None, :], ((0, 15), (0, 7), (0, cols - own_rows)))
+    gain_row = jnp.broadcast_to(gain_row[:, :1], (16, 8, cols))
+    sent = jnp.transpose(jnp.concatenate([sent, gain_row], 0), (1, 0, 2)).reshape(-1, cols)
+    got = lax.all_to_all(sent, "fsdp", split_axis=0, concat_axis=0, tiled=True)
+    got = got.reshape(8, own_rows + 16, cols)
+    gains = jnp.pad(got[:, own_rows, :own_rows].reshape(1, 8 * own_rows), ((0, 15), (0, 0)))
+    columns = {("own", 0): jnp.concatenate([got[:, :own_rows].reshape(-1, cols), gains], 0)}
+    hop_on(columns, 1)
+    low = flip(after(along_x[:half], columns["own", 0]), 4)
+    high = flip(after(along_y[half:], columns["own", 0]), 2)
+    down_use = lax.all_gather(
+        after(down_weight, columns["own", 0]), "fsdp", axis=0, tiled=True
+    )
+    core_x, core_y = flip(along_x, 1), flip(along_y, 1)
+    hop_on(columns, 2)
+    core_low, core_high = flip(low, 1), flip(high, 1)
+    hop_on(columns, 3)
+    pieces = [normed, along_x, along_y, low, high, on_core, core_x, core_y, core_low, core_high]
+
+    picked = jnp.sum(
+        jnp.where(jnp.arange(exit_scale.shape[0], dtype=jnp.int32) == group_ids[0], exit_scale, 0.0)
+    )
+    cotangent = output_grad[0].astype(f32) * picked
+    direct = keep * cotangent
+    directs = {("own", 0): direct.astype(bf16)}
+    hop_on(directs, 1, columns["up", 2], columns["down", 2])
+
+    half_dim = HEAD_DIM // 2
+    cosine, sine = rotary_tables(length)
+    cosine, sine = cosine[:, 0], sine[:, 0]
+    cosine = jnp.concatenate([cosine, cosine], 1)
+    sine = jnp.concatenate([-sine, sine], 1)
+    order = jnp.arange(doc_lengths.shape[1])
+    ends = jnp.sum(jnp.where(order[None, :] <= order[:, None], doc_lengths[0][None, :], 0), 1)
+    positions = jnp.arange(length, dtype=jnp.int32)
+    starts = jnp.max(jnp.where(positions[None, :] >= ends[:, None], ends[:, None], 0), 0)[None, :]
+
+    all_hops = [columns["own", 0]]
+    for step in (1, 2, 3):
+        all_hops += [columns["up", step], columns["down", step]]
+    queries, keys, values, mixed, norm, project, gains = front(
+        at, pieces, all_hops, cosine, sine, starts
+    )
+    gain_second = gains[:, 0, :].reshape(width).astype(f32)
+
+    hop_on(directs, 2, mixed)
+    attended_low = lax.all_to_all(mixed, "fsdp", split_axis=0, concat_axis=1, tiled=True)
+    branch_attention = dot_plain(attended_low, output_full)
+    middle = rows + branch_attention
+    inv_second = rms_scale(middle)
+    seconds = {("own", 0): (middle * inv_second * gain_second).astype(bf16)}
+
+    hop_on(seconds, 1)
+    hop_on(directs, 3, seconds["own", 0])
+    stacked, term_own = feed(at, 0, seconds, directs, both, down_use, None)
+    hop_on(seconds, 2)
+    stacked, term_1 = feed(at, 1, seconds, directs, both, down_use, stacked)
+    hop_on(seconds, 3)
+    stacked, term_2 = feed(at, 2, seconds, directs, both, down_use, stacked)
+    stacked, term_3 = feed(at, 3, seconds, directs, both, down_use, stacked)
+    second_all, direct_all, hidden_all, grads_all = stacked
+    grad_second = plane_scatter([term_own, term_1, term_2, term_3])
+
+    down_term = dot_left_t(hidden_all, direct_all).astype(bf16)
+    both_term = dot_left_t(second_all, grads_all).astype(bf16)
+    down_grad = lax.psum_scatter(down_term, "fsdp", scatter_dimension=0, tiled=True).astype(f32)
+    both_grad = lax.psum_scatter(both_term, "fsdp", scatter_dimension=0, tiled=True)
+    branch_terms = dot_plain(hidden_all, down_use).astype(bf16).reshape(4, tokens, width)
+
+    weighted = grad_second * gain_second
+    grad_middle = inv_second * weighted - middle * inv_second**3 * jnp.mean(
+        weighted * middle, -1, keepdims=True
+    )
+    grad_branch = (direct + grad_middle).astype(bf16)
+    grad_attended = dot_right_t(grad_branch, output_full).astype(bf16)
+    grad_heads = lax.all_to_all(grad_attended, "fsdp", split_axis=1, concat_axis=0, tiled=True)
+    gain_term = jnp.sum(grad_second * middle * inv_second, 0, keepdims=True)
+    gain_high = gain_term.astype(bf16)
+    gain_low = (gain_term - gain_high.astype(f32)).astype(bf16)
+    branch_block = jnp.concatenate(
+        [grad_branch, gain_high, gain_low, jnp.zeros((14, width), bf16)], 0
+    )
+    branch_x, branch_y, branch_core = flip(branch_block, 2), flip(branch_block, 4), flip(branch_block, 1)
+
+    core_terms, chip_terms, grad_cols = back(
+        at, queries, keys, values, mixed, norm, grad_heads, project, cosine, sine, starts
+    )
+    other = flip(core_terms, 1)
+    branch_low = flip(after(branch_x[:half], grad_cols), 4)
+    branch_high = flip(after(branch_y[half:], grad_cols), 2)
+    far = flip(add_low(chip_terms[0], other[0]), 6)
+    near_x = flip(add_low(chip_terms[1], other[1]), 2)
+    near_y = flip(add_low(chip_terms[2], other[2]), 4)
+    project_term = project_grad(at, pieces, grad_cols)
+    project_plane = plane_scatter(slots_of(project_term)).astype(bf16)
+    branch_pieces = [branch_block, branch_x, branch_y, branch_low, branch_high, branch_core]
+    branch_pieces += [flip(piece, 1) for piece in (branch_x, branch_y, branch_low, branch_high)]
+    output_term, gain_sum = output_grad_term(at, branch_pieces, mixed)
+    gain_own = lax.dynamic_slice_in_dim(gain_sum[0], place * 4 * own_rows, 4 * own_rows)
+    gain_own = jnp.pad(gain_own.reshape(4, 1, own_rows), ((0, 0), (0, 15), (0, width - own_rows)))
+    output_term = jnp.concatenate([output_term, gain_own.astype(bf16)], 1)
+    output_sum = output_rows(output_term.reshape(-1, width))
+    weighted_first = (
+        chip_terms[3].astype(f32)
+        + other[3].astype(f32)
+        + far.astype(f32)
+        + near_x.astype(f32)
+        + near_y.astype(f32)
+    )
+    grad_rows = inv_first * weighted_first - rows * inv_first**3 * jnp.mean(
+        weighted_first * rows, -1, keepdims=True
+    )
+    input_grad = cotangent + grad_middle + grad_rows
+
+    branch_terms = after(branch_terms, grad_branch)
+    branch_feed = plane_scatter([branch_terms[i] for i in range(4)])
+    output = (rows + keep * (branch_attention + branch_feed)).astype(bf16)
+
+    back_cols = lax.all_to_all(project_plane, "fsdp", split_axis=0, concat_axis=0, tiled=True)
+    back_cols = back_cols.reshape(8, own_rows, cols).astype(f32)
+
+    def collect(at_col):
+        parts = back_cols[:, :, at_col : at_col + HEAD_DIM].reshape(KV_HEADS, 2, own_rows, HEAD_DIM)
+        return jnp.transpose(jnp.sum(parts, 1), (1, 0, 2)).reshape(own_rows, KV_HEADS * HEAD_DIM)
+
+    query_plain = jnp.transpose(back_cols[:, :, :q_width], (1, 0, 2)).reshape(own_rows, width)
+    key_plain = collect(q_width)
+    value_plain = collect(q_width + HEAD_DIM)
+    first_gain_grad = (
+        jnp.sum(query_plain * query_weight.astype(f32), 1)
+        + jnp.sum(key_plain * key_weight.astype(f32), 1)
+        + jnp.sum(value_plain * value_weight.astype(f32), 1)
+    )
+    both_parts = both_grad.reshape(-1, ff_own // 128, 2, 128)
+    return (
+        output[None],
+        input_grad[None],
+        first_gain_grad,
+        query_plain * gain_mine,
+        key_plain * gain_mine,
+        value_plain * gain_mine,
+        output_sum[:own_rows],
+        output_sum[own_rows, :own_rows],
+        both_parts[:, :, 0].reshape(-1, ff_own).astype(f32),
+        both_parts[:, :, 1].reshape(-1, ff_own).astype(f32),
+        down_grad,
+    )
+
+
 def solution(mesh):
     both = ("dp", "fsdp")
+    fast = (mesh.shape["dp"], mesh.shape["fsdp"]) == (4, 8)
     return jax.shard_map(
-        per_device,
+        fast_device if fast else per_device,
         mesh=mesh,
         in_specs=(
             P("dp", "fsdp", None),

time: 898 us -> 673 us (0.75)
  waiting for transfers between devices: 463 us -> 212 us
  Pallas kernels: 22.1 us -> 125 us
  matrix products: 116 us -> 42.3 us
  blocking collectives: 66.9 us -> 18 us
  starting transfers between devices: 112 us -> 139 us
  other arithmetic: 57.6 us -> 70.7 us
  local copies, waits for them, and re-layouts: 24.8 us -> 34.4 us
    all_gather x4 -> x3, waiting for transfers between devices: 172 us -> 2.59 us  [the longest x1 2.57 us: fast_device(): both = lax.all_gather(both_mine, 'fsdp', axis=0, tiled=True)]
    pallas_call x2 -> x8, Pallas kernels: 22.1 us -> 125 us  [the longest x4 69.6 us: feed(): pl.pallas_call(functools.partial(feed_kernel, (chosen, names), len(so_far...]
    reduce_scatter x4 -> x2, waiting for transfers between devices: 76.9 us -> 0.01 us  [the longest x1 0.01 us: fast_device(): lax.psum_scatter(down_term, 'fsdp', scatter_dimension=0, tiled=True)]
    ppermute x18 -> x44, waiting for transfers between devices: 100 us -> 159 us  [the longest x18 78 us: hop_on(): lax.ppermute(block, 'dp', moves[step - 1:])]
    ppermute x4, waiting for transfers between devices: 36.7 us -> 0.91 us  [plane_scatter(): up3 = lax.ppermute(third, 'dp', UP[:1])]
    dot_general x4 -> x1, matrix products: 34.7 us -> 2.88 us  [dot_right_t(): lax.dot_general(left, right, (((1,), (1,)), ((), ())), preferred_element_...]
    dot_general x5 -> x2, matrix products: 42.7 us -> 14.8 us  [dot_plain(): return jnp.dot(left, right, preferred_element_type=f32)]
    ppermute x18 -> x44, starting transfers between devices: 28.2 us -> 51.5 us  [the longest x18 34.7 us: hop_on(): lax.ppermute(block, 'dp', moves[step - 1:])]
  transfers between devices with their start and end apart: 53 -> 76, of which waited for: 26 -> 31; matrix products, arithmetic and copies ran while one was open for 16% -> 17% of each run, Pallas kernels for 2% -> 16%
where the time goes in v3:
time: 673 us; the launch traced here: 665 us
  waiting for transfers between devices  212 us (32%)
  starting transfers between devices  139 us (21%)
  Pallas kernels  125 us (19%)
  other arithmetic  70.7 us (11%)
  matrix products  42.3 us (6%)
  local copies, waits for them, and re-layouts  34.4 us (5%)
  between operations  24.3 us (4%)
  blocking collectives  18 us (3%)
    ppermute x18, waiting for transfers between devices, hop_on(): lax.ppermute(block, 'dp', moves[step - 1:])  78 us
    pallas_call x4, Pallas kernels, feed(): pl.pallas_call(functools.partial(feed_kernel, (chosen, names), len(so_far...  69.6 us
    ppermute x22, waiting for transfers between devices, flip(): return lax.ppermute(block, 'fsdp', FLIP[bit])  56.6 us
    ppermute x18, starting transfers between devices, hop_on(): lax.ppermute(block, 'dp', moves[step - 1:])  34.7 us
    ppermute x4, starting transfers between devices, plane_scatter(): lax.ppermute(add_low(pick(plane, [first, first, second, second]), up2), '...  28.7 us
    ppermute x4, waiting for transfers between devices, output_rows(): got = lax.ppermute(sent, 'fsdp', moves)  24.6 us
    dot_general x2, matrix products, dot_left_t(): lax.dot_general(left, right, (((0,), (0,)), ((), ())), preferred_element_...  24.6 us
    convert_element_type x10, other arithmetic, add_low(): return (left.astype(f32) + right.astype(f32)).astype(left.dtype)  23.9 us
  transfers between devices with their start and end apart: 76, of which 31 were waited for; matrix products, arithmetic and copies ran while one was open for 17% of the time, Pallas kernels for 16%

profile of v3, /device:TPU:0, one launch (start us, length us, event | category | flops | bytes accessed | tf_op | source)
XLA Modules:
  0.0 664.8 jit_solution(14311819332590341450)
XLA Ops:
  11.3 18.0 %all_to_all.53 = bf16[8,80,512]{2,1,0:T(8,128)(2,1)S(1)} all-to-all(bf16[8,80,512]{2,1,0:T(8,128)(2,1)S(1)} %copy.73), channel_id=1, replica_groups=mesh['dp'=4,'fsdp'=8] {'fsdp'}, dimensions={0} | all-to-all | bytes 1310720 | tf_op jit(solution)/shard_map/all_to_all | solution.py:862
  37.7 3.5 collective-permute-start.9
  42.5 16.4 %collective-permute-done.1.refs_2_ = bf16[192,2048]{1,0:T(8,128)(2,1)} collective-permute-done((bf16[192,2048]{1,0:T(8,128)(2,1)S(1)}, bf16[192,2048]{1,0:T(8,128)(2,1)}, u32[]{:S(2)}, u32[]{:S(2)}) %collective-permute-start.1) | collective-permute-done | bytes 786464 | tf_op jit(solution)/shard_map/ppermute | solution.py:137
  60.3 4.9 collective-permute-done.refs_1_
  74.7 4.1 fusion.40
  80.5 28.1 %collective-permute-done.12.refs_14_ = bf16[528,512]{1,0:T(8,128)(2,1)} collective-permute-done((bf16[528,512]{1,0:T(8,128)(2,1)S(1)}, bf16[528,512]{1,0:T(8,128)(2,1)}, u32[]{:S(2)}, u32[]{:S(2)}) %collective-permute-start.12) | collective-permute-done | bytes 540704 | tf_op jit(solution)/shard_map/ppermute | solution.py:810
  116.7 8.3 %collective-permute-done.14.refs_16_ = bf16[528,512]{1,0:T(8,128)(2,1)} collective-permute-done((bf16[528,512]{1,0:T(8,128)(2,1)}, bf16[528,512]{1,0:T(8,128)(2,1)}, u32[]{:S(2)}, u32[]{:S(2)}) %collective-permute-start.14) | collective-permute-done | bytes 540704 | tf_op jit(solution)/shard_map/ppermute | solution.py:810
  125.0 19.4 %front.1 = (bf16[1536,256]{1,0:T(8,128)(2,1)}, bf16[1536,128]{1,0:T(8,128)(2,1)S(1)}, bf16[1536,128]{1,0:T(8,128)(2,1)S(1)}, bf16[1536,256]{1,0:T(8,128)(2,1)}, ...) custom-call(s32[2]{0:T(128)S(1)} %pad_add_fusion.at_ref, ...), custom_call_target="tpu_custom_call" | custom-call | flops 5637144576 | bytes 10485760 | tf_op jit(solution)/shard_map/front/pallas_call | solution.py:558
  145.8 3.7 all-to-all-start.1
  152.6 5.8 collective-permute-start.24
  158.5 3.6 all-to-all-done.1
  162.2 5.4 multiply_reduce_fusion.2
  170.0 4.6 collective-permute-start.18
  178.2 12.8 %collective-permute-done.15.refs_0_.refs_2_ = bf16[192,2048]{1,0:T(8,128)(2,1)S(1)} collective-permute-done((bf16[192,2048]{1,0:T(8,128)(2,1)S(1)}, bf16[192,2048]{1,0:T(8,128)(2,1)S(1)}, u32[]{:S(2)}, u32[]{:S(2)}) %collective-permute-start.15) | collective-permute-done | bytes 786464 | tf_op jit(solution)/shard_map/ppermute | solution.py:810
  195.5 12.5 %collective-permute-done.22.refs_4_.refs_5_ = bf16[192,2048]{1,0:T(8,128)(2,1)} collective-permute-done((bf16[192,2048]{1,0:T(8,128)(2,1)}, bf16[192,2048]{1,0:T(8,128)(2,1)}, u32[]{:S(2)}, u32[]{:S(2)}) %collective-permute-start.22) | collective-permute-done | bytes 786464 | tf_op jit(solution)/shard_map/ppermute | solution.py:810
  209.3 15.5 %collective-permute-done.16.refs_0_.refs_1_ = bf16[192,2048]{1,0:T(8,128)(2,1)S(1)} collective-permute-done((bf16[192,2048]{1,0:T(8,128)(2,1)S(1)}, bf16[192,2048]{1,0:T(8,128)(2,1)S(1)}, u32[]{:S(2)}, u32[]{:S(2)}) %collective-permute-start.16) | collective-permute-done | bytes 786464 | tf_op jit(solution)/shard_map/ppermute | solution.py:810
  230.2 16.5 %feed.4 = (bf16[768,2048]{1,0:T(8,128)(2,1)}, bf16[768,2048]{1,0:T(8,128)(2,1)}, bf16[768,1408]{1,0:T(8,128)(2,1)}, bf16[768,2816]{1,0:T(8,128)(2,1)}, bf16[192,2048]{1,0:T(8,128)(2,1)S(1)}) custom-call(s32[2]{0:T(128)S(1)} %pad_add_fusion.at_ref, bf16[192,2048]{1,0:T(8,128)(2,1)S(1)} %multiply_convert_fusion.refs_0_, bf16[192,2048]{1,0:T(8,128)(2,1)} %fusion.18.refs_1_, ...), custom_call_target="tpu_custom_call" | custom-call | flops 5536481280 | bytes 17301504 | tf_op jit(solution)/shard_map/feed/pallas_call | solution.py:766
  246.7 17.0 %feed.5 = (bf16[768,2048]{1,0:T(8,128)(2,1)}, bf16[768,2048]{1,0:T(8,128)(2,1)}, bf16[768,1408]{1,0:T(8,128)(2,1)}, bf16[768,2816]{1,0:T(8,128)(2,1)}, bf16[192,2048]{1,0:T(8,128)(2,1)S(1)}) custom-call(s32[2]{0:T(128)S(1)} %pad_add_fusion.at_ref, ...), custom_call_target="tpu_custom_call", output_to_operand_aliasing={{0}: (7, {}), {1}: (8, {}), {2}: (9, {}), {3}: (10, {})} | custom-call | flops 5536481280 | bytes 17301504 | tf_op jit(solution)/shard_map/feed/pallas_call | solution.py:766
  264.6 18.0 %feed.6 = (bf16[768,2048]{1,0:T(8,128)(2,1)}, bf16[768,2048]{1,0:T(8,128)(2,1)}, bf16[768,1408]{1,0:T(8,128)(2,1)}, bf16[768,2816]{1,0:T(8,128)(2,1)}, bf16[192,2048]{1,0:T(8,128)(2,1)S(1)}) custom-call(s32[2]{0:T(128)S(1)} %pad_add_fusion.at_ref, ...), custom_call_target="tpu_custom_call", output_to_operand_aliasing={{0}: (11, {}), {1}: (12, {}), {2}: (13, {}), {3}: (14, {})} | custom-call | flops 5536481280 | bytes 17301504 | tf_op jit(solution)/shard_map/feed/pallas_call | solution.py:766
  282.6 18.2 %feed.7 = (bf16[768,2048]{1,0:T(8,128)(2,1)}, bf16[768,2048]{1,0:T(8,128)(2,1)}, bf16[768,1408]{1,0:T(8,128)(2,1)}, bf16[768,2816]{1,0:T(8,128)(2,1)}, bf16[192,2048]{1,0:T(8,128)(2,1)S(1)}) custom-call(s32[2]{0:T(128)S(1)} %pad_add_fusion.at_ref, ...), custom_call_target="tpu_custom_call", output_to_operand_aliasing={{0}: (11, {}), {1}: (12, {}), {2}: (13, {}), {3}: (14, {})} | custom-call | flops 5536481280 | bytes 17301504 | tf_op jit(solution)/shard_map/feed/pallas_call | solution.py:766
  300.7 9.7 %convolution_convert_fusion.1 = bf16[1408,2048]{1,0:T(8,128)(2,1)} fusion(bf16[768,1408]{1,0:T(8,128)(2,1)} %get-tuple-element.76, bf16[768,2048]{1,0:T(8,128)(2,1)} %get-tuple-element.96), kind=kOutput, calls=%fused_computation.1 | convolution fusion | flops 4432068608 | bytes 11075584 | tf_op jit(solution)/shard_map/dot_general | solution.py:32
  315.7 14.9 %convolution_convert_fusion = bf16[2048,2816]{1,0:T(8,128)(2,1)} fusion(bf16[768,2048]{1,0:T(8,128)(2,1)} %get-tuple-element.94, bf16[768,2816]{1,0:T(8,128)(2,1)} %get-tuple-element.95), kind=kOutput, calls=%fused_computation | convolution fusion | flops 8864137216 | bytes 19005440 | tf_op jit(solution)/shard_map/dot_general | solution.py:32
  335.2 4.4 collective-permute-start.28
  345.2 11.1 %collective-permute-done.28 = bf16[192,2048]{1,0:T(8,128)(2,1)S(1)} collective-permute-done((bf16[192,2048]{1,0:T(8,128)(2,1)}, bf16[192,2048]{1,0:T(8,128)(2,1)S(1)}, u32[]{:S(2)}, u32[]{:S(2)}) %collective-permute-start.28) | collective-permute-done | bytes 786464 | tf_op jit(solution)/shard_map/ppermute | solution.py:107
  358.2 6.5 collective-permute-start.29
  366.3 9.5 %convolution_convert_fusion.2 = bf16[768,2048]{1,0:T(8,128)(2,1)} fusion(bf16[768,1408]{1,0:T(8,128)(2,1)S(1)} %copy-done.22, bf16[1408,2048]{1,0:T(8,128)(2,1)} %all-gather.8.cloned.1.call-done.refs_3_.refs_5_.refs_9_), kind=kOutput, calls=%fused_computation.8 | convolution fusion | flops 4430757888 | bytes 11075584 | tf_op jit(solution)/shard_map/dot_general | solution.py:24
  378.7 4.5 collective-permute-done.32
  390.2 4.2 all-to-all-start.2
  405.9 4.9 all-to-all-done.2
  412.5 18.9 %back.1 = (bf16[4,192,2048]{2,1,0:T(8,128)(2,1)}, bf16[4,192,2048]{2,1,0:T(8,128)(2,1)}, bf16[1536,512]{1,0:T(8,128)(2,1)}) custom-call(s32[2]{0:T(128)S(1)} %pad_add_fusion.at_ref, bf16[1536,256]{1,0:T(8,128)(2,1)S(1)} %copy-done.10, bf16[1536,128]{1,0:T(8,128)(2,1)S(1)} %copy-done.12, bf16[1536,128]{1,0:T(8,128)(2,1)S(1)} %copy-done.14, ...), custom_call_target="tpu_custom_call" | custom-call | flops 7449083904 | bytes 8388608 | tf_op jit(solution)/shard_map/back/pallas_call | solution.py:612
  431.3 10.2 %project_grad.1 = bf16[4,512,512]{2,1,0:T(8,128)(2,1)} custom-call(s32[2]{0:T(128)S(1)} %pad_add_fusion.at_ref, bf16[192,2048]{1,0:T(8,128)(2,1)} %copy-done.38, bf16[192,2048]{1,0:T(8,128)(2,1)} %collective-permute-done.refs_1_, bf16[192,2048]{1,0:T(8,128)(2,1)} %collective-permute-done.1.refs_2_, bf16[96,2048]{1,0:T(8,128)(2,1)S(1)} %copy-done.5, ...), custom_call_target="tpu_custom_call" | custom-call | flops 3221225472 | bytes 6291456 | tf_op jit(solution)/shard_map/project_grad/pallas_call | solution.py:651
  459.3 4.3 collective-permute-done.51.refs_3_
  479.1 6.6 output_grad_term.1
  494.6 6.2 collective-permute-done.44
  500.7 5.3 collective-permute-start.35
  509.2 6.9 %collective-permute-done.59 = bf16[80,2048]{1,0:T(8,128)(2,1)S(1)} collective-permute-done((bf16[80,2048]{1,0:T(8,128)(2,1)S(1)}, bf16[80,2048]{1,0:T(8,128)(2,1)S(1)}, u32[]{:S(2)}, u32[]{:S(2)}) %collective-permute-start.59) | collective-permute-done | bytes 327712 | tf_op jit(solution)/shard_map/ppermute | solution.py:153
  516.5 8.5 %collective-permute-done.60 = bf16[80,2048]{1,0:T(8,128)(2,1)S(1)} collective-permute-done((bf16[80,2048]{1,0:T(8,128)(2,1)S(1)}, bf16[80,2048]{1,0:T(8,128)(2,1)S(1)}, u32[]{:S(2)}, u32[]{:S(2)}) %collective-permute-start.60) | collective-permute-done | bytes 327712 | tf_op jit(solution)/shard_map/ppermute | solution.py:153
  525.1 9.2 %collective-permute-done.61 = bf16[80,2048]{1,0:T(8,128)(2,1)S(1)} collective-permute-done((bf16[80,2048]{1,0:T(8,128)(2,1)S(1)}, bf16[80,2048]{1,0:T(8,128)(2,1)S(1)}, u32[]{:S(2)}, u32[]{:S(2)}) %collective-permute-start.61) | collective-permute-done | bytes 327712 | tf_op jit(solution)/shard_map/ppermute | solution.py:153
  536.4 4.6 collective-permute-start.62
  540.9 9.1 %collective-permute-done.48 = bf16[512,512]{1,0:T(8,128)(2,1)S(1)} collective-permute-done((bf16[512,512]{1,0:T(8,128)(2,1)S(1)}, bf16[512,512]{1,0:T(8,128)(2,1)S(1)}, u32[]{:S(2)}, u32[]{:S(2)}) %collective-permute-start.48) | collective-permute-done | bytes 524320 | tf_op jit(solution)/shard_map/ppermute | solution.py:110
  552.4 4.1 all-to-all-start.3
  562.8 5.3 collective-permute-start.63
  576.2 15.5 %collective-permute-start.64 = (bf16[80,2048]{1,0:T(8,128)(2,1)S(1)}, bf16[80,2048]{1,0:T(8,128)(2,1)S(1)}, u32[]{:S(2)}, u32[]{:S(2)}) collective-permute-start(bf16[80,2048]{1,0:T(8,128)(2,1)S(1)} %get-tuple-element.118), channel_id=1, source_target_pairs={{0,8},{8,16},{16,24},{1,9},{9,17},{17,25},{2,10},{10,18},{18,26},{... | collective-permute-start | bytes 983048 | tf_op jit(solution)/shard_map/ppermute | solution.py:109
  606.0 10.9 %collective-permute-done.40 = bf16[192,2048]{1,0:T(8,128)(2,1)S(1)} collective-permute-done((bf16[192,2048]{1,0:T(8,128)(2,1)S(1)}, bf16[192,2048]{1,0:T(8,128)(2,1)S(1)}, u32[]{:S(2)}, u32[]{:S(2)}) %collective-permute-start.40) | collective-permute-done | bytes 786464 | tf_op jit(solution)/shard_map/ppermute | solution.py:137
  616.9 15.1 %collective-permute-done.41 = bf16[192,2048]{1,0:T(8,128)(2,1)S(1)} collective-permute-done((bf16[192,2048]{1,0:T(8,128)(2,1)S(1)}, bf16[192,2048]{1,0:T(8,128)(2,1)S(1)}, u32[]{:S(2)}, u32[]{:S(2)}) %collective-permute-start.41) | collective-permute-done | bytes 786464 | tf_op jit(solution)/shard_map/ppermute | solution.py:137
  632.0 4.0 fusion.12
  636.0 4.7 fusion.11
  646.3 8.4 %fusion.19 = (f32[256,11,128]{2,1,0:T(8,128)S(1)}, f32[256,11,128]{2,1,0:T(8,128)S(1)}) fusion(bf16[256,11,2,128]{3,2,1,0:T(2,128)(2,1)S(1)} %reshape.223), kind=kLoop, calls=%fused_computation.56 | loop fusion | flops 720896 | bytes 4325376 | tf_op jit(solution)/shard_map/convert_element_type | solution.py:1003
  (343 shorter events, 177.1 us)
Async XLA Ops:
  7.2 155.0 %all-gather.4.cloned.1.call-start = ((), (), s32[]{:S(2)}) async-start(), calls=%async_computation.6 | async-start | bytes 8650752 | tf_op jit(solution)/shard_map/all_gather | solution.py:842
  7.9 219.7 %all-gather.8.cloned.1.call-start = ((), (), s32[]{:S(2)}) async-start(), calls=%async_computation.8 | async-start | bytes 6488064 | tf_op jit(solution)/shard_map/all_gather | solution.py:869
  30.3 199.9 %all-gather.6.cloned.1.call-start = ((), (), s32[]{:S(2)}) async-start(), calls=%async_computation.7 | async-start | bytes 12976128 | tf_op jit(solution)/shard_map/all_gather | solution.py:846
  36.5 22.4 %collective-permute-start.1 = (bf16[192,2048]{1,0:T(8,128)(2,1)S(1)}, bf16[192,2048]{1,0:T(8,128)(2,1)}, u32[]{:S(2)}, u32[]{:S(2)}) collective-permute-start(bf16[192,2048]{1,0:T(8,128)(2,1)S(1)} %fusion.6.refs_0_), channel_id=1, source_target_pairs={{0,4},{1,5},{2,6},{3,7},{4,0},{5,1},{6,2},{7,3},{8,12},{9,13},{10,... | collective-permute-start | bytes 2359304 | tf_op jit(solution)/shard_map/ppermute | solution.py:137
  37.1 28.0 %collective-permute-start = (bf16[192,2048]{1,0:T(8,128)(2,1)S(1)}, bf16[192,2048]{1,0:T(8,128)(2,1)}, u32[]{:S(2)}, u32[]{:S(2)}) collective-permute-start(bf16[192,2048]{1,0:T(8,128)(2,1)S(1)} %fusion.6.refs_0_), channel_id=1, source_target_pairs={{0,2},{1,3},{2,0},{3,1},{4,6},{5,7},{6,4},{7,5},{8,10},{9,11},{10,... | collective-permute-start | bytes 2359304 | tf_op jit(solution)/shard_map/ppermute | solution.py:137
  37.7 30.1 %collective-permute-start.4 = (bf16[192,2048]{1,0:T(8,128)(2,1)S(1)}, bf16[192,2048]{1,0:T(8,128)(2,1)S(1)}, u32[]{:S(2)}, u32[]{:S(2)}) collective-permute-start(bf16[192,2048]{1,0:T(8,128)(2,1)S(1)} %fusion.6.refs_0_), channel_id=1, source_target_pairs={{0,1},{1,0},{2,3},{3,2},{4,5},{5,4},{6,7},{7,6},{8,9},{9,8},{10,11... | collective-permute-start | bytes 2359304 | tf_op jit(solution)/shard_map/ppermute | solution.py:137
  37.7 30.2 %collective-permute-start.9 = (bf16[528,512]{1,0:T(8,128)(2,1)S(1)}, bf16[528,512]{1,0:T(8,128)(2,1)S(1)}, u32[]{:S(2)}, u32[]{:S(2)}) collective-permute-start(bf16[528,512]{1,0:T(8,128)(2,1)S(1)} %copy-done.42), channel_id=1, source_target_pairs={{0,8},{8,16},{16,24},{1,9},{9,17},{17,25},{2,10},{10,18},{18,26},{... | collective-permute-start | bytes 1622024 | tf_op jit(solution)/shard_map/ppermute | solution.py:810
  41.2 27.2 %collective-permute-start.10 = (bf16[528,512]{1,0:T(8,128)(2,1)S(1)}, bf16[528,512]{1,0:T(8,128)(2,1)S(1)}, u32[]{:S(2)}, u32[]{:S(2)}) collective-permute-start(bf16[528,512]{1,0:T(8,128)(2,1)S(1)} %copy-done.42), channel_id=1, source_target_pairs={{24,16},{16,8},{8,0},{25,17},{17,9},{9,1},{26,18},{18,10},{10,2},{... | collective-permute-start | bytes 1622024 | tf_op jit(solution)/shard_map/ppermute | solution.py:810
  67.8 48.9 %collective-permute-start.5 = (bf16[192,2048]{1,0:T(8,128)(2,1)}, bf16[192,2048]{1,0:T(8,128)(2,1)}, u32[]{:S(2)}, u32[]{:S(2)}) collective-permute-start(bf16[192,2048]{1,0:T(8,128)(2,1)} %collective-permute-done.refs_1_), channel_id=1, source_target_pairs={{0,1},{1,0},{2,3},{3,2},{4,5},{5,4},{6,7},{7,6},{8,9},{9,8},{10,11... | collective-permute-start | bytes 2359304 | tf_op jit(solution)/shard_map/ppermute | solution.py:137
  67.9 48.8 %collective-permute-start.6 = (bf16[192,2048]{1,0:T(8,128)(2,1)}, bf16[192,2048]{1,0:T(8,128)(2,1)}, u32[]{:S(2)}, u32[]{:S(2)}) collective-permute-start(bf16[192,2048]{1,0:T(8,128)(2,1)} %collective-permute-done.1.refs_2_), channel_id=1, source_target_pairs={{0,1},{1,0},{2,3},{3,2},{4,5},{5,4},{6,7},{7,6},{8,9},{9,8},{10,11... | collective-permute-start | bytes 2359304 | tf_op jit(solution)/shard_map/ppermute | solution.py:137
  71.4 37.2 %collective-permute-start.12 = (bf16[528,512]{1,0:T(8,128)(2,1)S(1)}, bf16[528,512]{1,0:T(8,128)(2,1)}, u32[]{:S(2)}, u32[]{:S(2)}) collective-permute-start(bf16[528,512]{1,0:T(8,128)(2,1)S(1)} %collective-permute-done.10.refs_12_), channel_id=1, source_target_pairs={{16,8},{8,0},{17,9},{9,1},{18,10},{10,2},{19,11},{11,3},{20,12},{1... | collective-permute-start | bytes 1622024 | tf_op jit(solution)/shard_map/ppermute | solution.py:810
  74.7 35.9 %collective-permute-start.8 = (bf16[96,2048]{1,0:T(8,128)(2,1)S(1)}, bf16[96,2048]{1,0:T(8,128)(2,1)S(1)}, u32[]{:S(2)}, u32[]{:S(2)}) collective-permute-start(bf16[96,2048]{1,0:T(8,128)(2,1)S(1)} %collective-permute-done.3.refs_4_), channel_id=1, source_target_pairs={{0,1},{1,0},{2,3},{3,2},{4,5},{5,4},{6,7},{7,6},{8,9},{9,8},{10,11... | collective-permute-start | bytes 1179656 | tf_op jit(solution)/shard_map/ppermute | solution.py:137
  79.0 37.7 %collective-permute-start.13 = (bf16[528,512]{1,0:T(8,128)(2,1)}, bf16[528,512]{1,0:T(8,128)(2,1)}, u32[]{:S(2)}, u32[]{:S(2)}) collective-permute-start(bf16[528,512]{1,0:T(8,128)(2,1)} %collective-permute-done.11.refs_13_), channel_id=1, source_target_pairs={{16,24},{17,25},{18,26},{19,27},{20,28},{21,29},{22,30},{23,31}} | collective-permute-start | bytes 1622024 | tf_op jit(solution)/shard_map/ppermute | solution.py:810
  149.5 491.2 %reduce-scatter.5.cloned.1.call-start = ((), (), s32[]{:S(2)}) async-start(), calls=%async_computation.10 | async-start | bytes 6488064 | tf_op jit(solution)/shard_map/reduce_scatter | solution.py:924
  151.3 25.6 %collective-permute-start.21 = (bf16[192,2048]{1,0:T(8,128)(2,1)}, bf16[192,2048]{1,0:T(8,128)(2,1)}, u32[]{:S(2)}, u32[]{:S(2)}) collective-permute-start(bf16[192,2048]{1,0:T(8,128)(2,1)} %fusion.18.refs_1_), channel_id=1, source_target_pairs={{24,16},{16,8},{8,0},{25,17},{17,9},{9,1},{26,18},{18,10},{10,2},{... | collective-permute-start | bytes 2359304 | tf_op jit(solution)/shard_map/ppermute | solution.py:810
  152.6 22.8 %collective-permute-start.24 = (bf16[192,2048]{1,0:T(8,128)(2,1)}, bf16[192,2048]{1,0:T(8,128)(2,1)}, u32[]{:S(2)}, u32[]{:S(2)}) collective-permute-start(bf16[192,2048]{1,0:T(8,128)(2,1)} %fusion.18.refs_1_), channel_id=1, source_target_pairs={{0,8},{8,16},{16,24},{1,9},{9,17},{17,25},{2,10},{10,18},{18,26},{... | collective-permute-start | bytes 2359304 | tf_op jit(solution)/shard_map/ppermute | solution.py:810
  168.7 22.4 %collective-permute-start.15 = (bf16[192,2048]{1,0:T(8,128)(2,1)S(1)}, bf16[192,2048]{1,0:T(8,128)(2,1)S(1)}, u32[]{:S(2)}, u32[]{:S(2)}) collective-permute-start(bf16[192,2048]{1,0:T(8,128)(2,1)S(1)} %multiply_convert_fusion.refs_0_), channel_id=1, source_target_pairs={{24,16},{16,8},{8,0},{25,17},{17,9},{9,1},{26,18},{18,10},{10,2},{... | collective-permute-start | bytes 2359304 | tf_op jit(solution)/shard_map/ppermute | solution.py:810
  170.0 22.4 %collective-permute-start.18 = (bf16[192,2048]{1,0:T(8,128)(2,1)S(1)}, bf16[192,2048]{1,0:T(8,128)(2,1)S(1)}, u32[]{:S(2)}, u32[]{:S(2)}) collective-permute-start(bf16[192,2048]{1,0:T(8,128)(2,1)S(1)} %multiply_convert_fusion.refs_0_), channel_id=1, source_target_pairs={{0,8},{8,16},{16,24},{1,9},{9,17},{17,25},{2,10},{10,18},{18,26},{... | collective-permute-start | bytes 2359304 | tf_op jit(solution)/shard_map/ppermute | solution.py:810
  176.9 31.1 %collective-permute-start.22 = (bf16[192,2048]{1,0:T(8,128)(2,1)}, bf16[192,2048]{1,0:T(8,128)(2,1)}, u32[]{:S(2)}, u32[]{:S(2)}) collective-permute-start(bf16[192,2048]{1,0:T(8,128)(2,1)} %collective-permute-done.21.refs_2_.refs_6_), channel_id=1, source_target_pairs={{16,8},{8,0},{17,9},{9,1},{18,10},{10,2},{19,11},{11,3},{20,12},{1... | collective-permute-start | bytes 2359304 | tf_op jit(solution)/shard_map/ppermute | solution.py:810
  191.1 33.7 %collective-permute-start.16 = (bf16[192,2048]{1,0:T(8,128)(2,1)S(1)}, bf16[192,2048]{1,0:T(8,128)(2,1)S(1)}, u32[]{:S(2)}, u32[]{:S(2)}) collective-permute-start(bf16[192,2048]{1,0:T(8,128)(2,1)S(1)} %collective-permute-done.15.refs_0_.refs_2_), channel_id=1, source_target_pairs={{16,8},{8,0},{17,9},{9,1},{18,10},{10,2},{19,11},{11,3},{20,12},{1... | collective-permute-start | bytes 2359304 | tf_op jit(solution)/shard_map/ppermute | solution.py:810
  192.4 33.7 %collective-permute-start.19 = (bf16[192,2048]{1,0:T(8,128)(2,1)S(1)}, bf16[192,2048]{1,0:T(8,128)(2,1)}, u32[]{:S(2)}, u32[]{:S(2)}) collective-permute-start(bf16[192,2048]{1,0:T(8,128)(2,1)S(1)} %collective-permute-done.18.refs_1_), channel_id=1, source_target_pairs={{8,16},{16,24},{9,17},{17,25},{10,18},{18,26},{11,19},{19,27},{12,... | collective-permute-start | bytes 2359304 | tf_op jit(solution)/shard_map/ppermute | solution.py:810
  194.0 88.6 %collective-permute-start.26 = (bf16[192,2048]{1,0:T(8,128)(2,1)}, bf16[192,2048]{1,0:T(8,128)(2,1)}, u32[]{:S(2)}, u32[]{:S(2)}) collective-permute-start(bf16[192,2048]{1,0:T(8,128)(2,1)} %collective-permute-done.25.refs_7_.refs_6_), channel_id=1, source_target_pairs={{16,24},{17,25},{18,26},{19,27},{20,28},{21,29},{22,30},{23,31}} | collective-permute-start | bytes 2359304 | tf_op jit(solution)/shard_map/ppermute | solution.py:810
  208.0 74.5 %collective-permute-start.23 = (bf16[192,2048]{1,0:T(8,128)(2,1)}, bf16[192,2048]{1,0:T(8,128)(2,1)}, u32[]{:S(2)}, u32[]{:S(2)}) collective-permute-start(bf16[192,2048]{1,0:T(8,128)(2,1)} %collective-permute-done.22.refs_4_.refs_5_), channel_id=1, source_target_pairs={{8,0},{9,1},{10,2},{11,3},{12,4},{13,5},{14,6},{15,7}} | collective-permute-start | bytes 2359304 | tf_op jit(solution)/shard_map/ppermute | solution.py:810
  224.8 57.8 %collective-permute-start.17 = (bf16[192,2048]{1,0:T(8,128)(2,1)S(1)}, bf16[192,2048]{1,0:T(8,128)(2,1)}, u32[]{:S(2)}, u32[]{:S(2)}) collective-permute-start(bf16[192,2048]{1,0:T(8,128)(2,1)S(1)} %collective-permute-done.16.refs_0_.refs_1_), channel_id=1, source_target_pairs={{8,0},{9,1},{10,2},{11,3},{12,4},{13,5},{14,6},{15,7}} | collective-permute-start | bytes 2359304 | tf_op jit(solution)/shard_map/ppermute | solution.py:810
  226.1 56.5 %collective-permute-start.20 = (bf16[192,2048]{1,0:T(8,128)(2,1)}, bf16[192,2048]{1,0:T(8,128)(2,1)}, u32[]{:S(2)}, u32[]{:S(2)}) collective-permute-start(bf16[192,2048]{1,0:T(8,128)(2,1)} %collective-permute-done.19.refs_3_.refs_2_), channel_id=1, source_target_pairs={{16,24},{17,25},{18,26},{19,27},{20,28},{21,29},{22,30},{23,31}} | collective-permute-start | bytes 2359304 | tf_op jit(solution)/shard_map/ppermute | solution.py:810
  310.4 332.7 %reduce-scatter.3.cloned.1.call-start = ((), (), s32[]{:S(2)}) async-start(), calls=%async_computation.9 | async-start | bytes 12976128 | tf_op jit(solution)/shard_map/reduce_scatter | solution.py:925
  310.5 20.6 %collective-permute-start.27 = (bf16[192,2048]{1,0:T(8,128)(2,1)S(1)}, bf16[192,2048]{1,0:T(8,128)(2,1)S(1)}, u32[]{:S(2)}, u32[]{:S(2)}) collective-permute-start(bf16[192,2048]{1,0:T(8,128)(2,1)S(1)} %get-tuple-element.80), channel_id=1, source_target_pairs={{0,8},{1,9},{2,10},{3,11},{4,12},{5,13},{6,14},{7,15}} | collective-permute-start | bytes 2359304 | tf_op jit(solution)/shard_map/ppermute | solution.py:104
  335.2 21.1 %collective-permute-start.28 = (bf16[192,2048]{1,0:T(8,128)(2,1)}, bf16[192,2048]{1,0:T(8,128)(2,1)S(1)}, u32[]{:S(2)}, u32[]{:S(2)}) collective-permute-start(bf16[192,2048]{1,0:T(8,128)(2,1)} %get-tuple-element.116), channel_id=1, source_target_pairs={{0,8},{8,16},{1,9},{9,17},{2,10},{10,18},{3,11},{11,19},{4,12},{12... | collective-permute-start | bytes 2359304 | tf_op jit(solution)/shard_map/ppermute | solution.py:107
  358.2 20.5 %collective-permute-start.29 = (bf16[192,2048]{1,0:T(8,128)(2,1)S(1)}, bf16[192,2048]{1,0:T(8,128)(2,1)S(1)}, u32[]{:S(2)}, u32[]{:S(2)}) collective-permute-start(bf16[192,2048]{1,0:T(8,128)(2,1)S(1)} %get-tuple-element.114), channel_id=1, source_target_pairs={{0,8},{8,16},{16,24},{1,9},{9,17},{17,25},{2,10},{10,18},{18,26},{... | collective-permute-start | bytes 2359304 | tf_op jit(solution)/shard_map/ppermute | solution.py:109
  396.9 48.6 %collective-permute-start.50 = (bf16[208,2048]{1,0:T(8,128)(2,1)}, bf16[208,2048]{1,0:T(8,128)(2,1)}, u32[]{:S(2)}, u32[]{:S(2)}) collective-permute-start(bf16[208,2048]{1,0:T(8,128)(2,1)} %maximum_maximum_fusion.refs_0_), channel_id=1, source_target_pairs={{0,4},{1,5},{2,6},{3,7},{4,0},{5,1},{6,2},{7,3},{8,12},{9,13},{10,... | collective-permute-start | bytes 2555912 | tf_op jit(solution)/shard_map/ppermute | solution.py:137
  398.8 49.1 %collective-permute-start.49 = (bf16[208,2048]{1,0:T(8,128)(2,1)}, bf16[208,2048]{1,0:T(8,128)(2,1)}, u32[]{:S(2)}, u32[]{:S(2)}) collective-permute-start(bf16[208,2048]{1,0:T(8,128)(2,1)} %maximum_maximum_fusion.refs_0_), channel_id=1, source_target_pairs={{0,2},{1,3},{2,0},{3,1},{4,6},{5,7},{6,4},{7,5},{8,10},{9,11},{10,... | collective-permute-start | bytes 2555912 | tf_op jit(solution)/shard_map/ppermute | solution.py:137
  400.3 51.0 %collective-permute-start.53 = (bf16[208,2048]{1,0:T(8,128)(2,1)}, bf16[208,2048]{1,0:T(8,128)(2,1)}, u32[]{:S(2)}, u32[]{:S(2)}) collective-permute-start(bf16[208,2048]{1,0:T(8,128)(2,1)} %maximum_maximum_fusion.refs_0_), channel_id=1, source_target_pairs={{0,1},{1,0},{2,3},{3,2},{4,5},{5,4},{6,7},{7,6},{8,9},{9,8},{10,11... | collective-permute-start | bytes 2555912 | tf_op jit(solution)/shard_map/ppermute | solution.py:137
  402.6 48.6 %collective-permute-start.33 = (bf16[192,2048]{1,0:T(8,128)(2,1)}, bf16[192,2048]{1,0:T(8,128)(2,1)}, u32[]{:S(2)}, u32[]{:S(2)}) collective-permute-start(bf16[192,2048]{1,0:T(8,128)(2,1)} %slice_bitcast_fusion), channel_id=1, source_target_pairs={{0,8},{1,9},{2,10},{3,11},{4,12},{5,13},{6,14},{7,15}} | collective-permute-start | bytes 2359304 | tf_op jit(solution)/shard_map/ppermute | solution.py:104
  451.2 24.0 %collective-permute-start.54 = (bf16[208,2048]{1,0:T(8,128)(2,1)}, bf16[208,2048]{1,0:T(8,128)(2,1)S(1)}, u32[]{:S(2)}, u32[]{:S(2)}) collective-permute-start(bf16[208,2048]{1,0:T(8,128)(2,1)} %collective-permute-done.49.refs_1_), channel_id=1, source_target_pairs={{0,1},{1,0},{2,3},{3,2},{4,5},{5,4},{6,7},{7,6},{8,9},{9,8},{10,11... | collective-permute-start | bytes 2555912 | tf_op jit(solution)/shard_map/ppermute | solution.py:137
  451.2 24.2 %collective-permute-start.55 = (bf16[208,2048]{1,0:T(8,128)(2,1)}, bf16[208,2048]{1,0:T(8,128)(2,1)}, u32[]{:S(2)}, u32[]{:S(2)}) collective-permute-start(bf16[208,2048]{1,0:T(8,128)(2,1)} %collective-permute-done.50.refs_2_), channel_id=1, source_target_pairs={{0,1},{1,0},{2,3},{3,2},{4,5},{5,4},{6,7},{7,6},{8,9},{9,8},{10,11... | collective-permute-start | bytes 2555912 | tf_op jit(solution)/shard_map/ppermute | solution.py:137
  475.2 117.8 %collective-permute-start.39 = (bf16[4,192,2048]{2,1,0:T(8,128)(2,1)}, bf16[4,192,2048]{2,1,0:T(8,128)(2,1)}, u32[]{:S(2)}, u32[]{:S(2)}) collective-permute-start(bf16[4,192,2048]{2,1,0:T(8,128)(2,1)} %get-tuple-element.88), channel_id=1, source_target_pairs={{0,1},{1,0},{2,3},{3,2},{4,5},{5,4},{6,7},{7,6},{8,9},{9,8},{10,11... | collective-permute-start | bytes 9437192 | tf_op jit(solution)/shard_map/ppermute | solution.py:137
  475.4 25.3 %collective-permute-start.44 = (bf16[512,512]{1,0:T(8,128)(2,1)}, bf16[512,512]{1,0:T(8,128)(2,1)}, u32[]{:S(2)}, u32[]{:S(2)}) collective-permute-start(bf16[512,512]{1,0:T(8,128)(2,1)} %get-tuple-element.108), channel_id=1, source_target_pairs={{0,8},{8,16},{1,9},{9,17},{2,10},{10,18},{3,11},{11,19},{4,12},{12... | collective-permute-start | bytes 1572872 | tf_op jit(solution)/shard_map/ppermute | solution.py:107
  477.6 28.4 %collective-permute-start.47 = (bf16[512,512]{1,0:T(8,128)(2,1)}, bf16[512,512]{1,0:T(8,128)(2,1)}, u32[]{:S(2)}, u32[]{:S(2)}) collective-permute-start(bf16[512,512]{1,0:T(8,128)(2,1)} %get-tuple-element.109), channel_id=1, source_target_pairs={{24,16},{16,8},{25,17},{17,9},{26,18},{18,10},{27,19},{19,11},{28,... | collective-permute-start | bytes 1572872 | tf_op jit(solution)/shard_map/ppermute | solution.py:108
  487.4 21.5 %collective-permute-start.58 = (bf16[80,2048]{1,0:T(8,128)(2,1)S(1)}, bf16[80,2048]{1,0:T(8,128)(2,1)S(1)}, u32[]{:S(2)}, u32[]{:S(2)}) collective-permute-start(bf16[80,2048]{1,0:T(8,128)(2,1)S(1)} %get-tuple-element.123), channel_id=1, source_target_pairs={{0,0},{1,4},{2,2},{3,6},{4,1},{5,5},{6,3},{7,7},{8,8},{9,12},{10,1... | collective-permute-start | bytes 983048 | tf_op jit(solution)/shard_map/ppermute | solution.py:153
  493.0 63.5 %collective-permute-start.37 = (bf16[192,2048]{1,0:T(8,128)(2,1)}, bf16[192,2048]{1,0:T(8,128)(2,1)}, u32[]{:S(2)}, u32[]{:S(2)}) collective-permute-start(bf16[192,2048]{1,0:T(8,128)(2,1)} %get-tuple-element.107), channel_id=1, source_target_pairs={{24,16},{16,8},{25,17},{17,9},{26,18},{18,10},{27,19},{19,11},{28,... | collective-permute-start | bytes 2359304 | tf_op jit(solution)/shard_map/ppermute | solution.py:108
  500.7 105.2 %collective-permute-start.35 = (bf16[192,2048]{1,0:T(8,128)(2,1)}, bf16[192,2048]{1,0:T(8,128)(2,1)}, u32[]{:S(2)}, u32[]{:S(2)}) collective-permute-start(bf16[192,2048]{1,0:T(8,128)(2,1)} %get-tuple-element.106), channel_id=1, source_target_pairs={{0,8},{8,16},{16,24},{1,9},{9,17},{17,25},{2,10},{10,18},{18,26},{... | collective-permute-start | bytes 2359304 | tf_op jit(solution)/shard_map/ppermute | solution.py:109
  507.6 28.8 %collective-permute-start.45 = (bf16[512,512]{1,0:T(8,128)(2,1)S(1)}, bf16[512,512]{1,0:T(8,128)(2,1)S(1)}, u32[]{:S(2)}, u32[]{:S(2)}) collective-permute-start(bf16[512,512]{1,0:T(8,128)(2,1)S(1)} %get-tuple-element.110), channel_id=1, source_target_pairs={{0,8},{8,16},{16,24},{1,9},{9,17},{17,25},{2,10},{10,18},{18,26},{... | collective-permute-start | bytes 1572872 | tf_op jit(solution)/shard_map/ppermute | solution.py:109
  536.4 24.4 %collective-permute-start.62 = (bf16[80,2048]{1,0:T(8,128)(2,1)}, bf16[80,2048]{1,0:T(8,128)(2,1)S(1)}, u32[]{:S(2)}, u32[]{:S(2)}) collective-permute-start(bf16[80,2048]{1,0:T(8,128)(2,1)} %dynamic-slice_bitcast_fusion.1), channel_id=1, source_target_pairs={{0,8},{1,9},{2,10},{3,11},{4,12},{5,13},{6,14},{7,15}} | collective-permute-start | bytes 983048 | tf_op jit(solution)/shard_map/ppermute | solution.py:104
  559.5 46.5 %collective-permute-start.38 = (bf16[192,2048]{1,0:T(8,128)(2,1)}, bf16[192,2048]{1,0:T(8,128)(2,1)}, u32[]{:S(2)}, u32[]{:S(2)}) collective-permute-start(bf16[192,2048]{1,0:T(8,128)(2,1)} %add_convert_fusion.3), channel_id=1, source_target_pairs={{24,16},{16,8},{8,0},{25,17},{17,9},{9,1},{26,18},{18,10},{10,2},{... | collective-permute-start | bytes 2359304 | tf_op jit(solution)/shard_map/ppermute | solution.py:110
  576.2 22.2 %collective-permute-start.64 = (bf16[80,2048]{1,0:T(8,128)(2,1)S(1)}, bf16[80,2048]{1,0:T(8,128)(2,1)S(1)}, u32[]{:S(2)}, u32[]{:S(2)}) collective-permute-start(bf16[80,2048]{1,0:T(8,128)(2,1)S(1)} %get-tuple-element.118), channel_id=1, source_target_pairs={{0,8},{8,16},{16,24},{1,9},{9,17},{17,25},{2,10},{10,18},{18,26},{... | collective-permute-start | bytes 983048 | tf_op jit(solution)/shard_map/ppermute | solution.py:109
  595.4 21.5 %collective-permute-start.40 = (bf16[192,2048]{1,0:T(8,128)(2,1)S(1)}, bf16[192,2048]{1,0:T(8,128)(2,1)S(1)}, u32[]{:S(2)}, u32[]{:S(2)}) collective-permute-start(bf16[192,2048]{1,0:T(8,128)(2,1)S(1)} %get-tuple-element.103), channel_id=1, source_target_pairs={{0,6},{1,7},{2,4},{3,5},{4,2},{5,3},{6,0},{7,1},{8,14},{9,15},{10,... | collective-permute-start | bytes 2359304 | tf_op jit(solution)/shard_map/ppermute | solution.py:137
  598.4 33.6 %collective-permute-start.41 = (bf16[192,2048]{1,0:T(8,128)(2,1)S(1)}, bf16[192,2048]{1,0:T(8,128)(2,1)S(1)}, u32[]{:S(2)}, u32[]{:S(2)}) collective-permute-start(bf16[192,2048]{1,0:T(8,128)(2,1)S(1)} %get-tuple-element.105), channel_id=1, source_target_pairs={{0,2},{1,3},{2,0},{3,1},{4,6},{5,7},{6,4},{7,5},{8,10},{9,11},{10,... | collective-permute-start | bytes 2359304 | tf_op jit(solution)/shard_map/ppermute | solution.py:137
  602.5 29.5 %collective-permute-start.42 = (bf16[192,2048]{1,0:T(8,128)(2,1)S(1)}, bf16[192,2048]{1,0:T(8,128)(2,1)S(1)}, u32[]{:S(2)}, u32[]{:S(2)}) collective-permute-start(bf16[192,2048]{1,0:T(8,128)(2,1)S(1)} %get-tuple-element.104), channel_id=1, source_target_pairs={{0,4},{1,5},{2,6},{3,7},{4,0},{5,1},{6,2},{7,3},{8,12},{9,13},{10,... | collective-permute-start | bytes 2359304 | tf_op jit(solution)/shard_map/ppermute | solution.py:137
  (90 other events, 1384.1 us)
Sparse Core Ops, SparseCore 0:
  10.9 98.7 all-gather.3
  111.6 42.8 all-gather.7
  156.9 73.2 all-gather.5
  310.6 59.3 reduce-scatter.4
  373.6 112.8 reduce-scatter.2

commit v4 on v3

--- a/solution.py
+++ b/solution.py
@@ -60,74 +60,17 @@
     return lax.optimization_barrier((value, *earlier))[0]
 
 
-UP = [(0, 1), (1, 2), (2, 3)]
-DOWN = [(3, 2), (2, 1), (1, 0)]
-
-
-def pick(plane, options):
-    return lax.select_n(plane, *options)
-
-
 def plane_gather(block):
-    count = lax.axis_size("dp")
-    plane = lax.axis_index("dp")
-    if count != 4:
-        whole = lax.all_gather(block, "dp", axis=0)
-        return [whole[i] for i in range(count)], [jnp.int32(i) for i in range(count)]
-    up1 = lax.ppermute(block, "dp", UP)
-    down1 = lax.ppermute(block, "dp", DOWN)
-    up2 = lax.ppermute(up1, "dp", UP[1:])
-    down2 = lax.ppermute(down1, "dp", DOWN[1:])
-    up3 = lax.ppermute(up2, "dp", UP[2:])
-    down3 = lax.ppermute(down2, "dp", DOWN[2:])
-    blocks = [
-        block,
-        pick(plane, [down1, down1, up1, up1]),
-        pick(plane, [down2, up1, down1, up2]),
-        pick(plane, [down3, down2, up2, up3]),
-    ]
-    table = jnp.array([[0, 1, 2, 3], [1, 2, 0, 3], [2, 1, 3, 0], [3, 2, 1, 0]], jnp.int32)
-    mine = lax.dynamic_index_in_dim(table, plane, 0, keepdims=False)
-    return blocks, [mine[i] for i in range(4)]
+    whole = lax.all_gather(block, "dp", axis=0)
+    return [whole[i] for i in range(whole.shape[0])]
 
 
 def add_low(left, right):
     return (left.astype(f32) + right.astype(f32)).astype(left.dtype)
 
 
-def plane_scatter(parts):
-    count = lax.axis_size("dp")
-    plane = lax.axis_index("dp")
-    if count != 4:
-        return lax.psum_scatter(jnp.stack(parts), "dp", scatter_dimension=0, tiled=False).astype(f32)
-    own, first, second, third = parts
-    up3 = lax.ppermute(third, "dp", UP[:1])
-    down3 = lax.ppermute(third, "dp", DOWN[:1])
-    middle = pick(plane, [second, third, third, second])
-    up2 = lax.ppermute(add_low(middle, up3), "dp", UP[:2])
-    down2 = lax.ppermute(add_low(middle, down3), "dp", DOWN[:2])
-    up1 = lax.ppermute(add_low(pick(plane, [first, first, second, second]), up2), "dp", UP)
-    down1 = lax.ppermute(add_low(pick(plane, [second, second, first, first]), down2), "dp", DOWN)
-    return own.astype(f32) + up1.astype(f32) + down1.astype(f32)
-
-
-def slots_of(whole):
-    count = lax.axis_size("dp")
-    if count != 4:
-        return [whole[i] for i in range(count)]
-    plane = lax.axis_index("dp")
-    table = jnp.array([[0, 1, 2, 3], [1, 2, 0, 3], [2, 1, 3, 0], [3, 2, 1, 0]], jnp.int32)
-    mine = lax.dynamic_index_in_dim(table, plane, 0, keepdims=False)
-    return [lax.dynamic_index_in_dim(whole, mine[i], 0, keepdims=False) for i in range(4)]
-
-
-def in_order(blocks, planes):
-    if lax.axis_size("dp") != 4:
-        return jnp.stack(blocks)
-    whole = jnp.zeros((4, *blocks[0].shape), blocks[0].dtype)
-    for block, plane in zip(blocks, planes):
-        whole = lax.dynamic_update_index_in_dim(whole, block, plane, 0)
-    return whole
+def plane_scatter(whole):
+    return lax.psum_scatter(whole, "dp", scatter_dimension=0, tiled=False).astype(f32)
 
 
 FLIP = {bit: [(i, i ^ bit) for i in range(8)] for bit in (1, 2, 4, 6)}
@@ -137,22 +80,36 @@
     return lax.ppermute(block, "fsdp", FLIP[bit])
 
 
-def output_rows(term):
-    place = lax.axis_index("fsdp")
-    plane = lax.axis_index("dp")
-    rows = term.shape[0] // 4
-    blocks = term.reshape(4, rows, term.shape[1])
-    y, x, core = place // 4, (place // 2) % 2, place % 2
-    by_group = jnp.zeros_like(blocks)
-    for a in (0, 1):
-        for b in (0, 1):
-            sent = lax.dynamic_index_in_dim(blocks, 2 * (x ^ a) + (y ^ b), 0, keepdims=False)
-            moves = [
-                (i, 4 * (i % 2) + 2 * ((i // 2) % 2 ^ a) + ((i // 4) ^ b)) for i in range(8)
-            ]
-            got = lax.ppermute(sent, "fsdp", moves)
-            by_group = lax.dynamic_update_index_in_dim(by_group, got, 2 * (core ^ b) + (x ^ a), 0)
-    return plane_scatter(slots_of(by_group))
+def shift(block, step):
+    return lax.ppermute(block, "dp", [(i, (i + step) % 4) for i in range(4)])
+
+
+def gather_planes(block):
+    copies = jnp.broadcast_to(block[None], (4, *block.shape))
+    return lax.all_to_all(copies, "dp", split_axis=0, concat_axis=0)
+
+
+def swap_planes(whole):
+    return lax.all_to_all(whole, "dp", split_axis=0, concat_axis=0)
+
+
+def output_rows(mine, others, *earlier):
+    group, plane = lax.axis_index("fsdp") // 2, lax.axis_index("dp")
+    whole = add_low(mine, flip(others, 1))
+
+    def to(bit):
+        return lax.dynamic_index_in_dim(whole, group ^ bit, 0, keepdims=False)
+
+    parts = [to(0)] + [flip(to(bit), 2 * bit) for bit in (1, 2, 3)]
+    by_group = jnp.zeros_like(whole)
+    for bit, part in enumerate(parts):
+        by_group = lax.dynamic_update_index_in_dim(by_group, part, group ^ bit, 0)
+    by_group = after(by_group, *earlier)
+    ahead = [lax.dynamic_index_in_dim(by_group, (plane + k) % 4, 0, keepdims=False) for k in range(4)]
+    total = ahead[0].astype(f32)
+    for k in (1, 2, 3):
+        total = total + shift(ahead[k], k).astype(f32)
+    return total
 
 
 def block_rows_of(length):
@@ -321,15 +278,14 @@
     sent = jnp.concatenate([query_scaled, spread(key_weight), spread(value_weight)], -1)
     sent = jnp.transpose(sent, (1, 0, 2)).reshape(ring * own_rows, cols)
     plane_cols = lax.all_to_all(sent, "fsdp", split_axis=0, concat_axis=0, tiled=True)
-    project = in_order(*plane_gather(plane_cols)).reshape(width, cols)
+    project = jnp.concatenate(plane_gather(plane_cols), 0)
 
     picked = jnp.sum(
         jnp.where(jnp.arange(exit_scale.shape[0], dtype=jnp.int32) == group_ids[0], exit_scale, 0.0)
     )
     cotangent = output_grad[0].astype(f32) * picked
     direct = keep * cotangent
-    direct_all = plane_gather(after(direct.astype(bf16), project))[0]
-    direct_all = jnp.concatenate(direct_all, 0)
+    direct_all = jnp.concatenate(plane_gather(direct.astype(bf16)), 0)
 
     gain_second = lax.all_gather(
         lax.all_gather(feedforward_gain, "fsdp", axis=0, tiled=False), "dp", axis=0, tiled=False
@@ -365,7 +321,7 @@
     inv_second = rms_scale(middle)
     second_mine = (middle * inv_second * gain_second).astype(bf16)
 
-    second_all = jnp.concatenate(plane_gather(second_mine)[0], 0)
+    second_all = jnp.concatenate(plane_gather(second_mine), 0)
     gate_use, up_use = gate_up[:, :ff_own], gate_up[:, ff_own:]
     gate_pre = dot_plain(second_all, gate_use)
     upward = dot_plain(second_all, up_use)
@@ -379,7 +335,7 @@
     grad_up_low = (grad_hidden * silu_gate).astype(bf16)
     grad_both = jnp.concatenate([grad_gate_low, grad_up_low], 1)
     second_terms = dot_right_t(grad_both, gate_up).astype(bf16).reshape(planes, tokens, width)
-    grad_second = plane_scatter([second_terms[i] for i in range(planes)])
+    grad_second = plane_scatter(second_terms)
 
     down_term = dot_left_t(hidden_low, direct_all).astype(bf16)
     gate_up_term = dot_left_t(second_all, grad_both).astype(bf16)
@@ -389,7 +345,7 @@
     ).astype(f32)
     branch_terms = dot_plain(hidden_low, down_use).astype(bf16).reshape(planes, tokens, width)
     branch_terms = after(branch_terms, grad_second)
-    branch_feed = plane_scatter([branch_terms[i] for i in range(planes)])
+    branch_feed = plane_scatter(branch_terms)
     output = (rows + keep * (branch_attention + branch_feed)).astype(bf16)
 
     second_gain_term = jnp.sum(grad_second * middle * inv_second, 0)
@@ -415,7 +371,7 @@
     input_grad = cotangent + grad_middle + grad_rows
 
     project_term = dot_left_t(normed, grad_cols).astype(bf16).reshape(planes, ring * own_rows, cols)
-    project_plane = plane_scatter(slots_of(project_term)).astype(bf16)
+    project_plane = plane_scatter(project_term).astype(bf16)
     back = lax.all_to_all(project_plane, "fsdp", split_axis=0, concat_axis=0, tiled=True)
     back = back.reshape(ring, own_rows, cols).astype(f32)
 
@@ -436,9 +392,7 @@
     ).reshape(tokens, width)
     output_term = dot_left_t(attended_by_owner, grad_branch_low).astype(bf16)
     output_plane = lax.psum_scatter(output_term, "fsdp", scatter_dimension=0, tiled=True)
-    output_grad_weight = plane_scatter(
-        slots_of(output_plane.reshape(planes, own_rows, width))
-    )
+    output_grad_weight = plane_scatter(output_plane.reshape(planes, own_rows, width))
     second_gain_all = lax.psum(lax.psum(second_gain_term, "fsdp"), "dp")
     mine = (lax.axis_index("dp") * ring + place) * own_rows
     second_gain_grad = lax.dynamic_slice_in_dim(second_gain_all, mine, own_rows)
@@ -460,11 +414,6 @@
 PIECES = ((0, 0), (2, 0), (4, 0), (6, 0), (6, 1), (1, 0), (3, 0), (5, 0), (7, 0), (7, 1))
 TO_CORE = (7, 3, 5, 1)
 TO_CHIPS = (6, 2, 4, 0)
-SLOT_HOPS = (
-    (("down", 1), ("down", 1), ("up", 1), ("up", 1)),
-    (("down", 2), ("up", 1), ("down", 1), ("up", 2)),
-    (("down", 3), ("down", 2), ("up", 2), ("up", 3)),
-)
 VMEM = pl.BlockSpec(memory_space=pltpu.VMEM)
 SMEM = pl.BlockSpec(memory_space=pltpu.SMEM)
 log2_e = math.log2(math.e)
@@ -487,34 +436,35 @@
     return scores, (key_pos <= query_pos) & (key_pos >= starts)
 
 
-def front_kernel(tokens, at_ref, *refs):
-    pieces, refs = refs[:10], refs[10:]
-    hops, refs = refs[:7], refs[7:]
+def front_kernel(at_ref, normed_ref, *refs):
+    columns_refs, refs = refs[:2], refs[2:]
     cos_ref, sin_ref, starts_ref, refs = refs[0], refs[1], refs[2], refs[3:]
     q_ref, k_ref, v_ref, mixed_ref, norm_ref, project_ref, gain_ref, vt_ref = refs
-    place, plane = at_ref[0], at_ref[1]
-    length = 8 * tokens
-    plane_rows = hops[0].shape[0] - 16
-
-    def put(ref, owner):
-        project_ref[pl.ds(pl.multiple_of(owner * plane_rows, plane_rows), plane_rows), :] = ref[:plane_rows, :]
-        gain_ref[owner] = ref[plane_rows:, :]
-
-    put(hops[0], plane)
-    for hop in (1, 2, 3):
-
-        @pl.when(plane >= hop)
-        def _():
-            put(hops[2 * hop - 1], plane - hop)
-
-        @pl.when(plane + hop <= 3)
-        def _():
-            put(hops[2 * hop], plane + hop)
-
+    place = at_ref[0]
+    length = normed_ref.shape[0]
+    core = place & 1
+    group = place >> 1
+    rows = columns_refs[0].shape[2] - 16
     q_width = q_ref.shape[1]
-    for piece in range(10):
-        here = pl.ds(start_of(place, piece, tokens), pieces[piece].shape[0])
-        raw = dot_plain(pieces[piece][...], project_ref[...])
+    q_all = 2 * q_width
+    for owner in range(4):
+        for bit in range(4):
+            for side in range(2):
+                block = columns_refs[side]
+                device = 2 * (group ^ bit) + (core ^ side)
+                here = pl.ds(pl.multiple_of((owner * 8 + device) * rows, rows), rows)
+                for which in range(2):
+
+                    @pl.when(core == which)
+                    def _():
+                        project_ref[here, :q_width] = block[owner, bit, :rows, which * q_width : (which + 1) * q_width]
+
+                project_ref[here, q_width:] = block[owner, bit, :rows, q_all:]
+                gain_ref[owner * 8 + device] = block[owner, bit, rows:, :HEAD_DIM]
+
+    for low_row in range(0, length, 256):
+        here = slice(low_row, low_row + 256)
+        raw = dot_plain(normed_ref[here, :], project_ref[...])
         cosine, sine = cos_ref[here, :], sin_ref[here, :]
         for low in range(0, q_width, HEAD_DIM):
             q_ref[here, low : low + HEAD_DIM] = turn(
@@ -540,12 +490,11 @@
             norm_ref[head, :, low:high] = top + jnp.log2(total)
 
 
-def front(at, pieces, hops, cosine, sine, starts):
-    tokens = pieces[0].shape[0]
-    length = 8 * tokens
-    plane_rows, cols = hops[0].shape[0] - 16, hops[0].shape[1]
-    q_width = cols - 2 * HEAD_DIM
-    width = 4 * plane_rows
+def front(at, normed, columns, columns_other, cosine, sine, starts):
+    length = normed.shape[0]
+    q_width = (columns.shape[3] - 2 * HEAD_DIM) // 2
+    cols = q_width + 2 * HEAD_DIM
+    width = 32 * (columns.shape[2] - 16)
     shapes = [
         jax.ShapeDtypeStruct((length, q_width), bf16),
         jax.ShapeDtypeStruct((length, HEAD_DIM), bf16),
@@ -553,11 +502,11 @@
         jax.ShapeDtypeStruct((length, q_width), bf16),
         jax.ShapeDtypeStruct((q_width // HEAD_DIM, 1, length), f32),
         jax.ShapeDtypeStruct((width, cols), bf16),
-        jax.ShapeDtypeStruct((4, 16, cols), bf16),
+        jax.ShapeDtypeStruct((32, 16, HEAD_DIM), bf16),
     ]
     return pl.pallas_call(
-        functools.partial(front_kernel, tokens),
-        in_specs=[SMEM] + [VMEM] * 20,
+        front_kernel,
+        in_specs=[SMEM] + [VMEM] * 6,
         out_specs=[VMEM] * 7,
         out_shape=shapes,
         scratch_shapes=[pltpu.VMEM((HEAD_DIM, length), bf16)],
@@ -568,7 +517,7 @@
             transcendentals=length * length,
         ),
         name="front",
-    )(at, *pieces, *hops, cosine, sine, starts)
+    )(at, normed, columns, columns_other, cosine, sine, starts)
 
 
 def back_kernel(tokens, at_ref, q_ref, k_ref, v_ref, mixed_ref, norm_ref, grad_ref, project_ref,
@@ -625,7 +574,7 @@
         ],
         compiler_params=pltpu.CompilerParams(vmem_limit_bytes=52 << 20),
         cost_estimate=pl.CostEstimate(
-            flops=2 * length * width * cols + 7 * length * length * q_width,
+            flops=140 * length * width * cols + 7 * length * length * q_width,
             bytes_accessed=2 * length * width + 2 * width * cols,
             transcendentals=length * length,
         ),
@@ -633,181 +582,181 @@
     )(at, queries, keys, values, mixed, norm, grads, project, cosine, sine, starts)
 
 
-def project_grad_kernel(tokens, at_ref, *refs):
-    pieces, (cols_ref, out_ref) = refs[:10], refs[10:]
-    place = at_ref[0]
-    total = None
-    for piece in range(10):
-        here = pl.ds(start_of(place, piece, tokens), pieces[piece].shape[0])
-        term = dot_left_t(cols_ref[here, :], pieces[piece][...])
-        total = term if total is None else total + term
-    turned = jnp.transpose(total).astype(bf16)
-    out_ref[...] = turned.reshape(out_ref.shape)
-
-
-def project_grad(at, pieces, grad_cols):
-    tokens, width = pieces[0].shape
+def project_grad_kernel(normed_ref, cols_ref, out_ref):
+    out_ref[...] = jnp.transpose(dot_left_t(cols_ref[...], normed_ref[...])).astype(bf16)
+
+
+def project_grad(normed, grad_cols):
+    length, width = normed.shape
     cols = grad_cols.shape[1]
+    part = 512
     return pl.pallas_call(
-        functools.partial(project_grad_kernel, tokens),
-        in_specs=[SMEM] + [VMEM] * 11,
-        out_specs=VMEM,
-        out_shape=jax.ShapeDtypeStruct((4, width // 4, cols), bf16),
+        project_grad_kernel,
+        grid=(width // part,),
+        in_specs=[
+            pl.BlockSpec((length, part), lambda i: (0, i)),
+            pl.BlockSpec((length, cols), lambda i: (0, 0)),
+        ],
+        out_specs=pl.BlockSpec((part, cols), lambda i: (i, 0)),
+        out_shape=jax.ShapeDtypeStruct((width, cols), bf16),
         compiler_params=pltpu.CompilerParams(vmem_limit_bytes=52 << 20),
         cost_estimate=pl.CostEstimate(
-            flops=16 * tokens * width * cols, bytes_accessed=16 * tokens * width, transcendentals=0
+            flops=10 * length * width * cols, bytes_accessed=2 * length * width, transcendentals=0
         ),
         name="project_grad",
-    )(at, *pieces, grad_cols)
+    )(normed, grad_cols)
 
 
 def output_grad_kernel(tokens, at_ref, *refs):
-    pieces, (mixed_ref, out_ref, gain_ref) = refs[:10], refs[10:]
+    pieces, (mixed_ref, other_ref, out_ref, rest_ref, gain_ref) = refs[:5], refs[5:]
     place = at_ref[0]
-    total = None
+    core = place & 1
+    totals = [None, None]
     gain = None
-    for piece in range(10):
+    for piece in range(5):
         bit, half = PIECES[piece]
         rows = tokens // 2 if bit >= 6 else tokens
         here = pl.ds(start_of(place, piece, tokens), rows)
-        term = dot_left_t(mixed_ref[here, :], pieces[piece][:rows, :])
-        total = term if total is None else total + term
+        block = pieces[piece][:rows, :]
+        for side, ref in enumerate((mixed_ref, other_ref)):
+            term = dot_left_t(ref[here, :], block)
+            totals[side] = term if totals[side] is None else totals[side] + term
         if pieces[piece].shape[0] > rows:
             extra = jnp.sum(pieces[piece][rows:, :].astype(f32), 0, keepdims=True)
             gain = extra if gain is None else gain + extra
-    out_ref[...] = total.astype(bf16).reshape(out_ref.shape)
     gain_ref[...] = gain
-
-
-def output_grad_term(at, pieces, mixed):
+    rows = out_ref.shape[1]
+    for side, total in enumerate(totals):
+        blocks = total.astype(bf16).reshape(4, rows, total.shape[1])
+        first = 2 * (core ^ side)
+        for head in range(2):
+            for which in range(2):
+
+                @pl.when(core == which)
+                def _():
+                    out_ref[first + head] = blocks[2 * head + which]
+                    rest_ref[first + head] = blocks[2 * head + 1 - which]
+
+
+def output_grad_term(at, pieces, mixed, mixed_other):
     length, own = mixed.shape
     tokens, width = length // 8, pieces[0].shape[1]
+    shape = jax.ShapeDtypeStruct((4, own // 4, width), bf16)
     return pl.pallas_call(
         functools.partial(output_grad_kernel, tokens),
-        in_specs=[SMEM] + [VMEM] * 11,
-        out_specs=[VMEM] * 2,
-        out_shape=[
-            jax.ShapeDtypeStruct((4, own // 4, width), bf16),
-            jax.ShapeDtypeStruct((1, width), f32),
-        ],
+        in_specs=[SMEM] + [VMEM] * 7,
+        out_specs=[VMEM] * 3,
+        out_shape=[shape, shape, jax.ShapeDtypeStruct((1, width), f32)],
         compiler_params=pltpu.CompilerParams(vmem_limit_bytes=52 << 20),
         cost_estimate=pl.CostEstimate(
             flops=2 * length * own * width, bytes_accessed=2 * length * width, transcendentals=0
         ),
         name="output_grad_term",
-    )(at, *pieces, mixed)
-
-
-def feed_kernel(chosen, count, at_ref, *refs):
-    n_ins = len(chosen[1])
-    n_opts, d_opts, refs = refs[:n_ins], refs[n_ins : 2 * n_ins], refs[2 * n_ins :]
-    both_ref, down_ref, refs = refs[0], refs[1], refs[2 + count :]
-    second_ref, direct_ref, hidden_ref, grads_ref, term_ref, total_ref = refs
+    )(at, *pieces, mixed, mixed_other)
+
+
+def feed_kernel(units, count, at_ref, *refs):
+    d_refs, n_ref, both_ref, down_ref, rows_ref, refs = refs[:4], *refs[4:8], refs[8 + count :]
+    second_ref, direct_ref, hidden_ref, grads_ref, term_ref, held_ref = refs
     step = pl.program_id(0)
-    plane = at_ref[1]
 
     @pl.when(step == 0)
     def _():
-        total_ref[...] = jnp.zeros_like(total_ref)
-        if n_ins == 1:
-            second_ref[...] = n_opts[0][...]
-            direct_ref[...] = d_opts[0][...]
-        else:
-            for p in range(4):
-
-                @pl.when(plane == p)
-                def _():
-                    second_ref[...] = n_opts[chosen[0][p]][...]
-                    direct_ref[...] = d_opts[chosen[0][p]][...]
-
-    second, direct = second_ref[...], direct_ref[...]
-    both = both_ref[...]
-    raw = dot_plain(second, both)
-    half = raw.shape[1] // 2
-    gate, upward = raw[:, :half], raw[:, half:]
-    sig = 1.0 / (1.0 + jnp.exp(-gate))
-    silu = gate * sig
-    hidden_ref[...] = (silu * upward).astype(bf16)
-    grad_hidden = dot_right_t(direct, down_ref[...])
-    grads = jnp.concatenate(
-        [
-            (grad_hidden * upward * sig * (1.0 + gate * (1.0 - sig))).astype(bf16),
-            (grad_hidden * silu).astype(bf16),
-        ],
-        1,
-    )
-    grads_ref[...] = grads
-    total_ref[...] += dot_right_t(grads, both)
-
-    @pl.when(step == pl.num_programs(0) - 1)
+        second_ref[...] = n_ref[...].reshape(second_ref.shape)
+        tokens = n_ref.shape[1]
+        for slot in range(4):
+            owner = (at_ref[1] - slot) & 3
+            direct_ref[pl.ds(pl.multiple_of(owner * tokens, tokens), tokens), :] = d_refs[slot][...]
+
+    @pl.when(step < units)
     def _():
-        term_ref[...] = total_ref[...].astype(bf16)
-
-
-def feed(at, slot, second_hops, direct_hops, both, down, so_far):
-    if slot == 0:
-        names, chosen = [("own", 0)], [0] * 4
-    else:
-        names = list(dict.fromkeys(SLOT_HOPS[slot - 1]))
-        chosen = [names.index(name) for name in SLOT_HOPS[slot - 1]]
-    tokens, width = second_hops["own", 0].shape
+        raw = dot_plain(second_ref[...], both_ref[...])
+        half = raw.shape[1] // 2
+        gate, upward = raw[:, :half], raw[:, half:]
+        sig = 1.0 / (1.0 + jnp.exp(-gate))
+        silu = gate * sig
+        hidden_ref[...] = (silu * upward).astype(bf16)
+        grad_hidden = dot_right_t(direct_ref[...], down_ref[...])
+        grad_gate = (grad_hidden * upward * sig * (1.0 + gate * (1.0 - sig))).astype(bf16)
+        grads = jnp.concatenate([grad_gate, (grad_hidden * silu).astype(bf16)], 1)
+        grads_ref[...] = grads
+        held_ref[step] = grads
+
+    @pl.when(step >= units)
+    def _():
+        total = None
+        for unit in range(units):
+            cols = slice(unit * held_ref.shape[2], (unit + 1) * held_ref.shape[2])
+            part = dot_right_t(held_ref[unit], rows_ref[:, cols])
+            total = part if total is None else total + part
+        term_ref[...] = total.astype(bf16).reshape(term_ref.shape)
+
+
+def feed(at, part_at, parts_of, seconds, directs, both, down, so_far):
+    tokens, width = seconds.shape[1:]
+    some = 4 * tokens
     ff = down.shape[0]
-    unit = 128
+    unit, part = 128, 256
+    units, parts = ff // unit, width // part
     so_far = so_far or []
-    whole = pl.BlockSpec((tokens, width), lambda i: (0, 0))
-    shapes = [
-        jax.ShapeDtypeStruct((4 * tokens, width), bf16),
-        jax.ShapeDtypeStruct((4 * tokens, width), bf16),
-        jax.ShapeDtypeStruct((4 * tokens, ff), bf16),
-        jax.ShapeDtypeStruct((4 * tokens, 2 * ff), bf16),
-        jax.ShapeDtypeStruct((tokens, width), bf16),
-    ]
-    first = 1 + 2 * len(names) + 2
+    total = parts_of * some
     outs = pl.pallas_call(
-        functools.partial(feed_kernel, (chosen, names), len(so_far)),
-        grid=(ff // unit,),
-        in_specs=[SMEM]
-        + [whole] * (2 * len(names))
-        + [
-            pl.BlockSpec((width, 2 * unit), lambda i: (0, i)),
-            pl.BlockSpec((unit, width), lambda i: (i, 0)),
+        functools.partial(feed_kernel, units, len(so_far)),
+        grid=(units + parts,),
+        in_specs=[
+            SMEM,
+            *[pl.BlockSpec((tokens, width), lambda i: (part_at, 0))] * 4,
+            pl.BlockSpec((4, tokens, width), lambda i: (0, 0, 0)),
+            pl.BlockSpec((width, 2 * unit), lambda i: (0, jnp.minimum(i, units - 1))),
+            pl.BlockSpec((unit, width), lambda i: (jnp.minimum(i, units - 1), 0)),
+            pl.BlockSpec((part, 2 * ff), lambda i: (jnp.maximum(i - units, 0), 0)),
         ]
         + [pl.BlockSpec(memory_space=pl.ANY)] * len(so_far),
         out_specs=[
-            pl.BlockSpec((tokens, width), lambda i: (slot, 0)),
-            pl.BlockSpec((tokens, width), lambda i: (slot, 0)),
-            pl.BlockSpec((tokens, unit), lambda i: (slot, i)),
-            pl.BlockSpec((tokens, 2 * unit), lambda i: (slot, i)),
-            whole,
+            pl.BlockSpec((some, width), lambda i: (part_at, 0)),
+            pl.BlockSpec((some, width), lambda i: (part_at, 0)),
+            pl.BlockSpec((some, unit), lambda i: (part_at, jnp.minimum(i, units - 1))),
+            pl.BlockSpec((some, 2 * unit), lambda i: (part_at, jnp.minimum(i, units - 1))),
+            pl.BlockSpec((4, tokens, part), lambda i: (0, 0, jnp.maximum(i - units, 0))),
         ],
-        out_shape=shapes,
-        scratch_shapes=[pltpu.VMEM((tokens, width), f32)],
-        input_output_aliases={first + i: i for i in range(len(so_far))},
+        out_shape=[
+            jax.ShapeDtypeStruct((total, width), bf16),
+            jax.ShapeDtypeStruct((total, width), bf16),
+            jax.ShapeDtypeStruct((total, ff), bf16),
+            jax.ShapeDtypeStruct((total, 2 * ff), bf16),
+            jax.ShapeDtypeStruct((4, tokens, width), bf16),
+        ],
+        scratch_shapes=[pltpu.VMEM((units, some, 2 * unit), bf16)],
+        input_output_aliases={9 + i: i for i in range(len(so_far))},
         compiler_params=pltpu.CompilerParams(vmem_limit_bytes=52 << 20),
         cost_estimate=pl.CostEstimate(
-            flops=10 * tokens * width * ff,
-            bytes_accessed=6 * width * ff,
-            transcendentals=tokens * ff,
+            flops=10 * some * width * ff,
+            bytes_accessed=10 * width * ff,
+            transcendentals=some * ff,
         ),
         name="feed",
-    )(
-        at,
-        *[second_hops[name] for name in names],
-        *[direct_hops[name] for name in names],
-        both,
-        down,
-        *so_far,
-    )
+    )(at, *directs, seconds, both, down, both, *so_far)
     return outs[:4], outs[4]
 
 
-def hop_on(hops, step, *earlier):
-    before = (("own", 0), ("own", 0)) if step == 1 else (("up", step - 1), ("down", step - 1))
-    for name, moves in ((0, UP), (1, DOWN)):
-        block = hops[before[name]]
-        if earlier:
-            block = after(block, *earlier)
-        hops[("up", "down")[name], step] = lax.ppermute(block, "dp", moves[step - 1 :])
+def split_kernel(both_ref, gate_ref, up_ref):
+    half = gate_ref.shape[1]
+    gate_ref[...] = both_ref[:, :half].astype(f32)
+    up_ref[...] = both_ref[:, half:].astype(f32)
+
+
+def split(both):
+    rows, cols = both.shape
+    out = jax.ShapeDtypeStruct((rows, cols // 2), f32)
+    half = pl.BlockSpec((rows, 128), lambda i: (0, i))
+    return pl.pallas_call(
+        split_kernel,
+        grid=(cols // 256,),
+        in_specs=[pl.BlockSpec((rows, 256), lambda i: (0, i))],
+        out_specs=[half, half],
+        out_shape=[out, out],
+        name="split",
+    )(both)
 
 
 def fast_device(
@@ -839,49 +788,41 @@
     rows = layer_input[0].astype(f32)
     keep = layer_keep[0].astype(f32)
 
-    output_full = lax.all_gather(output_weight, ("dp", "fsdp"), axis=0, tiled=True)
     both_mine = jnp.stack(
         [gate_weight.reshape(-1, ff_own // 128, 128), up_weight.reshape(-1, ff_own // 128, 128)], 2
     ).reshape(-1, 2 * ff_own)
-    both = lax.all_gather(both_mine, "fsdp", axis=0, tiled=True)
-
     inv_first = rms_scale(rows)
     normed = (rows * inv_first).astype(bf16)
-    along_x, along_y, on_core = flip(normed, 2), flip(normed, 4), flip(normed, 1)
+    first = lax.all_gather(jnp.concatenate([normed, down_weight], 0), "fsdp", axis=0, tiled=False)
+    normed_all = first[:, :tokens].reshape(length, width)
+    down_use = first[:, tokens:].reshape(ff_own, width)
     gain_mine = attention_gain.astype(f32)[:, None]
 
-    def spread(weight):
-        scaled = (weight.astype(f32) * gain_mine).astype(bf16).reshape(own_rows, KV_HEADS, 1, HEAD_DIM)
-        return jnp.broadcast_to(scaled, (own_rows, KV_HEADS, 2, HEAD_DIM)).reshape(own_rows, 8, HEAD_DIM)
-
-    query_scaled = (query_weight.astype(f32) * gain_mine).astype(bf16).reshape(own_rows, 8, q_width)
-    sent = jnp.concatenate([query_scaled, spread(key_weight), spread(value_weight)], -1)
-    gain_row = jnp.pad(feedforward_gain[None, None, :], ((0, 15), (0, 7), (0, cols - own_rows)))
-    gain_row = jnp.broadcast_to(gain_row[:, :1], (16, 8, cols))
-    sent = jnp.transpose(jnp.concatenate([sent, gain_row], 0), (1, 0, 2)).reshape(-1, cols)
-    got = lax.all_to_all(sent, "fsdp", split_axis=0, concat_axis=0, tiled=True)
-    got = got.reshape(8, own_rows + 16, cols)
-    gains = jnp.pad(got[:, own_rows, :own_rows].reshape(1, 8 * own_rows), ((0, 15), (0, 0)))
-    columns = {("own", 0): jnp.concatenate([got[:, :own_rows].reshape(-1, cols), gains], 0)}
-    hop_on(columns, 1)
-    low = flip(after(along_x[:half], columns["own", 0]), 4)
-    high = flip(after(along_y[half:], columns["own", 0]), 2)
-    down_use = lax.all_gather(
-        after(down_weight, columns["own", 0]), "fsdp", axis=0, tiled=True
-    )
-    core_x, core_y = flip(along_x, 1), flip(along_y, 1)
-    hop_on(columns, 2)
-    core_low, core_high = flip(low, 1), flip(high, 1)
-    hop_on(columns, 3)
-    pieces = [normed, along_x, along_y, low, high, on_core, core_x, core_y, core_low, core_high]
-
+    def by_chip(weight):
+        scaled = (weight.astype(f32) * gain_mine).astype(bf16)
+        return scaled.reshape(own_rows, 4, weight.shape[1] // 4)
+
+    sent = jnp.concatenate([by_chip(query_weight), by_chip(key_weight), by_chip(value_weight)], -1)
+    sent = jnp.transpose(sent, (1, 0, 2))
+    wide = sent.shape[2]
+    gain_rows = jnp.pad(feedforward_gain[None, :], ((0, 15), (0, wide - own_rows)))
+    group = place // 2
+
+    def to_chip(bit):
+        block = lax.dynamic_index_in_dim(sent, group ^ bit, 0, keepdims=False)
+        return jnp.concatenate([block, gain_rows], 0)
+
+    columns = jnp.stack([to_chip(0)] + [flip(to_chip(bit), 2 * bit) for bit in (1, 2, 3)])
+    output_plane = gather_planes(after(output_weight, columns))
+    columns = gather_planes(after(columns, output_plane))
+    columns_other = flip(columns, 1)
+    output_full = lax.all_gather(output_plane, "fsdp", axis=1, tiled=True).reshape(width, width)
+    both = lax.all_gather(after(both_mine, columns), "fsdp", axis=0, tiled=True)
     picked = jnp.sum(
         jnp.where(jnp.arange(exit_scale.shape[0], dtype=jnp.int32) == group_ids[0], exit_scale, 0.0)
     )
     cotangent = output_grad[0].astype(f32) * picked
     direct = keep * cotangent
-    directs = {("own", 0): direct.astype(bf16)}
-    hop_on(directs, 1, columns["up", 2], columns["down", 2])
 
     half_dim = HEAD_DIM // 2
     cosine, sine = rotary_tables(length)
@@ -893,37 +834,42 @@
     positions = jnp.arange(length, dtype=jnp.int32)
     starts = jnp.max(jnp.where(positions[None, :] >= ends[:, None], ends[:, None], 0), 0)[None, :]
 
-    all_hops = [columns["own", 0]]
-    for step in (1, 2, 3):
-        all_hops += [columns["up", step], columns["down", step]]
+    direct_low = after(direct.astype(bf16), columns)
+    direct_1 = shift(direct_low, 1)
     queries, keys, values, mixed, norm, project, gains = front(
-        at, pieces, all_hops, cosine, sine, starts
-    )
-    gain_second = gains[:, 0, :].reshape(width).astype(f32)
-
-    hop_on(directs, 2, mixed)
+        at, normed_all, columns, columns_other, cosine, sine, starts
+    )
+    mixed = after(mixed, direct_1)
+    direct_2 = shift(direct_low, 2)
+    mixed_other = flip(mixed, 1)
+    gain_second = gains[:, 0, :own_rows].reshape(width).astype(f32)
+
     attended_low = lax.all_to_all(mixed, "fsdp", split_axis=0, concat_axis=1, tiled=True)
+    direct_3 = shift(direct_low, 3)
+    attended_low = after(attended_low, direct_2)
     branch_attention = dot_plain(attended_low, output_full)
     middle = rows + branch_attention
     inv_second = rms_scale(middle)
-    seconds = {("own", 0): (middle * inv_second * gain_second).astype(bf16)}
-
-    hop_on(seconds, 1)
-    hop_on(directs, 3, seconds["own", 0])
-    stacked, term_own = feed(at, 0, seconds, directs, both, down_use, None)
-    hop_on(seconds, 2)
-    stacked, term_1 = feed(at, 1, seconds, directs, both, down_use, stacked)
-    hop_on(seconds, 3)
-    stacked, term_2 = feed(at, 2, seconds, directs, both, down_use, stacked)
-    stacked, term_3 = feed(at, 3, seconds, directs, both, down_use, stacked)
+    directs = [direct_low, direct_1, direct_2, direct_3]
+    second_mine = (middle * inv_second * gain_second).astype(bf16)
+    seconds_low = gather_planes(after(second_mine[:half], direct_3, mixed_other))
+    seconds_high = gather_planes(after(second_mine[half:], seconds_low))
+
+    stacked, terms_low = feed(at, 0, 2, seconds_low, directs, both, down_use, None)
+    stacked, terms_high = feed(at, 1, 2, seconds_high, directs, both, down_use, stacked)
     second_all, direct_all, hidden_all, grads_all = stacked
-    grad_second = plane_scatter([term_own, term_1, term_2, term_3])
+    got_low = swap_planes(terms_low)
 
     down_term = dot_left_t(hidden_all, direct_all).astype(bf16)
+    got_high = swap_planes(after(terms_high, got_low))
+    grad_second = jnp.concatenate(
+        [jnp.sum(got_low.astype(f32), 0), jnp.sum(got_high.astype(f32), 0)], 0
+    )
     both_term = dot_left_t(second_all, grads_all).astype(bf16)
     down_grad = lax.psum_scatter(down_term, "fsdp", scatter_dimension=0, tiled=True).astype(f32)
     both_grad = lax.psum_scatter(both_term, "fsdp", scatter_dimension=0, tiled=True)
-    branch_terms = dot_plain(hidden_all, down_use).astype(bf16).reshape(4, tokens, width)
+    branch_terms = dot_plain(hidden_all, down_use).astype(bf16).reshape(2, 4, half, width)
+    branch_terms = jnp.transpose(branch_terms, (1, 0, 2, 3)).reshape(4, tokens, width)
 
     weighted = grad_second * gain_second
     grad_middle = inv_second * weighted - middle * inv_second**3 * jnp.mean(
@@ -938,26 +884,37 @@
     branch_block = jnp.concatenate(
         [grad_branch, gain_high, gain_low, jnp.zeros((14, width), bf16)], 0
     )
-    branch_x, branch_y, branch_core = flip(branch_block, 2), flip(branch_block, 4), flip(branch_block, 1)
-
+    ahead = [
+        lax.dynamic_index_in_dim(branch_terms, (plane + k) % 4, 0, keepdims=False) for k in range(4)
+    ]
+    branch_1, branch_3 = shift(after(ahead[1], grad_branch), 1), shift(after(ahead[3], grad_branch), 3)
+    branch_x, branch_y = flip(branch_block, 2), flip(branch_block, 4)
+    grad_heads = after(grad_heads, branch_x, branch_y, branch_1, branch_3)
+    branch_2 = shift(after(ahead[2], grad_branch), 2)
+    branch_low, branch_high = flip(branch_x[:half], 4), flip(branch_y[half:], 2)
     core_terms, chip_terms, grad_cols = back(
         at, queries, keys, values, mixed, norm, grad_heads, project, cosine, sine, starts
     )
+    core_terms = after(core_terms, branch_2, branch_low, branch_high)
     other = flip(core_terms, 1)
-    branch_low = flip(after(branch_x[:half], grad_cols), 4)
-    branch_high = flip(after(branch_y[half:], grad_cols), 2)
-    far = flip(add_low(chip_terms[0], other[0]), 6)
-    near_x = flip(add_low(chip_terms[1], other[1]), 2)
-    near_y = flip(add_low(chip_terms[2], other[2]), 4)
-    project_term = project_grad(at, pieces, grad_cols)
-    project_plane = plane_scatter(slots_of(project_term)).astype(bf16)
-    branch_pieces = [branch_block, branch_x, branch_y, branch_low, branch_high, branch_core]
-    branch_pieces += [flip(piece, 1) for piece in (branch_x, branch_y, branch_low, branch_high)]
-    output_term, gain_sum = output_grad_term(at, branch_pieces, mixed)
-    gain_own = lax.dynamic_slice_in_dim(gain_sum[0], place * 4 * own_rows, 4 * own_rows)
-    gain_own = jnp.pad(gain_own.reshape(4, 1, own_rows), ((0, 0), (0, 15), (0, width - own_rows)))
-    output_term = jnp.concatenate([output_term, gain_own.astype(bf16)], 1)
-    output_sum = output_rows(output_term.reshape(-1, width))
+    branch_pieces = [branch_block, branch_x, branch_y, branch_low, branch_high]
+    mine, others, gain_sum = output_grad_term(at, branch_pieces, after(mixed, core_terms), mixed_other)
+    other = after(other, mine)
+    sums = [add_low(chip_terms[i], other[i]) for i in range(3)]
+    far, near_x, near_y = flip(sums[0], 6), flip(sums[1], 2), flip(sums[2], 4)
+    project_term = project_grad(normed_all, after(grad_cols, *sums)).reshape(4, width // 4, cols)
+    project_got = swap_planes(project_term)
+    branch_feed = (
+        ahead[0].astype(f32) + branch_1.astype(f32) + branch_2.astype(f32) + branch_3.astype(f32)
+    )
+    group, core = place // 2, place % 2
+    gain_own = lax.dynamic_slice_in_dim(gain_sum[0], group * 8 * own_rows, 8 * own_rows)
+    gain_own = gain_own.reshape(4, 2, own_rows).astype(bf16)
+    gain_own = jnp.pad(gain_own[:, :, None, :], ((0, 0), (0, 0), (0, 15), (0, width - own_rows)))
+    mine = jnp.concatenate([mine, lax.dynamic_index_in_dim(gain_own, core, 1, keepdims=False)], 1)
+    others = jnp.concatenate([others, lax.dynamic_index_in_dim(gain_own, 1 - core, 1, keepdims=False)], 1)
+    output_sum = output_rows(after(mine, far, near_x, near_y), others, project_got)
+    project_plane = jnp.sum(project_got.astype(f32), 0).astype(bf16)
     weighted_first = (
         chip_terms[3].astype(f32)
         + other[3].astype(f32)
@@ -970,8 +927,6 @@
     )
     input_grad = cotangent + grad_middle + grad_rows
 
-    branch_terms = after(branch_terms, grad_branch)
-    branch_feed = plane_scatter([branch_terms[i] for i in range(4)])
     output = (rows + keep * (branch_attention + branch_feed)).astype(bf16)
 
     back_cols = lax.all_to_all(project_plane, "fsdp", split_axis=0, concat_axis=0, tiled=True)
@@ -989,7 +944,7 @@
         + jnp.sum(key_plain * key_weight.astype(f32), 1)
         + jnp.sum(value_plain * value_weight.astype(f32), 1)
     )
-    both_parts = both_grad.reshape(-1, ff_own // 128, 2, 128)
+    gate_grad, up_grad = split(both_grad)
     return (
         output[None],
         input_grad[None],
@@ -999,8 +954,8 @@
         value_plain * gain_mine,
         output_sum[:own_rows],
         output_sum[own_rows, :own_rows],
-        both_parts[:, :, 0].reshape(-1, ff_own).astype(f32),
-        both_parts[:, :, 1].reshape(-1, ff_own).astype(f32),
+        gate_grad,
+        up_grad,
         down_grad,
     )
 

time: 673 us -> 580 us (0.86)
  the two profiles are of different devices: /device:TPU:0 before, /device:TPU:9 now
where the time goes in v4:
time: 580 us; the launch traced here: 570 us
  waiting for transfers between devices  153 us (26%)
  Pallas kernels  115 us (20%)
  starting transfers between devices  76.7 us (13%)
  blocking collectives  66.6 us (11%)
  other arithmetic  47.7 us (8%)
  local copies, waits for them, and re-layouts  47.1 us (8%)
  matrix products  47.1 us (8%)
  between operations  16.5 us (3%)
    all_to_all x2, blocking collectives, gather_planes(): return lax.all_to_all(copies, 'dp', split_axis=0, concat_axis=0)  66.6 us
    pallas_call x2, Pallas kernels, feed(): pl.pallas_call(functools.partial(feed_kernel, units, len(so_far)), grid=(...  55.5 us
    ppermute x17, waiting for transfers between devices, flip(): return lax.ppermute(block, 'fsdp', FLIP[bit])  46.3 us
    ppermute x9, waiting for transfers between devices, shift(): return lax.ppermute(block, 'dp', [(i, (i + step) % 4) for i in range(4)])  41.5 us
    all_to_all x2, waiting for transfers between devices, gather_planes(): return lax.all_to_all(copies, 'dp', split_axis=0, concat_axis=0)  35.3 us
    dot_general x2, matrix products, dot_left_t(): lax.dot_general(left, right, (((0,), (0,)), ((), ())), preferred_element_...  24.6 us
    pallas_call x1, Pallas kernels, back(): pl.pallas_call(functools.partial(back_kernel, tokens), in_specs=[SMEM] +...  19.8 us
    pallas_call x1, Pallas kernels, front(): pl.pallas_call(front_kernel, in_specs=[SMEM] + [VMEM] * 6, out_specs=[VME...  18.6 us
  transfers between devices with their start and end apart: 39, of which 15 were waited for; matrix products, arithmetic and copies ran while one was open for 23% of the time, Pallas kernels for 19%

profile of v4, /device:TPU:9, one launch (start us, length us, event | category | flops | bytes accessed | tf_op | source)
XLA Modules:
  0.0 569.8 jit_solution(8358568060094517675)
XLA Ops:
  23.0 27.5 %all_to_all.82 = bf16[4,64,2048]{2,1,0:T(8,128)(2,1)} all-to-all(bf16[4,64,2048]{2,1,0:T(8,128)(2,1)S(1)} %broadcast_in_dim.98), channel_id=1, replica_groups=mesh['dp'=4,'fsdp'=8] {'dp'}, dimensions={0} | all-to-all | bytes 2097152 | tf_op jit(solution)/shard_map/all_to_all | solution.py:89
  51.9 6.4 %all-to-all-start.1 = ((bf16[4,4,80,768]{3,2,1,0:T(8,128)(2,1)}), bf16[4,4,80,768]{3,2,1,0:T(8,128)(2,1)}, u32[]{:S(2)}, u32[]{:S(2)}) async-start(bf16[4,4,80,768]{3,2,1,0:T(8,128)(2,1)} %broadcast_in_dim.99), calls=%async_computation.1 | async-start | bytes 3932160 | tf_op jit(solution)/shard_map/all_to_all | solution.py:89
  63.4 35.3 %all-to-all-done.1.refs_0_ = bf16[4,4,80,768]{3,2,1,0:T(8,128)(2,1)} async-done(((bf16[4,4,80,768]{3,2,1,0:T(8,128)(2,1)}), bf16[4,4,80,768]{3,2,1,0:T(8,128)(2,1)}, u32[]{:S(2)}, u32[]{:S(2)}) %all-to-all-start.1) | async-done | bytes 1966112 | tf_op jit(solution)/shard_map/all_to_all | solution.py:89
  98.8 3.0 collective-permute-start.3
  104.8 2.8 fusion.23
  110.5 4.0 collective-permute-start.5
  114.5 6.8 %slice.80 = bf16[8,192,2048]{2,1,0:T(8,128)(2,1)} slice(bf16[8,368,2048]{2,1,0:T(8,128)(2,1)} %bitcast.171), slice={[0:8], [0:192], [0:2048]} | slice | bytes 12582912 | tf_op jit(solution)/shard_map/slice | solution.py:797
  121.3 18.6 %front.1 = (bf16[1536,256]{1,0:T(8,128)(2,1)S(1)}, bf16[1536,128]{1,0:T(8,128)(2,1)S(1)}, bf16[1536,128]{1,0:T(8,128)(2,1)S(1)}, bf16[1536,256]{1,0:T(8,128)(2,1...) custom-call(s32[2]{0:T(128)S(1)} %pad_add_fusion.at_ref, ...), custom_call_target="tpu_custom_call" | custom-call | flops 5637144576 | bytes 10485760 | tf_op jit(solution)/shard_map/front/pallas_call | solution.py:507
  141.5 4.6 all-to-all-start.2
  146.9 11.3 %all-to-all-done.2 = bf16[8,192,256]{2,1,0:T(8,128)(2,1)} async-done(((bf16[8,192,256]{2,1,0:T(8,128)(2,1)}), bf16[8,192,256]{2,1,0:T(8,128)(2,1)}, u32[]{:S(2)}, u32[]{:S(2)}) %all-to-all-start.2) | async-done | bytes 786464 | tf_op jit(solution)/shard_map/all_to_all | solution.py:847
  160.3 16.2 %collective-permute-done.5.refs_2_ = bf16[192,2048]{1,0:T(8,128)(2,1)} collective-permute-done((bf16[192,2048]{1,0:T(8,128)(2,1)S(1)}, bf16[192,2048]{1,0:T(8,128)(2,1)}, u32[]{:S(2)}, u32[]{:S(2)}) %collective-permute-start.5) | collective-permute-done | bytes 786464 | tf_op jit(solution)/shard_map/ppermute | solution.py:84
  176.5 7.6 %multiply_reduce_fusion.2 = (f32[192]{0:T(256)S(1)}, f32[192,2048]{1,0:T(8,128)S(1)}) fusion(bf16[1,192,2048]{2,1,0:T(8,128)(2,1)} %param.15, bf16[192,2048]{1,0:T(8,128)(2,1)} %bitcast.183, bf16[2048,2048]{1,0:T(8,128)(2,1)} %bitcast.191), kind=kOutput, calls=%fused_computation.40 | convolution fusion | flops 1612185344 | bytes 11535104 | tf_op jit(solution)/shard_map/dot_general | solution.py:24
  185.6 39.2 %all_to_all.83.refs_4_ = bf16[4,96,2048]{2,1,0:T(8,128)(2,1)} all-to-all(bf16[4,96,2048]{2,1,0:T(8,128)(2,1)S(1)} %broadcast_in_dim.106), channel_id=1, replica_groups=mesh['dp'=4,'fsdp'=8] {'dp'}, dimensions={0} | all-to-all | bytes 3145728 | tf_op jit(solution)/shard_map/all_to_all | solution.py:89
  226.1 6.2 %all-to-all-start.4 = ((bf16[4,96,2048]{2,1,0:T(8,128)(2,1)}), bf16[4,96,2048]{2,1,0:T(8,128)(2,1)}, u32[]{:S(2)}, u32[]{:S(2)}) async-start(bf16[4,96,2048]{2,1,0:T(8,128)(2,1)} %broadcast_in_dim.107), calls=%async_computation.4 | async-start | bytes 3145728 | tf_op jit(solution)/shard_map/all_to_all | solution.py:89
  232.3 6.0 %slice.83 = bf16[8,176,2048]{2,1,0:T(8,128)(2,1)} slice(bf16[8,368,2048]{2,1,0:T(8,128)(2,1)} %bitcast.172), slice={[0:8], [192:368], [0:2048]} | slice | bytes 11534336 | tf_op jit(solution)/shard_map/slice | solution.py:798
  238.4 27.8 %feed.2 = (bf16[768,2048]{1,0:T(8,128)(2,1)}, bf16[768,2048]{1,0:T(8,128)(2,1)}, bf16[768,1408]{1,0:T(8,128)(2,1)}, bf16[768,2816]{1,0:T(8,128)(2,1)}, bf16[4,96,2048]{2,1,0:T(8,128)(2,1)}) custom-call(s32[2]{0:T(128)S(1)} %pad_add_fusion.at_ref, bf16[192,2048]{1,0:T(8,128)(2,1)S(1)} %fusion.14.refs_0_, ...), custom_call_target="tpu_custom_call" | custom-call | flops 11072962560 | bytes 28835840 | tf_op jit(solution)/shard_map/feed/pallas_call | solution.py:703
  266.1 7.1 %all-to-all-start.5 = ((bf16[4,96,2048]{2,1,0:T(8,128)(2,1)}), bf16[4,96,2048]{2,1,0:T(8,128)(2,1)}, u32[]{:S(2)}, u32[]{:S(2)}) async-start(bf16[4,96,2048]{2,1,0:T(8,128)(2,1)} %get-tuple-element.70), calls=%async_computation.5 | async-start | bytes 3145728 | tf_op jit(solution)/shard_map/all_to_all | solution.py:93
  273.2 27.8 %feed.3 = (bf16[768,2048]{1,0:T(8,128)(2,1)}, bf16[768,2048]{1,0:T(8,128)(2,1)}, bf16[768,1408]{1,0:T(8,128)(2,1)}, bf16[768,2816]{1,0:T(8,128)(2,1)}, bf16[4,96,2048]{2,1,0:T(8,128)(2,1)}) custom-call(s32[2]{0:T(128)S(1)} %pad_add_fusion.at_ref, ...), custom_call_target="tpu_custom_call", output_to_operand_aliasing={{0}: (9, {}), {1}: (10, {}), {2}: (11, {}), {3}: (12, {})} | custom-call | flops 11072962560 | bytes 28835840 | tf_op jit(solution)/shard_map/feed/pallas_call | solution.py:703
  301.0 9.8 %convolution_convert_fusion.1 = bf16[1408,2048]{1,0:T(8,128)(2,1)} fusion(bf16[768,1408]{1,0:T(8,128)(2,1)} %get-tuple-element.69, bf16[768,2048]{1,0:T(8,128)(2,1)} %get-tuple-element.98), kind=kOutput, calls=%fused_computation.1 | convolution fusion | flops 4432068608 | bytes 11075584 | tf_op jit(solution)/shard_map/dot_general | solution.py:32
  310.8 4.9 all-to-all-start.6
  315.8 8.0 %convolution_convert_fusion.2 = bf16[768,2048]{1,0:T(8,128)(2,1)S(1)} fusion(bf16[768,1408]{1,0:T(8,128)(2,1)S(1)} %copy-done.25, bf16[1408,2048]{1,0:T(8,128)(2,1)} %bitcast.168), kind=kOutput, calls=%fused_computation.8 | convolution fusion | flops 4430757888 | bytes 11075584 | tf_op jit(solution)/shard_map/dot_general | solution.py:24
  326.9 2.7 convert_reduce_fusion.1
  329.6 18.0 %all-to-all-done.6 = bf16[4,96,2048]{2,1,0:T(8,128)(2,1)} async-done(((bf16[4,96,2048]{2,1,0:T(8,128)(2,1)}), bf16[4,96,2048]{2,1,0:T(8,128)(2,1)}, u32[]{:S(2)}, u32[]{:S(2)}) %all-to-all-start.6) | async-done | bytes 1572896 | tf_op jit(solution)/shard_map/all_to_all | solution.py:93
  355.6 4.6 collective-permute-start.10
  360.2 6.8 %convolution_convert_fusion.3 = bf16[192,2048]{1,0:T(8,128)(2,1)S(1)} fusion(bf16[192,2048]{1,0:T(8,128)(2,1)S(1)} %add_convert_fusion.4, bf16[2048,2048]{1,0:T(8,128)(2,1)} %bitcast.192), kind=kOutput, calls=%fused_computation.12 | convolution fusion | flops 1611005952 | bytes 9961472 | tf_op jit(solution)/shard_map/dot_general | solution.py:28
  367.9 5.2 all-to-all-start.7
  373.1 14.8 %convolution_convert_fusion = bf16[2048,2816]{1,0:T(8,128)(2,1)} fusion(bf16[768,2048]{1,0:T(8,128)(2,1)} %get-tuple-element.94, bf16[768,2816]{1,0:T(8,128)(2,1)} %get-tuple-element.95), kind=kOutput, calls=%fused_computation | convolution fusion | flops 8864137216 | bytes 19005440 | tf_op jit(solution)/shard_map/dot_general | solution.py:32
  388.0 3.7 collective-permute-start.9
  391.7 5.6 collective-permute-done.8
  401.0 19.8 %back.1 = (bf16[4,192,2048]{2,1,0:T(8,128)(2,1)}, bf16[4,192,2048]{2,1,0:T(8,128)(2,1)}, bf16[1536,512]{1,0:T(8,128)(2,1)}) custom-call(s32[2]{0:T(128)S(1)} %pad_add_fusion.at_ref, bf16[1536,256]{1,0:T(8,128)(2,1)S(1)} %get-tuple-element.76.q_ref, bf16[1536,128]{1,0:T(8,128)(2,1)S(1)} %copy-done.3, bf16[1536,128]{1,0:T(8,128)(2,1)S(1)} %copy-done.5, ...), custom_call_target="tpu_custom_call" | custom-call | flops 229713641472 | bytes 8388608 | tf_op jit(solution)/shard_map/back/pallas_call | solution.py:561
  420.8 7.2 %collective-permute-done.9 = bf16[192,2048]{1,0:T(8,128)(2,1)} collective-permute-done((bf16[192,2048]{1,0:T(8,128)(2,1)}, bf16[192,2048]{1,0:T(8,128)(2,1)}, u32[]{:S(2)}, u32[]{:S(2)}) %collective-permute-start.9) | collective-permute-done | bytes 786464 | tf_op jit(solution)/shard_map/ppermute | solution.py:84
  428.5 7.2 %output_grad_term.1 = (bf16[4,64,2048]{2,1,0:T(8,128)(2,1)}, bf16[4,64,2048]{2,1,0:T(8,128)(2,1)}, f32[1,2048]{1,0:T(1,128)S(1)}) custom-call(s32[2]{0:T(128)S(1)} %pad_add_fusion.at_ref, bf16[208,2048]{1,0:T(8,128)(2,1)} %copy-done.29, bf16[208,2048]{1,0:T(8,128)(2,1)} %collective-permute-done.11.refs_1_, ...), custom_call_target="tpu_custom_call" | custom-call | flops 1610612736 | bytes 6291456 | tf_op jit(solution)/shard_map/output_grad_term/pallas_call | solution.py:645
  439.5 3.8 fusion.15
  446.0 7.2 %project_grad.1 = bf16[2048,512]{1,0:T(8,128)(2,1)} custom-call(bf16[1536,2048]{1,0:T(8,128)(2,1)} %bitcast.174, bf16[1536,512]{1,0:T(8,128)(2,1)S(1)} %copy-done.6), custom_call_target="tpu_custom_call" | custom-call | flops 16106127360 | bytes 6291456 | tf_op jit(solution)/shard_map/project_grad/pallas_call | solution.py:593
  453.2 5.5 all-to-all-start.8
  460.0 8.7 %collective-permute-done.16 = bf16[192,2048]{1,0:T(8,128)(2,1)S(1)} collective-permute-done((bf16[192,2048]{1,0:T(8,128)(2,1)}, bf16[192,2048]{1,0:T(8,128)(2,1)S(1)}, u32[]{:S(2)}, u32[]{:S(2)}) %collective-permute-start.16) | collective-permute-done | bytes 786464 | tf_op jit(solution)/shard_map/ppermute | solution.py:80
  468.7 18.3 %collective-permute-done.17 = bf16[192,2048]{1,0:T(8,128)(2,1)S(1)} collective-permute-done((bf16[192,2048]{1,0:T(8,128)(2,1)}, bf16[192,2048]{1,0:T(8,128)(2,1)S(1)}, u32[]{:S(2)}, u32[]{:S(2)}) %collective-permute-start.17) | collective-permute-done | bytes 786464 | tf_op jit(solution)/shard_map/ppermute | solution.py:80
  487.0 2.4 add_convert_fusion
  494.1 5.0 fusion.7
  499.1 7.8 %collective-permute-done.20 = bf16[80,2048]{1,0:T(8,128)(2,1)S(1)} collective-permute-done((bf16[80,2048]{1,0:T(8,128)(2,1)S(1)}, bf16[80,2048]{1,0:T(8,128)(2,1)S(1)}, u32[]{:S(2)}, u32[]{:S(2)}) %collective-permute-start.20) | collective-permute-done | bytes 327712 | tf_op jit(solution)/shard_map/ppermute | solution.py:80
  508.5 6.3 %collective-permute-done.22 = bf16[80,2048]{1,0:T(8,128)(2,1)S(1)} collective-permute-done((bf16[80,2048]{1,0:T(8,128)(2,1)S(1)}, bf16[80,2048]{1,0:T(8,128)(2,1)S(1)}, u32[]{:S(2)}, u32[]{:S(2)}) %collective-permute-start.22) | collective-permute-done | bytes 327712 | tf_op jit(solution)/shard_map/ppermute | solution.py:80
  521.3 5.4 fusion.6
  526.6 2.4 convert_element_type.318
  529.0 2.9 reduce_sum.150
  531.9 5.2 all-to-all-start.9
  537.0 9.6 %collective-permute-done.24 = bf16[80,2048]{1,0:T(8,128)(2,1)} collective-permute-done((bf16[80,2048]{1,0:T(8,128)(2,1)}, bf16[80,2048]{1,0:T(8,128)(2,1)}, u32[]{:S(2)}, u32[]{:S(2)}) %collective-permute-start.24) | collective-permute-done | bytes 327712 | tf_op jit(solution)/shard_map/ppermute | solution.py:84
  546.6 3.0 collective-permute-done.25
  555.8 7.0 %split.1 = (f32[256,1408]{1,0:T(8,128)}, f32[256,1408]{1,0:T(8,128)}) custom-call(bf16[256,2816]{1,0:T(8,128)(2,1)} %reduce-scatter.3.cloned.1.call-done.both_ref), custom_call_target="tpu_custom_call" | custom-call | tf_op jit(solution)/shard_map/split/pallas_call | solution.py:752
  (251 shorter events, 76.5 us)
Async XLA Ops:
  7.2 107.3 %all-gather.9.cloned.1.call-start = ((), (), s32[]{:S(2)}) async-start(), calls=%async_computation.16 | async-start | bytes 13565952 | tf_op jit(solution)/shard_map/all_gather | solution.py:796
  12.4 164.0 %all-gather.5.cloned.1.call-start = ((), (), s32[]{:S(2)}) async-start(), calls=%async_computation.12 | async-start | bytes 9437184 | tf_op jit(solution)/shard_map/all_gather | solution.py:819
  14.9 4.3 collective-permute-start.1
  16.2 4.7 collective-permute-start.2
  17.4 5.4 collective-permute-start
  51.9 46.9 %all-to-all-start.1 = ((bf16[4,4,80,768]{3,2,1,0:T(8,128)(2,1)}), bf16[4,4,80,768]{3,2,1,0:T(8,128)(2,1)}, u32[]{:S(2)}, u32[]{:S(2)}) async-start(bf16[4,4,80,768]{3,2,1,0:T(8,128)(2,1)} %broadcast_in_dim.99), calls=%async_computation.1 | async-start | bytes 3932160 | tf_op jit(solution)/shard_map/all_to_all | solution.py:89
  58.3 180.0 %all-gather.7.cloned.1.call-start = ((), (), s32[]{:S(2)}) async-start(), calls=%async_computation.13 | async-start | bytes 12976128 | tf_op jit(solution)/shard_map/all_gather | solution.py:820
  61.9 39.8 %copy-start.54 = (s32[1,4]{1,0:T(1,128)S(1)}, s32[1,4]{1,0:T(1,128)}, u32[]{:S(2)}) copy-start(s32[1,4]{1,0:T(1,128)} %param.20) | copy-start | bytes 52
  62.0 41.4 %copy-start.55 = (f32[2]{0:T(128)S(1)}, f32[2]{0:T(128)}, u32[]{:S(2)}) copy-start(f32[2]{0:T(128)} %param.19) | copy-start | bytes 28
  62.0 42.0 %copy-start.18 = (bf16[1,192,2048]{2,1,0:T(8,128)(2,1)S(1)}, bf16[1,192,2048]{2,1,0:T(8,128)(2,1)}, u32[]{:S(2)}) copy-start(bf16[1,192,2048]{2,1,0:T(8,128)(2,1)} %param.16) | copy-start | bytes 2359300
  98.8 22.5 %collective-permute-start.3 = (bf16[4,4,80,768]{3,2,1,0:T(8,128)(2,1)}, bf16[4,4,80,768]{3,2,1,0:T(8,128)(2,1)}, u32[]{:S(2)}, u32[]{:S(2)}) collective-permute-start(bf16[4,4,80,768]{3,2,1,0:T(8,128)(2,1)} %all-to-all-done.1.refs_0_), channel_id=1, source_target_pairs={{0,1},{1,0},{2,3},{3,2},{4,5},{5,4},{6,7},{7,6},{8,9},{9,8},{10,11... | collective-permute-start | bytes 5898248 | tf_op jit(solution)/shard_map/ppermute | solution.py:80
  107.7 33.8 %collective-permute-start.4 = (bf16[192,2048]{1,0:T(8,128)(2,1)S(1)}, bf16[192,2048]{1,0:T(8,128)(2,1)S(1)}, u32[]{:S(2)}, u32[]{:S(2)}) collective-permute-start(bf16[192,2048]{1,0:T(8,128)(2,1)S(1)} %fusion.14.refs_0_), channel_id=1, source_target_pairs={{0,8},{8,16},{16,24},{24,0},{1,9},{9,17},{17,25},{25,1},{2,10},{10... | collective-permute-start | bytes 2359304 | tf_op jit(solution)/shard_map/ppermute | solution.py:84
  110.5 65.9 %collective-permute-start.5 = (bf16[192,2048]{1,0:T(8,128)(2,1)S(1)}, bf16[192,2048]{1,0:T(8,128)(2,1)}, u32[]{:S(2)}, u32[]{:S(2)}) collective-permute-start(bf16[192,2048]{1,0:T(8,128)(2,1)S(1)} %fusion.14.refs_0_), channel_id=1, source_target_pairs={{0,16},{8,24},{16,0},{24,8},{1,17},{9,25},{17,1},{25,9},{2,18},{10... | collective-permute-start | bytes 2359304 | tf_op jit(solution)/shard_map/ppermute | solution.py:84
  141.5 16.7 %all-to-all-start.2 = ((bf16[8,192,256]{2,1,0:T(8,128)(2,1)}), bf16[8,192,256]{2,1,0:T(8,128)(2,1)}, u32[]{:S(2)}, u32[]{:S(2)}) async-start(bf16[8,192,256]{2,1,0:T(8,128)(2,1)} %bitcast.165), calls=%async_computation.2 | async-start | bytes 1572864 | tf_op jit(solution)/shard_map/all_to_all | solution.py:847
  146.1 39.3 %collective-permute-start.6 = (bf16[192,2048]{1,0:T(8,128)(2,1)S(1)}, bf16[192,2048]{1,0:T(8,128)(2,1)}, u32[]{:S(2)}, u32[]{:S(2)}) collective-permute-start(bf16[192,2048]{1,0:T(8,128)(2,1)S(1)} %fusion.14.refs_0_), channel_id=1, source_target_pairs={{0,24},{8,0},{16,8},{24,16},{1,25},{9,1},{17,9},{25,17},{2,26},{10... | collective-permute-start | bytes 2359304 | tf_op jit(solution)/shard_map/ppermute | solution.py:84
  146.5 38.9 %collective-permute-start.7 = (bf16[1536,256]{1,0:T(8,128)(2,1)S(1)}, bf16[1536,256]{1,0:T(8,128)(2,1)}, u32[]{:S(2)}, u32[]{:S(2)}) collective-permute-start(bf16[1536,256]{1,0:T(8,128)(2,1)S(1)} %copy-done), channel_id=1, source_target_pairs={{0,1},{1,0},{2,3},{3,2},{4,5},{5,4},{6,7},{7,6},{8,9},{9,8},{10,11... | collective-permute-start | bytes 2359304 | tf_op jit(solution)/shard_map/ppermute | solution.py:80
  146.9 204.6 %copy-start.39 = (f32[2048]{0:T(1024)}, f32[2048]{0:T(1024)S(1)}, u32[]{:S(2)}) copy-start(f32[2048]{0:T(1024)S(1)} %reshape.224) | copy-start | bytes 24580
  184.1 167.3 %copy-start.41 = (f32[192]{0:T(256)}, f32[192]{0:T(256)S(1)}, u32[]{:S(2)}) copy-start(f32[192]{0:T(256)S(1)} %get-tuple-element.138) | copy-start | bytes 2308
  184.1 167.3 %copy-start.43 = (f32[192]{0:T(256)}, f32[192]{0:T(256)S(1)}, u32[]{:S(2)}) copy-start(f32[192]{0:T(256)S(1)} %get-tuple-element.137) | copy-start | bytes 2308
  226.1 40.0 %all-to-all-start.4 = ((bf16[4,96,2048]{2,1,0:T(8,128)(2,1)}), bf16[4,96,2048]{2,1,0:T(8,128)(2,1)}, u32[]{:S(2)}, u32[]{:S(2)}) async-start(bf16[4,96,2048]{2,1,0:T(8,128)(2,1)} %broadcast_in_dim.107), calls=%async_computation.4 | async-start | bytes 3145728 | tf_op jit(solution)/shard_map/all_to_all | solution.py:89
  266.1 44.7 %all-to-all-start.5 = ((bf16[4,96,2048]{2,1,0:T(8,128)(2,1)}), bf16[4,96,2048]{2,1,0:T(8,128)(2,1)}, u32[]{:S(2)}, u32[]{:S(2)}) async-start(bf16[4,96,2048]{2,1,0:T(8,128)(2,1)} %get-tuple-element.70), calls=%async_computation.5 | async-start | bytes 3145728 | tf_op jit(solution)/shard_map/all_to_all | solution.py:93
  273.2 253.5 %reduce-scatter.5.cloned.1.call-start = ((), (), s32[]{:S(2)}) async-start(), calls=%async_computation.15 | async-start | bytes 6488064 | tf_op jit(solution)/shard_map/reduce_scatter | solution.py:869
  310.8 36.8 %all-to-all-start.6 = ((bf16[4,96,2048]{2,1,0:T(8,128)(2,1)}), bf16[4,96,2048]{2,1,0:T(8,128)(2,1)}, u32[]{:S(2)}, u32[]{:S(2)}) async-start(bf16[4,96,2048]{2,1,0:T(8,128)(2,1)} %get-tuple-element.72), calls=%async_computation.6 | async-start | bytes 3145728 | tf_op jit(solution)/shard_map/all_to_all | solution.py:93
  329.6 19.8 %copy-start.11 = (bf16[1,192,2048]{2,1,0:T(8,128)(2,1)S(1)}, bf16[1,192,2048]{2,1,0:T(8,128)(2,1)}, u32[]{:S(2)}) copy-start(bf16[1,192,2048]{2,1,0:T(8,128)(2,1)} %param.15) | copy-start | bytes 2359300
  353.1 44.2 %collective-permute-start.11 = (bf16[208,2048]{1,0:T(8,128)(2,1)S(1)}, bf16[208,2048]{1,0:T(8,128)(2,1)}, u32[]{:S(2)}, u32[]{:S(2)}) collective-permute-start(bf16[208,2048]{1,0:T(8,128)(2,1)S(1)} %maximum_maximum_fusion.refs_0_), channel_id=1, source_target_pairs={{0,2},{1,3},{2,0},{3,1},{4,6},{5,7},{6,4},{7,5},{8,10},{9,11},{10,... | collective-permute-start | bytes 2555912 | tf_op jit(solution)/shard_map/ppermute | solution.py:80
  354.3 43.0 %collective-permute-start.12 = (bf16[208,2048]{1,0:T(8,128)(2,1)S(1)}, bf16[208,2048]{1,0:T(8,128)(2,1)}, u32[]{:S(2)}, u32[]{:S(2)}) collective-permute-start(bf16[208,2048]{1,0:T(8,128)(2,1)S(1)} %maximum_maximum_fusion.refs_0_), channel_id=1, source_target_pairs={{0,4},{1,5},{2,6},{3,7},{4,0},{5,1},{6,2},{7,3},{8,12},{9,13},{10,... | collective-permute-start | bytes 2555912 | tf_op jit(solution)/shard_map/ppermute | solution.py:80
  355.6 36.1 %collective-permute-start.10 = (bf16[192,2048]{1,0:T(8,128)(2,1)}, bf16[192,2048]{1,0:T(8,128)(2,1)}, u32[]{:S(2)}, u32[]{:S(2)}) collective-permute-start(bf16[192,2048]{1,0:T(8,128)(2,1)} %get-tuple-element.75), channel_id=1, source_target_pairs={{0,24},{8,0},{16,8},{24,16},{1,25},{9,1},{17,9},{25,17},{2,26},{10... | collective-permute-start | bytes 2359304 | tf_op jit(solution)/shard_map/ppermute | solution.py:84
  360.2 37.1 %collective-permute-start.8 = (bf16[192,2048]{1,0:T(8,128)(2,1)}, bf16[192,2048]{1,0:T(8,128)(2,1)}, u32[]{:S(2)}, u32[]{:S(2)}) collective-permute-start(bf16[192,2048]{1,0:T(8,128)(2,1)} %get-tuple-element.73), channel_id=1, source_target_pairs={{0,8},{8,16},{16,24},{24,0},{1,9},{9,17},{17,25},{25,1},{2,10},{10... | collective-permute-start | bytes 2359304 | tf_op jit(solution)/shard_map/ppermute | solution.py:84
  367.9 23.8 %all-to-all-start.7 = ((bf16[192,8,256]{2,0,1:T(8,128)(2,1)}), bf16[192,8,256]{2,0,1:T(8,128)(2,1)S(1)}, u32[]{:S(2)}, u32[]{:S(2)}) async-start(bf16[192,8,256]{2,0,1:T(8,128)(2,1)} %bitcast.161), calls=%async_computation.7 | async-start | bytes 1572864 | tf_op jit(solution)/shard_map/all_to_all | solution.py:880
  373.1 182.7 %reduce-scatter.3.cloned.1.call-start = ((), (), s32[]{:S(2)}) async-start(), calls=%async_computation.14 | async-start | bytes 12976128 | tf_op jit(solution)/shard_map/reduce_scatter | solution.py:870
  388.0 40.0 %collective-permute-start.9 = (bf16[192,2048]{1,0:T(8,128)(2,1)}, bf16[192,2048]{1,0:T(8,128)(2,1)}, u32[]{:S(2)}, u32[]{:S(2)}) collective-permute-start(bf16[192,2048]{1,0:T(8,128)(2,1)} %get-tuple-element.74), channel_id=1, source_target_pairs={{0,16},{8,24},{16,0},{24,8},{1,17},{9,25},{17,1},{25,9},{2,18},{10... | collective-permute-start | bytes 2359304 | tf_op jit(solution)/shard_map/ppermute | solution.py:84
  399.2 28.9 %collective-permute-start.14 = (bf16[112,2048]{1,0:T(8,128)(2,1)}, bf16[112,2048]{1,0:T(8,128)(2,1)}, u32[]{:S(2)}, u32[]{:S(2)}) collective-permute-start(bf16[112,2048]{1,0:T(8,128)(2,1)} %slice.85), channel_id=1, source_target_pairs={{0,2},{1,3},{2,0},{3,1},{4,6},{5,7},{6,4},{7,5},{8,10},{9,11},{10,... | collective-permute-start | bytes 1376264 | tf_op jit(solution)/shard_map/ppermute | solution.py:80
  401.0 27.1 %collective-permute-start.13 = (bf16[96,2048]{1,0:T(8,128)(2,1)}, bf16[96,2048]{1,0:T(8,128)(2,1)}, u32[]{:S(2)}, u32[]{:S(2)}) collective-permute-start(bf16[96,2048]{1,0:T(8,128)(2,1)} %slice.84), channel_id=1, source_target_pairs={{0,4},{1,5},{2,6},{3,7},{4,0},{5,1},{6,2},{7,3},{8,12},{9,13},{10,... | collective-permute-start | bytes 1179656 | tf_op jit(solution)/shard_map/ppermute | solution.py:80
  401.0 27.5 %copy-start.1 = (bf16[1536,256]{1,0:T(8,128)(2,1)S(1)}, bf16[1536,256]{1,0:T(8,128)(2,1)}, u32[]{:S(2)}) copy-start(bf16[1536,256]{1,0:T(8,128)(2,1)} %get-tuple-element.85.mixed_ref.refs_5_) | copy-start | bytes 2359300
  428.0 10.6 %collective-permute-start.15 = (bf16[4,192,2048]{2,1,0:T(8,128)(2,1)}, bf16[4,192,2048]{2,1,0:T(8,128)(2,1)}, u32[]{:S(2)}, u32[]{:S(2)}) collective-permute-start(bf16[4,192,2048]{2,1,0:T(8,128)(2,1)} %get-tuple-element.84), channel_id=1, source_target_pairs={{0,1},{1,0},{2,3},{3,2},{4,5},{5,4},{6,7},{7,6},{8,9},{9,8},{10,11... | collective-permute-start | bytes 9437192 | tf_op jit(solution)/shard_map/ppermute | solution.py:80
  438.6 48.4 %collective-permute-start.19 = (bf16[4,80,2048]{2,1,0:T(8,128)(2,1)}, bf16[4,80,2048]{2,1,0:T(8,128)(2,1)}, u32[]{:S(2)}, u32[]{:S(2)}) collective-permute-start(bf16[4,80,2048]{2,1,0:T(8,128)(2,1)} %pad_maximum_fusion.4), channel_id=1, source_target_pairs={{0,1},{1,0},{2,3},{3,2},{4,5},{5,4},{6,7},{7,6},{8,9},{9,8},{10,11... | collective-permute-start | bytes 3932168 | tf_op jit(solution)/shard_map/ppermute | solution.py:80
  443.4 25.3 %collective-permute-start.16 = (bf16[192,2048]{1,0:T(8,128)(2,1)}, bf16[192,2048]{1,0:T(8,128)(2,1)S(1)}, u32[]{:S(2)}, u32[]{:S(2)}) collective-permute-start(bf16[192,2048]{1,0:T(8,128)(2,1)} %get-tuple-element.103), channel_id=1, source_target_pairs={{0,6},{1,7},{2,4},{3,5},{4,2},{5,3},{6,0},{7,1},{8,14},{9,15},{10,... | collective-permute-start | bytes 2359304 | tf_op jit(solution)/shard_map/ppermute | solution.py:80
  443.6 43.4 %collective-permute-start.17 = (bf16[192,2048]{1,0:T(8,128)(2,1)}, bf16[192,2048]{1,0:T(8,128)(2,1)S(1)}, u32[]{:S(2)}, u32[]{:S(2)}) collective-permute-start(bf16[192,2048]{1,0:T(8,128)(2,1)} %get-tuple-element.105), channel_id=1, source_target_pairs={{0,2},{1,3},{2,0},{3,1},{4,6},{5,7},{6,4},{7,5},{8,10},{9,11},{10,... | collective-permute-start | bytes 2359304 | tf_op jit(solution)/shard_map/ppermute | solution.py:80
  444.9 42.2 %collective-permute-start.18 = (bf16[192,2048]{1,0:T(8,128)(2,1)}, bf16[192,2048]{1,0:T(8,128)(2,1)S(1)}, u32[]{:S(2)}, u32[]{:S(2)}) collective-permute-start(bf16[192,2048]{1,0:T(8,128)(2,1)} %get-tuple-element.104), channel_id=1, source_target_pairs={{0,4},{1,5},{2,6},{3,7},{4,0},{5,1},{6,2},{7,3},{8,12},{9,13},{10,... | collective-permute-start | bytes 2359304 | tf_op jit(solution)/shard_map/ppermute | solution.py:80
  453.2 62.3 %all-to-all-start.8 = ((bf16[4,512,512]{2,1,0:T(8,128)(2,1)}), bf16[4,512,512]{2,1,0:T(8,128)(2,1)}, u32[]{:S(2)}, u32[]{:S(2)}) async-start(bf16[4,512,512]{2,1,0:T(8,128)(2,1)} %bitcast.178), calls=%async_computation.8 | async-start | bytes 4194304 | tf_op jit(solution)/shard_map/all_to_all | solution.py:93
  468.7 25.5 %copy-start.22 = (bf16[192,2048]{1,0:T(8,128)(2,1)}, bf16[192,2048]{1,0:T(8,128)(2,1)S(1)}, u32[]{:S(2)}) copy-start(bf16[192,2048]{1,0:T(8,128)(2,1)S(1)} %collective-permute-done.16) | copy-start | bytes 2359300
  491.5 15.5 %collective-permute-start.20 = (bf16[80,2048]{1,0:T(8,128)(2,1)S(1)}, bf16[80,2048]{1,0:T(8,128)(2,1)S(1)}, u32[]{:S(2)}, u32[]{:S(2)}) collective-permute-start(bf16[80,2048]{1,0:T(8,128)(2,1)S(1)} %get-tuple-element.114), channel_id=1, source_target_pairs={{0,2},{1,3},{2,0},{3,1},{4,6},{5,7},{6,4},{7,5},{8,10},{9,11},{10,... | collective-permute-start | bytes 983048 | tf_op jit(solution)/shard_map/ppermute | solution.py:80
  492.3 15.5 %collective-permute-start.21 = (bf16[80,2048]{1,0:T(8,128)(2,1)S(1)}, bf16[80,2048]{1,0:T(8,128)(2,1)S(1)}, u32[]{:S(2)}, u32[]{:S(2)}) collective-permute-start(bf16[80,2048]{1,0:T(8,128)(2,1)S(1)} %get-tuple-element.113), channel_id=1, source_target_pairs={{0,4},{1,5},{2,6},{3,7},{4,0},{5,1},{6,2},{7,3},{8,12},{9,13},{10,... | collective-permute-start | bytes 983048 | tf_op jit(solution)/shard_map/ppermute | solution.py:80
  493.0 21.8 %collective-permute-start.22 = (bf16[80,2048]{1,0:T(8,128)(2,1)S(1)}, bf16[80,2048]{1,0:T(8,128)(2,1)S(1)}, u32[]{:S(2)}, u32[]{:S(2)}) collective-permute-start(bf16[80,2048]{1,0:T(8,128)(2,1)S(1)} %get-tuple-element.112), channel_id=1, source_target_pairs={{0,6},{1,7},{2,4},{3,5},{4,2},{5,3},{6,0},{7,1},{8,14},{9,15},{10,... | collective-permute-start | bytes 983048 | tf_op jit(solution)/shard_map/ppermute | solution.py:80
  517.7 19.3 %collective-permute-start.23 = (bf16[80,2048]{1,0:T(8,128)(2,1)}, bf16[80,2048]{1,0:T(8,128)(2,1)}, u32[]{:S(2)}, u32[]{:S(2)}) collective-permute-start(bf16[80,2048]{1,0:T(8,128)(2,1)} %get-tuple-element.109), channel_id=1, source_target_pairs={{0,8},{8,16},{16,24},{24,0},{1,9},{9,17},{17,25},{25,1},{2,10},{10... | collective-permute-start | bytes 983048 | tf_op jit(solution)/shard_map/ppermute | solution.py:84
  519.0 27.6 %collective-permute-start.24 = (bf16[80,2048]{1,0:T(8,128)(2,1)}, bf16[80,2048]{1,0:T(8,128)(2,1)}, u32[]{:S(2)}, u32[]{:S(2)}) collective-permute-start(bf16[80,2048]{1,0:T(8,128)(2,1)} %get-tuple-element.111), channel_id=1, source_target_pairs={{0,16},{8,24},{16,0},{24,8},{1,17},{9,25},{17,1},{25,9},{2,18},{10... | collective-permute-start | bytes 983048 | tf_op jit(solution)/shard_map/ppermute | solution.py:84
  520.0 29.6 %collective-permute-start.25 = (bf16[80,2048]{1,0:T(8,128)(2,1)S(1)}, bf16[80,2048]{1,0:T(8,128)(2,1)}, u32[]{:S(2)}, u32[]{:S(2)}) collective-permute-start(bf16[80,2048]{1,0:T(8,128)(2,1)S(1)} %get-tuple-element.110), channel_id=1, source_target_pairs={{0,24},{8,0},{16,8},{24,16},{1,25},{9,1},{17,9},{25,17},{2,26},{10... | collective-permute-start | bytes 983048 | tf_op jit(solution)/shard_map/ppermute | solution.py:84
  531.9 20.5 %all-to-all-start.9 = ((bf16[8,64,512]{2,1,0:T(8,128)(2,1)}), bf16[8,64,512]{2,1,0:T(8,128)(2,1)S(1)}, u32[]{:S(2)}, u32[]{:S(2)}) async-start(bf16[8,64,512]{2,1,0:T(8,128)(2,1)} %bitcast.39), calls=%async_computation.9 | async-start | bytes 1048576 | tf_op jit(solution)/shard_map/all_to_all | solution.py:932
  (47 other events, 261.1 us)
Sparse Core Ops, SparseCore 0:
  12.6 71.4 all-gather.8
  86.0 54.3 all-gather.4
  142.9 69.2 all-gather.6
  310.9 69.0 reduce-scatter.4
  388.1 119.4 reduce-scatter.2

commit v5 on v4

--- a/solution.py
+++ b/solution.py
@@ -56,6 +56,10 @@
     return lax.rsqrt(jnp.mean(rows * rows, -1, keepdims=True) + norm_eps)
 
 
+def after_all(values, *earlier):
+    return lax.optimization_barrier((*values, *earlier))[: len(values)]
+
+
 def after(value, *earlier):
     return lax.optimization_barrier((value, *earlier))[0]
 
@@ -84,6 +88,25 @@
     return lax.ppermute(block, "dp", [(i, (i + step) % 4) for i in range(4)])
 
 
+UP = [(0, 1), (1, 2), (2, 3)]
+DOWN = [(1, 0), (2, 1), (3, 2)]
+LINE = (0, -1, 1, -2, 2, 3)
+
+
+def line_first(block):
+    return lax.ppermute(block, "dp", UP), lax.ppermute(block, "dp", DOWN)
+
+
+def line_second(up, down):
+    plane = lax.axis_index("dp")
+    far = jnp.where(plane == 2, down, up)
+    return (
+        lax.ppermute(up, "dp", UP[1:]),
+        lax.ppermute(down, "dp", DOWN[:2]),
+        lax.ppermute(far, "dp", [(2, 0), (1, 3)]),
+    )
+
+
 def gather_planes(block):
     copies = jnp.broadcast_to(block[None], (4, *block.shape))
     return lax.all_to_all(copies, "dp", split_axis=0, concat_axis=0)
@@ -91,25 +114,6 @@
 
 def swap_planes(whole):
     return lax.all_to_all(whole, "dp", split_axis=0, concat_axis=0)
-
-
-def output_rows(mine, others, *earlier):
-    group, plane = lax.axis_index("fsdp") // 2, lax.axis_index("dp")
-    whole = add_low(mine, flip(others, 1))
-
-    def to(bit):
-        return lax.dynamic_index_in_dim(whole, group ^ bit, 0, keepdims=False)
-
-    parts = [to(0)] + [flip(to(bit), 2 * bit) for bit in (1, 2, 3)]
-    by_group = jnp.zeros_like(whole)
-    for bit, part in enumerate(parts):
-        by_group = lax.dynamic_update_index_in_dim(by_group, part, group ^ bit, 0)
-    by_group = after(by_group, *earlier)
-    ahead = [lax.dynamic_index_in_dim(by_group, (plane + k) % 4, 0, keepdims=False) for k in range(4)]
-    total = ahead[0].astype(f32)
-    for k in (1, 2, 3):
-        total = total + shift(ahead[k], k).astype(f32)
-    return total
 
 
 def block_rows_of(length):
@@ -411,7 +415,6 @@
     )
 
 
-PIECES = ((0, 0), (2, 0), (4, 0), (6, 0), (6, 1), (1, 0), (3, 0), (5, 0), (7, 0), (7, 1))
 TO_CORE = (7, 3, 5, 1)
 TO_CHIPS = (6, 2, 4, 0)
 VMEM = pl.BlockSpec(memory_space=pltpu.VMEM)
@@ -419,11 +422,6 @@
 log2_e = math.log2(math.e)
 
 
-def start_of(place, piece, rows):
-    bit, half = PIECES[piece]
-    return pl.multiple_of((place ^ bit) * rows + half * (rows // 2), rows // 2)
-
-
 def turn(block, cosine, sine, forward):
     rolled = pltpu.roll(block, HEAD_DIM // 2, 1)
     return block * cosine + rolled * sine if forward else block * cosine - rolled * sine
@@ -436,12 +434,46 @@
     return scores, (key_pos <= query_pos) & (key_pos >= starts)
 
 
+anywhere = pl.BlockSpec(memory_space=pl.ANY)
+
+
+def whole_of(array):
+    return pl.BlockSpec(array.shape, lambda i: (0,) * len(array.shape))
+
+
 def front_kernel(at_ref, normed_ref, *refs):
+    first_ref, refs = refs[0], refs[1:]
+    down_ref, held_ref, sem, refs = refs[-4], refs[-2], refs[-1], (*refs[:-4], refs[-3])
+    devices, tokens = normed_ref.shape[:2]
+    chunk = first_ref.shape[1] - tokens
+    copies = [
+        pltpu.make_async_copy(
+            first_ref.at[device, pl.ds(tokens, chunk)],
+            held_ref.at[pl.ds(device * chunk, chunk)],
+            sem.at[device],
+        )
+        for device in range(devices)
+    ]
+    for copy in copies:
+        copy.start()
+    out = pltpu.make_async_copy(held_ref, down_ref, sem.at[devices])
+
+    def midway():
+        for copy in copies:
+            copy.wait()
+        out.start()
+
+    front_body(midway, at_ref, normed_ref, *refs)
+    out.wait()
+
+
+def front_body(midway, at_ref, normed_ref, *refs):
     columns_refs, refs = refs[:2], refs[2:]
     cos_ref, sin_ref, starts_ref, refs = refs[0], refs[1], refs[2], refs[3:]
     q_ref, k_ref, v_ref, mixed_ref, norm_ref, project_ref, gain_ref, vt_ref = refs
     place = at_ref[0]
-    length = normed_ref.shape[0]
+    devices, tokens = normed_ref.shape[:2]
+    length = devices * tokens
     core = place & 1
     group = place >> 1
     rows = columns_refs[0].shape[2] - 16
@@ -462,9 +494,9 @@
                 project_ref[here, q_width:] = block[owner, bit, :rows, q_all:]
                 gain_ref[owner * 8 + device] = block[owner, bit, rows:, :HEAD_DIM]
 
-    for low_row in range(0, length, 256):
-        here = slice(low_row, low_row + 256)
-        raw = dot_plain(normed_ref[here, :], project_ref[...])
+    for device in range(devices):
+        here = slice(device * tokens, (device + 1) * tokens)
+        raw = dot_plain(normed_ref[device], project_ref[...])
         cosine, sine = cos_ref[here, :], sin_ref[here, :]
         for low in range(0, q_width, HEAD_DIM):
             q_ref[here, low : low + HEAD_DIM] = turn(
@@ -472,6 +504,7 @@
             ).astype(bf16)
         k_ref[here, :] = turn(raw[:, q_width : q_width + HEAD_DIM], cosine, sine, True).astype(bf16)
         v_ref[here, :] = raw[:, q_width + HEAD_DIM :].astype(bf16)
+    midway()
     vt_ref[...] = jnp.transpose(v_ref[...].astype(f32)).astype(bf16)
     block = 256
     for head in range(q_width // HEAD_DIM):
@@ -490,8 +523,8 @@
             norm_ref[head, :, low:high] = top + jnp.log2(total)
 
 
-def front(at, normed, columns, columns_other, cosine, sine, starts):
-    length = normed.shape[0]
+def front(at, first, tokens, columns, columns_other, cosine, sine, starts):
+    length = 8 * tokens
     q_width = (columns.shape[3] - 2 * HEAD_DIM) // 2
     cols = q_width + 2 * HEAD_DIM
     width = 32 * (columns.shape[2] - 16)
@@ -506,10 +539,16 @@
     ]
     return pl.pallas_call(
         front_kernel,
-        in_specs=[SMEM] + [VMEM] * 6,
-        out_specs=[VMEM] * 7,
-        out_shape=shapes,
-        scratch_shapes=[pltpu.VMEM((HEAD_DIM, length), bf16)],
+        grid=(1,),
+        in_specs=[SMEM, pl.BlockSpec((8, tokens, width), lambda i: (0, 0, 0)), anywhere]
+        + [whole_of(x) for x in (columns, columns_other, cosine, sine, starts)],
+        out_specs=[whole_of(x) for x in shapes] + [anywhere],
+        out_shape=shapes + [jax.ShapeDtypeStruct((8 * (first.shape[1] - tokens), width), bf16)],
+        scratch_shapes=[
+            pltpu.VMEM((HEAD_DIM, length), bf16),
+            pltpu.VMEM((8 * (first.shape[1] - tokens), width), bf16),
+            pltpu.SemaphoreType.DMA((9,)),
+        ],
         compiler_params=pltpu.CompilerParams(vmem_limit_bytes=52 << 20),
         cost_estimate=pl.CostEstimate(
             flops=2 * length * width * cols + 4 * length * length * q_width,
@@ -517,13 +556,16 @@
             transcendentals=length * length,
         ),
         name="front",
-    )(at, normed, columns, columns_other, cosine, sine, starts)
-
-
-def back_kernel(tokens, at_ref, q_ref, k_ref, v_ref, mixed_ref, norm_ref, grad_ref, project_ref,
-                cos_ref, sin_ref, starts_ref, core_ref, chips_ref, cols_ref, kt_ref, dk_ref, dv_ref):
+    )(at, first, first, columns, columns_other, cosine, sine, starts)
+
+
+def back_kernel(tokens, at_ref, q_ref, k_ref, v_ref, mixed_ref, norm_ref, packed_ref, project_ref,
+                cos_ref, sin_ref, starts_ref, core_ref, chips_ref, cols_ref, kt_ref, dk_ref, dv_ref,
+                grad_ref):
     place = at_ref[0]
     length, q_width = q_ref.shape
+    for device in range(8):
+        grad_ref[device * tokens : (device + 1) * tokens, :] = packed_ref[device, :tokens, :q_width]
     block = 256
     kt_ref[...] = jnp.transpose(k_ref[...].astype(f32)).astype(bf16)
     dk_ref[...] = jnp.zeros_like(dk_ref)
@@ -571,10 +613,11 @@
             pltpu.VMEM((HEAD_DIM, length), bf16),
             pltpu.VMEM((length, HEAD_DIM), f32),
             pltpu.VMEM((length, HEAD_DIM), f32),
+            pltpu.VMEM((length, q_width), bf16),
         ],
         compiler_params=pltpu.CompilerParams(vmem_limit_bytes=52 << 20),
         cost_estimate=pl.CostEstimate(
-            flops=140 * length * width * cols + 7 * length * length * q_width,
+            flops=600 * length * width * cols + 7 * length * length * q_width,
             bytes_accessed=2 * length * width + 2 * width * cols,
             transcendentals=length * length,
         ),
@@ -582,91 +625,94 @@
     )(at, queries, keys, values, mixed, norm, grads, project, cosine, sine, starts)
 
 
-def project_grad_kernel(normed_ref, cols_ref, out_ref):
-    out_ref[...] = jnp.transpose(dot_left_t(cols_ref[...], normed_ref[...])).astype(bf16)
-
-
-def project_grad(normed, grad_cols):
-    length, width = normed.shape
-    cols = grad_cols.shape[1]
+def project_grad_kernel(first_ref, cols_ref, out_ref):
+    normed = first_ref[...].reshape(cols_ref.shape[0], first_ref.shape[2])
+    out_ref[...] = jnp.transpose(dot_left_t(cols_ref[...], normed)).astype(bf16)
+
+
+def project_grad(first, grad_cols):
+    length, cols = grad_cols.shape
+    width = first.shape[2]
     part = 512
     return pl.pallas_call(
         project_grad_kernel,
         grid=(width // part,),
         in_specs=[
-            pl.BlockSpec((length, part), lambda i: (0, i)),
+            pl.BlockSpec((8, length // 8, part), lambda i: (0, 0, i)),
             pl.BlockSpec((length, cols), lambda i: (0, 0)),
         ],
         out_specs=pl.BlockSpec((part, cols), lambda i: (i, 0)),
         out_shape=jax.ShapeDtypeStruct((width, cols), bf16),
         compiler_params=pltpu.CompilerParams(vmem_limit_bytes=52 << 20),
         cost_estimate=pl.CostEstimate(
-            flops=10 * length * width * cols, bytes_accessed=2 * length * width, transcendentals=0
+            flops=20 * length * width * cols, bytes_accessed=2 * length * width, transcendentals=0
         ),
         name="project_grad",
-    )(normed, grad_cols)
-
-
-def output_grad_kernel(tokens, at_ref, *refs):
-    pieces, (mixed_ref, other_ref, out_ref, rest_ref, gain_ref) = refs[:5], refs[5:]
-    place = at_ref[0]
-    core = place & 1
-    totals = [None, None]
+    )(first, grad_cols)
+
+
+def output_grad_kernel(at_ref, packed_ref, attended_ref, out_ref):
+    own = packed_ref.shape[2] // 2
+    rows = out_ref.shape[1] - 16
+    tokens = packed_ref.shape[1] - 16
+    total = None
     gain = None
-    for piece in range(5):
-        bit, half = PIECES[piece]
-        rows = tokens // 2 if bit >= 6 else tokens
-        here = pl.ds(start_of(place, piece, tokens), rows)
-        block = pieces[piece][:rows, :]
-        for side, ref in enumerate((mixed_ref, other_ref)):
-            term = dot_left_t(ref[here, :], block)
-            totals[side] = term if totals[side] is None else totals[side] + term
-        if pieces[piece].shape[0] > rows:
-            extra = jnp.sum(pieces[piece][rows:, :].astype(f32), 0, keepdims=True)
-            gain = extra if gain is None else gain + extra
-    gain_ref[...] = gain
-    rows = out_ref.shape[1]
-    for side, total in enumerate(totals):
-        blocks = total.astype(bf16).reshape(4, rows, total.shape[1])
-        first = 2 * (core ^ side)
-        for head in range(2):
-            for which in range(2):
-
-                @pl.when(core == which)
-                def _():
-                    out_ref[first + head] = blocks[2 * head + which]
-                    rest_ref[first + head] = blocks[2 * head + 1 - which]
-
-
-def output_grad_term(at, pieces, mixed, mixed_other):
-    length, own = mixed.shape
-    tokens, width = length // 8, pieces[0].shape[1]
-    shape = jax.ShapeDtypeStruct((4, own // 4, width), bf16)
+    for device in range(8):
+        term = dot_left_t(
+            packed_ref[device, :tokens, own:], attended_ref[device * tokens : (device + 1) * tokens, :]
+        )
+        extra = jnp.sum(packed_ref[device, tokens:, own:].astype(f32), 0, keepdims=True)
+        total = term if total is None else total + term
+        gain = extra if gain is None else gain + extra
+    turned = jnp.transpose(total).astype(bf16)
+    first = lax.broadcasted_iota(jnp.int32, (16, own), 0) == 0
+    gain_rows = jnp.where(first, jnp.broadcast_to(gain, (16, own)), 0.0)
+    for owner in range(4):
+        out_ref[owner, :rows, :] = turned[owner * rows : (owner + 1) * rows, :]
+        here = jnp.where(at_ref[0] // 2 == owner, 1.0, 0.0)
+        out_ref[owner, rows:, :] = (gain_rows * here).astype(bf16)
+
+
+def output_grad_term(at, packed, attended):
+    length, width = attended.shape
+    own = packed.shape[2] // 2
     return pl.pallas_call(
-        functools.partial(output_grad_kernel, tokens),
-        in_specs=[SMEM] + [VMEM] * 7,
-        out_specs=[VMEM] * 3,
-        out_shape=[shape, shape, jax.ShapeDtypeStruct((1, width), f32)],
+        output_grad_kernel,
+        in_specs=[SMEM] + [VMEM] * 2,
+        out_specs=VMEM,
+        out_shape=jax.ShapeDtypeStruct((4, width // 4 + 16, own), bf16),
         compiler_params=pltpu.CompilerParams(vmem_limit_bytes=52 << 20),
         cost_estimate=pl.CostEstimate(
-            flops=2 * length * own * width, bytes_accessed=2 * length * width, transcendentals=0
+            flops=60 * length * own * width, bytes_accessed=2 * length * width, transcendentals=0
         ),
         name="output_grad_term",
-    )(at, *pieces, mixed, mixed_other)
-
-
-def feed_kernel(units, count, at_ref, *refs):
-    d_refs, n_ref, both_ref, down_ref, rows_ref, refs = refs[:4], *refs[4:8], refs[8 + count :]
+    )(at, packed, attended)
+
+
+def place_blocks(plane, blocks, out_ref):
+    tokens = blocks[0].shape[0]
+    for block, move in zip(blocks, LINE):
+        owner = plane + move if move != 3 else 3 - plane
+        valid = (owner >= 0) & (owner <= 3) if move != 3 else (plane == 0) | (plane == 3)
+
+        @pl.when(valid)
+        def _():
+            out_ref[pl.ds(pl.multiple_of(owner * tokens, tokens), tokens), :] = block[...]
+
+
+def feed_kernel(units, count, n_count, at_ref, *refs):
+    d_refs, n_refs, refs = refs[:6], refs[6 : 6 + n_count], refs[6 + n_count :]
+    both_ref, down_ref, rows_ref, refs = *refs[:3], refs[3 + count :]
     second_ref, direct_ref, hidden_ref, grads_ref, term_ref, held_ref = refs
     step = pl.program_id(0)
 
     @pl.when(step == 0)
     def _():
-        second_ref[...] = n_ref[...].reshape(second_ref.shape)
-        tokens = n_ref.shape[1]
-        for slot in range(4):
-            owner = (at_ref[1] - slot) & 3
-            direct_ref[pl.ds(pl.multiple_of(owner * tokens, tokens), tokens), :] = d_refs[slot][...]
+        place_blocks(at_ref[1], d_refs, direct_ref)
+        if n_count == 6:
+            place_blocks(at_ref[1], n_refs, second_ref)
+        else:
+            second_ref[...] = n_refs[0][...].reshape(second_ref.shape)
 
     @pl.when(step < units)
     def _():
@@ -693,20 +739,23 @@
 
 
 def feed(at, part_at, parts_of, seconds, directs, both, down, so_far):
-    tokens, width = seconds.shape[1:]
+    tokens, width = seconds[0].shape[-2:]
     some = 4 * tokens
     ff = down.shape[0]
+    n_count = len(seconds)
+    gathered = pl.BlockSpec((4, tokens, width), lambda i: (0, 0, 0))
+    single = pl.BlockSpec((tokens, width), lambda i: (0, 0))
     unit, part = 128, 256
     units, parts = ff // unit, width // part
     so_far = so_far or []
     total = parts_of * some
     outs = pl.pallas_call(
-        functools.partial(feed_kernel, units, len(so_far)),
+        functools.partial(feed_kernel, units, len(so_far), n_count),
         grid=(units + parts,),
         in_specs=[
             SMEM,
-            *[pl.BlockSpec((tokens, width), lambda i: (part_at, 0))] * 4,
-            pl.BlockSpec((4, tokens, width), lambda i: (0, 0, 0)),
+            *[pl.BlockSpec((tokens, width), lambda i: (part_at, 0))] * 6,
+            *[single if n_count == 6 else gathered] * n_count,
             pl.BlockSpec((width, 2 * unit), lambda i: (0, jnp.minimum(i, units - 1))),
             pl.BlockSpec((unit, width), lambda i: (jnp.minimum(i, units - 1), 0)),
             pl.BlockSpec((part, 2 * ff), lambda i: (jnp.maximum(i - units, 0), 0)),
@@ -727,7 +776,7 @@
             jax.ShapeDtypeStruct((4, tokens, width), bf16),
         ],
         scratch_shapes=[pltpu.VMEM((units, some, 2 * unit), bf16)],
-        input_output_aliases={9 + i: i for i in range(len(so_far))},
+        input_output_aliases={10 + n_count + i: i for i in range(len(so_far))},
         compiler_params=pltpu.CompilerParams(vmem_limit_bytes=52 << 20),
         cost_estimate=pl.CostEstimate(
             flops=10 * some * width * ff,
@@ -735,25 +784,48 @@
             transcendentals=some * ff,
         ),
         name="feed",
-    )(at, *directs, seconds, both, down, both, *so_far)
+    )(at, *directs, *seconds, both, down, both, *so_far)
     return outs[:4], outs[4]
 
 
+def branch_kernel(hidden_ref, down_ref, out_ref):
+    out_ref[...] = dot_plain(hidden_ref[...], down_ref[...]).astype(bf16).reshape(out_ref.shape)
+
+
+def branch(hidden, down, parts):
+    rows, ff = hidden.shape
+    width = down.shape[1]
+    tokens = rows // (4 * parts)
+    return pl.pallas_call(
+        branch_kernel,
+        grid=(parts, 4),
+        in_specs=[
+            pl.BlockSpec((4 * tokens, ff), lambda h, i: (h, 0)),
+            pl.BlockSpec((ff, width // 4), lambda h, i: (0, i)),
+        ],
+        out_specs=pl.BlockSpec((4, tokens, width // 4), lambda h, i: (0, h, i)),
+        out_shape=jax.ShapeDtypeStruct((4, parts * tokens, width), bf16),
+        compiler_params=pltpu.CompilerParams(vmem_limit_bytes=52 << 20),
+        cost_estimate=pl.CostEstimate(flops=1 << 20, bytes_accessed=1 << 16, transcendentals=0),
+        name="branch",
+    )(hidden, down)
+
+
 def split_kernel(both_ref, gate_ref, up_ref):
-    half = gate_ref.shape[1]
-    gate_ref[...] = both_ref[:, :half].astype(f32)
-    up_ref[...] = both_ref[:, half:].astype(f32)
+    for low in range(0, gate_ref.shape[1], 128):
+        gate_ref[:, low : low + 128] = both_ref[:, 2 * low : 2 * low + 128].astype(f32)
+        up_ref[:, low : low + 128] = both_ref[:, 2 * low + 128 : 2 * low + 256].astype(f32)
 
 
 def split(both):
     rows, cols = both.shape
     out = jax.ShapeDtypeStruct((rows, cols // 2), f32)
-    half = pl.BlockSpec((rows, 128), lambda i: (0, i))
+    part = pl.BlockSpec((64, cols // 2), lambda i: (i, 0))
     return pl.pallas_call(
         split_kernel,
-        grid=(cols // 256,),
-        in_specs=[pl.BlockSpec((rows, 256), lambda i: (0, i))],
-        out_specs=[half, half],
+        grid=(rows // 64,),
+        in_specs=[pl.BlockSpec((64, cols), lambda i: (i, 0))],
+        out_specs=[part, part],
         out_shape=[out, out],
         name="split",
     )(both)
@@ -794,8 +866,6 @@
     inv_first = rms_scale(rows)
     normed = (rows * inv_first).astype(bf16)
     first = lax.all_gather(jnp.concatenate([normed, down_weight], 0), "fsdp", axis=0, tiled=False)
-    normed_all = first[:, :tokens].reshape(length, width)
-    down_use = first[:, tokens:].reshape(ff_own, width)
     gain_mine = attention_gain.astype(f32)[:, None]
 
     def by_chip(weight):
@@ -812,18 +882,19 @@
         block = lax.dynamic_index_in_dim(sent, group ^ bit, 0, keepdims=False)
         return jnp.concatenate([block, gain_rows], 0)
 
+    picked = jnp.sum(
+        jnp.where(jnp.arange(exit_scale.shape[0], dtype=jnp.int32) == group_ids[0], exit_scale, 0.0)
+    )
+    cotangent = output_grad[0].astype(f32) * picked
+    direct = keep * cotangent
+    direct_low = direct.astype(bf16)
+    direct_near = line_first(direct_low)
     columns = jnp.stack([to_chip(0)] + [flip(to_chip(bit), 2 * bit) for bit in (1, 2, 3)])
-    output_plane = gather_planes(after(output_weight, columns))
+    output_plane = gather_planes(after(output_weight, columns, *direct_near))
     columns = gather_planes(after(columns, output_plane))
     columns_other = flip(columns, 1)
     output_full = lax.all_gather(output_plane, "fsdp", axis=1, tiled=True).reshape(width, width)
     both = lax.all_gather(after(both_mine, columns), "fsdp", axis=0, tiled=True)
-    picked = jnp.sum(
-        jnp.where(jnp.arange(exit_scale.shape[0], dtype=jnp.int32) == group_ids[0], exit_scale, 0.0)
-    )
-    cotangent = output_grad[0].astype(f32) * picked
-    direct = keep * cotangent
-
     half_dim = HEAD_DIM // 2
     cosine, sine = rotary_tables(length)
     cosine, sine = cosine[:, 0], sine[:, 0]
@@ -834,42 +905,39 @@
     positions = jnp.arange(length, dtype=jnp.int32)
     starts = jnp.max(jnp.where(positions[None, :] >= ends[:, None], ends[:, None], 0), 0)[None, :]
 
-    direct_low = after(direct.astype(bf16), columns)
-    direct_1 = shift(direct_low, 1)
-    queries, keys, values, mixed, norm, project, gains = front(
-        at, normed_all, columns, columns_other, cosine, sine, starts
-    )
-    mixed = after(mixed, direct_1)
-    direct_2 = shift(direct_low, 2)
-    mixed_other = flip(mixed, 1)
+    direct_second = line_second(*after_all(direct_near, columns))
+    queries, keys, values, mixed, norm, project, gains, down_use = front(
+        at, first, tokens, columns, columns_other, cosine, sine, starts
+    )
     gain_second = gains[:, 0, :own_rows].reshape(width).astype(f32)
 
     attended_low = lax.all_to_all(mixed, "fsdp", split_axis=0, concat_axis=1, tiled=True)
-    direct_3 = shift(direct_low, 3)
-    attended_low = after(attended_low, direct_2)
+    attended_low = after(attended_low, *direct_second)
     branch_attention = dot_plain(attended_low, output_full)
     middle = rows + branch_attention
     inv_second = rms_scale(middle)
-    directs = [direct_low, direct_1, direct_2, direct_3]
+    directs = [direct_low, *direct_near, *direct_second]
     second_mine = (middle * inv_second * gain_second).astype(bf16)
-    seconds_low = gather_planes(after(second_mine[:half], direct_3, mixed_other))
-    seconds_high = gather_planes(after(second_mine[half:], seconds_low))
+    second_half = second_mine[:half]
+    second_near = line_first(second_half)
+    seconds_low = [second_half, *second_near, *line_second(*second_near)]
+    attended_all = lax.all_gather(after(attended_low, *seconds_low), "fsdp", axis=0, tiled=True)
+    seconds_high = gather_planes(after(second_mine[half:], *seconds_low))
 
     stacked, terms_low = feed(at, 0, 2, seconds_low, directs, both, down_use, None)
-    stacked, terms_high = feed(at, 1, 2, seconds_high, directs, both, down_use, stacked)
+    stacked, terms_high = feed(at, 1, 2, [seconds_high], directs, both, down_use, stacked)
     second_all, direct_all, hidden_all, grads_all = stacked
     got_low = swap_planes(terms_low)
 
+    branch_terms = branch(hidden_all, down_use, 2)
     down_term = dot_left_t(hidden_all, direct_all).astype(bf16)
     got_high = swap_planes(after(terms_high, got_low))
     grad_second = jnp.concatenate(
-        [jnp.sum(got_low.astype(f32), 0), jnp.sum(got_high.astype(f32), 0)], 0
+        [jnp.sum(after(got_low, got_high).astype(f32), 0), jnp.sum(got_high.astype(f32), 0)], 0
     )
     both_term = dot_left_t(second_all, grads_all).astype(bf16)
     down_grad = lax.psum_scatter(down_term, "fsdp", scatter_dimension=0, tiled=True).astype(f32)
     both_grad = lax.psum_scatter(both_term, "fsdp", scatter_dimension=0, tiled=True)
-    branch_terms = dot_plain(hidden_all, down_use).astype(bf16).reshape(2, 4, half, width)
-    branch_terms = jnp.transpose(branch_terms, (1, 0, 2, 3)).reshape(4, tokens, width)
 
     weighted = grad_second * gain_second
     grad_middle = inv_second * weighted - middle * inv_second**3 * jnp.mean(
@@ -877,44 +945,67 @@
     )
     grad_branch = (direct + grad_middle).astype(bf16)
     grad_attended = dot_right_t(grad_branch, output_full).astype(bf16)
-    grad_heads = lax.all_to_all(grad_attended, "fsdp", split_axis=1, concat_axis=0, tiled=True)
     gain_term = jnp.sum(grad_second * middle * inv_second, 0, keepdims=True)
     gain_high = gain_term.astype(bf16)
     gain_low = (gain_term - gain_high.astype(f32)).astype(bf16)
-    branch_block = jnp.concatenate(
-        [grad_branch, gain_high, gain_low, jnp.zeros((14, width), bf16)], 0
-    )
-    ahead = [
-        lax.dynamic_index_in_dim(branch_terms, (plane + k) % 4, 0, keepdims=False) for k in range(4)
-    ]
-    branch_1, branch_3 = shift(after(ahead[1], grad_branch), 1), shift(after(ahead[3], grad_branch), 3)
-    branch_x, branch_y = flip(branch_block, 2), flip(branch_block, 4)
-    grad_heads = after(grad_heads, branch_x, branch_y, branch_1, branch_3)
-    branch_2 = shift(after(ahead[2], grad_branch), 2)
-    branch_low, branch_high = flip(branch_x[:half], 4), flip(branch_y[half:], 2)
+    gain_rows = jnp.concatenate([gain_high, gain_low, jnp.zeros((14, width), bf16)], 0)
+    packed = jnp.concatenate(
+        [
+            jnp.concatenate([grad_attended, jnp.zeros((16, width), bf16)], 0).reshape(-1, 8, q_width),
+            jnp.concatenate([grad_branch, gain_rows], 0).reshape(-1, 8, q_width),
+        ],
+        2,
+    )
+    packed = lax.all_to_all(jnp.transpose(packed, (1, 0, 2)), "fsdp", split_axis=0, concat_axis=0)
+    def ahead(step):
+        return lax.dynamic_index_in_dim(branch_terms, jnp.clip(step, 0, 3), 0, keepdims=False)
+
+    branch_up2 = lax.ppermute(after(ahead(plane + 2), grad_branch), "dp", UP[:2])
+    branch_down2 = lax.ppermute(after(ahead(plane - 2), grad_branch), "dp", DOWN[1:])
+    branch_far = lax.ppermute(after(ahead(3 - plane), grad_branch), "dp", [(3, 1), (0, 2)])
+    zero = jnp.zeros((), bf16)
+    sent_up = (
+        ahead(plane + 1).astype(f32)
+        + branch_up2.astype(f32)
+        + jnp.where(plane == 2, branch_far, zero).astype(f32)
+    ).astype(bf16)
+    sent_down = (
+        ahead(plane - 1).astype(f32)
+        + branch_down2.astype(f32)
+        + jnp.where(plane == 1, branch_far, zero).astype(f32)
+    ).astype(bf16)
+    packed = after(packed, sent_up, sent_down)
+    branch_up1 = lax.ppermute(sent_up, "dp", UP)
+    branch_down1 = lax.ppermute(sent_down, "dp", DOWN)
+    output_term = output_grad_term(at, packed, attended_all)
+    output_got = swap_planes(output_term)
+    packed = after(packed, output_term)
     core_terms, chip_terms, grad_cols = back(
-        at, queries, keys, values, mixed, norm, grad_heads, project, cosine, sine, starts
-    )
-    core_terms = after(core_terms, branch_2, branch_low, branch_high)
+        at, queries, keys, values, mixed, norm, packed, project, cosine, sine, starts
+    )
     other = flip(core_terms, 1)
-    branch_pieces = [branch_block, branch_x, branch_y, branch_low, branch_high]
-    mine, others, gain_sum = output_grad_term(at, branch_pieces, after(mixed, core_terms), mixed_other)
-    other = after(other, mine)
+    project_term = project_grad(first, after(grad_cols, branch_up1, branch_down1))
+    other = after(other, project_term)
     sums = [add_low(chip_terms[i], other[i]) for i in range(3)]
     far, near_x, near_y = flip(sums[0], 6), flip(sums[1], 2), flip(sums[2], 4)
-    project_term = project_grad(normed_all, after(grad_cols, *sums)).reshape(4, width // 4, cols)
-    project_got = swap_planes(project_term)
-    branch_feed = (
-        ahead[0].astype(f32) + branch_1.astype(f32) + branch_2.astype(f32) + branch_3.astype(f32)
-    )
-    group, core = place // 2, place % 2
-    gain_own = lax.dynamic_slice_in_dim(gain_sum[0], group * 8 * own_rows, 8 * own_rows)
-    gain_own = gain_own.reshape(4, 2, own_rows).astype(bf16)
-    gain_own = jnp.pad(gain_own[:, :, None, :], ((0, 0), (0, 0), (0, 15), (0, width - own_rows)))
-    mine = jnp.concatenate([mine, lax.dynamic_index_in_dim(gain_own, core, 1, keepdims=False)], 1)
-    others = jnp.concatenate([others, lax.dynamic_index_in_dim(gain_own, 1 - core, 1, keepdims=False)], 1)
-    output_sum = output_rows(after(mine, far, near_x, near_y), others, project_got)
+    core = place % 2
+    keys_term, values_term = project_term[:, q_width : q_width + HEAD_DIM], project_term[:, q_width + HEAD_DIM :]
+    kept = jnp.where(core == 0, keys_term, values_term)
+    kept = add_low(kept, flip(jnp.where(core == 0, values_term, keys_term), 1))
+    project_term = jnp.concatenate([project_term[:, :q_width], kept], 1)
+    kept_cols = q_width + HEAD_DIM
+    project_got = swap_planes(after(project_term.reshape(4, width // 4, kept_cols), output_got))
+    branch_feed = ahead(plane).astype(f32) + branch_up1.astype(f32) + branch_down1.astype(f32)
     project_plane = jnp.sum(project_got.astype(f32), 0).astype(bf16)
+    output_plane_sum = jnp.sum(output_got.astype(f32), 0).astype(bf16)
+    both_plane = jnp.concatenate([project_plane, output_plane_sum[: 8 * own_rows]], 1)
+    gain_four = output_plane_sum[8 * own_rows].reshape(4, own_rows)
+    low_half = place % 2 == 0
+    gain_eight = jnp.concatenate(
+        [jnp.where(low_half, gain_four, 0), jnp.where(low_half, 0, gain_four)], 0
+    )
+    gain_eight = jnp.pad(gain_eight[:, None, :], ((0, 0), (0, 15), (0, kept_cols + q_width - own_rows)))
+    final = jnp.concatenate([both_plane.reshape(8, own_rows, kept_cols + q_width), gain_eight], 1)
     weighted_first = (
         chip_terms[3].astype(f32)
         + other[3].astype(f32)
@@ -929,22 +1020,25 @@
 
     output = (rows + keep * (branch_attention + branch_feed)).astype(bf16)
 
-    back_cols = lax.all_to_all(project_plane, "fsdp", split_axis=0, concat_axis=0, tiled=True)
-    back_cols = back_cols.reshape(8, own_rows, cols).astype(f32)
-
-    def collect(at_col):
-        parts = back_cols[:, :, at_col : at_col + HEAD_DIM].reshape(KV_HEADS, 2, own_rows, HEAD_DIM)
-        return jnp.transpose(jnp.sum(parts, 1), (1, 0, 2)).reshape(own_rows, KV_HEADS * HEAD_DIM)
+    gate_grad, up_grad = split(both_grad)
+    final = lax.all_to_all(after(final, input_grad), "fsdp", split_axis=0, concat_axis=0)
+    final = after(final, gate_grad)
+    back_cols = final[:, :own_rows].astype(f32)
+    output_sum = jnp.transpose(back_cols[:, :, kept_cols:], (1, 0, 2)).reshape(own_rows, width)
+    second_gain_grad = jnp.sum(final[:, own_rows, :own_rows].astype(f32), 0)
+
+    def collect(side):
+        parts = back_cols[side::2, :, q_width:kept_cols]
+        return jnp.transpose(parts, (1, 0, 2)).reshape(own_rows, KV_HEADS * HEAD_DIM)
 
     query_plain = jnp.transpose(back_cols[:, :, :q_width], (1, 0, 2)).reshape(own_rows, width)
-    key_plain = collect(q_width)
-    value_plain = collect(q_width + HEAD_DIM)
+    key_plain = collect(0)
+    value_plain = collect(1)
     first_gain_grad = (
         jnp.sum(query_plain * query_weight.astype(f32), 1)
         + jnp.sum(key_plain * key_weight.astype(f32), 1)
         + jnp.sum(value_plain * value_weight.astype(f32), 1)
     )
-    gate_grad, up_grad = split(both_grad)
     return (
         output[None],
         input_grad[None],
@@ -952,8 +1046,8 @@
         query_plain * gain_mine,
         key_plain * gain_mine,
         value_plain * gain_mine,
-        output_sum[:own_rows],
-        output_sum[own_rows, :own_rows],
+        output_sum,
+        second_gain_grad,
         gate_grad,
         up_grad,
         down_grad,

time: 580 us -> 558 us (0.962)
  the two profiles are of different devices: /device:TPU:9 before, /device:TPU:0 now
where the time goes in v5:
time: 558 us; the launch traced here: 547 us
  waiting for transfers between devices  165 us (30%)
  Pallas kernels  127 us (23%)
  starting transfers between devices  89.5 us (16%)
  other arithmetic  51.9 us (9%)
  matrix products  36.2 us (6%)
  local copies, waits for them, and re-layouts  31.4 us (6%)
  blocking collectives  28.3 us (5%)
  between operations  17.1 us (3%)
    pallas_call x2, Pallas kernels, feed(): pl.pallas_call(functools.partial(feed_kernel, units, len(so_far), n_count...  56.1 us
    ppermute x9, waiting for transfers between devices, flip(): return lax.ppermute(block, 'fsdp', FLIP[bit])  53.3 us
    all_to_all x2, waiting for transfers between devices, gather_planes(): return lax.all_to_all(copies, 'dp', split_axis=0, concat_axis=0)  41.1 us
    all_to_all x1, blocking collectives, gather_planes(): return lax.all_to_all(copies, 'dp', split_axis=0, concat_axis=0)  28.3 us
    dot_general x2, matrix products, dot_left_t(): lax.dot_general(left, right, (((0,), (0,)), ((), ())), preferred_element_...  24.3 us
    all_to_all x4, waiting for transfers between devices, swap_planes(): return lax.all_to_all(whole, 'dp', split_axis=0, concat_axis=0)  20.5 us
    pallas_call x1, Pallas kernels, back(): pl.pallas_call(functools.partial(back_kernel, tokens), in_specs=[SMEM] +...  19.7 us
    all_to_all x4, starting transfers between devices, swap_planes(): return lax.all_to_all(whole, 'dp', split_axis=0, concat_axis=0)  19.3 us
  transfers between devices with their start and end apart: 39, of which 15 were waited for; matrix products, arithmetic and copies ran while one was open for 19% of the time, Pallas kernels for 23%

profile of v5, /device:TPU:0, one launch (start us, length us, event | category | flops | bytes accessed | tf_op | source)
XLA Modules:
  0.0 546.9 jit_solution(6860997877319416581)
XLA Ops:
  15.4 5.0 collective-permute-start.3
  27.0 5.7 %collective-permute-done.2 = bf16[80,768]{1,0:T(8,128)(2,1)S(1)} collective-permute-done((bf16[80,768]{1,0:T(8,128)(2,1)S(1)}, bf16[80,768]{1,0:T(8,128)(2,1)S(1)}, u32[]{:S(2)}, u32[]{:S(2)}) %collective-permute-start.2) | collective-permute-done | bytes 122912 | tf_op jit(solution)/shard_map/ppermute | solution.py:84
  32.7 5.3 collective-permute-done
  38.1 3.4 collective-permute-done.4.refs_2_
  41.5 28.3 %all_to_all.64 = bf16[4,64,2048]{2,1,0:T(8,128)(2,1)} all-to-all(bf16[4,64,2048]{2,1,0:T(8,128)(2,1)S(1)} %broadcast_in_dim.93), channel_id=1, replica_groups=mesh['dp'=4,'fsdp'=8] {'dp'}, dimensions={0} | all-to-all | bytes 2097152 | tf_op jit(solution)/shard_map/all_to_all | solution.py:112
  71.2 4.6 all-to-all-start.1
  79.3 3.1 copy.64
  82.5 4.5 reshape.206
  87.0 33.2 %all-to-all-done.1.refs_1_ = bf16[4,4,80,768]{3,2,1,0:T(8,128)(2,1)} async-done(((bf16[4,4,80,768]{3,2,1,0:T(8,128)(2,1)}), bf16[4,4,80,768]{3,2,1,0:T(8,128)(2,1)}, u32[]{:S(2)}, u32[]{:S(2)}) %all-to-all-start.1) | async-done | bytes 1966112 | tf_op jit(solution)/shard_map/all_to_all | solution.py:112
  120.7 2.8 fusion.25
  130.3 19.3 %front.1 = (bf16[1536,256]{1,0:T(8,128)(2,1)S(1)}, bf16[1536,128]{1,0:T(8,128)(2,1)S(1)}, bf16[1536,128]{1,0:T(8,128)(2,1)S(1)}, bf16[1536,256]{1,0:T(8,128)(2,1...) custom-call(s32[2]{0:T(128)S(1)} %pad_add_fusion.at_ref, ...), custom_call_target="tpu_custom_call" | custom-call | flops 5637144576 | bytes 10485760 | tf_op jit(solution)/shard_map/front/pallas_call | solution.py:540
  149.6 4.4 all-to-all-start.2
  154.6 17.6 %all-to-all-done.2 = bf16[8,192,256]{2,1,0:T(8,128)(2,1)} async-done(((bf16[8,192,256]{2,1,0:T(8,128)(2,1)}), bf16[8,192,256]{2,1,0:T(8,128)(2,1)}, u32[]{:S(2)}, u32[]{:S(2)}) %all-to-all-start.2) | async-done | bytes 786464 | tf_op jit(solution)/shard_map/all_to_all | solution.py:914
  174.3 5.6 %multiply_reduce_fusion.2 = (f32[192]{0:T(256)S(1)}, f32[192,2048]{1,0:T(8,128)S(1)}) fusion(bf16[1,192,2048]{2,1,0:T(8,128)(2,1)S(1)} %copy-done.10, bf16[192,2048]{1,0:T(8,128)(2,1)} %bitcast.143, bf16[2048,2048]{1,0:T(8,128)(2,1)} %bitcast.158), kind=kOutput, calls=%fused_computation.46 | convolution fusion | flops 1612185344 | bytes 11535104 | tf_op jit(solution)/shard_map/dot_general | solution.py:24
  183.2 8.4 %collective-permute-start.9 = (bf16[96,2048]{1,0:T(8,128)(2,1)S(1)}, bf16[96,2048]{1,0:T(8,128)(2,1)S(1)}, u32[]{:S(2)}, u32[]{:S(2)}) collective-permute-start(bf16[96,2048]{1,0:T(8,128)(2,1)S(1)} %get-tuple-element.115.refs_6_), channel_id=1, source_target_pairs={{0,8},{8,16},{16,24},{1,9},{9,17},{17,25},{2,10},{10,18},{18,26},{... | collective-permute-start | bytes 1179656 | tf_op jit(solution)/shard_map/ppermute | solution.py:97
  191.5 3.8 collective-permute-done.10.refs_8_
  200.1 12.3 %collective-permute-done.13.refs_11_ = bf16[96,2048]{1,0:T(8,128)(2,1)S(1)} collective-permute-done((bf16[96,2048]{1,0:T(8,128)(2,1)S(1)}, bf16[96,2048]{1,0:T(8,128)(2,1)S(1)}, u32[]{:S(2)}, u32[]{:S(2)}) %collective-permute-start.13) | collective-permute-done | bytes 393248 | tf_op jit(solution)/shard_map/ppermute | solution.py:106
  213.1 5.2 collective-permute-done.12.refs_10_
  220.7 5.1 all-to-all-start.3
  225.7 28.0 %feed.2 = (bf16[768,2048]{1,0:T(8,128)(2,1)}, bf16[768,2048]{1,0:T(8,128)(2,1)}, bf16[768,1408]{1,0:T(8,128)(2,1)}, bf16[768,2816]{1,0:T(8,128)(2,1)}, bf16[4,96,2048]{2,1,0:T(8,128)(2,1)}) custom-call(s32[2]{0:T(128)S(1)} %pad_add_fusion.at_ref, bf16[192,2048]{1,0:T(8,128)(2,1)} %copy-done.2, bf16[192,2048]{1,0:T(8,128)(2,1)} %copy-done, ...), custom_call_target="tpu_custom_call" | custom-call | flops 11072962560 | bytes 28835840 | tf_op jit(solution)/shard_map/feed/pallas_call | solution.py:752
  253.7 7.9 %all-to-all-done.3.refs_6_ = bf16[4,96,2048]{2,1,0:T(8,128)(2,1)} async-done(((bf16[4,96,2048]{2,1,0:T(8,128)(2,1)}), bf16[4,96,2048]{2,1,0:T(8,128)(2,1)}, u32[]{:S(2)}, u32[]{:S(2)}) %all-to-all-start.3) | async-done | bytes 1572896 | tf_op jit(solution)/shard_map/all_to_all | solution.py:112
  261.7 4.5 all-to-all-start.4
  266.2 28.1 %feed.3 = (bf16[768,2048]{1,0:T(8,128)(2,1)}, bf16[768,2048]{1,0:T(8,128)(2,1)}, bf16[768,1408]{1,0:T(8,128)(2,1)}, bf16[768,2816]{1,0:T(8,128)(2,1)}, bf16[4,96,2048]{2,1,0:T(8,128)(2,1)}) custom-call(s32[2]{0:T(128)S(1)} %pad_add_fusion.at_ref, ...), custom_call_target="tpu_custom_call", output_to_operand_aliasing={{0}: (11, {}), {1}: (12, {}), {2}: (13, {}), {3}: (14, {})} | custom-call | flops 11072962560 | bytes 28835840 | tf_op jit(solution)/shard_map/feed/pallas_call | solution.py:752
  294.3 9.7 %convolution_convert_fusion.1 = bf16[1408,2048]{1,0:T(8,128)(2,1)} fusion(bf16[768,1408]{1,0:T(8,128)(2,1)} %get-tuple-element.68.hidden_ref, bf16[768,2048]{1,0:T(8,128)(2,1)} %get-tuple-element.96), kind=kOutput, calls=%fused_computation.1 | convolution fusion | flops 4432068608 | bytes 11075584 | tf_op jit(solution)/shard_map/dot_general | solution.py:32
  304.0 5.1 all-to-all-start.5
  309.2 12.2 %branch.1 = bf16[4,192,2048]{2,1,0:T(8,128)(2,1)} custom-call(bf16[768,1408]{1,0:T(8,128)(2,1)} %get-tuple-element.68.hidden_ref, bf16[1408,2048]{1,0:T(8,128)(2,1)} %get-tuple-element.63.refs_13_.refs_8_.down_ref), custom_call_target="tpu_custom_call" | custom-call | flops 1048576 | bytes 65536 | tf_op jit(solution)/shard_map/branch/pallas_call | solution.py:799
  321.4 3.3 dynamic-slice_bitcast_fusion.2
  324.7 20.4 %all-to-all-done.5 = bf16[4,96,2048]{2,1,0:T(8,128)(2,1)S(1)} async-done(((bf16[4,96,2048]{2,1,0:T(8,128)(2,1)}), bf16[4,96,2048]{2,1,0:T(8,128)(2,1)S(1)}, u32[]{:S(2)}, u32[]{:S(2)}) %all-to-all-start.5) | async-done | bytes 1572896 | tf_op jit(solution)/shard_map/all_to_all | solution.py:116
  353.2 3.5 collective-permute-start.15
  358.8 6.3 %convolution_convert_fusion.2 = bf16[192,2048]{1,0:T(8,128)(2,1)S(1)} fusion(bf16[192,2048]{1,0:T(8,128)(2,1)S(1)} %add_convert_fusion.3, bf16[2048,2048]{1,0:T(8,128)(2,1)} %bitcast.159), kind=kOutput, calls=%fused_computation.10 | convolution fusion | flops 1611005952 | bytes 9961472 | tf_op jit(solution)/shard_map/dot_general | solution.py:28
  367.0 6.7 %all-to-all-start.6 = ((bf16[8,208,512]{2,1,0:T(8,128)(2,1)}), bf16[8,208,512]{2,1,0:T(8,128)(2,1)S(1)}, u32[]{:S(2)}, u32[]{:S(2)}) async-start(bf16[8,208,512]{2,1,0:T(8,128)(2,1)} %maximum_bitcast_fusion), calls=%async_computation.6 | async-start | bytes 3407872 | tf_op jit(solution)/shard_map/all_to_all | solution.py:959
  373.8 14.6 %convolution_convert_fusion = bf16[2048,2816]{1,0:T(8,128)(2,1)} fusion(bf16[768,2048]{1,0:T(8,128)(2,1)} %get-tuple-element.91, bf16[768,2816]{1,0:T(8,128)(2,1)} %get-tuple-element.92), kind=kOutput, calls=%fused_computation | convolution fusion | flops 8864137216 | bytes 19005440 | tf_op jit(solution)/shard_map/dot_general | solution.py:32
  388.4 4.0 fusion.11
  392.5 5.1 collective-permute-start.16
  400.1 8.5 %output_grad_term.1 = bf16[4,528,256]{2,1,0:T(8,128)(2,1)} custom-call(s32[2]{0:T(128)S(1)} %pad_add_fusion.at_ref, bf16[8,208,512]{2,1,0:T(8,128)(2,1)} %copy-done.22, bf16[1536,2048]{1,0:T(8,128)(2,1)} %all-gather.10.cloned.1.call-done.attended_ref), custom_call_target="tpu_custom_call" | custom-call | flops 48318382080 | bytes 6291456 | tf_op jit(solution)/shard_map/output_grad_term/pallas_call | solution.py:679
  408.6 4.6 all-to-all-start.7
  413.3 19.7 %back.1 = (bf16[4,192,2048]{2,1,0:T(8,128)(2,1)}, bf16[4,192,2048]{2,1,0:T(8,128)(2,1)}, bf16[1536,512]{1,0:T(8,128)(2,1)}) custom-call(s32[2]{0:T(128)S(1)} %pad_add_fusion.at_ref, bf16[1536,256]{1,0:T(8,128)(2,1)S(1)} %get-tuple-element.76.q_ref, bf16[1536,128]{1,0:T(8,128)(2,1)S(1)} %get-tuple-element.77.k_ref, ...), custom_call_target="tpu_custom_call" | custom-call | flops 970595500032 | bytes 8388608 | tf_op jit(solution)/shard_map/back/pallas_call | solution.py:603
  434.7 7.5 %project_grad.1 = bf16[2048,512]{1,0:T(8,128)(2,1)} custom-call(bf16[8,368,2048]{2,1,0:T(8,128)(2,1)} %bitcast.138, bf16[1536,512]{1,0:T(8,128)(2,1)S(1)} %copy-done.6), custom_call_target="tpu_custom_call" | custom-call | flops 32212254720 | bytes 6291456 | tf_op jit(solution)/shard_map/project_grad/pallas_call | solution.py:637
  447.2 5.1 all-to-all-start.8
  453.9 5.3 fusion.19
  459.2 3.5 collective-permute-start.20
  465.2 24.9 %collective-permute-done.20 = bf16[192,2048]{1,0:T(8,128)(2,1)S(1)} collective-permute-done((bf16[192,2048]{1,0:T(8,128)(2,1)}, bf16[192,2048]{1,0:T(8,128)(2,1)S(1)}, u32[]{:S(2)}, u32[]{:S(2)}) %collective-permute-start.20) | collective-permute-done | bytes 786464 | tf_op jit(solution)/shard_map/ppermute | solution.py:84
  490.1 15.8 %collective-permute-done.21 = bf16[192,2048]{1,0:T(8,128)(2,1)} collective-permute-done((bf16[192,2048]{1,0:T(8,128)(2,1)}, bf16[192,2048]{1,0:T(8,128)(2,1)}, u32[]{:S(2)}, u32[]{:S(2)}) %collective-permute-start.21) | collective-permute-done | bytes 786464 | tf_op jit(solution)/shard_map/ppermute | solution.py:84
  506.0 4.6 fusion.7
  510.7 5.2 fusion.6
  518.8 3.5 all-to-all-start.9
  524.8 3.8 split.1
  528.6 6.7 %all-to-all-done.9 = bf16[8,80,640]{2,1,0:T(8,128)(2,1)S(1)} async-done(((bf16[8,80,640]{2,1,0:T(8,128)(2,1)}), bf16[8,80,640]{2,1,0:T(8,128)(2,1)S(1)}, u32[]{:S(2)}, u32[]{:S(2)}) %all-to-all-start.9) | async-done | bytes 819232 | tf_op jit(solution)/shard_map/all_to_all | solution.py:1024
  (244 shorter events, 74.0 us)
Async XLA Ops:
  7.2 123.1 %all-gather.12.cloned.1.call-start = ((), (), s32[]{:S(2)}) async-start(), calls=%async_computation.17 | async-start | bytes 13565952 | tf_op jit(solution)/shard_map/all_gather | solution.py:868
  12.4 161.9 %all-gather.6.cloned.1.call-start = ((), (), s32[]{:S(2)}) async-start(), calls=%async_computation.12 | async-start | bytes 9437184 | tf_op jit(solution)/shard_map/all_gather | solution.py:896
  15.4 22.6 %collective-permute-start.3 = (bf16[192,2048]{1,0:T(8,128)(2,1)S(1)}, bf16[192,2048]{1,0:T(8,128)(2,1)S(1)}, u32[]{:S(2)}, u32[]{:S(2)}) collective-permute-start(bf16[192,2048]{1,0:T(8,128)(2,1)S(1)} %fusion.17.refs_0_), channel_id=1, source_target_pairs={{0,8},{8,16},{16,24},{1,9},{9,17},{17,25},{2,10},{10,18},{18,26},{... | collective-permute-start | bytes 2359304 | tf_op jit(solution)/shard_map/ppermute | solution.py:97
  20.4 21.0 %collective-permute-start.4 = (bf16[192,2048]{1,0:T(8,128)(2,1)S(1)}, bf16[192,2048]{1,0:T(8,128)(2,1)}, u32[]{:S(2)}, u32[]{:S(2)}) collective-permute-start(bf16[192,2048]{1,0:T(8,128)(2,1)S(1)} %fusion.17.refs_0_), channel_id=1, source_target_pairs={{8,0},{16,8},{24,16},{9,1},{17,9},{25,17},{10,2},{18,10},{26,18},{... | collective-permute-start | bytes 2359304 | tf_op jit(solution)/shard_map/ppermute | solution.py:97
  23.5 9.2 %collective-permute-start.2 = (bf16[80,768]{1,0:T(8,128)(2,1)S(1)}, bf16[80,768]{1,0:T(8,128)(2,1)S(1)}, u32[]{:S(2)}, u32[]{:S(2)}) collective-permute-start(bf16[80,768]{1,0:T(8,128)(2,1)S(1)} %get-tuple-element.139), channel_id=1, source_target_pairs={{0,6},{1,7},{2,4},{3,5},{4,2},{5,3},{6,0},{7,1},{8,14},{9,15},{10,... | collective-permute-start | bytes 368648 | tf_op jit(solution)/shard_map/ppermute | solution.py:84
  26.0 12.0 %collective-permute-start = (bf16[80,768]{1,0:T(8,128)(2,1)S(1)}, bf16[80,768]{1,0:T(8,128)(2,1)S(1)}, u32[]{:S(2)}, u32[]{:S(2)}) collective-permute-start(bf16[80,768]{1,0:T(8,128)(2,1)S(1)} %get-tuple-element.137), channel_id=1, source_target_pairs={{0,2},{1,3},{2,0},{3,1},{4,6},{5,7},{6,4},{7,5},{8,10},{9,11},{10,... | collective-permute-start | bytes 368648 | tf_op jit(solution)/shard_map/ppermute | solution.py:84
  26.5 11.4 %collective-permute-start.1 = (bf16[80,768]{1,0:T(8,128)(2,1)S(1)}, bf16[80,768]{1,0:T(8,128)(2,1)S(1)}, u32[]{:S(2)}, u32[]{:S(2)}) collective-permute-start(bf16[80,768]{1,0:T(8,128)(2,1)S(1)} %get-tuple-element.138), channel_id=1, source_target_pairs={{0,4},{1,5},{2,6},{3,7},{4,0},{5,1},{6,2},{7,3},{8,12},{9,13},{10,... | collective-permute-start | bytes 368648 | tf_op jit(solution)/shard_map/ppermute | solution.py:84
  38.0 89.9 %copy-start = (bf16[192,2048]{1,0:T(8,128)(2,1)}, bf16[192,2048]{1,0:T(8,128)(2,1)S(1)}, u32[]{:S(2)}) copy-start(bf16[192,2048]{1,0:T(8,128)(2,1)S(1)} %collective-permute-done.3.refs_1_) | copy-start | bytes 2359300
  71.2 49.0 %all-to-all-start.1 = ((bf16[4,4,80,768]{3,2,1,0:T(8,128)(2,1)}), bf16[4,4,80,768]{3,2,1,0:T(8,128)(2,1)}, u32[]{:S(2)}, u32[]{:S(2)}) async-start(bf16[4,4,80,768]{3,2,1,0:T(8,128)(2,1)} %broadcast_in_dim.94), calls=%async_computation.1 | async-start | bytes 3932160 | tf_op jit(solution)/shard_map/all_to_all | solution.py:112
  75.8 149.9 %all-gather.8.cloned.1.call-start = ((), (), s32[]{:S(2)}) async-start(), calls=%async_computation.13 | async-start | bytes 12976128 | tf_op jit(solution)/shard_map/all_gather | solution.py:897
  120.2 10.0 %collective-permute-start.5 = (bf16[4,4,80,768]{3,2,1,0:T(8,128)(2,1)}, bf16[4,4,80,768]{3,2,1,0:T(8,128)(2,1)}, u32[]{:S(2)}, u32[]{:S(2)}) collective-permute-start(bf16[4,4,80,768]{3,2,1,0:T(8,128)(2,1)} %all-to-all-done.1.refs_1_), channel_id=1, source_target_pairs={{0,1},{1,0},{2,3},{3,2},{4,5},{5,4},{6,7},{7,6},{8,9},{9,8},{10,11... | collective-permute-start | bytes 5898248 | tf_op jit(solution)/shard_map/ppermute | solution.py:84
  125.1 49.2 %collective-permute-start.6 = (bf16[192,2048]{1,0:T(8,128)(2,1)S(1)}, bf16[192,2048]{1,0:T(8,128)(2,1)}, u32[]{:S(2)}, u32[]{:S(2)}) collective-permute-start(bf16[192,2048]{1,0:T(8,128)(2,1)S(1)} %collective-permute-done.3.refs_1_), channel_id=1, source_target_pairs={{8,16},{16,24},{9,17},{17,25},{10,18},{18,26},{11,19},{19,27},{12,... | collective-permute-start | bytes 2359304 | tf_op jit(solution)/shard_map/ppermute | solution.py:104
  126.7 47.6 %collective-permute-start.7 = (bf16[192,2048]{1,0:T(8,128)(2,1)}, bf16[192,2048]{1,0:T(8,128)(2,1)}, u32[]{:S(2)}, u32[]{:S(2)}) collective-permute-start(bf16[192,2048]{1,0:T(8,128)(2,1)} %collective-permute-done.4.refs_2_), channel_id=1, source_target_pairs={{8,0},{16,8},{9,1},{17,9},{10,2},{18,10},{11,3},{19,11},{12,4},{20... | collective-permute-start | bytes 2359304 | tf_op jit(solution)/shard_map/ppermute | solution.py:105
  128.9 45.3 %collective-permute-start.8 = (bf16[192,2048]{1,0:T(8,128)(2,1)}, bf16[192,2048]{1,0:T(8,128)(2,1)}, u32[]{:S(2)}, u32[]{:S(2)}) collective-permute-start(bf16[192,2048]{1,0:T(8,128)(2,1)} %broadcast_select_fusion), channel_id=1, source_target_pairs={{16,0},{8,24},{17,1},{9,25},{18,2},{10,26},{19,3},{11,27},{20,4},{... | collective-permute-start | bytes 2359304 | tf_op jit(solution)/shard_map/ppermute | solution.py:106
  149.6 22.5 %all-to-all-start.2 = ((bf16[8,192,256]{2,1,0:T(8,128)(2,1)}), bf16[8,192,256]{2,1,0:T(8,128)(2,1)}, u32[]{:S(2)}, u32[]{:S(2)}) async-start(bf16[8,192,256]{2,1,0:T(8,128)(2,1)} %bitcast.150), calls=%async_computation.2 | async-start | bytes 1572864 | tf_op jit(solution)/shard_map/all_to_all | solution.py:914
  154.0 245.0 %all-gather.10.cloned.1.call-start = ((), (), s32[]{:S(2)}) async-start(), calls=%async_computation.14 | async-start | bytes 7077888 | tf_op jit(solution)/shard_map/all_gather | solution.py:924
  180.6 168.8 %copy-start.37 = (f32[192]{0:T(256)}, f32[192]{0:T(256)S(1)}, u32[]{:S(2)}) copy-start(f32[192]{0:T(256)S(1)} %get-tuple-element.133) | copy-start | bytes 2308
  181.9 13.4 %collective-permute-start.10 = (bf16[96,2048]{1,0:T(8,128)(2,1)S(1)}, bf16[96,2048]{1,0:T(8,128)(2,1)S(1)}, u32[]{:S(2)}, u32[]{:S(2)}) collective-permute-start(bf16[96,2048]{1,0:T(8,128)(2,1)S(1)} %get-tuple-element.115.refs_6_), channel_id=1, source_target_pairs={{8,0},{16,8},{24,16},{9,1},{17,9},{25,17},{10,2},{18,10},{26,18},{... | collective-permute-start | bytes 1179656 | tf_op jit(solution)/shard_map/ppermute | solution.py:97
  183.2 13.6 %collective-permute-start.9 = (bf16[96,2048]{1,0:T(8,128)(2,1)S(1)}, bf16[96,2048]{1,0:T(8,128)(2,1)S(1)}, u32[]{:S(2)}, u32[]{:S(2)}) collective-permute-start(bf16[96,2048]{1,0:T(8,128)(2,1)S(1)} %get-tuple-element.115.refs_6_), channel_id=1, source_target_pairs={{0,8},{8,16},{16,24},{1,9},{9,17},{17,25},{2,10},{10,18},{18,26},{... | collective-permute-start | bytes 1179656 | tf_op jit(solution)/shard_map/ppermute | solution.py:97
  196.8 15.5 %collective-permute-start.13 = (bf16[96,2048]{1,0:T(8,128)(2,1)S(1)}, bf16[96,2048]{1,0:T(8,128)(2,1)S(1)}, u32[]{:S(2)}, u32[]{:S(2)}) collective-permute-start(bf16[96,2048]{1,0:T(8,128)(2,1)S(1)} %broadcast_select_fusion.2), channel_id=1, source_target_pairs={{16,0},{8,24},{17,1},{9,25},{18,2},{10,26},{19,3},{11,27},{20,4},{... | collective-permute-start | bytes 1179656 | tf_op jit(solution)/shard_map/ppermute | solution.py:106
  198.1 14.3 %collective-permute-start.11 = (bf16[96,2048]{1,0:T(8,128)(2,1)S(1)}, bf16[96,2048]{1,0:T(8,128)(2,1)S(1)}, u32[]{:S(2)}, u32[]{:S(2)}) collective-permute-start(bf16[96,2048]{1,0:T(8,128)(2,1)S(1)} %collective-permute-done.9.refs_7_), channel_id=1, source_target_pairs={{8,16},{16,24},{9,17},{17,25},{10,18},{18,26},{11,19},{19,27},{12,... | collective-permute-start | bytes 1179656 | tf_op jit(solution)/shard_map/ppermute | solution.py:104
  198.8 19.5 %collective-permute-start.12 = (bf16[96,2048]{1,0:T(8,128)(2,1)S(1)}, bf16[96,2048]{1,0:T(8,128)(2,1)S(1)}, u32[]{:S(2)}, u32[]{:S(2)}) collective-permute-start(bf16[96,2048]{1,0:T(8,128)(2,1)S(1)} %collective-permute-done.10.refs_8_), channel_id=1, source_target_pairs={{8,0},{16,8},{9,1},{17,9},{10,2},{18,10},{11,3},{19,11},{12,4},{20... | collective-permute-start | bytes 1179656 | tf_op jit(solution)/shard_map/ppermute | solution.py:105
  220.7 41.0 %all-to-all-start.3 = ((bf16[4,96,2048]{2,1,0:T(8,128)(2,1)}), bf16[4,96,2048]{2,1,0:T(8,128)(2,1)}, u32[]{:S(2)}, u32[]{:S(2)}) async-start(bf16[4,96,2048]{2,1,0:T(8,128)(2,1)} %broadcast_in_dim.100), calls=%async_computation.3 | async-start | bytes 3145728 | tf_op jit(solution)/shard_map/all_to_all | solution.py:112
  261.7 42.4 %all-to-all-start.4 = ((bf16[4,96,2048]{2,1,0:T(8,128)(2,1)}), bf16[4,96,2048]{2,1,0:T(8,128)(2,1)}, u32[]{:S(2)}, u32[]{:S(2)}) async-start(bf16[4,96,2048]{2,1,0:T(8,128)(2,1)} %get-tuple-element.69), calls=%async_computation.4 | async-start | bytes 3145728 | tf_op jit(solution)/shard_map/all_to_all | solution.py:116
  266.1 256.3 %reduce-scatter.5.cloned.1.call-start = ((), (), s32[]{:S(2)}) async-start(), calls=%async_computation.16 | async-start | bytes 6488064 | tf_op jit(solution)/shard_map/reduce_scatter | solution.py:939
  304.0 41.1 %all-to-all-start.5 = ((bf16[4,96,2048]{2,1,0:T(8,128)(2,1)}), bf16[4,96,2048]{2,1,0:T(8,128)(2,1)S(1)}, u32[]{:S(2)}, u32[]{:S(2)}) async-start(bf16[4,96,2048]{2,1,0:T(8,128)(2,1)} %get-tuple-element.71), calls=%async_computation.5 | async-start | bytes 3145728 | tf_op jit(solution)/shard_map/all_to_all | solution.py:116
  351.6 36.8 %collective-permute-start.17 = (bf16[192,2048]{1,0:T(8,128)(2,1)}, bf16[192,2048]{1,0:T(8,128)(2,1)}, u32[]{:S(2)}, u32[]{:S(2)}) collective-permute-start(bf16[192,2048]{1,0:T(8,128)(2,1)} %get-tuple-element.75), channel_id=1, source_target_pairs={{16,8},{24,16},{17,9},{25,17},{18,10},{26,18},{19,11},{27,19},{20,... | collective-permute-start | bytes 2359304 | tf_op jit(solution)/shard_map/ppermute | solution.py:964
  353.2 35.2 %collective-permute-start.15 = (bf16[192,2048]{1,0:T(8,128)(2,1)}, bf16[192,2048]{1,0:T(8,128)(2,1)}, u32[]{:S(2)}, u32[]{:S(2)}) collective-permute-start(bf16[192,2048]{1,0:T(8,128)(2,1)} %get-tuple-element.74), channel_id=1, source_target_pairs={{24,8},{0,16},{25,9},{1,17},{26,10},{2,18},{27,11},{3,19},{28,12},... | collective-permute-start | bytes 2359304 | tf_op jit(solution)/shard_map/ppermute | solution.py:965
  356.7 31.8 %collective-permute-start.14 = (bf16[192,2048]{1,0:T(8,128)(2,1)}, bf16[192,2048]{1,0:T(8,128)(2,1)}, u32[]{:S(2)}, u32[]{:S(2)}) collective-permute-start(bf16[192,2048]{1,0:T(8,128)(2,1)} %get-tuple-element.73), channel_id=1, source_target_pairs={{0,8},{8,16},{1,9},{9,17},{2,10},{10,18},{3,11},{11,19},{4,12},{12... | collective-permute-start | bytes 2359304 | tf_op jit(solution)/shard_map/ppermute | solution.py:963
  367.0 31.9 %all-to-all-start.6 = ((bf16[8,208,512]{2,1,0:T(8,128)(2,1)}), bf16[8,208,512]{2,1,0:T(8,128)(2,1)S(1)}, u32[]{:S(2)}, u32[]{:S(2)}) async-start(bf16[8,208,512]{2,1,0:T(8,128)(2,1)} %maximum_bitcast_fusion), calls=%async_computation.6 | async-start | bytes 3407872 | tf_op jit(solution)/shard_map/all_to_all | solution.py:959
  373.7 151.0 %reduce-scatter.3.cloned.1.call-start = ((), (), s32[]{:S(2)}) async-start(), calls=%async_computation.15 | async-start | bytes 12976128 | tf_op jit(solution)/shard_map/reduce_scatter | solution.py:940
  392.5 40.5 %collective-permute-start.16 = (bf16[192,2048]{1,0:T(8,128)(2,1)}, bf16[192,2048]{1,0:T(8,128)(2,1)}, u32[]{:S(2)}, u32[]{:S(2)}) collective-permute-start(bf16[192,2048]{1,0:T(8,128)(2,1)} %get-tuple-element.104), channel_id=1, source_target_pairs={{0,8},{8,16},{16,24},{1,9},{9,17},{17,25},{2,10},{10,18},{18,26},{... | collective-permute-start | bytes 2359304 | tf_op jit(solution)/shard_map/ppermute | solution.py:978
  397.6 35.4 %collective-permute-start.18 = (bf16[192,2048]{1,0:T(8,128)(2,1)}, bf16[192,2048]{1,0:T(8,128)(2,1)}, u32[]{:S(2)}, u32[]{:S(2)}) collective-permute-start(bf16[192,2048]{1,0:T(8,128)(2,1)} %get-tuple-element.105), channel_id=1, source_target_pairs={{8,0},{16,8},{24,16},{9,1},{17,9},{25,17},{10,2},{18,10},{26,18},{... | collective-permute-start | bytes 2359304 | tf_op jit(solution)/shard_map/ppermute | solution.py:979
  408.6 38.6 %all-to-all-start.7 = ((bf16[4,528,256]{2,1,0:T(8,128)(2,1)}), bf16[4,528,256]{2,1,0:T(8,128)(2,1)}, u32[]{:S(2)}, u32[]{:S(2)}) async-start(bf16[4,528,256]{2,1,0:T(8,128)(2,1)} %output_grad_term.1), calls=%async_computation.7 | async-start | bytes 2162688 | tf_op jit(solution)/shard_map/all_to_all | solution.py:116
  433.0 19.3 %collective-permute-start.19 = (bf16[4,192,2048]{2,1,0:T(8,128)(2,1)}, bf16[4,192,2048]{2,1,0:T(8,128)(2,1)S(1)}, u32[]{:S(2)}, u32[]{:S(2)}) collective-permute-start(bf16[4,192,2048]{2,1,0:T(8,128)(2,1)} %get-tuple-element.85), channel_id=1, source_target_pairs={{0,1},{1,0},{2,3},{3,2},{4,5},{5,4},{6,7},{7,6},{8,9},{9,8},{10,11... | collective-permute-start | bytes 9437192 | tf_op jit(solution)/shard_map/ppermute | solution.py:84
  443.6 2.0 collective-permute-start.23
  447.2 68.7 %all-to-all-start.8 = ((bf16[4,512,384]{2,1,0:T(8,128)(2,1)}), bf16[4,512,384]{2,1,0:T(8,128)(2,1)}, u32[]{:S(2)}, u32[]{:S(2)}) async-start(bf16[4,512,384]{2,1,0:T(8,128)(2,1)} %bitcast.33), calls=%async_computation.8 | async-start | bytes 3145728 | tf_op jit(solution)/shard_map/all_to_all | solution.py:116
  453.9 52.1 %copy-start.12 = (bf16[1,192,2048]{2,1,0:T(8,128)(2,1)S(1)}, bf16[1,192,2048]{2,1,0:T(8,128)(2,1)}, u32[]{:S(2)}) copy-start(bf16[1,192,2048]{2,1,0:T(8,128)(2,1)} %param.15) | copy-start | bytes 2359300
  459.2 46.8 %copy-start.9 = (f32[192,2048]{1,0:T(8,128)S(1)}, f32[192,2048]{1,0:T(8,128)}, u32[]{:S(2)}) copy-start(f32[192,2048]{1,0:T(8,128)} %copy-done.7) | copy-start | bytes 4718596
  459.2 30.9 %collective-permute-start.20 = (bf16[192,2048]{1,0:T(8,128)(2,1)}, bf16[192,2048]{1,0:T(8,128)(2,1)S(1)}, u32[]{:S(2)}, u32[]{:S(2)}) collective-permute-start(bf16[192,2048]{1,0:T(8,128)(2,1)} %get-tuple-element.101), channel_id=1, source_target_pairs={{0,6},{1,7},{2,4},{3,5},{4,2},{5,3},{6,0},{7,1},{8,14},{9,15},{10,... | collective-permute-start | bytes 2359304 | tf_op jit(solution)/shard_map/ppermute | solution.py:84
  462.8 43.2 %collective-permute-start.21 = (bf16[192,2048]{1,0:T(8,128)(2,1)}, bf16[192,2048]{1,0:T(8,128)(2,1)}, u32[]{:S(2)}, u32[]{:S(2)}) collective-permute-start(bf16[192,2048]{1,0:T(8,128)(2,1)} %get-tuple-element.103), channel_id=1, source_target_pairs={{0,2},{1,3},{2,0},{3,1},{4,6},{5,7},{6,4},{7,5},{8,10},{9,11},{10,... | collective-permute-start | bytes 2359304 | tf_op jit(solution)/shard_map/ppermute | solution.py:84
  462.8 43.2 %collective-permute-start.22 = (bf16[192,2048]{1,0:T(8,128)(2,1)}, bf16[192,2048]{1,0:T(8,128)(2,1)}, u32[]{:S(2)}, u32[]{:S(2)}) collective-permute-start(bf16[192,2048]{1,0:T(8,128)(2,1)} %get-tuple-element.102), channel_id=1, source_target_pairs={{0,4},{1,5},{2,6},{3,7},{4,0},{5,1},{6,2},{7,3},{8,12},{9,13},{10,... | collective-permute-start | bytes 2359304 | tf_op jit(solution)/shard_map/ppermute | solution.py:84
  464.9 45.7 %copy-start.23 = (bf16[528,256]{1,0:T(8,128)(2,1)}, bf16[528,256]{1,0:T(8,128)(2,1)S(1)}, u32[]{:S(2)}) copy-start(bf16[528,256]{1,0:T(8,128)(2,1)S(1)} %reduce_sum.154) | copy-start | bytes 811012
  465.1 45.5 %copy-start.14 = (f32[96,2048]{1,0:T(8,128)S(1)}, f32[96,2048]{1,0:T(8,128)}, u32[]{:S(2)}) copy-start(f32[96,2048]{1,0:T(8,128)} %copy-done.13) | copy-start | bytes 2359300
  465.1 45.5 %copy-start.16 = (f32[96,2048]{1,0:T(8,128)S(1)}, f32[96,2048]{1,0:T(8,128)}, u32[]{:S(2)}) copy-start(f32[96,2048]{1,0:T(8,128)} %copy-done.15) | copy-start | bytes 2359300
  465.1 45.5 %copy-start.19 = (bf16[1,192,2048]{2,1,0:T(8,128)(2,1)S(1)}, bf16[1,192,2048]{2,1,0:T(8,128)(2,1)}, u32[]{:S(2)}) copy-start(bf16[1,192,2048]{2,1,0:T(8,128)(2,1)} %param.16) | copy-start | bytes 2359300
  465.1 45.5 %copy-start.36 = (f32[2048]{0:T(1024)S(1)}, f32[2048]{0:T(1024)}, u32[]{:S(2)}) copy-start(f32[2048]{0:T(1024)} %copy-done.34) | copy-start | bytes 24580
  518.8 16.4 %all-to-all-start.9 = ((bf16[8,80,640]{2,1,0:T(8,128)(2,1)}), bf16[8,80,640]{2,1,0:T(8,128)(2,1)S(1)}, u32[]{:S(2)}, u32[]{:S(2)}) async-start(bf16[8,80,640]{2,1,0:T(8,128)(2,1)} %fusion.18), calls=%async_computation.9 | async-start | bytes 1638400 | tf_op jit(solution)/shard_map/all_to_all | solution.py:1024
  (46 other events, 470.7 us)
Sparse Core Ops, SparseCore 0:
  12.6 77.8 all-gather.11
  92.4 54.3 all-gather.5
  149.3 75.1 all-gather.7
  226.2 45.5 all-gather.9
  304.1 63.2 reduce-scatter.4
  388.5 109.6 reduce-scatter.2

commit v6 on v5

--- a/solution.py
+++ b/solution.py
@@ -3,6 +3,7 @@
 
 import jax
 import jax.numpy as jnp
+import numpy as np
 from jax import lax
 from jax.experimental import pallas as pl
 from jax.experimental.pallas import tpu as pltpu
@@ -701,14 +702,17 @@
 
 
 def feed_kernel(units, count, n_count, at_ref, *refs):
-    d_refs, n_refs, refs = refs[:6], refs[6 : 6 + n_count], refs[6 + n_count :]
+    d_refs, n_refs, refs = refs[:4], refs[4 : 4 + n_count], refs[4 + n_count :]
     both_ref, down_ref, rows_ref, refs = *refs[:3], refs[3 + count :]
     second_ref, direct_ref, hidden_ref, grads_ref, term_ref, held_ref = refs
     step = pl.program_id(0)
 
     @pl.when(step == 0)
     def _():
-        place_blocks(at_ref[1], d_refs, direct_ref)
+        tokens = d_refs[0].shape[0]
+        for slot in range(4):
+            owner = (at_ref[1] - slot) & 3
+            direct_ref[pl.ds(pl.multiple_of(owner * tokens, tokens), tokens), :] = d_refs[slot][...]
         if n_count == 6:
             place_blocks(at_ref[1], n_refs, second_ref)
         else:
@@ -754,7 +758,7 @@
         grid=(units + parts,),
         in_specs=[
             SMEM,
-            *[pl.BlockSpec((tokens, width), lambda i: (part_at, 0))] * 6,
+            *[pl.BlockSpec((tokens, width), lambda i: (part_at, 0))] * 4,
             *[single if n_count == 6 else gathered] * n_count,
             pl.BlockSpec((width, 2 * unit), lambda i: (0, jnp.minimum(i, units - 1))),
             pl.BlockSpec((unit, width), lambda i: (jnp.minimum(i, units - 1), 0)),
@@ -776,7 +780,7 @@
             jax.ShapeDtypeStruct((4, tokens, width), bf16),
         ],
         scratch_shapes=[pltpu.VMEM((units, some, 2 * unit), bf16)],
-        input_output_aliases={10 + n_count + i: i for i in range(len(so_far))},
+        input_output_aliases={8 + n_count + i: i for i in range(len(so_far))},
         compiler_params=pltpu.CompilerParams(vmem_limit_bytes=52 << 20),
         cost_estimate=pl.CostEstimate(
             flops=10 * some * width * ff,
@@ -829,6 +833,183 @@
         out_shape=[out, out],
         name="split",
     )(both)
+
+
+def finish_kernel(final_ref, gain_ref, qw_ref, kw_ref, vw_ref, q_ref, k_ref, v_ref, o_ref, first_ref, second_ref):
+    rows = q_ref.shape[0]
+    own = q_ref.shape[1] // 8
+    gain = gain_ref[...]
+    first = None
+    second = None
+    for device in range(8):
+        block = final_ref[device, :rows, :].astype(f32)
+        cols = slice(device * own, (device + 1) * own)
+        head = slice(device // 2 * HEAD_DIM, (device // 2 + 1) * HEAD_DIM)
+        out_ref, weight_ref = ((k_ref, kw_ref), (v_ref, vw_ref))[device % 2]
+        query, shared = block[:, :own], block[:, own : own + HEAD_DIM]
+        q_ref[:, cols] = query * gain
+        out_ref[:, head] = shared * gain
+        o_ref[:, cols] = block[:, own + HEAD_DIM :]
+        term = jnp.sum(query * qw_ref[:, cols].astype(f32), 1, keepdims=True) + jnp.sum(
+            shared * weight_ref[:, head].astype(f32), 1, keepdims=True
+        )
+        extra = jnp.sum(final_ref[device, rows:, :HEAD_DIM].astype(f32), 0, keepdims=True)
+        first = term if first is None else first + term
+        second = extra if second is None else second + extra
+    first_ref[...] = first
+    second_ref[...] = second
+
+
+def finish(final, gain, query_weight, key_weight, value_weight):
+    def like(weight):
+        return jax.ShapeDtypeStruct(weight.shape, f32)
+
+    rows = query_weight.shape[0]
+    return pl.pallas_call(
+        finish_kernel,
+        in_specs=[VMEM] * 5,
+        out_specs=[VMEM] * 6,
+        out_shape=[
+            like(query_weight),
+            like(key_weight),
+            like(value_weight),
+            like(query_weight),
+            jax.ShapeDtypeStruct((rows, 1), f32),
+            jax.ShapeDtypeStruct((1, HEAD_DIM), f32),
+        ],
+        compiler_params=pltpu.CompilerParams(vmem_limit_bytes=32 << 20),
+        name="finish",
+    )(final, gain, query_weight, key_weight, value_weight)
+
+
+def middle_back_kernel(low_ref, high_ref, middle_ref, inv_ref, gain_ref, direct_ref, weight_ref,
+                       packed_ref, grad_ref, branch_ref):
+    tokens, width = grad_ref.shape
+    half = tokens // 2
+    own = weight_ref.shape[0]
+    step = pl.program_id(0)
+
+    @pl.when(step == 0)
+    def _():
+        for first, ref in ((0, low_ref), (half, high_ref)):
+            here = slice(first, first + half)
+            total = ref[0].astype(f32)
+            for plane in (1, 2, 3):
+                total = total + ref[plane].astype(f32)
+            middle, inv = middle_ref[here, :], inv_ref[here, :]
+            weighted = total * gain_ref[...]
+            grad = inv * weighted - middle * inv**3 * jnp.mean(weighted * middle, -1, keepdims=True)
+            grad_ref[here, :] = grad
+            branch_ref[here, :] = (direct_ref[here, :] + grad).astype(bf16)
+            term = jnp.sum(total * middle * inv, 0, keepdims=True)
+            gain_term = term if first == 0 else gain_term + term
+        gain_high = gain_term.astype(bf16).astype(f32)
+        row = lax.broadcasted_iota(jnp.int32, (16, width), 0)
+        branch_ref[tokens:, :] = jnp.where(
+            row == 0, gain_high, jnp.where(row == 1, gain_term - gain_high, 0.0)
+        ).astype(bf16)
+
+    packed_ref[0, :tokens, :own] = dot_right_t(branch_ref[:tokens, :], weight_ref[...]).astype(bf16)
+    packed_ref[0, tokens:, :own] = jnp.zeros((16, own), bf16)
+    packed_ref[0, :, own:] = branch_ref[:, pl.ds(pl.multiple_of(step * own, own), own)]
+
+
+def middle_back(low, high, middle, inv, gain, direct, weight):
+    tokens, width = middle.shape
+    own = width // 8
+    whole = pl.BlockSpec((4, tokens // 2, width), lambda i: (0, 0, 0))
+    rows = pl.BlockSpec((tokens, width), lambda i: (0, 0))
+    return pl.pallas_call(
+        middle_back_kernel,
+        grid=(8,),
+        in_specs=[
+            whole,
+            whole,
+            rows,
+            pl.BlockSpec((tokens, 1), lambda i: (0, 0)),
+            pl.BlockSpec((1, width), lambda i: (0, 0)),
+            rows,
+            pl.BlockSpec((own, width), lambda i: (i, 0)),
+        ],
+        out_specs=[pl.BlockSpec((1, tokens + 16, 2 * own), lambda i: (i, 0, 0)), rows],
+        out_shape=[
+            jax.ShapeDtypeStruct((8, tokens + 16, 2 * own), bf16),
+            jax.ShapeDtypeStruct((tokens, width), f32),
+        ],
+        scratch_shapes=[pltpu.VMEM((tokens + 16, width), bf16)],
+        compiler_params=pltpu.CompilerParams(vmem_limit_bytes=48 << 20),
+        cost_estimate=pl.CostEstimate(
+            flops=2 * tokens * width * width, bytes_accessed=3 * width * width, transcendentals=0
+        ),
+        name="middle_back",
+    )(low, high, middle, inv, gain, direct, weight)
+
+
+def middle_kernel(parts_ref, weight_ref, rows_ref, gain_ref, attended_ref, branch_ref, middle_ref, inv_ref,
+                  low_ref, high_ref, total_ref):
+    step = pl.program_id(0)
+    term = dot_plain(parts_ref[0], weight_ref[...])
+    attended_ref[...] = parts_ref[0]
+
+    @pl.when(step == 0)
+    def _():
+        total_ref[...] = term
+
+    @pl.when(step > 0)
+    def _():
+        total_ref[...] += term
+
+    @pl.when(step == pl.num_programs(0) - 1)
+    def _():
+        half = low_ref.shape[0]
+        branch = total_ref[...]
+        middle = rows_ref[...].astype(f32) + branch
+        inv = rms_scale(middle)
+        branch_ref[...] = branch
+        middle_ref[...] = middle
+        inv_ref[...] = inv
+        second = (middle * inv * gain_ref[...]).astype(bf16)
+        low_ref[...] = second[:half]
+        high_ref[...] = second[half:]
+
+
+def middle_forward(parts, weight, rows, gain):
+    devices, tokens, own = parts.shape
+    width = weight.shape[1]
+    half = pl.BlockSpec((tokens // 2, width), lambda i: (0, 0))
+    whole = pl.BlockSpec((tokens, width), lambda i: (0, 0))
+    return pl.pallas_call(
+        middle_kernel,
+        grid=(devices,),
+        in_specs=[
+            pl.BlockSpec((1, tokens, own), lambda i: (i, 0, 0)),
+            pl.BlockSpec((own, width), lambda i: (i, 0)),
+            whole,
+            pl.BlockSpec((1, width), lambda i: (0, 0)),
+        ],
+        out_specs=[
+            pl.BlockSpec((tokens, own), lambda i: (0, i)),
+            whole,
+            whole,
+            pl.BlockSpec((tokens, 1), lambda i: (0, 0)),
+            half,
+            half,
+        ],
+        out_shape=[
+            jax.ShapeDtypeStruct((tokens, devices * own), bf16),
+            jax.ShapeDtypeStruct((tokens, width), f32),
+            jax.ShapeDtypeStruct((tokens, width), f32),
+            jax.ShapeDtypeStruct((tokens, 1), f32),
+            jax.ShapeDtypeStruct((tokens // 2, width), bf16),
+            jax.ShapeDtypeStruct((tokens // 2, width), bf16),
+        ],
+        scratch_shapes=[pltpu.VMEM((tokens, width), f32)],
+        compiler_params=pltpu.CompilerParams(vmem_limit_bytes=48 << 20),
+        cost_estimate=pl.CostEstimate(
+            flops=2 * tokens * width * width, bytes_accessed=3 * width * width, transcendentals=0
+        ),
+        name="middle_forward",
+    )(parts, weight, rows, gain)
 
 
 def fast_device(
@@ -888,41 +1069,41 @@
     cotangent = output_grad[0].astype(f32) * picked
     direct = keep * cotangent
     direct_low = direct.astype(bf16)
-    direct_near = line_first(direct_low)
+    direct_1 = shift(direct_low, 1)
     columns = jnp.stack([to_chip(0)] + [flip(to_chip(bit), 2 * bit) for bit in (1, 2, 3)])
-    output_plane = gather_planes(after(output_weight, columns, *direct_near))
+    output_plane = gather_planes(after(output_weight, columns, direct_1))
     columns = gather_planes(after(columns, output_plane))
     columns_other = flip(columns, 1)
     output_full = lax.all_gather(output_plane, "fsdp", axis=1, tiled=True).reshape(width, width)
     both = lax.all_gather(after(both_mine, columns), "fsdp", axis=0, tiled=True)
     half_dim = HEAD_DIM // 2
-    cosine, sine = rotary_tables(length)
-    cosine, sine = cosine[:, 0], sine[:, 0]
-    cosine = jnp.concatenate([cosine, cosine], 1)
-    sine = jnp.concatenate([-sine, sine], 1)
+    frequency = rope_base ** (-(2.0 * np.arange(HEAD_DIM // 2, dtype=np.float32)) / HEAD_DIM)
+    angles = np.arange(length, dtype=np.float32)[:, None] * frequency.astype(np.float32)[None, :]
+    cosine = jnp.asarray(np.concatenate([np.cos(angles), np.cos(angles)], 1).astype(np.float32))
+    sine = jnp.asarray(np.concatenate([-np.sin(angles), np.sin(angles)], 1).astype(np.float32))
     order = jnp.arange(doc_lengths.shape[1])
     ends = jnp.sum(jnp.where(order[None, :] <= order[:, None], doc_lengths[0][None, :], 0), 1)
     positions = jnp.arange(length, dtype=jnp.int32)
     starts = jnp.max(jnp.where(positions[None, :] >= ends[:, None], ends[:, None], 0), 0)[None, :]
 
-    direct_second = line_second(*after_all(direct_near, columns))
+    direct_2 = shift(after(direct_low, columns), 2)
     queries, keys, values, mixed, norm, project, gains, down_use = front(
         at, first, tokens, columns, columns_other, cosine, sine, starts
     )
     gain_second = gains[:, 0, :own_rows].reshape(width).astype(f32)
 
-    attended_low = lax.all_to_all(mixed, "fsdp", split_axis=0, concat_axis=1, tiled=True)
-    attended_low = after(attended_low, *direct_second)
-    branch_attention = dot_plain(attended_low, output_full)
-    middle = rows + branch_attention
-    inv_second = rms_scale(middle)
-    directs = [direct_low, *direct_near, *direct_second]
-    second_mine = (middle * inv_second * gain_second).astype(bf16)
-    second_half = second_mine[:half]
+    parts = lax.all_to_all(mixed.reshape(8, tokens, q_width), "fsdp", split_axis=0, concat_axis=0)
+    direct_3 = shift(after(direct_low, columns), 3)
+    parts = after(parts, direct_2)
+    attended_low, branch_attention, middle, inv_second, second_low, second_high = middle_forward(
+        parts, output_full, layer_input[0], gain_second[None, :]
+    )
+    directs = [direct_low, direct_1, direct_2, direct_3]
+    second_half = after(second_low, direct_3)
     second_near = line_first(second_half)
     seconds_low = [second_half, *second_near, *line_second(*second_near)]
     attended_all = lax.all_gather(after(attended_low, *seconds_low), "fsdp", axis=0, tiled=True)
-    seconds_high = gather_planes(after(second_mine[half:], *seconds_low))
+    seconds_high = gather_planes(after(second_high, *seconds_low))
 
     stacked, terms_low = feed(at, 0, 2, seconds_low, directs, both, down_use, None)
     stacked, terms_high = feed(at, 1, 2, [seconds_high], directs, both, down_use, stacked)
@@ -930,40 +1111,46 @@
     got_low = swap_planes(terms_low)
 
     branch_terms = branch(hidden_all, down_use, 2)
-    down_term = dot_left_t(hidden_all, direct_all).astype(bf16)
-    got_high = swap_planes(after(terms_high, got_low))
-    grad_second = jnp.concatenate(
-        [jnp.sum(after(got_low, got_high).astype(f32), 0), jnp.sum(got_high.astype(f32), 0)], 0
-    )
+    down_term = dot_left_t(after(hidden_all, got_low), direct_all).astype(bf16)
     both_term = dot_left_t(second_all, grads_all).astype(bf16)
+    got_high = after(swap_planes(after(terms_high, got_low)), branch_terms, both_term)
     down_grad = lax.psum_scatter(down_term, "fsdp", scatter_dimension=0, tiled=True).astype(f32)
     both_grad = lax.psum_scatter(both_term, "fsdp", scatter_dimension=0, tiled=True)
 
-    weighted = grad_second * gain_second
-    grad_middle = inv_second * weighted - middle * inv_second**3 * jnp.mean(
-        weighted * middle, -1, keepdims=True
-    )
-    grad_branch = (direct + grad_middle).astype(bf16)
-    grad_attended = dot_right_t(grad_branch, output_full).astype(bf16)
-    gain_term = jnp.sum(grad_second * middle * inv_second, 0, keepdims=True)
-    gain_high = gain_term.astype(bf16)
-    gain_low = (gain_term - gain_high.astype(f32)).astype(bf16)
-    gain_rows = jnp.concatenate([gain_high, gain_low, jnp.zeros((14, width), bf16)], 0)
-    packed = jnp.concatenate(
-        [
-            jnp.concatenate([grad_attended, jnp.zeros((16, width), bf16)], 0).reshape(-1, 8, q_width),
-            jnp.concatenate([grad_branch, gain_rows], 0).reshape(-1, 8, q_width),
-        ],
-        2,
-    )
-    packed = lax.all_to_all(jnp.transpose(packed, (1, 0, 2)), "fsdp", split_axis=0, concat_axis=0)
+    to_send, grad_middle = middle_back(
+        got_low, got_high, middle, inv_second, gain_second[None, :], direct, output_full
+    )
+    packed = lax.all_to_all(to_send, "fsdp", split_axis=0, concat_axis=0)
+
     def ahead(step):
         return lax.dynamic_index_in_dim(branch_terms, jnp.clip(step, 0, 3), 0, keepdims=False)
 
-    branch_up2 = lax.ppermute(after(ahead(plane + 2), grad_branch), "dp", UP[:2])
-    branch_down2 = lax.ppermute(after(ahead(plane - 2), grad_branch), "dp", DOWN[1:])
-    branch_far = lax.ppermute(after(ahead(3 - plane), grad_branch), "dp", [(3, 1), (0, 2)])
+    branch_up2 = lax.ppermute(after(ahead(plane + 2), to_send), "dp", UP[:2])
+    branch_down2 = lax.ppermute(after(ahead(plane - 2), to_send), "dp", DOWN[1:])
+    branch_far = lax.ppermute(after(ahead(3 - plane), to_send), "dp", [(3, 1), (0, 2)])
+    output_term = output_grad_term(at, packed, attended_all)
+    output_got = swap_planes(output_term)
+    packed = after(packed, output_term)
+    core_terms, chip_terms, grad_cols = back(
+        at, queries, keys, values, mixed, norm, packed, project, cosine, sine, starts
+    )
+    core_terms, branch_up2, branch_down2, branch_far = after_all(
+        (core_terms, branch_up2, branch_down2, branch_far)
+    )
+    other = flip(core_terms, 1)
+    project_term = project_grad(first, grad_cols)
+    other = after(other, project_term)
+    sums = [add_low(chip_terms[i], other[i]) for i in range(3)]
+    far, near_x, near_y = flip(sums[0], 6), flip(sums[1], 2), flip(sums[2], 4)
+    core = place % 2
+    keys_term, values_term = project_term[:, q_width : q_width + HEAD_DIM], project_term[:, q_width + HEAD_DIM :]
+    kept = jnp.where(core == 0, keys_term, values_term)
+    kept = add_low(kept, flip(jnp.where(core == 0, values_term, keys_term), 1))
+    project_term = jnp.concatenate([project_term[:, :q_width], kept], 1)
+    kept_cols = q_width + HEAD_DIM
+    project_got = swap_planes(after(project_term.reshape(4, width // 4, kept_cols), output_got))
     zero = jnp.zeros((), bf16)
+    branch_up2, branch_down2, branch_far = after_all((branch_up2, branch_down2, branch_far), *sums)
     sent_up = (
         ahead(plane + 1).astype(f32)
         + branch_up2.astype(f32)
@@ -974,27 +1161,8 @@
         + branch_down2.astype(f32)
         + jnp.where(plane == 1, branch_far, zero).astype(f32)
     ).astype(bf16)
-    packed = after(packed, sent_up, sent_down)
     branch_up1 = lax.ppermute(sent_up, "dp", UP)
     branch_down1 = lax.ppermute(sent_down, "dp", DOWN)
-    output_term = output_grad_term(at, packed, attended_all)
-    output_got = swap_planes(output_term)
-    packed = after(packed, output_term)
-    core_terms, chip_terms, grad_cols = back(
-        at, queries, keys, values, mixed, norm, packed, project, cosine, sine, starts
-    )
-    other = flip(core_terms, 1)
-    project_term = project_grad(first, after(grad_cols, branch_up1, branch_down1))
-    other = after(other, project_term)
-    sums = [add_low(chip_terms[i], other[i]) for i in range(3)]
-    far, near_x, near_y = flip(sums[0], 6), flip(sums[1], 2), flip(sums[2], 4)
-    core = place % 2
-    keys_term, values_term = project_term[:, q_width : q_width + HEAD_DIM], project_term[:, q_width + HEAD_DIM :]
-    kept = jnp.where(core == 0, keys_term, values_term)
-    kept = add_low(kept, flip(jnp.where(core == 0, values_term, keys_term), 1))
-    project_term = jnp.concatenate([project_term[:, :q_width], kept], 1)
-    kept_cols = q_width + HEAD_DIM
-    project_got = swap_planes(after(project_term.reshape(4, width // 4, kept_cols), output_got))
     branch_feed = ahead(plane).astype(f32) + branch_up1.astype(f32) + branch_down1.astype(f32)
     project_plane = jnp.sum(project_got.astype(f32), 0).astype(bf16)
     output_plane_sum = jnp.sum(output_got.astype(f32), 0).astype(bf16)
@@ -1006,6 +1174,8 @@
     )
     gain_eight = jnp.pad(gain_eight[:, None, :], ((0, 0), (0, 15), (0, kept_cols + q_width - own_rows)))
     final = jnp.concatenate([both_plane.reshape(8, own_rows, kept_cols + q_width), gain_eight], 1)
+    gate_grad, up_grad = split(both_grad)
+    final = lax.all_to_all(after(final, far, near_x, near_y, sent_up, sent_down, gate_grad), "fsdp", split_axis=0, concat_axis=0)
     weighted_first = (
         chip_terms[3].astype(f32)
         + other[3].astype(f32)
@@ -1020,34 +1190,19 @@
 
     output = (rows + keep * (branch_attention + branch_feed)).astype(bf16)
 
-    gate_grad, up_grad = split(both_grad)
-    final = lax.all_to_all(after(final, input_grad), "fsdp", split_axis=0, concat_axis=0)
-    final = after(final, gate_grad)
-    back_cols = final[:, :own_rows].astype(f32)
-    output_sum = jnp.transpose(back_cols[:, :, kept_cols:], (1, 0, 2)).reshape(own_rows, width)
-    second_gain_grad = jnp.sum(final[:, own_rows, :own_rows].astype(f32), 0)
-
-    def collect(side):
-        parts = back_cols[side::2, :, q_width:kept_cols]
-        return jnp.transpose(parts, (1, 0, 2)).reshape(own_rows, KV_HEADS * HEAD_DIM)
-
-    query_plain = jnp.transpose(back_cols[:, :, :q_width], (1, 0, 2)).reshape(own_rows, width)
-    key_plain = collect(0)
-    value_plain = collect(1)
-    first_gain_grad = (
-        jnp.sum(query_plain * query_weight.astype(f32), 1)
-        + jnp.sum(key_plain * key_weight.astype(f32), 1)
-        + jnp.sum(value_plain * value_weight.astype(f32), 1)
+    final = after(final, branch_up1, branch_down1)
+    query_grad, key_grad, value_grad, output_sum, first_gain, second_gain = finish(
+        final, gain_mine, query_weight, key_weight, value_weight
     )
     return (
         output[None],
         input_grad[None],
-        first_gain_grad,
-        query_plain * gain_mine,
-        key_plain * gain_mine,
-        value_plain * gain_mine,
+        first_gain[:, 0],
+        query_grad,
+        key_grad,
+        value_grad,
         output_sum,
-        second_gain_grad,
+        second_gain[0, :own_rows],
         gate_grad,
         up_grad,
         down_grad,

time: 558 us -> 536 us (0.961)
  Pallas kernels: 127 us -> 149 us
  starting transfers between devices: 89.5 us -> 74.3 us
  matrix products: 36.2 us -> 21.6 us
  other arithmetic: 51.9 us -> 38.3 us
    pallas_call x0 -> x3, Pallas kernels: none -> 22.9 us  [the longest x1 12.1 us: middle_back(): pl.pallas_call(middle_back_kernel, grid=(8,), in_specs=[whole, whole, row...]
    dot_general x2 -> x0, matrix products: 12 us -> none  [the longest x1 6.34 us: dot_right_t(): lax.dot_general(left, right, (((1,), (1,)), ((), ())), preferred_element_...]
    broadcast_in_dim x0 -> x2, other arithmetic: none -> 8.17 us  [the longest x1 7.58 us: fast_device(): input_grad[None]]
    ppermute x4 -> x2, starting transfers between devices: 15.9 us -> 7.82 us  [line_first(): return (lax.ppermute(block, 'dp', UP), lax.ppermute(block, 'dp', DOWN))]
    ppermute x3 -> x6, waiting for transfers between devices: 0.01 us -> 7.78 us  [the longest x3 7.78 us: shift(): return lax.ppermute(block, 'dp', [(i, (i + step) % 4) for i in range(4)])]
    ppermute x9, waiting for transfers between devices: 53.3 us -> 46 us  [flip(): return lax.ppermute(block, 'fsdp', FLIP[bit])]
    add x2 -> x0, other arithmetic: 5.68 us -> none  [the longest x1 5.16 us: fast_device(): input_grad = cotangent + grad_middle + grad_rows]
    ppermute x3 -> x6, starting transfers between devices: 7.2 us -> 11.3 us  [the longest x1 4.3 us: fast_device(): lax.ppermute(after(ahead(3 - plane), to_send), 'dp', [(3, 1), (0, 2)])]
  transfers between devices with their start and end apart: 39 -> 37, of which waited for: 15 -> 21; matrix products, arithmetic and copies ran while one was open for 19% -> 14% of each run, Pallas kernels for 23% -> 28%
where the time goes in v6:
time: 536 us; the launch traced here: 528 us
  waiting for transfers between devices  167 us (31%)
  Pallas kernels  149 us (28%)
  starting transfers between devices  74.3 us (14%)
  other arithmetic  38.3 us (7%)
  local copies, waits for them, and re-layouts  32.5 us (6%)
  blocking collectives  28.6 us (5%)
  matrix products  21.6 us (4%)
  between operations  16.4 us (3%)
    pallas_call x2, Pallas kernels, feed(): pl.pallas_call(functools.partial(feed_kernel, units, len(so_far), n_count...  55.9 us
    ppermute x9, waiting for transfers between devices, flip(): return lax.ppermute(block, 'fsdp', FLIP[bit])  46 us
    all_to_all x2, waiting for transfers between devices, gather_planes(): return lax.all_to_all(copies, 'dp', split_axis=0, concat_axis=0)  36.7 us
    all_to_all x1, blocking collectives, gather_planes(): return lax.all_to_all(copies, 'dp', split_axis=0, concat_axis=0)  28.6 us
    dot_general x2, matrix products, dot_left_t(): lax.dot_general(left, right, (((0,), (0,)), ((), ())), preferred_element_...  21.6 us
    pallas_call x1, Pallas kernels, front(): pl.pallas_call(front_kernel, grid=(1,), in_specs=[SMEM, pl.BlockSpec((8,...  19.4 us
    pallas_call x1, Pallas kernels, back(): pl.pallas_call(functools.partial(back_kernel, tokens), in_specs=[SMEM] +...  18.7 us
    all_to_all x4, starting transfers between devices, swap_planes(): return lax.all_to_all(whole, 'dp', split_axis=0, concat_axis=0)  18.2 us
  transfers between devices with their start and end apart: 37, of which 21 were waited for; matrix products, arithmetic and copies ran while one was open for 14% of the time, Pallas kernels for 28%

profile of v6, /device:TPU:0, one launch (start us, length us, event | category | flops | bytes accessed | tf_op | source)
XLA Modules:
  0.0 527.7 jit_solution(14349741040068329474)
XLA Ops:
  25.3 4.9 collective-permute-done.2
  35.5 3.5 collective-permute-done.3.refs_1_
  39.1 28.6 %all_to_all.50 = bf16[4,64,2048]{2,1,0:T(8,128)(2,1)} all-to-all(bf16[4,64,2048]{2,1,0:T(8,128)(2,1)S(1)} %broadcast_in_dim.86), channel_id=1, replica_groups=mesh['dp'=4,'fsdp'=8] {'dp'}, dimensions={0} | all-to-all | bytes 2097152 | tf_op jit(solution)/shard_map/all_to_all | solution.py:113
  69.1 3.6 all-to-all-start.1
  78.8 4.9 copy.47
  83.7 4.5 reshape.125
  88.2 28.9 %all-to-all-done.1.refs_1_ = bf16[4,4,80,768]{3,2,1,0:T(8,128)(2,1)S(1)} async-done(((bf16[4,4,80,768]{3,2,1,0:T(8,128)(2,1)}), bf16[4,4,80,768]{3,2,1,0:T(8,128)(2,1)S(1)}, u32[]{:S(2)}, u32[]{:S(2)}) %all-to-all-start.1) | async-done | bytes 1966112 | tf_op jit(solution)/shard_map/all_to_all | solution.py:113
  117.6 6.2 %collective-permute-done.4.refs_2_ = bf16[4,4,80,768]{3,2,1,0:T(8,128)(2,1)} collective-permute-done((bf16[4,4,80,768]{3,2,1,0:T(8,128)(2,1)S(1)}, bf16[4,4,80,768]{3,2,1,0:T(8,128)(2,1)}, u32[]{:S(2)}, u32[]{:S(2)}) %collective-permute-start.4) | collective-permute-done | bytes 1966112 | tf_op jit(solution)/shard_map/ppermute | solution.py:85
  123.9 19.4 %front.1 = (bf16[1536,256]{1,0:T(8,128)(2,1)S(1)}, bf16[1536,128]{1,0:T(8,128)(2,1)S(1)}, bf16[1536,128]{1,0:T(8,128)(2,1)S(1)}, bf16[1536,256]{1,0:T(8,128)(2,1...) custom-call(s32[2]{0:T(128)S(1)} %pad_add_fusion.at_ref, ...), custom_call_target="tpu_custom_call" | custom-call | flops 5637144576 | bytes 10485760 | tf_op jit(solution)/shard_map/front/pallas_call | solution.py:541
  145.6 3.9 all-to-all-start.2
  150.0 4.3 collective-permute-done.5.refs_2_
  154.3 11.6 %all-to-all-done.2.parts_ref = bf16[8,192,256]{2,1,0:T(8,128)(2,1)S(1)} async-done(((bf16[8,192,256]{2,1,0:T(8,128)(2,1)}), bf16[8,192,256]{2,1,0:T(8,128)(2,1)S(1)}, u32[]{:S(2)}, u32[]{:S(2)}) %all-to-all-start.2) | async-done | bytes 786464 | tf_op jit(solution)/shard_map/all_to_all | solution.py:1095
  165.9 9.7 %middle_forward.1 = (bf16[192,2048]{1,0:T(8,128)(2,1)}, f32[192,2048]{1,0:T(8,128)S(1)}, f32[192,2048]{1,0:T(8,128)}, f32[192,1]{1,0:T(8,128)S(1)}, bf16[96,2048...) custom-call(bf16[8,192,256]{2,1,0:T(8,128)(2,1)S(1)} %all-to-all-done.2.parts_ref, bf16[2048,2048]{1,0:T(8,128)(2,1)} %bitcast.89, ...), custom_call_target="tpu_custom_call" | custom-call | flops 1610612736 | bytes 12582912 | tf_op jit(solution)/shard_map/middle_forward/pallas_call | solution.py:981
  176.8 6.5 %collective-permute-start.7 = (bf16[96,2048]{1,0:T(8,128)(2,1)S(1)}, bf16[96,2048]{1,0:T(8,128)(2,1)S(1)}, u32[]{:S(2)}, u32[]{:S(2)}) collective-permute-start(bf16[96,2048]{1,0:T(8,128)(2,1)S(1)} %get-tuple-element.83.refs_4_), channel_id=1, source_target_pairs={{0,8},{8,16},{16,24},{1,9},{9,17},{17,25},{2,10},{10,18},{18,26},{... | collective-permute-start | bytes 1179656 | tf_op jit(solution)/shard_map/ppermute | solution.py:98
  184.6 7.2 %collective-permute-done.7.refs_5_ = bf16[96,2048]{1,0:T(8,128)(2,1)S(1)} collective-permute-done((bf16[96,2048]{1,0:T(8,128)(2,1)S(1)}, bf16[96,2048]{1,0:T(8,128)(2,1)S(1)}, u32[]{:S(2)}, u32[]{:S(2)}) %collective-permute-start.7) | collective-permute-done | bytes 393248 | tf_op jit(solution)/shard_map/ppermute | solution.py:98
  192.5 3.5 collective-permute-done.8.refs_6_
  198.6 10.7 %collective-permute-done.10.refs_8_ = bf16[96,2048]{1,0:T(8,128)(2,1)S(1)} collective-permute-done((bf16[96,2048]{1,0:T(8,128)(2,1)S(1)}, bf16[96,2048]{1,0:T(8,128)(2,1)S(1)}, u32[]{:S(2)}, u32[]{:S(2)}) %collective-permute-start.10) | collective-permute-done | bytes 393248 | tf_op jit(solution)/shard_map/ppermute | solution.py:106
  209.3 9.1 %collective-permute-done.11.refs_9_ = bf16[96,2048]{1,0:T(8,128)(2,1)S(1)} collective-permute-done((bf16[96,2048]{1,0:T(8,128)(2,1)S(1)}, bf16[96,2048]{1,0:T(8,128)(2,1)S(1)}, u32[]{:S(2)}, u32[]{:S(2)}) %collective-permute-start.11) | collective-permute-done | bytes 393248 | tf_op jit(solution)/shard_map/ppermute | solution.py:107
  220.6 4.3 all-to-all-start.3
  225.0 28.1 %feed.2 = (bf16[768,2048]{1,0:T(8,128)(2,1)}, bf16[768,2048]{1,0:T(8,128)(2,1)}, bf16[768,1408]{1,0:T(8,128)(2,1)}, bf16[768,2816]{1,0:T(8,128)(2,1)}, bf16[4,96,2048]{2,1,0:T(8,128)(2,1)}) custom-call(s32[2]{0:T(128)S(1)} %pad_add_fusion.at_ref, bf16[192,2048]{1,0:T(8,128)(2,1)} %copy-done.1, bf16[192,2048]{1,0:T(8,128)(2,1)} %copy-done.8, ...), custom_call_target="tpu_custom_call" | custom-call | flops 11072962560 | bytes 28835840 | tf_op jit(solution)/shard_map/feed/pallas_call | solution.py:756
  253.1 7.7 %all-to-all-done.3.refs_4_ = bf16[4,96,2048]{2,1,0:T(8,128)(2,1)} async-done(((bf16[4,96,2048]{2,1,0:T(8,128)(2,1)}), bf16[4,96,2048]{2,1,0:T(8,128)(2,1)}, u32[]{:S(2)}, u32[]{:S(2)}) %all-to-all-start.3) | async-done | bytes 1572896 | tf_op jit(solution)/shard_map/all_to_all | solution.py:113
  260.8 3.7 all-to-all-start.4
  265.7 27.7 %feed.3 = (bf16[768,2048]{1,0:T(8,128)(2,1)}, bf16[768,2048]{1,0:T(8,128)(2,1)}, bf16[768,1408]{1,0:T(8,128)(2,1)}, bf16[768,2816]{1,0:T(8,128)(2,1)}, bf16[4,96,2048]{2,1,0:T(8,128)(2,1)}) custom-call(s32[2]{0:T(128)S(1)} %pad_add_fusion.at_ref, ...), custom_call_target="tpu_custom_call", output_to_operand_aliasing={{0}: (9, {}), {1}: (10, {}), {2}: (11, {}), {3}: (12, {})} | custom-call | flops 11072962560 | bytes 28835840 | tf_op jit(solution)/shard_map/feed/pallas_call | solution.py:756
  293.4 7.5 %all-to-all-done.4.low_ref = bf16[4,96,2048]{2,1,0:T(8,128)(2,1)S(1)} async-done(((bf16[4,96,2048]{2,1,0:T(8,128)(2,1)}), bf16[4,96,2048]{2,1,0:T(8,128)(2,1)S(1)}, u32[]{:S(2)}, u32[]{:S(2)}) %all-to-all-start.4) | async-done | bytes 1572896 | tf_op jit(solution)/shard_map/all_to_all | solution.py:117
  300.9 9.7 %convolution_convert_fusion.1 = bf16[1408,2048]{1,0:T(8,128)(2,1)} fusion(bf16[768,1408]{1,0:T(8,128)(2,1)} %get-tuple-element.135.hidden_ref, bf16[768,2048]{1,0:T(8,128)(2,1)} %get-tuple-element.136), kind=kOutput, calls=%fused_computation.1 | convolution fusion | flops 4432068608 | bytes 11075584 | tf_op jit(solution)/shard_map/dot_general | solution.py:33
  310.7 4.9 all-to-all-start.5
  315.6 14.2 %branch.1 = bf16[4,192,2048]{2,1,0:T(8,128)(2,1)} custom-call(bf16[768,1408]{1,0:T(8,128)(2,1)} %get-tuple-element.135.hidden_ref, bf16[1408,2048]{1,0:T(8,128)(2,1)} %get-tuple-element.86.refs_11_.refs_6_.down_ref), custom_call_target="tpu_custom_call" | custom-call | flops 1048576 | bytes 65536 | tf_op jit(solution)/shard_map/branch/pallas_call | solution.py:803
  329.8 11.9 %convolution_convert_fusion = bf16[2048,2816]{1,0:T(8,128)(2,1)} fusion(bf16[768,2048]{1,0:T(8,128)(2,1)S(1)} %copy-done.23, bf16[768,2816]{1,0:T(8,128)(2,1)S(1)} %bitcast.92), kind=kOutput, calls=%fused_computation | convolution fusion | flops 8864137216 | bytes 19005440 | tf_op jit(solution)/shard_map/dot_general | solution.py:33
  341.7 10.4 %all-to-all-done.5.high_ref = bf16[4,96,2048]{2,1,0:T(8,128)(2,1)} async-done(((bf16[4,96,2048]{2,1,0:T(8,128)(2,1)}), bf16[4,96,2048]{2,1,0:T(8,128)(2,1)}, u32[]{:S(2)}, u32[]{:S(2)}) %all-to-all-start.5) | async-done | bytes 1572896 | tf_op jit(solution)/shard_map/all_to_all | solution.py:117
  352.1 12.1 %middle_back.1 = (bf16[8,208,512]{2,1,0:T(8,128)(2,1)}, f32[192,2048]{1,0:T(8,128)S(1)}) custom-call(bf16[4,96,2048]{2,1,0:T(8,128)(2,1)S(1)} %all-to-all-done.4.low_ref, bf16[4,96,2048]{2,1,0:T(8,128)(2,1)} %all-to-all-done.5.high_ref, f32[192,2048]{1,0:T(8,128)} %get-tuple-element.102.middle_ref, f32[192,1]{1,0:T(8,128)S(1)} %get-tuple-element.103.inv_ref, ...), custom_call_target="tpu_custom_call" | custom-call | flops 1610612736 | bytes 12582912 | tf_op jit(solution)/shard_map/middle_back/pallas_call | solution.py:922
  365.3 3.6 all-to-all-start.6
  369.4 3.1 dynamic-slice_bitcast_fusion
  376.3 4.3 collective-permute-start.14
  380.6 10.6 %all-to-all-done.6.packed_ref = bf16[8,208,512]{2,1,0:T(8,128)(2,1)S(1)} async-done(((bf16[8,208,512]{2,1,0:T(8,128)(2,1)}), bf16[8,208,512]{2,1,0:T(8,128)(2,1)S(1)}, u32[]{:S(2)}, u32[]{:S(2)}) %all-to-all-start.6) | async-done | bytes 1703968 | tf_op jit(solution)/shard_map/all_to_all | solution.py:1123
  392.4 6.7 %output_grad_term.1 = bf16[4,528,256]{2,1,0:T(8,128)(2,1)} custom-call(s32[2]{0:T(128)S(1)} %pad_add_fusion.at_ref, bf16[8,208,512]{2,1,0:T(8,128)(2,1)} %copy-done.26, bf16[1536,2048]{1,0:T(8,128)(2,1)} %all-gather.10.cloned.1.call-done.attended_ref), custom_call_target="tpu_custom_call" | custom-call | flops 48318382080 | bytes 6291456 | tf_op jit(solution)/shard_map/output_grad_term/pallas_call | solution.py:680
  399.2 4.6 all-to-all-start.7
  403.8 18.7 %back.1 = (bf16[4,192,2048]{2,1,0:T(8,128)(2,1)}, bf16[4,192,2048]{2,1,0:T(8,128)(2,1)}, bf16[1536,512]{1,0:T(8,128)(2,1)}) custom-call(s32[2]{0:T(128)S(1)} %pad_add_fusion.at_ref, bf16[1536,256]{1,0:T(8,128)(2,1)S(1)} %copy-done.15, bf16[1536,128]{1,0:T(8,128)(2,1)S(1)} %copy-done.17, bf16[1536,128]{1,0:T(8,128)(2,1)S(1)} %copy-done.19, ...), custom_call_target="tpu_custom_call" | custom-call | flops 970595500032 | bytes 8388608 | tf_op jit(solution)/shard_map/back/pallas_call | solution.py:604
  424.0 7.5 %project_grad.1 = bf16[2048,512]{1,0:T(8,128)(2,1)} custom-call(bf16[8,368,2048]{2,1,0:T(8,128)(2,1)} %bitcast.88, bf16[1536,512]{1,0:T(8,128)(2,1)S(1)} %copy-done.20), custom_call_target="tpu_custom_call" | custom-call | flops 32212254720 | bytes 6291456 | tf_op jit(solution)/shard_map/project_grad/pallas_call | solution.py:638
  436.5 5.1 all-to-all-start.8
  441.6 4.4 fusion.21
  453.7 4.1 fusion.12
  459.0 5.5 %collective-permute-start.16 = (bf16[192,2048]{1,0:T(8,128)(2,1)}, bf16[192,2048]{1,0:T(8,128)(2,1)}, u32[]{:S(2)}, u32[]{:S(2)}) collective-permute-start(bf16[192,2048]{1,0:T(8,128)(2,1)} %get-tuple-element.142), channel_id=1, source_target_pairs={{0,8},{8,16},{16,24},{1,9},{9,17},{17,25},{2,10},{10,18},{18,26},{... | collective-permute-start | bytes 2359304 | tf_op jit(solution)/shard_map/ppermute | solution.py:1164
  464.5 10.2 %collective-permute-done.20 = bf16[192,2048]{1,0:T(8,128)(2,1)S(1)} collective-permute-done((bf16[192,2048]{1,0:T(8,128)(2,1)}, bf16[192,2048]{1,0:T(8,128)(2,1)S(1)}, u32[]{:S(2)}, u32[]{:S(2)}) %collective-permute-start.20) | collective-permute-done | bytes 786464 | tf_op jit(solution)/shard_map/ppermute | solution.py:85
  475.2 17.4 %collective-permute-done.18 = bf16[192,2048]{1,0:T(8,128)(2,1)} collective-permute-done((bf16[192,2048]{1,0:T(8,128)(2,1)}, bf16[192,2048]{1,0:T(8,128)(2,1)}, u32[]{:S(2)}, u32[]{:S(2)}) %collective-permute-start.18) | collective-permute-done | bytes 786464 | tf_op jit(solution)/shard_map/ppermute | solution.py:85
  497.1 3.9 split.1
  501.0 3.5 all-to-all-start.9
  504.7 7.6 %fusion.7 = (f32[1,192,2048]{2,1,0:T(8,128)}, bf16[1,192,2048]{2,1,0:T(8,128)(2,1)}) fusion(f32[192,2048]{1,0:T(8,128)} %copy-done.5, bf16[1,192,2048]{2,1,0:T(8,128)(2,1)} %param.18, f32[192]{0:T(256)S(1)} %broadcast_multiply_fusion, f32[192]{0:T(256)S(1)} %copy-done.32, f32[]{:T(128)} %fusion.32, f32[192]{0:T(256)S(1)} %copy-done.31, ...), kind=kLoop, calls=%fused_computation.15 | loop fusion | flops 10616832 | bytes 13371660 | tf_op jit(solution)/shard_map/broadcast_in_dim | solution.py:1199
  512.2 5.2 all-to-all-done.9.final_ref
  (190 shorter events, 72.2 us)
Async XLA Ops:
  7.2 116.7 %all-gather.12.cloned.1.call-start = ((), (), s32[]{:S(2)}) async-start(), calls=%async_computation.17 | async-start | bytes 13565952 | tf_op jit(solution)/shard_map/all_gather | solution.py:1049
  12.4 153.5 %all-gather.6.cloned.1.call-start = ((), (), s32[]{:S(2)}) async-start(), calls=%async_computation.12 | async-start | bytes 9437184 | tf_op jit(solution)/shard_map/all_gather | solution.py:1077
  16.4 133.2 %copy-start.1 = (bf16[192,2048]{1,0:T(8,128)(2,1)}, bf16[192,2048]{1,0:T(8,128)(2,1)S(1)}, u32[]{:S(2)}) copy-start(bf16[192,2048]{1,0:T(8,128)(2,1)S(1)} %get-tuple-element.77.refs_0_) | copy-start | bytes 2359300
  16.4 22.6 %collective-permute-start.3 = (bf16[192,2048]{1,0:T(8,128)(2,1)S(1)}, bf16[192,2048]{1,0:T(8,128)(2,1)S(1)}, u32[]{:S(2)}, u32[]{:S(2)}) collective-permute-start(bf16[192,2048]{1,0:T(8,128)(2,1)S(1)} %get-tuple-element.77.refs_0_), channel_id=1, source_target_pairs={{0,8},{8,16},{16,24},{24,0},{1,9},{9,17},{17,25},{25,1},{2,10},{10... | collective-permute-start | bytes 2359304 | tf_op jit(solution)/shard_map/ppermute | solution.py:89
  21.6 17.4 %copy-start.29 = (bf16[64,2048]{1,0:T(8,128)(2,1)S(1)}, bf16[64,2048]{1,0:T(8,128)(2,1)}, u32[]{:S(2)}) copy-start(bf16[64,2048]{1,0:T(8,128)(2,1)} %param.27) | copy-start | bytes 786436
  21.7 8.5 %collective-permute-start.2 = (bf16[80,768]{1,0:T(8,128)(2,1)S(1)}, bf16[80,768]{1,0:T(8,128)(2,1)S(1)}, u32[]{:S(2)}, u32[]{:S(2)}) collective-permute-start(bf16[80,768]{1,0:T(8,128)(2,1)S(1)} %get-tuple-element.162), channel_id=1, source_target_pairs={{0,6},{1,7},{2,4},{3,5},{4,2},{5,3},{6,0},{7,1},{8,14},{9,15},{10,... | collective-permute-start | bytes 368648 | tf_op jit(solution)/shard_map/ppermute | solution.py:85
  24.2 8.5 %collective-permute-start.1 = (bf16[80,768]{1,0:T(8,128)(2,1)S(1)}, bf16[80,768]{1,0:T(8,128)(2,1)S(1)}, u32[]{:S(2)}, u32[]{:S(2)}) collective-permute-start(bf16[80,768]{1,0:T(8,128)(2,1)S(1)} %get-tuple-element.161), channel_id=1, source_target_pairs={{0,4},{1,5},{2,6},{3,7},{4,0},{5,1},{6,2},{7,3},{8,12},{9,13},{10,... | collective-permute-start | bytes 368648 | tf_op jit(solution)/shard_map/ppermute | solution.py:85
  24.7 10.7 %collective-permute-start = (bf16[80,768]{1,0:T(8,128)(2,1)S(1)}, bf16[80,768]{1,0:T(8,128)(2,1)S(1)}, u32[]{:S(2)}, u32[]{:S(2)}) collective-permute-start(bf16[80,768]{1,0:T(8,128)(2,1)S(1)} %get-tuple-element.160), channel_id=1, source_target_pairs={{0,2},{1,3},{2,0},{3,1},{4,6},{5,7},{6,4},{7,5},{8,10},{9,11},{10,... | collective-permute-start | bytes 368648 | tf_op jit(solution)/shard_map/ppermute | solution.py:85
  39.0 28.7 %copy-start.8 = (bf16[192,2048]{1,0:T(8,128)(2,1)}, bf16[192,2048]{1,0:T(8,128)(2,1)S(1)}, u32[]{:S(2)}) copy-start(bf16[192,2048]{1,0:T(8,128)(2,1)S(1)} %collective-permute-done.3.refs_1_) | copy-start | bytes 2359300
  69.1 48.0 %all-to-all-start.1 = ((bf16[4,4,80,768]{3,2,1,0:T(8,128)(2,1)}), bf16[4,4,80,768]{3,2,1,0:T(8,128)(2,1)S(1)}, u32[]{:S(2)}, u32[]{:S(2)}) async-start(bf16[4,4,80,768]{3,2,1,0:T(8,128)(2,1)} %broadcast_in_dim.87), calls=%async_computation.1 | async-start | bytes 3932160 | tf_op jit(solution)/shard_map/all_to_all | solution.py:113
  72.7 152.2 %all-gather.8.cloned.1.call-start = ((), (), s32[]{:S(2)}) async-start(), calls=%async_computation.13 | async-start | bytes 12976128 | tf_op jit(solution)/shard_map/all_gather | solution.py:1078
  83.7 33.6 %copy-start.38 = (s32[1,4]{1,0:T(1,128)S(1)}, s32[1,4]{1,0:T(1,128)}, u32[]{:S(2)}) copy-start(s32[1,4]{1,0:T(1,128)} %param.22) | copy-start | bytes 52
  117.2 6.7 %collective-permute-start.4 = (bf16[4,4,80,768]{3,2,1,0:T(8,128)(2,1)S(1)}, bf16[4,4,80,768]{3,2,1,0:T(8,128)(2,1)}, u32[]{:S(2)}, u32[]{:S(2)}) collective-permute-start(bf16[4,4,80,768]{3,2,1,0:T(8,128)(2,1)S(1)} %all-to-all-done.1.refs_1_), channel_id=1, source_target_pairs={{0,1},{1,0},{2,3},{3,2},{4,5},{5,4},{6,7},{7,6},{8,9},{9,8},{10,11... | collective-permute-start | bytes 5898248 | tf_op jit(solution)/shard_map/ppermute | solution.py:85
  117.6 36.7 %collective-permute-start.5 = (bf16[192,2048]{1,0:T(8,128)(2,1)S(1)}, bf16[192,2048]{1,0:T(8,128)(2,1)}, u32[]{:S(2)}, u32[]{:S(2)}) collective-permute-start(bf16[192,2048]{1,0:T(8,128)(2,1)S(1)} %get-tuple-element.77.refs_0_), channel_id=1, source_target_pairs={{0,16},{8,24},{16,0},{24,8},{1,17},{9,25},{17,1},{25,9},{2,18},{10... | collective-permute-start | bytes 2359304 | tf_op jit(solution)/shard_map/ppermute | solution.py:89
  145.6 20.3 %copy-start = (bf16[1,192,2048]{2,1,0:T(8,128)(2,1)S(1)}, bf16[1,192,2048]{2,1,0:T(8,128)(2,1)}, u32[]{:S(2)}) copy-start(bf16[1,192,2048]{2,1,0:T(8,128)(2,1)} %param.17) | copy-start | bytes 2359300
  145.6 20.3 %all-to-all-start.2 = ((bf16[8,192,256]{2,1,0:T(8,128)(2,1)}), bf16[8,192,256]{2,1,0:T(8,128)(2,1)S(1)}, u32[]{:S(2)}, u32[]{:S(2)}) async-start(bf16[8,192,256]{2,1,0:T(8,128)(2,1)} %bitcast.96), calls=%async_computation.2 | async-start | bytes 1572864 | tf_op jit(solution)/shard_map/all_to_all | solution.py:1095
  149.5 241.7 %all-gather.10.cloned.1.call-start = ((), (), s32[]{:S(2)}) async-start(), calls=%async_computation.14 | async-start | bytes 7077888 | tf_op jit(solution)/shard_map/all_gather | solution.py:1105
  149.6 27.2 %collective-permute-start.6 = (bf16[192,2048]{1,0:T(8,128)(2,1)S(1)}, bf16[192,2048]{1,0:T(8,128)(2,1)}, u32[]{:S(2)}, u32[]{:S(2)}) collective-permute-start(bf16[192,2048]{1,0:T(8,128)(2,1)S(1)} %get-tuple-element.77.refs_0_), channel_id=1, source_target_pairs={{0,24},{8,0},{16,8},{24,16},{1,25},{9,1},{17,9},{25,17},{2,26},{10... | collective-permute-start | bytes 2359304 | tf_op jit(solution)/shard_map/ppermute | solution.py:89
  176.8 15.1 %collective-permute-start.7 = (bf16[96,2048]{1,0:T(8,128)(2,1)S(1)}, bf16[96,2048]{1,0:T(8,128)(2,1)S(1)}, u32[]{:S(2)}, u32[]{:S(2)}) collective-permute-start(bf16[96,2048]{1,0:T(8,128)(2,1)S(1)} %get-tuple-element.83.refs_4_), channel_id=1, source_target_pairs={{0,8},{8,16},{16,24},{1,9},{9,17},{17,25},{2,10},{10,18},{18,26},{... | collective-permute-start | bytes 1179656 | tf_op jit(solution)/shard_map/ppermute | solution.py:98
  183.3 12.7 %collective-permute-start.8 = (bf16[96,2048]{1,0:T(8,128)(2,1)S(1)}, bf16[96,2048]{1,0:T(8,128)(2,1)S(1)}, u32[]{:S(2)}, u32[]{:S(2)}) collective-permute-start(bf16[96,2048]{1,0:T(8,128)(2,1)S(1)} %get-tuple-element.83.refs_4_), channel_id=1, source_target_pairs={{8,0},{16,8},{24,16},{9,1},{17,9},{25,17},{10,2},{18,10},{26,18},{... | collective-permute-start | bytes 1179656 | tf_op jit(solution)/shard_map/ppermute | solution.py:98
  191.8 6.8 %collective-permute-start.9 = (bf16[96,2048]{1,0:T(8,128)(2,1)S(1)}, bf16[96,2048]{1,0:T(8,128)(2,1)S(1)}, u32[]{:S(2)}, u32[]{:S(2)}) collective-permute-start(bf16[96,2048]{1,0:T(8,128)(2,1)S(1)} %collective-permute-done.7.refs_5_), channel_id=1, source_target_pairs={{8,16},{16,24},{9,17},{17,25},{10,18},{18,26},{11,19},{19,27},{12,... | collective-permute-start | bytes 1179656 | tf_op jit(solution)/shard_map/ppermute | solution.py:105
  196.0 13.3 %collective-permute-start.10 = (bf16[96,2048]{1,0:T(8,128)(2,1)S(1)}, bf16[96,2048]{1,0:T(8,128)(2,1)S(1)}, u32[]{:S(2)}, u32[]{:S(2)}) collective-permute-start(bf16[96,2048]{1,0:T(8,128)(2,1)S(1)} %collective-permute-done.8.refs_6_), channel_id=1, source_target_pairs={{8,0},{16,8},{9,1},{17,9},{10,2},{18,10},{11,3},{19,11},{12,4},{20... | collective-permute-start | bytes 1179656 | tf_op jit(solution)/shard_map/ppermute | solution.py:106
  197.3 21.1 %collective-permute-start.11 = (bf16[96,2048]{1,0:T(8,128)(2,1)S(1)}, bf16[96,2048]{1,0:T(8,128)(2,1)S(1)}, u32[]{:S(2)}, u32[]{:S(2)}) collective-permute-start(bf16[96,2048]{1,0:T(8,128)(2,1)S(1)} %broadcast_select_fusion.1), channel_id=1, source_target_pairs={{16,0},{8,24},{17,1},{9,25},{18,2},{10,26},{19,3},{11,27},{20,4},{... | collective-permute-start | bytes 1179656 | tf_op jit(solution)/shard_map/ppermute | solution.py:107
  220.6 40.2 %all-to-all-start.3 = ((bf16[4,96,2048]{2,1,0:T(8,128)(2,1)}), bf16[4,96,2048]{2,1,0:T(8,128)(2,1)}, u32[]{:S(2)}, u32[]{:S(2)}) async-start(bf16[4,96,2048]{2,1,0:T(8,128)(2,1)} %broadcast_in_dim.93), calls=%async_computation.3 | async-start | bytes 3145728 | tf_op jit(solution)/shard_map/all_to_all | solution.py:113
  260.8 40.1 %all-to-all-start.4 = ((bf16[4,96,2048]{2,1,0:T(8,128)(2,1)}), bf16[4,96,2048]{2,1,0:T(8,128)(2,1)S(1)}, u32[]{:S(2)}, u32[]{:S(2)}) async-start(bf16[4,96,2048]{2,1,0:T(8,128)(2,1)} %get-tuple-element.96), calls=%async_computation.4 | async-start | bytes 3145728 | tf_op jit(solution)/shard_map/all_to_all | solution.py:117
  264.5 186.8 %reduce-scatter.5.cloned.1.call-start = ((), (), s32[]{:S(2)}) async-start(), calls=%async_computation.16 | async-start | bytes 6488064 | tf_op jit(solution)/shard_map/reduce_scatter | solution.py:1117
  310.6 19.1 %slice-start.1 = ((s8[4325376]{0:T(1024)(128)(4,1)}), s8[131072]{0:T(1024)(128)(4,1)S(1)}, s32[]{:S(2)}) async-start(s8[4325376]{0:T(1024)(128)(4,1)} %bitcast.91), calls=%async_computation.19 | async-start | bytes 262144
  310.7 41.4 %all-to-all-start.5 = ((bf16[4,96,2048]{2,1,0:T(8,128)(2,1)}), bf16[4,96,2048]{2,1,0:T(8,128)(2,1)}, u32[]{:S(2)}, u32[]{:S(2)}) async-start(bf16[4,96,2048]{2,1,0:T(8,128)(2,1)} %get-tuple-element.98), calls=%async_computation.5 | async-start | bytes 3145728 | tf_op jit(solution)/shard_map/all_to_all | solution.py:117
  315.6 14.2 %slice-start.2 = ((s8[4325376]{0:T(1024)(128)(4,1)}), s8[4194304]{0:T(1024)(128)(4,1)S(1)}, s32[]{:S(2)}) async-start(s8[4325376]{0:T(1024)(128)(4,1)} %bitcast.91), calls=%async_computation.20 | async-start | bytes 8388608
  315.6 14.2 %copy-start.23 = (bf16[768,2048]{1,0:T(8,128)(2,1)S(1)}, bf16[768,2048]{1,0:T(8,128)(2,1)}, u32[]{:S(2)}) copy-start(bf16[768,2048]{1,0:T(8,128)(2,1)} %get-tuple-element.99) | copy-start | bytes 9437188
  365.3 26.0 %all-to-all-start.6 = ((bf16[8,208,512]{2,1,0:T(8,128)(2,1)}), bf16[8,208,512]{2,1,0:T(8,128)(2,1)S(1)}, u32[]{:S(2)}, u32[]{:S(2)}) async-start(bf16[8,208,512]{2,1,0:T(8,128)(2,1)} %get-tuple-element.104), calls=%async_computation.6 | async-start | bytes 3407872 | tf_op jit(solution)/shard_map/all_to_all | solution.py:1123
  368.9 128.2 %reduce-scatter.3.cloned.1.call-start = ((), (), s32[]{:S(2)}) async-start(), calls=%async_computation.15 | async-start | bytes 12976128 | tf_op jit(solution)/shard_map/reduce_scatter | solution.py:1118
  372.6 49.9 %collective-permute-start.12 = (bf16[192,2048]{1,0:T(8,128)(2,1)}, bf16[192,2048]{1,0:T(8,128)(2,1)}, u32[]{:S(2)}, u32[]{:S(2)}) collective-permute-start(bf16[192,2048]{1,0:T(8,128)(2,1)} %get-tuple-element.110), channel_id=1, source_target_pairs={{0,8},{8,16},{1,9},{9,17},{2,10},{10,18},{3,11},{11,19},{4,12},{12... | collective-permute-start | bytes 2359304 | tf_op jit(solution)/shard_map/ppermute | solution.py:1128
  374.7 47.7 %collective-permute-start.13 = (bf16[192,2048]{1,0:T(8,128)(2,1)}, bf16[192,2048]{1,0:T(8,128)(2,1)}, u32[]{:S(2)}, u32[]{:S(2)}) collective-permute-start(bf16[192,2048]{1,0:T(8,128)(2,1)} %get-tuple-element.111), channel_id=1, source_target_pairs={{16,8},{24,16},{17,9},{25,17},{18,10},{26,18},{19,11},{27,19},{20,... | collective-permute-start | bytes 2359304 | tf_op jit(solution)/shard_map/ppermute | solution.py:1129
  376.3 46.2 %collective-permute-start.14 = (bf16[192,2048]{1,0:T(8,128)(2,1)}, bf16[192,2048]{1,0:T(8,128)(2,1)}, u32[]{:S(2)}, u32[]{:S(2)}) collective-permute-start(bf16[192,2048]{1,0:T(8,128)(2,1)} %get-tuple-element.112), channel_id=1, source_target_pairs={{24,8},{0,16},{25,9},{1,17},{26,10},{2,18},{27,11},{3,19},{28,12},... | collective-permute-start | bytes 2359304 | tf_op jit(solution)/shard_map/ppermute | solution.py:1130
  399.2 37.3 %all-to-all-start.7 = ((bf16[4,528,256]{2,1,0:T(8,128)(2,1)}), bf16[4,528,256]{2,1,0:T(8,128)(2,1)}, u32[]{:S(2)}, u32[]{:S(2)}) async-start(bf16[4,528,256]{2,1,0:T(8,128)(2,1)} %output_grad_term.1), calls=%async_computation.7 | async-start | bytes 2162688 | tf_op jit(solution)/shard_map/all_to_all | solution.py:117
  422.5 19.1 %collective-permute-start.15 = (bf16[4,192,2048]{2,1,0:T(8,128)(2,1)}, bf16[4,192,2048]{2,1,0:T(8,128)(2,1)}, u32[]{:S(2)}, u32[]{:S(2)}) collective-permute-start(bf16[4,192,2048]{2,1,0:T(8,128)(2,1)} %get-tuple-element.117), channel_id=1, source_target_pairs={{0,1},{1,0},{2,3},{3,2},{4,5},{5,4},{6,7},{7,6},{8,9},{9,8},{10,11... | collective-permute-start | bytes 9437192 | tf_op jit(solution)/shard_map/ppermute | solution.py:85
  432.9 2.0 collective-permute-start.21
  436.5 58.6 %all-to-all-start.8 = ((bf16[4,512,384]{2,1,0:T(8,128)(2,1)}), bf16[4,512,384]{2,1,0:T(8,128)(2,1)S(1)}, u32[]{:S(2)}, u32[]{:S(2)}) async-start(bf16[4,512,384]{2,1,0:T(8,128)(2,1)} %bitcast.29), calls=%async_computation.8 | async-start | bytes 3145728 | tf_op jit(solution)/shard_map/all_to_all | solution.py:117
  446.0 28.7 %collective-permute-start.20 = (bf16[192,2048]{1,0:T(8,128)(2,1)}, bf16[192,2048]{1,0:T(8,128)(2,1)S(1)}, u32[]{:S(2)}, u32[]{:S(2)}) collective-permute-start(bf16[192,2048]{1,0:T(8,128)(2,1)} %get-tuple-element.139), channel_id=1, source_target_pairs={{0,4},{1,5},{2,6},{3,7},{4,0},{5,1},{6,2},{7,3},{8,12},{9,13},{10,... | collective-permute-start | bytes 2359304 | tf_op jit(solution)/shard_map/ppermute | solution.py:85
  446.9 28.2 %collective-permute-start.19 = (bf16[192,2048]{1,0:T(8,128)(2,1)}, bf16[192,2048]{1,0:T(8,128)(2,1)}, u32[]{:S(2)}, u32[]{:S(2)}) collective-permute-start(bf16[192,2048]{1,0:T(8,128)(2,1)} %get-tuple-element.140), channel_id=1, source_target_pairs={{0,2},{1,3},{2,0},{3,1},{4,6},{5,7},{6,4},{7,5},{8,10},{9,11},{10,... | collective-permute-start | bytes 2359304 | tf_op jit(solution)/shard_map/ppermute | solution.py:85
  448.2 44.4 %collective-permute-start.18 = (bf16[192,2048]{1,0:T(8,128)(2,1)}, bf16[192,2048]{1,0:T(8,128)(2,1)}, u32[]{:S(2)}, u32[]{:S(2)}) collective-permute-start(bf16[192,2048]{1,0:T(8,128)(2,1)} %get-tuple-element.141), channel_id=1, source_target_pairs={{0,6},{1,7},{2,4},{3,5},{4,2},{5,3},{6,0},{7,1},{8,14},{9,15},{10,... | collective-permute-start | bytes 2359304 | tf_op jit(solution)/shard_map/ppermute | solution.py:85
  457.7 46.8 %collective-permute-start.17 = (bf16[192,2048]{1,0:T(8,128)(2,1)}, bf16[192,2048]{1,0:T(8,128)(2,1)}, u32[]{:S(2)}, u32[]{:S(2)}) collective-permute-start(bf16[192,2048]{1,0:T(8,128)(2,1)} %get-tuple-element.143), channel_id=1, source_target_pairs={{8,0},{16,8},{24,16},{9,1},{17,9},{25,17},{10,2},{18,10},{26,18},{... | collective-permute-start | bytes 2359304 | tf_op jit(solution)/shard_map/ppermute | solution.py:1165
  459.0 45.6 %collective-permute-start.16 = (bf16[192,2048]{1,0:T(8,128)(2,1)}, bf16[192,2048]{1,0:T(8,128)(2,1)}, u32[]{:S(2)}, u32[]{:S(2)}) collective-permute-start(bf16[192,2048]{1,0:T(8,128)(2,1)} %get-tuple-element.142), channel_id=1, source_target_pairs={{0,8},{8,16},{16,24},{1,9},{9,17},{17,25},{2,10},{10,18},{18,26},{... | collective-permute-start | bytes 2359304 | tf_op jit(solution)/shard_map/ppermute | solution.py:1164
  474.7 20.4 %copy-start.24 = (bf16[192,2048]{1,0:T(8,128)(2,1)}, bf16[192,2048]{1,0:T(8,128)(2,1)S(1)}, u32[]{:S(2)}) copy-start(bf16[192,2048]{1,0:T(8,128)(2,1)S(1)} %collective-permute-done.20) | copy-start | bytes 2359300
  501.0 16.4 %all-to-all-start.9 = ((bf16[8,80,640]{2,1,0:T(8,128)(2,1)}), bf16[8,80,640]{2,1,0:T(8,128)(2,1)S(1)}, u32[]{:S(2)}, u32[]{:S(2)}) async-start(bf16[8,80,640]{2,1,0:T(8,128)(2,1)} %fusion.18), calls=%async_computation.10 | async-start | bytes 1638400 | tf_op jit(solution)/shard_map/all_to_all | solution.py:1178
  504.6 12.8 %copy-start.7 = (bf16[64,2048]{1,0:T(8,128)(2,1)S(1)}, bf16[64,2048]{1,0:T(8,128)(2,1)}, u32[]{:S(2)}) copy-start(bf16[64,2048]{1,0:T(8,128)(2,1)} %qw_ref.1) | copy-start | bytes 786436
  504.6 12.8 %copy-start.11 = (bf16[64,512]{1,0:T(8,128)(2,1)S(1)}, bf16[64,512]{1,0:T(8,128)(2,1)}, u32[]{:S(2)}) copy-start(bf16[64,512]{1,0:T(8,128)(2,1)} %vw_ref.1) | copy-start | bytes 196612
  (32 other events, 111.7 us)
Sparse Core Ops, SparseCore 0:
  12.5 75.4 all-gather.11
  89.9 54.3 all-gather.5
  146.8 67.8 all-gather.7
  219.3 43.4 all-gather.9
  310.8 57.8 reduce-scatter.4
  373.3 95.0 reduce-scatter.2

commit v7 on v6

--- a/solution.py
+++ b/solution.py
@@ -886,7 +886,7 @@
                        packed_ref, grad_ref, branch_ref):
     tokens, width = grad_ref.shape
     half = tokens // 2
-    own = weight_ref.shape[0]
+    own = weight_ref.shape[0] // 2
     step = pl.program_id(0)
 
     @pl.when(step == 0)
@@ -909,9 +909,12 @@
             row == 0, gain_high, jnp.where(row == 1, gain_term - gain_high, 0.0)
         ).astype(bf16)
 
-    packed_ref[0, :tokens, :own] = dot_right_t(branch_ref[:tokens, :], weight_ref[...]).astype(bf16)
-    packed_ref[0, tokens:, :own] = jnp.zeros((16, own), bf16)
-    packed_ref[0, :, own:] = branch_ref[:, pl.ds(pl.multiple_of(step * own, own), own)]
+    grads = dot_right_t(branch_ref[:tokens, :], weight_ref[...]).astype(bf16)
+    for which in range(2):
+        packed_ref[which, :tokens, :own] = grads[:, which * own : (which + 1) * own]
+        packed_ref[which, tokens:, :own] = jnp.zeros((16, own), bf16)
+        at_col = pl.multiple_of((2 * step + which) * own, own)
+        packed_ref[which, :, own:] = branch_ref[:, pl.ds(at_col, own)]
 
 
 def middle_back(low, high, middle, inv, gain, direct, weight):
@@ -921,7 +924,7 @@
     rows = pl.BlockSpec((tokens, width), lambda i: (0, 0))
     return pl.pallas_call(
         middle_back_kernel,
-        grid=(8,),
+        grid=(4,),
         in_specs=[
             whole,
             whole,
@@ -929,9 +932,9 @@
             pl.BlockSpec((tokens, 1), lambda i: (0, 0)),
             pl.BlockSpec((1, width), lambda i: (0, 0)),
             rows,
-            pl.BlockSpec((own, width), lambda i: (i, 0)),
-        ],
-        out_specs=[pl.BlockSpec((1, tokens + 16, 2 * own), lambda i: (i, 0, 0)), rows],
+            pl.BlockSpec((2 * own, width), lambda i: (i, 0)),
+        ],
+        out_specs=[pl.BlockSpec((2, tokens + 16, 2 * own), lambda i: (i, 0, 0)), rows],
         out_shape=[
             jax.ShapeDtypeStruct((8, tokens + 16, 2 * own), bf16),
             jax.ShapeDtypeStruct((tokens, width), f32),
@@ -948,8 +951,10 @@
 def middle_kernel(parts_ref, weight_ref, rows_ref, gain_ref, attended_ref, branch_ref, middle_ref, inv_ref,
                   low_ref, high_ref, total_ref):
     step = pl.program_id(0)
-    term = dot_plain(parts_ref[0], weight_ref[...])
-    attended_ref[...] = parts_ref[0]
+    own = parts_ref.shape[2]
+    attended_ref[:, :own] = parts_ref[0]
+    attended_ref[:, own:] = parts_ref[1]
+    term = dot_plain(attended_ref[...], weight_ref[...])
 
     @pl.when(step == 0)
     def _():
@@ -980,15 +985,15 @@
     whole = pl.BlockSpec((tokens, width), lambda i: (0, 0))
     return pl.pallas_call(
         middle_kernel,
-        grid=(devices,),
+        grid=(devices // 2,),
         in_specs=[
-            pl.BlockSpec((1, tokens, own), lambda i: (i, 0, 0)),
-            pl.BlockSpec((own, width), lambda i: (i, 0)),
+            pl.BlockSpec((2, tokens, own), lambda i: (i, 0, 0)),
+            pl.BlockSpec((2 * own, width), lambda i: (i, 0)),
             whole,
             pl.BlockSpec((1, width), lambda i: (0, 0)),
         ],
         out_specs=[
-            pl.BlockSpec((tokens, own), lambda i: (0, i)),
+            pl.BlockSpec((tokens, 2 * own), lambda i: (0, i)),
             whole,
             whole,
             pl.BlockSpec((tokens, 1), lambda i: (0, 0)),
@@ -1175,7 +1180,7 @@
     gain_eight = jnp.pad(gain_eight[:, None, :], ((0, 0), (0, 15), (0, kept_cols + q_width - own_rows)))
     final = jnp.concatenate([both_plane.reshape(8, own_rows, kept_cols + q_width), gain_eight], 1)
     gate_grad, up_grad = split(both_grad)
-    final = lax.all_to_all(after(final, far, near_x, near_y, sent_up, sent_down, gate_grad), "fsdp", split_axis=0, concat_axis=0)
+    final = lax.all_to_all(after(final, far, near_x, near_y, sent_up, sent_down), "fsdp", split_axis=0, concat_axis=0)
     weighted_first = (
         chip_terms[3].astype(f32)
         + other[3].astype(f32)
@@ -1190,7 +1195,7 @@
 
     output = (rows + keep * (branch_attention + branch_feed)).astype(bf16)
 
-    final = after(final, branch_up1, branch_down1)
+    final = after(final, branch_up1, branch_down1, gate_grad)
     query_grad, key_grad, value_grad, output_sum, first_gain, second_gain = finish(
         final, gain_mine, query_weight, key_weight, value_weight
     )

time: 536 us -> 533 us (level)
  no operation moved by 1% of the time
where the time goes in v7:
time: 533 us; the launch traced here: 525 us
  waiting for transfers between devices  166 us (31%)
  Pallas kernels  147 us (28%)
  starting transfers between devices  74.3 us (14%)
  other arithmetic  38.4 us (7%)
  local copies, waits for them, and re-layouts  31.9 us (6%)
  blocking collectives  28.6 us (5%)
  matrix products  21.6 us (4%)
  between operations  16.6 us (3%)
    pallas_call x2, Pallas kernels, feed(): pl.pallas_call(functools.partial(feed_kernel, units, len(so_far), n_count...  56 us
    ppermute x9, waiting for transfers between devices, flip(): return lax.ppermute(block, 'fsdp', FLIP[bit])  49.5 us
    all_to_all x2, waiting for transfers between devices, gather_planes(): return lax.all_to_all(copies, 'dp', split_axis=0, concat_axis=0)  36.5 us
    all_to_all x1, blocking collectives, gather_planes(): return lax.all_to_all(copies, 'dp', split_axis=0, concat_axis=0)  28.6 us
    dot_general x2, matrix products, dot_left_t(): lax.dot_general(left, right, (((0,), (0,)), ((), ())), preferred_element_...  21.6 us
    pallas_call x1, Pallas kernels, back(): pl.pallas_call(functools.partial(back_kernel, tokens), in_specs=[SMEM] +...  19.6 us
    pallas_call x1, Pallas kernels, front(): pl.pallas_call(front_kernel, grid=(1,), in_specs=[SMEM, pl.BlockSpec((8,...  19.4 us
    all_to_all x4, starting transfers between devices, swap_planes(): return lax.all_to_all(whole, 'dp', split_axis=0, concat_axis=0)  18 us
  transfers between devices with their start and end apart: 37, of which 21 were waited for; matrix products, arithmetic and copies ran while one was open for 14% of the time, Pallas kernels for 28%

profile of v7, /device:TPU:0, one launch (start us, length us, event | category | flops | bytes accessed | tf_op | source)
XLA Modules:
  0.0 525.0 jit_solution(9345917601124804931)
XLA Ops:
  16.4 3.0 collective-permute-start.3
  25.3 4.9 collective-permute-done.2
  35.5 3.5 collective-permute-done.3.refs_1_
  39.1 28.6 %all_to_all.50 = bf16[4,64,2048]{2,1,0:T(8,128)(2,1)} all-to-all(bf16[4,64,2048]{2,1,0:T(8,128)(2,1)S(1)} %broadcast_in_dim.86), channel_id=1, replica_groups=mesh['dp'=4,'fsdp'=8] {'dp'}, dimensions={0} | all-to-all | bytes 2097152 | tf_op jit(solution)/shard_map/all_to_all | solution.py:113
  69.1 3.6 all-to-all-start.1
  78.8 4.9 copy.47
  83.7 4.5 reshape.125
  88.2 28.9 %all-to-all-done.1.refs_1_ = bf16[4,4,80,768]{3,2,1,0:T(8,128)(2,1)S(1)} async-done(((bf16[4,4,80,768]{3,2,1,0:T(8,128)(2,1)}), bf16[4,4,80,768]{3,2,1,0:T(8,128)(2,1)S(1)}, u32[]{:S(2)}, u32[]{:S(2)}) %all-to-all-start.1) | async-done | bytes 1966112 | tf_op jit(solution)/shard_map/all_to_all | solution.py:113
  117.6 6.2 %collective-permute-done.4.refs_2_ = bf16[4,4,80,768]{3,2,1,0:T(8,128)(2,1)} collective-permute-done((bf16[4,4,80,768]{3,2,1,0:T(8,128)(2,1)S(1)}, bf16[4,4,80,768]{3,2,1,0:T(8,128)(2,1)}, u32[]{:S(2)}, u32[]{:S(2)}) %collective-permute-start.4) | collective-permute-done | bytes 1966112 | tf_op jit(solution)/shard_map/ppermute | solution.py:85
  123.9 19.4 %front.1 = (bf16[1536,256]{1,0:T(8,128)(2,1)S(1)}, bf16[1536,128]{1,0:T(8,128)(2,1)S(1)}, bf16[1536,128]{1,0:T(8,128)(2,1)S(1)}, bf16[1536,256]{1,0:T(8,128)(2,1...) custom-call(s32[2]{0:T(128)S(1)} %pad_add_fusion.at_ref, ...), custom_call_target="tpu_custom_call" | custom-call | flops 5637144576 | bytes 10485760 | tf_op jit(solution)/shard_map/front/pallas_call | solution.py:541
  145.7 3.9 all-to-all-start.2
  150.2 4.1 collective-permute-done.5.refs_2_
  154.3 11.7 %all-to-all-done.2.parts_ref = bf16[8,192,256]{2,1,0:T(8,128)(2,1)S(1)} async-done(((bf16[8,192,256]{2,1,0:T(8,128)(2,1)}), bf16[8,192,256]{2,1,0:T(8,128)(2,1)S(1)}, u32[]{:S(2)}, u32[]{:S(2)}) %all-to-all-start.2) | async-done | bytes 786464 | tf_op jit(solution)/shard_map/all_to_all | solution.py:1100
  166.0 7.4 %middle_forward.1 = (bf16[192,2048]{1,0:T(8,128)(2,1)}, f32[192,2048]{1,0:T(8,128)S(1)}, f32[192,2048]{1,0:T(8,128)}, f32[192,1]{1,0:T(8,128)S(1)}, bf16[96,2048...) custom-call(bf16[8,192,256]{2,1,0:T(8,128)(2,1)S(1)} %all-to-all-done.2.parts_ref, bf16[2048,2048]{1,0:T(8,128)(2,1)} %bitcast.89, ...), custom_call_target="tpu_custom_call" | custom-call | flops 1610612736 | bytes 12582912 | tf_op jit(solution)/shard_map/middle_forward/pallas_call | solution.py:986
  174.6 6.4 %collective-permute-start.7 = (bf16[96,2048]{1,0:T(8,128)(2,1)S(1)}, bf16[96,2048]{1,0:T(8,128)(2,1)S(1)}, u32[]{:S(2)}, u32[]{:S(2)}) collective-permute-start(bf16[96,2048]{1,0:T(8,128)(2,1)S(1)} %get-tuple-element.83.refs_4_), channel_id=1, source_target_pairs={{0,8},{8,16},{16,24},{1,9},{9,17},{17,25},{2,10},{10,18},{18,26},{... | collective-permute-start | bytes 1179656 | tf_op jit(solution)/shard_map/ppermute | solution.py:98
  182.4 7.2 %collective-permute-done.7.refs_5_ = bf16[96,2048]{1,0:T(8,128)(2,1)S(1)} collective-permute-done((bf16[96,2048]{1,0:T(8,128)(2,1)S(1)}, bf16[96,2048]{1,0:T(8,128)(2,1)S(1)}, u32[]{:S(2)}, u32[]{:S(2)}) %collective-permute-start.7) | collective-permute-done | bytes 393248 | tf_op jit(solution)/shard_map/ppermute | solution.py:98
  190.3 3.5 collective-permute-done.8.refs_6_
  196.4 10.7 %collective-permute-done.10.refs_8_ = bf16[96,2048]{1,0:T(8,128)(2,1)S(1)} collective-permute-done((bf16[96,2048]{1,0:T(8,128)(2,1)S(1)}, bf16[96,2048]{1,0:T(8,128)(2,1)S(1)}, u32[]{:S(2)}, u32[]{:S(2)}) %collective-permute-start.10) | collective-permute-done | bytes 393248 | tf_op jit(solution)/shard_map/ppermute | solution.py:106
  207.1 9.1 %collective-permute-done.11.refs_9_ = bf16[96,2048]{1,0:T(8,128)(2,1)S(1)} collective-permute-done((bf16[96,2048]{1,0:T(8,128)(2,1)S(1)}, bf16[96,2048]{1,0:T(8,128)(2,1)S(1)}, u32[]{:S(2)}, u32[]{:S(2)}) %collective-permute-start.11) | collective-permute-done | bytes 393248 | tf_op jit(solution)/shard_map/ppermute | solution.py:107
  218.3 4.3 all-to-all-start.3
  222.7 28.3 %feed.2 = (bf16[768,2048]{1,0:T(8,128)(2,1)}, bf16[768,2048]{1,0:T(8,128)(2,1)}, bf16[768,1408]{1,0:T(8,128)(2,1)}, bf16[768,2816]{1,0:T(8,128)(2,1)}, bf16[4,96,2048]{2,1,0:T(8,128)(2,1)}) custom-call(s32[2]{0:T(128)S(1)} %pad_add_fusion.at_ref, bf16[192,2048]{1,0:T(8,128)(2,1)} %copy-done.1, bf16[192,2048]{1,0:T(8,128)(2,1)} %copy-done.8, ...), custom_call_target="tpu_custom_call" | custom-call | flops 11072962560 | bytes 28835840 | tf_op jit(solution)/shard_map/feed/pallas_call | solution.py:756
  250.9 7.6 %all-to-all-done.3.refs_4_ = bf16[4,96,2048]{2,1,0:T(8,128)(2,1)} async-done(((bf16[4,96,2048]{2,1,0:T(8,128)(2,1)}), bf16[4,96,2048]{2,1,0:T(8,128)(2,1)}, u32[]{:S(2)}, u32[]{:S(2)}) %all-to-all-start.3) | async-done | bytes 1572896 | tf_op jit(solution)/shard_map/all_to_all | solution.py:113
  258.5 3.8 all-to-all-start.4
  263.5 27.7 %feed.3 = (bf16[768,2048]{1,0:T(8,128)(2,1)}, bf16[768,2048]{1,0:T(8,128)(2,1)}, bf16[768,1408]{1,0:T(8,128)(2,1)}, bf16[768,2816]{1,0:T(8,128)(2,1)}, bf16[4,96,2048]{2,1,0:T(8,128)(2,1)}) custom-call(s32[2]{0:T(128)S(1)} %pad_add_fusion.at_ref, ...), custom_call_target="tpu_custom_call", output_to_operand_aliasing={{0}: (9, {}), {1}: (10, {}), {2}: (11, {}), {3}: (12, {})} | custom-call | flops 11072962560 | bytes 28835840 | tf_op jit(solution)/shard_map/feed/pallas_call | solution.py:756
  291.2 7.4 %all-to-all-done.4.low_ref = bf16[4,96,2048]{2,1,0:T(8,128)(2,1)S(1)} async-done(((bf16[4,96,2048]{2,1,0:T(8,128)(2,1)}), bf16[4,96,2048]{2,1,0:T(8,128)(2,1)S(1)}, u32[]{:S(2)}, u32[]{:S(2)}) %all-to-all-start.4) | async-done | bytes 1572896 | tf_op jit(solution)/shard_map/all_to_all | solution.py:117
  298.7 9.7 %convolution_convert_fusion.1 = bf16[1408,2048]{1,0:T(8,128)(2,1)} fusion(bf16[768,1408]{1,0:T(8,128)(2,1)} %get-tuple-element.135.hidden_ref, bf16[768,2048]{1,0:T(8,128)(2,1)} %get-tuple-element.136), kind=kOutput, calls=%fused_computation.1 | convolution fusion | flops 4432068608 | bytes 11075584 | tf_op jit(solution)/shard_map/dot_general | solution.py:33
  308.4 4.7 all-to-all-start.5
  313.1 14.1 %branch.1 = bf16[4,192,2048]{2,1,0:T(8,128)(2,1)} custom-call(bf16[768,1408]{1,0:T(8,128)(2,1)} %get-tuple-element.135.hidden_ref, bf16[1408,2048]{1,0:T(8,128)(2,1)} %get-tuple-element.86.refs_11_.refs_6_.down_ref), custom_call_target="tpu_custom_call" | custom-call | flops 1048576 | bytes 65536 | tf_op jit(solution)/shard_map/branch/pallas_call | solution.py:803
  327.2 11.9 %convolution_convert_fusion = bf16[2048,2816]{1,0:T(8,128)(2,1)} fusion(bf16[768,2048]{1,0:T(8,128)(2,1)S(1)} %copy-done.23, bf16[768,2816]{1,0:T(8,128)(2,1)S(1)} %bitcast.92), kind=kOutput, calls=%fused_computation | convolution fusion | flops 8864137216 | bytes 19005440 | tf_op jit(solution)/shard_map/dot_general | solution.py:33
  339.1 10.5 %all-to-all-done.5.high_ref = bf16[4,96,2048]{2,1,0:T(8,128)(2,1)} async-done(((bf16[4,96,2048]{2,1,0:T(8,128)(2,1)}), bf16[4,96,2048]{2,1,0:T(8,128)(2,1)}, u32[]{:S(2)}, u32[]{:S(2)}) %all-to-all-start.5) | async-done | bytes 1572896 | tf_op jit(solution)/shard_map/all_to_all | solution.py:117
  349.6 9.9 %middle_back.1 = (bf16[8,208,512]{2,1,0:T(8,128)(2,1)}, f32[192,2048]{1,0:T(8,128)S(1)}) custom-call(bf16[4,96,2048]{2,1,0:T(8,128)(2,1)S(1)} %all-to-all-done.4.low_ref, bf16[4,96,2048]{2,1,0:T(8,128)(2,1)} %all-to-all-done.5.high_ref, f32[192,2048]{1,0:T(8,128)} %get-tuple-element.102.middle_ref, f32[192,1]{1,0:T(8,128)S(1)} %get-tuple-element.103.inv_ref, ...), custom_call_target="tpu_custom_call" | custom-call | flops 1610612736 | bytes 12582912 | tf_op jit(solution)/shard_map/middle_back/pallas_call | solution.py:925
  360.6 3.8 all-to-all-start.6
  365.0 3.1 dynamic-slice_bitcast_fusion
  371.9 4.3 collective-permute-start.14
  376.2 10.7 %all-to-all-done.6.packed_ref = bf16[8,208,512]{2,1,0:T(8,128)(2,1)S(1)} async-done(((bf16[8,208,512]{2,1,0:T(8,128)(2,1)}), bf16[8,208,512]{2,1,0:T(8,128)(2,1)S(1)}, u32[]{:S(2)}, u32[]{:S(2)}) %all-to-all-start.6) | async-done | bytes 1703968 | tf_op jit(solution)/shard_map/all_to_all | solution.py:1128
  388.1 8.3 %output_grad_term.1 = bf16[4,528,256]{2,1,0:T(8,128)(2,1)} custom-call(s32[2]{0:T(128)S(1)} %pad_add_fusion.at_ref, bf16[8,208,512]{2,1,0:T(8,128)(2,1)} %copy-done.26, bf16[1536,2048]{1,0:T(8,128)(2,1)} %all-gather.10.cloned.1.call-done.attended_ref), custom_call_target="tpu_custom_call" | custom-call | flops 48318382080 | bytes 6291456 | tf_op jit(solution)/shard_map/output_grad_term/pallas_call | solution.py:680
  396.3 4.6 all-to-all-start.7
  401.0 19.6 %back.1 = (bf16[4,192,2048]{2,1,0:T(8,128)(2,1)}, bf16[4,192,2048]{2,1,0:T(8,128)(2,1)}, bf16[1536,512]{1,0:T(8,128)(2,1)}) custom-call(s32[2]{0:T(128)S(1)} %pad_add_fusion.at_ref, bf16[1536,256]{1,0:T(8,128)(2,1)S(1)} %copy-done.15, bf16[1536,128]{1,0:T(8,128)(2,1)S(1)} %copy-done.17, bf16[1536,128]{1,0:T(8,128)(2,1)S(1)} %copy-done.19, ...), custom_call_target="tpu_custom_call" | custom-call | flops 970595500032 | bytes 8388608 | tf_op jit(solution)/shard_map/back/pallas_call | solution.py:604
  422.4 7.5 %project_grad.1 = bf16[2048,512]{1,0:T(8,128)(2,1)} custom-call(bf16[8,368,2048]{2,1,0:T(8,128)(2,1)} %bitcast.88, bf16[1536,512]{1,0:T(8,128)(2,1)S(1)} %copy-done.20), custom_call_target="tpu_custom_call" | custom-call | flops 32212254720 | bytes 6291456 | tf_op jit(solution)/shard_map/project_grad/pallas_call | solution.py:638
  434.8 5.0 all-to-all-start.8
  439.8 4.5 fusion.21
  452.0 4.1 fusion.12
  457.3 5.6 %collective-permute-start.16 = (bf16[192,2048]{1,0:T(8,128)(2,1)}, bf16[192,2048]{1,0:T(8,128)(2,1)}, u32[]{:S(2)}, u32[]{:S(2)}) collective-permute-start(bf16[192,2048]{1,0:T(8,128)(2,1)} %get-tuple-element.142), channel_id=1, source_target_pairs={{0,8},{8,16},{16,24},{1,9},{9,17},{17,25},{2,10},{10,18},{18,26},{... | collective-permute-start | bytes 2359304 | tf_op jit(solution)/shard_map/ppermute | solution.py:1169
  462.9 13.6 %collective-permute-done.20 = bf16[192,2048]{1,0:T(8,128)(2,1)S(1)} collective-permute-done((bf16[192,2048]{1,0:T(8,128)(2,1)}, bf16[192,2048]{1,0:T(8,128)(2,1)S(1)}, u32[]{:S(2)}, u32[]{:S(2)}) %collective-permute-start.20) | collective-permute-done | bytes 786464 | tf_op jit(solution)/shard_map/ppermute | solution.py:85
  477.0 17.3 %collective-permute-done.18 = bf16[192,2048]{1,0:T(8,128)(2,1)} collective-permute-done((bf16[192,2048]{1,0:T(8,128)(2,1)}, bf16[192,2048]{1,0:T(8,128)(2,1)}, u32[]{:S(2)}, u32[]{:S(2)}) %collective-permute-start.18) | collective-permute-done | bytes 786464 | tf_op jit(solution)/shard_map/ppermute | solution.py:85
  498.9 3.5 all-to-all-start.9
  502.6 7.6 %fusion.7 = (f32[1,192,2048]{2,1,0:T(8,128)}, bf16[1,192,2048]{2,1,0:T(8,128)(2,1)}) fusion(f32[192,2048]{1,0:T(8,128)} %copy-done.5, bf16[1,192,2048]{2,1,0:T(8,128)(2,1)} %param.18, f32[192]{0:T(256)S(1)} %broadcast_multiply_fusion, f32[192]{0:T(256)S(1)} %copy-done.32, f32[]{:T(128)} %fusion.32, f32[192]{0:T(256)S(1)} %copy-done.31, ...), kind=kLoop, calls=%fused_computation.15 | loop fusion | flops 10616832 | bytes 13371660 | tf_op jit(solution)/shard_map/broadcast_in_dim | solution.py:1204
  510.1 3.8 split.1
  (190 shorter events, 70.1 us)
Async XLA Ops:
  7.2 116.7 %all-gather.12.cloned.1.call-start = ((), (), s32[]{:S(2)}) async-start(), calls=%async_computation.17 | async-start | bytes 13565952 | tf_op jit(solution)/shard_map/all_gather | solution.py:1054
  12.4 153.6 %all-gather.6.cloned.1.call-start = ((), (), s32[]{:S(2)}) async-start(), calls=%async_computation.12 | async-start | bytes 9437184 | tf_op jit(solution)/shard_map/all_gather | solution.py:1082
  16.4 133.2 %copy-start.1 = (bf16[192,2048]{1,0:T(8,128)(2,1)}, bf16[192,2048]{1,0:T(8,128)(2,1)S(1)}, u32[]{:S(2)}) copy-start(bf16[192,2048]{1,0:T(8,128)(2,1)S(1)} %get-tuple-element.77.refs_0_) | copy-start | bytes 2359300
  16.4 22.6 %collective-permute-start.3 = (bf16[192,2048]{1,0:T(8,128)(2,1)S(1)}, bf16[192,2048]{1,0:T(8,128)(2,1)S(1)}, u32[]{:S(2)}, u32[]{:S(2)}) collective-permute-start(bf16[192,2048]{1,0:T(8,128)(2,1)S(1)} %get-tuple-element.77.refs_0_), channel_id=1, source_target_pairs={{0,8},{8,16},{16,24},{24,0},{1,9},{9,17},{17,25},{25,1},{2,10},{10... | collective-permute-start | bytes 2359304 | tf_op jit(solution)/shard_map/ppermute | solution.py:89
  21.6 17.4 %copy-start.29 = (bf16[64,2048]{1,0:T(8,128)(2,1)S(1)}, bf16[64,2048]{1,0:T(8,128)(2,1)}, u32[]{:S(2)}) copy-start(bf16[64,2048]{1,0:T(8,128)(2,1)} %param.27) | copy-start | bytes 786436
  21.7 8.5 %collective-permute-start.2 = (bf16[80,768]{1,0:T(8,128)(2,1)S(1)}, bf16[80,768]{1,0:T(8,128)(2,1)S(1)}, u32[]{:S(2)}, u32[]{:S(2)}) collective-permute-start(bf16[80,768]{1,0:T(8,128)(2,1)S(1)} %get-tuple-element.162), channel_id=1, source_target_pairs={{0,6},{1,7},{2,4},{3,5},{4,2},{5,3},{6,0},{7,1},{8,14},{9,15},{10,... | collective-permute-start | bytes 368648 | tf_op jit(solution)/shard_map/ppermute | solution.py:85
  24.2 8.5 %collective-permute-start.1 = (bf16[80,768]{1,0:T(8,128)(2,1)S(1)}, bf16[80,768]{1,0:T(8,128)(2,1)S(1)}, u32[]{:S(2)}, u32[]{:S(2)}) collective-permute-start(bf16[80,768]{1,0:T(8,128)(2,1)S(1)} %get-tuple-element.161), channel_id=1, source_target_pairs={{0,4},{1,5},{2,6},{3,7},{4,0},{5,1},{6,2},{7,3},{8,12},{9,13},{10,... | collective-permute-start | bytes 368648 | tf_op jit(solution)/shard_map/ppermute | solution.py:85
  24.7 10.7 %collective-permute-start = (bf16[80,768]{1,0:T(8,128)(2,1)S(1)}, bf16[80,768]{1,0:T(8,128)(2,1)S(1)}, u32[]{:S(2)}, u32[]{:S(2)}) collective-permute-start(bf16[80,768]{1,0:T(8,128)(2,1)S(1)} %get-tuple-element.160), channel_id=1, source_target_pairs={{0,2},{1,3},{2,0},{3,1},{4,6},{5,7},{6,4},{7,5},{8,10},{9,11},{10,... | collective-permute-start | bytes 368648 | tf_op jit(solution)/shard_map/ppermute | solution.py:85
  39.0 28.7 %copy-start.8 = (bf16[192,2048]{1,0:T(8,128)(2,1)}, bf16[192,2048]{1,0:T(8,128)(2,1)S(1)}, u32[]{:S(2)}) copy-start(bf16[192,2048]{1,0:T(8,128)(2,1)S(1)} %collective-permute-done.3.refs_1_) | copy-start | bytes 2359300
  69.1 48.0 %all-to-all-start.1 = ((bf16[4,4,80,768]{3,2,1,0:T(8,128)(2,1)}), bf16[4,4,80,768]{3,2,1,0:T(8,128)(2,1)S(1)}, u32[]{:S(2)}, u32[]{:S(2)}) async-start(bf16[4,4,80,768]{3,2,1,0:T(8,128)(2,1)} %broadcast_in_dim.87), calls=%async_computation.1 | async-start | bytes 3932160 | tf_op jit(solution)/shard_map/all_to_all | solution.py:113
  72.7 149.9 %all-gather.8.cloned.1.call-start = ((), (), s32[]{:S(2)}) async-start(), calls=%async_computation.13 | async-start | bytes 12976128 | tf_op jit(solution)/shard_map/all_gather | solution.py:1083
  83.7 33.6 %copy-start.38 = (s32[1,4]{1,0:T(1,128)S(1)}, s32[1,4]{1,0:T(1,128)}, u32[]{:S(2)}) copy-start(s32[1,4]{1,0:T(1,128)} %param.22) | copy-start | bytes 52
  117.2 6.7 %collective-permute-start.4 = (bf16[4,4,80,768]{3,2,1,0:T(8,128)(2,1)S(1)}, bf16[4,4,80,768]{3,2,1,0:T(8,128)(2,1)}, u32[]{:S(2)}, u32[]{:S(2)}) collective-permute-start(bf16[4,4,80,768]{3,2,1,0:T(8,128)(2,1)S(1)} %all-to-all-done.1.refs_1_), channel_id=1, source_target_pairs={{0,1},{1,0},{2,3},{3,2},{4,5},{5,4},{6,7},{7,6},{8,9},{9,8},{10,11... | collective-permute-start | bytes 5898248 | tf_op jit(solution)/shard_map/ppermute | solution.py:85
  117.6 36.7 %collective-permute-start.5 = (bf16[192,2048]{1,0:T(8,128)(2,1)S(1)}, bf16[192,2048]{1,0:T(8,128)(2,1)}, u32[]{:S(2)}, u32[]{:S(2)}) collective-permute-start(bf16[192,2048]{1,0:T(8,128)(2,1)S(1)} %get-tuple-element.77.refs_0_), channel_id=1, source_target_pairs={{0,16},{8,24},{16,0},{24,8},{1,17},{9,25},{17,1},{25,9},{2,18},{10... | collective-permute-start | bytes 2359304 | tf_op jit(solution)/shard_map/ppermute | solution.py:89
  145.7 20.4 %copy-start = (bf16[1,192,2048]{2,1,0:T(8,128)(2,1)S(1)}, bf16[1,192,2048]{2,1,0:T(8,128)(2,1)}, u32[]{:S(2)}) copy-start(bf16[1,192,2048]{2,1,0:T(8,128)(2,1)} %param.17) | copy-start | bytes 2359300
  145.7 20.3 %all-to-all-start.2 = ((bf16[8,192,256]{2,1,0:T(8,128)(2,1)}), bf16[8,192,256]{2,1,0:T(8,128)(2,1)S(1)}, u32[]{:S(2)}, u32[]{:S(2)}) async-start(bf16[8,192,256]{2,1,0:T(8,128)(2,1)} %bitcast.96), calls=%async_computation.2 | async-start | bytes 1572864 | tf_op jit(solution)/shard_map/all_to_all | solution.py:1100
  149.6 237.3 %all-gather.10.cloned.1.call-start = ((), (), s32[]{:S(2)}) async-start(), calls=%async_computation.14 | async-start | bytes 7077888 | tf_op jit(solution)/shard_map/all_gather | solution.py:1110
  149.6 25.0 %collective-permute-start.6 = (bf16[192,2048]{1,0:T(8,128)(2,1)S(1)}, bf16[192,2048]{1,0:T(8,128)(2,1)}, u32[]{:S(2)}, u32[]{:S(2)}) collective-permute-start(bf16[192,2048]{1,0:T(8,128)(2,1)S(1)} %get-tuple-element.77.refs_0_), channel_id=1, source_target_pairs={{0,24},{8,0},{16,8},{24,16},{1,25},{9,1},{17,9},{25,17},{2,26},{10... | collective-permute-start | bytes 2359304 | tf_op jit(solution)/shard_map/ppermute | solution.py:89
  174.6 15.0 %collective-permute-start.7 = (bf16[96,2048]{1,0:T(8,128)(2,1)S(1)}, bf16[96,2048]{1,0:T(8,128)(2,1)S(1)}, u32[]{:S(2)}, u32[]{:S(2)}) collective-permute-start(bf16[96,2048]{1,0:T(8,128)(2,1)S(1)} %get-tuple-element.83.refs_4_), channel_id=1, source_target_pairs={{0,8},{8,16},{16,24},{1,9},{9,17},{17,25},{2,10},{10,18},{18,26},{... | collective-permute-start | bytes 1179656 | tf_op jit(solution)/shard_map/ppermute | solution.py:98
  181.1 12.7 %collective-permute-start.8 = (bf16[96,2048]{1,0:T(8,128)(2,1)S(1)}, bf16[96,2048]{1,0:T(8,128)(2,1)S(1)}, u32[]{:S(2)}, u32[]{:S(2)}) collective-permute-start(bf16[96,2048]{1,0:T(8,128)(2,1)S(1)} %get-tuple-element.83.refs_4_), channel_id=1, source_target_pairs={{8,0},{16,8},{24,16},{9,1},{17,9},{25,17},{10,2},{18,10},{26,18},{... | collective-permute-start | bytes 1179656 | tf_op jit(solution)/shard_map/ppermute | solution.py:98
  189.6 6.8 %collective-permute-start.9 = (bf16[96,2048]{1,0:T(8,128)(2,1)S(1)}, bf16[96,2048]{1,0:T(8,128)(2,1)S(1)}, u32[]{:S(2)}, u32[]{:S(2)}) collective-permute-start(bf16[96,2048]{1,0:T(8,128)(2,1)S(1)} %collective-permute-done.7.refs_5_), channel_id=1, source_target_pairs={{8,16},{16,24},{9,17},{17,25},{10,18},{18,26},{11,19},{19,27},{12,... | collective-permute-start | bytes 1179656 | tf_op jit(solution)/shard_map/ppermute | solution.py:105
  193.7 13.3 %collective-permute-start.10 = (bf16[96,2048]{1,0:T(8,128)(2,1)S(1)}, bf16[96,2048]{1,0:T(8,128)(2,1)S(1)}, u32[]{:S(2)}, u32[]{:S(2)}) collective-permute-start(bf16[96,2048]{1,0:T(8,128)(2,1)S(1)} %collective-permute-done.8.refs_6_), channel_id=1, source_target_pairs={{8,0},{16,8},{9,1},{17,9},{10,2},{18,10},{11,3},{19,11},{12,4},{20... | collective-permute-start | bytes 1179656 | tf_op jit(solution)/shard_map/ppermute | solution.py:106
  195.1 21.1 %collective-permute-start.11 = (bf16[96,2048]{1,0:T(8,128)(2,1)S(1)}, bf16[96,2048]{1,0:T(8,128)(2,1)S(1)}, u32[]{:S(2)}, u32[]{:S(2)}) collective-permute-start(bf16[96,2048]{1,0:T(8,128)(2,1)S(1)} %broadcast_select_fusion.1), channel_id=1, source_target_pairs={{16,0},{8,24},{17,1},{9,25},{18,2},{10,26},{19,3},{11,27},{20,4},{... | collective-permute-start | bytes 1179656 | tf_op jit(solution)/shard_map/ppermute | solution.py:107
  218.3 40.2 %all-to-all-start.3 = ((bf16[4,96,2048]{2,1,0:T(8,128)(2,1)}), bf16[4,96,2048]{2,1,0:T(8,128)(2,1)}, u32[]{:S(2)}, u32[]{:S(2)}) async-start(bf16[4,96,2048]{2,1,0:T(8,128)(2,1)} %broadcast_in_dim.93), calls=%async_computation.3 | async-start | bytes 3145728 | tf_op jit(solution)/shard_map/all_to_all | solution.py:113
  258.5 40.1 %all-to-all-start.4 = ((bf16[4,96,2048]{2,1,0:T(8,128)(2,1)}), bf16[4,96,2048]{2,1,0:T(8,128)(2,1)S(1)}, u32[]{:S(2)}, u32[]{:S(2)}) async-start(bf16[4,96,2048]{2,1,0:T(8,128)(2,1)} %get-tuple-element.96), calls=%async_computation.4 | async-start | bytes 3145728 | tf_op jit(solution)/shard_map/all_to_all | solution.py:117
  262.3 187.3 %reduce-scatter.5.cloned.1.call-start = ((), (), s32[]{:S(2)}) async-start(), calls=%async_computation.16 | async-start | bytes 6488064 | tf_op jit(solution)/shard_map/reduce_scatter | solution.py:1122
  308.4 18.8 %slice-start.1 = ((s8[4325376]{0:T(1024)(128)(4,1)}), s8[131072]{0:T(1024)(128)(4,1)S(1)}, s32[]{:S(2)}) async-start(s8[4325376]{0:T(1024)(128)(4,1)} %bitcast.91), calls=%async_computation.19 | async-start | bytes 262144
  308.4 41.2 %all-to-all-start.5 = ((bf16[4,96,2048]{2,1,0:T(8,128)(2,1)}), bf16[4,96,2048]{2,1,0:T(8,128)(2,1)}, u32[]{:S(2)}, u32[]{:S(2)}) async-start(bf16[4,96,2048]{2,1,0:T(8,128)(2,1)} %get-tuple-element.98), calls=%async_computation.5 | async-start | bytes 3145728 | tf_op jit(solution)/shard_map/all_to_all | solution.py:117
  313.1 14.1 %slice-start.2 = ((s8[4325376]{0:T(1024)(128)(4,1)}), s8[4194304]{0:T(1024)(128)(4,1)S(1)}, s32[]{:S(2)}) async-start(s8[4325376]{0:T(1024)(128)(4,1)} %bitcast.91), calls=%async_computation.20 | async-start | bytes 8388608
  313.1 14.1 %copy-start.23 = (bf16[768,2048]{1,0:T(8,128)(2,1)S(1)}, bf16[768,2048]{1,0:T(8,128)(2,1)}, u32[]{:S(2)}) copy-start(bf16[768,2048]{1,0:T(8,128)(2,1)} %get-tuple-element.99) | copy-start | bytes 9437188
  360.6 26.2 %all-to-all-start.6 = ((bf16[8,208,512]{2,1,0:T(8,128)(2,1)}), bf16[8,208,512]{2,1,0:T(8,128)(2,1)S(1)}, u32[]{:S(2)}, u32[]{:S(2)}) async-start(bf16[8,208,512]{2,1,0:T(8,128)(2,1)} %get-tuple-element.104), calls=%async_computation.6 | async-start | bytes 3407872 | tf_op jit(solution)/shard_map/all_to_all | solution.py:1128
  364.5 145.7 %reduce-scatter.3.cloned.1.call-start = ((), (), s32[]{:S(2)}) async-start(), calls=%async_computation.15 | async-start | bytes 12976128 | tf_op jit(solution)/shard_map/reduce_scatter | solution.py:1123
  368.2 52.5 %collective-permute-start.12 = (bf16[192,2048]{1,0:T(8,128)(2,1)}, bf16[192,2048]{1,0:T(8,128)(2,1)}, u32[]{:S(2)}, u32[]{:S(2)}) collective-permute-start(bf16[192,2048]{1,0:T(8,128)(2,1)} %get-tuple-element.110), channel_id=1, source_target_pairs={{0,8},{8,16},{1,9},{9,17},{2,10},{10,18},{3,11},{11,19},{4,12},{12... | collective-permute-start | bytes 2359304 | tf_op jit(solution)/shard_map/ppermute | solution.py:1133
  370.3 50.3 %collective-permute-start.13 = (bf16[192,2048]{1,0:T(8,128)(2,1)}, bf16[192,2048]{1,0:T(8,128)(2,1)}, u32[]{:S(2)}, u32[]{:S(2)}) collective-permute-start(bf16[192,2048]{1,0:T(8,128)(2,1)} %get-tuple-element.111), channel_id=1, source_target_pairs={{16,8},{24,16},{17,9},{25,17},{18,10},{26,18},{19,11},{27,19},{20,... | collective-permute-start | bytes 2359304 | tf_op jit(solution)/shard_map/ppermute | solution.py:1134
  371.9 48.7 %collective-permute-start.14 = (bf16[192,2048]{1,0:T(8,128)(2,1)}, bf16[192,2048]{1,0:T(8,128)(2,1)}, u32[]{:S(2)}, u32[]{:S(2)}) collective-permute-start(bf16[192,2048]{1,0:T(8,128)(2,1)} %get-tuple-element.112), channel_id=1, source_target_pairs={{24,8},{0,16},{25,9},{1,17},{26,10},{2,18},{27,11},{3,19},{28,12},... | collective-permute-start | bytes 2359304 | tf_op jit(solution)/shard_map/ppermute | solution.py:1135
  396.3 38.5 %all-to-all-start.7 = ((bf16[4,528,256]{2,1,0:T(8,128)(2,1)}), bf16[4,528,256]{2,1,0:T(8,128)(2,1)}, u32[]{:S(2)}, u32[]{:S(2)}) async-start(bf16[4,528,256]{2,1,0:T(8,128)(2,1)} %output_grad_term.1), calls=%async_computation.7 | async-start | bytes 2162688 | tf_op jit(solution)/shard_map/all_to_all | solution.py:117
  420.6 19.2 %collective-permute-start.15 = (bf16[4,192,2048]{2,1,0:T(8,128)(2,1)}, bf16[4,192,2048]{2,1,0:T(8,128)(2,1)}, u32[]{:S(2)}, u32[]{:S(2)}) collective-permute-start(bf16[4,192,2048]{2,1,0:T(8,128)(2,1)} %get-tuple-element.117), channel_id=1, source_target_pairs={{0,1},{1,0},{2,3},{3,2},{4,5},{5,4},{6,7},{7,6},{8,9},{9,8},{10,11... | collective-permute-start | bytes 9437192 | tf_op jit(solution)/shard_map/ppermute | solution.py:85
  431.3 2.0 collective-permute-start.21
  434.8 62.1 %all-to-all-start.8 = ((bf16[4,512,384]{2,1,0:T(8,128)(2,1)}), bf16[4,512,384]{2,1,0:T(8,128)(2,1)S(1)}, u32[]{:S(2)}, u32[]{:S(2)}) async-start(bf16[4,512,384]{2,1,0:T(8,128)(2,1)} %bitcast.29), calls=%async_computation.8 | async-start | bytes 3145728 | tf_op jit(solution)/shard_map/all_to_all | solution.py:117
  444.3 32.2 %collective-permute-start.20 = (bf16[192,2048]{1,0:T(8,128)(2,1)}, bf16[192,2048]{1,0:T(8,128)(2,1)S(1)}, u32[]{:S(2)}, u32[]{:S(2)}) collective-permute-start(bf16[192,2048]{1,0:T(8,128)(2,1)} %get-tuple-element.139), channel_id=1, source_target_pairs={{0,4},{1,5},{2,6},{3,7},{4,0},{5,1},{6,2},{7,3},{8,12},{9,13},{10,... | collective-permute-start | bytes 2359304 | tf_op jit(solution)/shard_map/ppermute | solution.py:85
  445.2 31.8 %collective-permute-start.19 = (bf16[192,2048]{1,0:T(8,128)(2,1)}, bf16[192,2048]{1,0:T(8,128)(2,1)}, u32[]{:S(2)}, u32[]{:S(2)}) collective-permute-start(bf16[192,2048]{1,0:T(8,128)(2,1)} %get-tuple-element.140), channel_id=1, source_target_pairs={{0,2},{1,3},{2,0},{3,1},{4,6},{5,7},{6,4},{7,5},{8,10},{9,11},{10,... | collective-permute-start | bytes 2359304 | tf_op jit(solution)/shard_map/ppermute | solution.py:85
  445.3 49.0 %collective-permute-start.18 = (bf16[192,2048]{1,0:T(8,128)(2,1)}, bf16[192,2048]{1,0:T(8,128)(2,1)}, u32[]{:S(2)}, u32[]{:S(2)}) collective-permute-start(bf16[192,2048]{1,0:T(8,128)(2,1)} %get-tuple-element.141), channel_id=1, source_target_pairs={{0,6},{1,7},{2,4},{3,5},{4,2},{5,3},{6,0},{7,1},{8,14},{9,15},{10,... | collective-permute-start | bytes 2359304 | tf_op jit(solution)/shard_map/ppermute | solution.py:85
  456.1 46.4 %collective-permute-start.17 = (bf16[192,2048]{1,0:T(8,128)(2,1)}, bf16[192,2048]{1,0:T(8,128)(2,1)}, u32[]{:S(2)}, u32[]{:S(2)}) collective-permute-start(bf16[192,2048]{1,0:T(8,128)(2,1)} %get-tuple-element.143), channel_id=1, source_target_pairs={{8,0},{16,8},{24,16},{9,1},{17,9},{25,17},{10,2},{18,10},{26,18},{... | collective-permute-start | bytes 2359304 | tf_op jit(solution)/shard_map/ppermute | solution.py:1170
  457.3 45.2 %collective-permute-start.16 = (bf16[192,2048]{1,0:T(8,128)(2,1)}, bf16[192,2048]{1,0:T(8,128)(2,1)}, u32[]{:S(2)}, u32[]{:S(2)}) collective-permute-start(bf16[192,2048]{1,0:T(8,128)(2,1)} %get-tuple-element.142), channel_id=1, source_target_pairs={{0,8},{8,16},{16,24},{1,9},{9,17},{17,25},{2,10},{10,18},{18,26},{... | collective-permute-start | bytes 2359304 | tf_op jit(solution)/shard_map/ppermute | solution.py:1169
  476.5 20.4 %copy-start.24 = (bf16[192,2048]{1,0:T(8,128)(2,1)}, bf16[192,2048]{1,0:T(8,128)(2,1)S(1)}, u32[]{:S(2)}) copy-start(bf16[192,2048]{1,0:T(8,128)(2,1)S(1)} %collective-permute-done.20) | copy-start | bytes 2359300
  498.9 16.4 %all-to-all-start.9 = ((bf16[8,80,640]{2,1,0:T(8,128)(2,1)}), bf16[8,80,640]{2,1,0:T(8,128)(2,1)S(1)}, u32[]{:S(2)}, u32[]{:S(2)}) async-start(bf16[8,80,640]{2,1,0:T(8,128)(2,1)} %fusion.18), calls=%async_computation.9 | async-start | bytes 1638400 | tf_op jit(solution)/shard_map/all_to_all | solution.py:1183
  502.5 12.8 %copy-start.11 = (bf16[64,512]{1,0:T(8,128)(2,1)S(1)}, bf16[64,512]{1,0:T(8,128)(2,1)}, u32[]{:S(2)}) copy-start(bf16[64,512]{1,0:T(8,128)(2,1)} %vw_ref.1) | copy-start | bytes 196612
  502.5 12.8 %copy-start.13 = (bf16[64,512]{1,0:T(8,128)(2,1)S(1)}, bf16[64,512]{1,0:T(8,128)(2,1)}, u32[]{:S(2)}) copy-start(bf16[64,512]{1,0:T(8,128)(2,1)} %kw_ref.1) | copy-start | bytes 196612
  (32 other events, 107.8 us)
Sparse Core Ops, SparseCore 0:
  12.5 75.4 all-gather.11
  89.9 54.3 all-gather.5
  146.8 67.9 all-gather.7
  217.0 44.9 all-gather.9
  308.5 57.9 reduce-scatter.4
  370.2 103.5 reduce-scatter.2
